TPU v7x, 32 devices: a whole 2x2x4 slice. The times are simulated.
32 devices in a mesh: dom: 8 (over z, x), edge: 4 (over y, core).
Axes of the slice: x: 2, y: 2, z: 4, core: 2. Of those that a mesh axis runs over, the one named last changes fastest.
Arguments:
- node_feats: bfloat16 [4096, 1024], P(('dom', 'edge')), may hold values from -6 to 6
- gat_weight: bfloat16 [1024, 1024], P('edge'), may hold values from -0.1875 to 0.1875
- attn_src: float32 [8, 128], replicated
- attn_dst: float32 [8, 128], replicated
- neighbours: int32 [4096, 16], P(('dom', 'edge')), may hold values from 0 to 383
- degree: int32 [4096], P(('dom', 'edge')), may hold values from 0 to 16
- halo_rows: int32 [8, 4, 8, 32], P('dom', 'edge'), may hold values from 0 to 127
- halo_count: int32 [8, 4, 8], P('dom', 'edge'), may hold values from 1 to 32, as said below
- endpoint_rows: int32 [8, 4, 8, 4, 2], P('dom', 'edge'), may hold values from 0 to 127
- cand_ends: int32 [8, 4, 2, 256], P('dom', 'edge'), may hold values from 0 to 63
- cand_count: int32 [8, 4], P('dom', 'edge'), may hold values from 16 to 256, as said below
- labels: int32 [8, 4, 256], P('dom', 'edge'), may hold values 0 or 1
- mlp_weight: bfloat16 [2048, 512], P('edge'), may hold values from -0.125 to 0.125
- out_weight: float32 [512], replicated, may hold values from -0.6 to 0.6
Outputs:
- node_out: bfloat16 [4096, 1024], P(('dom', 'edge'))
- scores: float32 [8, 4, 256], P('dom', 'edge')
- node_grad: float32 [4096, 1024], P(('dom', 'edge'))
Inputs may be any that keep to these rules, and one draw needn't show every extreme that they name: `neighbours`: an entry below 128 names the device's own row; entry 128 + s * 32 + k names row k of the boundary block from dom index s. `halo_count`: in every draw some dom index receives full blocks from every sender. `cand_ends`: slot (s * 4 + r) * 2 + k is row k that device (s, r) sends. `cand_count`: some device has all 256 candidate slots live.
All inputs are finite; a program needn't handle non-finite values. No bound on the sum of `labels` on one device may be relied on, other than what follows from the above.
Results may differ from a plain program's by a relative error of at most 0.012.
The roundings to bfloat16 on the way count: a program that leaves them out, or rounds other values in their place, can miss the bound.
Values may be sent and summed in bfloat16 or wider, within the bound.
No kernel may reach another device: no remote copies, remote signals or barrier semaphores. Data moves between devices by JAX's collectives and lax.ppermute only.
A program may use at most 64 MiB of HBM per device.

v0:
```python
import jax
import jax.numpy as jnp
from jax import lax
from jax.sharding import PartitionSpec as P


def leaky_relu(values):
    return jnp.where(values > 0, values, 0.2 * values)


def silu_grad(pre_act):
    sigmoid_at = jax.nn.sigmoid(pre_act)
    return sigmoid_at * (1.0 + pre_act * (1.0 - sigmoid_at))


def head_scores(row_block, attn_vector):
    head_count, head_size = attn_vector.shape
    split_rows = row_block.astype(jnp.float32).reshape(
        row_block.shape[:-1] + (head_count, head_size)
    )
    return jnp.einsum("...hc,hc->...h", split_rows, attn_vector, precision=lax.Precision.HIGHEST)


def local(
    node_feats,
    gat_weight,
    attn_src,
    attn_dst,
    neighbours,
    degree,
    halo_rows,
    halo_count,
    endpoint_rows,
    cand_ends,
    cand_count,
    labels,
    mlp_weight,
    out_weight,
):
    node_count, feat_width = node_feats.shape
    head_count, head_size = attn_src.shape
    dom_count = lax.axis_size("dom")
    edge_count = lax.axis_size("edge")
    block_rows = halo_rows.shape[-1]
    slot_depth = endpoint_rows.shape[-1]
    cand_total = labels.shape[-1]
    degree_slots = neighbours.shape[1]
    projected = jnp.dot(
        node_feats,
        lax.all_gather(gat_weight, "edge", axis=0, tiled=True),
        preferred_element_type=jnp.float32,
    ).astype(jnp.bfloat16)
    src_own = head_scores(projected, attn_src).astype(jnp.bfloat16)
    dst_own = head_scores(projected, attn_dst)
    pick_rows = halo_rows[0, 0]
    send_rows = projected[pick_rows]
    send_count = halo_count[0, 0]
    send_src = src_own[pick_rows]
    got_rows, got_src, got_count = (
        lax.all_to_all(send_rows, "dom", split_axis=0, concat_axis=0, tiled=True),
        lax.all_to_all(send_src, "dom", split_axis=0, concat_axis=0, tiled=True),
        lax.all_to_all(send_count, "dom", split_axis=0, concat_axis=0, tiled=True),
    )
    halo_total = dom_count * block_rows
    key_table = jnp.concatenate([projected, got_rows.reshape(halo_total, feat_width)], axis=0)
    table_src = jnp.concatenate([src_own, got_src.reshape(halo_total, head_count)], axis=0).astype(
        jnp.float32
    )
    halo_live = (jnp.arange(block_rows)[None, :] < got_count[:, None]).reshape(halo_total)
    table_live = jnp.concatenate([jnp.ones((node_count,), jnp.bool_), halo_live])
    self_logit_all = leaky_relu(dst_own + src_own.astype(jnp.float32))
    row_block = min(node_count, 64)
    block_count = node_count // row_block

    def attend(block_index):
        first_row = block_index * row_block
        neighbour_ids = lax.dynamic_slice_in_dim(neighbours, first_row, row_block, 0)
        degree_here = lax.dynamic_slice_in_dim(degree, first_row, row_block, 0)
        dst_here = lax.dynamic_slice_in_dim(dst_own, first_row, row_block, 0)
        self_logit = lax.dynamic_slice_in_dim(self_logit_all, first_row, row_block, 0)
        own_rows = lax.dynamic_slice_in_dim(projected, first_row, row_block, 0)
        live_mask = (jnp.arange(degree_slots)[None, :] < degree_here[:, None]) & table_live[
            neighbour_ids
        ]
        logits = leaky_relu(dst_here[:, None, :] + table_src[neighbour_ids])
        row_peak = jnp.maximum(
            self_logit, jnp.max(jnp.where(live_mask[:, :, None], logits, -jnp.inf), axis=1)
        )
        exp_terms = jnp.where(live_mask[:, :, None], jnp.exp(logits - row_peak[:, None, :]), 0.0)
        self_exp = jnp.exp(self_logit - row_peak)
        running = self_exp + jnp.sum(exp_terms, axis=1)
        weights = (exp_terms / running[:, None, :]).astype(jnp.bfloat16)
        self_weight = (self_exp / running).astype(jnp.bfloat16)
        gathered = key_table[neighbour_ids].reshape(row_block, degree_slots, head_count, head_size)
        aggregate = jnp.einsum(
            "rjh,rjhc->rhc", weights, gathered, preferred_element_type=jnp.float32
        )
        aggregate = aggregate + self_weight.astype(jnp.float32)[:, :, None] * own_rows.reshape(
            row_block, head_count, head_size
        ).astype(jnp.float32)
        return jax.nn.elu(aggregate).reshape(row_block, feat_width).astype(jnp.bfloat16)

    node_out = lax.map(attend, jnp.arange(block_count)).reshape(node_count, feat_width)

    def route(payload):
        return lax.all_to_all(
            lax.all_to_all(payload, "dom", split_axis=0, concat_axis=0, tiled=True),
            "edge",
            split_axis=1,
            concat_axis=1,
            tiled=True,
        )

    owner_rows = endpoint_rows[0, 0]
    slot_total = dom_count * edge_count * slot_depth
    slot_rows = route(node_out[owner_rows]).reshape(slot_total, feat_width)
    end_slots = cand_ends[0, 0]
    pair_rows = jnp.concatenate([slot_rows[end_slots[0]], slot_rows[end_slots[1]]], axis=1)
    mlp_full = lax.all_gather(mlp_weight, "edge", axis=0, tiled=True)
    pre_act = jnp.dot(pair_rows, mlp_full, preferred_element_type=jnp.float32)
    edge_score = jnp.dot(jax.nn.silu(pre_act), out_weight, precision=lax.Precision.HIGHEST)
    live_mask = jnp.arange(cand_total) < cand_count[0, 0]
    edge_score = jnp.where(live_mask, edge_score, 0.0)
    grad_score = jnp.where(
        live_mask, jax.nn.sigmoid(edge_score) - labels[0, 0].astype(jnp.float32), 0.0
    )
    grad_pre = (grad_score[:, None] * out_weight[None, :] * silu_grad(pre_act)).astype(jnp.bfloat16)
    grad_pair = lax.dot_general(
        grad_pre, mlp_full, (((1,), (1,)), ((), ())), preferred_element_type=jnp.float32
    )
    slot_grad = jax.ops.segment_sum(
        grad_pair[:, :feat_width], end_slots[0], num_segments=slot_total
    )
    slot_grad = (
        slot_grad
        + jax.ops.segment_sum(grad_pair[:, feat_width:], end_slots[1], num_segments=slot_total)
    ).astype(jnp.bfloat16)
    returned = route(slot_grad.reshape(dom_count, edge_count, slot_depth, feat_width))
    node_grad = jax.ops.segment_sum(
        returned.reshape(slot_total, feat_width).astype(jnp.float32),
        owner_rows.reshape(slot_total),
        num_segments=node_count,
    )
    return (node_out, edge_score.reshape(1, 1, cand_total), node_grad)


def solution(mesh):
    in_specs = (
        P(("dom", "edge"), None),
        P("edge", None),
        P(),
        P(),
        P(("dom", "edge"), None),
        P(("dom", "edge")),
        P("dom", "edge", None, None),
        P("dom", "edge", None),
        P("dom", "edge", None, None, None),
        P("dom", "edge", None, None),
        P("dom", "edge"),
        P("dom", "edge", None),
        P("edge", None),
        P(),
    )
    out_specs = (P(("dom", "edge"), None), P("dom", "edge", None), P(("dom", "edge"), None))
    return jax.shard_map(local, mesh=mesh, in_specs=in_specs, out_specs=out_specs, check_vma=False)
```

profile of v0, /device:TPU:0, one launch (start us, length us, event | category | flops | bytes accessed | tf_op | source)
XLA Modules:
  0.0 171.3 jit_solution(17171330082397368396)
XLA Ops:
  7.9 1.3 copy.60
  9.3 7.3 %all-to-all-start = ((s32[8,1,1]{2,1,0:T(1,128)}), s32[8,1,1]{2,1,0:T(1,128)S(1)}, u32[]{:S(2)}, u32[]{:S(2)}) async-start(s32[8,1,1]{2,1,0:T(1,128)} %copy.60), calls=%async_computation | async-start | bytes 8192 | tf_op jit(solution)/shard_map/all_to_all | solution.py:62
  17.3 17.6 %all-gather.3.cloned.1.call-done = bf16[1024,1024]{1,0:T(8,128)(2,1)} async-done(((bf16[256,1024]{1,0:T(8,128)(2,1)}), bf16[1024,1024]{1,0:T(8,128)(2,1)}) %all-gather.3.cloned.1.call-update) | async-done | bytes 2097168 | tf_op jit(solution)/shard_map/all_gather | solution.py:50
  34.9 2.0 %convolution_convert_fusion = bf16[128,1024]{1,0:T(8,128)(2,1)S(1)} fusion(bf16[128,1024]{1,0:T(8,128)(2,1)S(1)} %copy-done, bf16[1024,1024]{1,0:T(8,128)(2,1)} %all-gather.3.cloned.1.call-done), kind=kOutput, calls=%fused_computation.38 | convolution fusion | flops 268566528 | bytes 2621440 | tf_op jit(solution)/shard_map/dot_general | solution.py:48
  39.9 5.6 %all-to-all-start.1 = ((bf16[8,2,128]{2,1,0:T(2,128)(2,1)}), bf16[8,2,128]{2,1,0:T(2,128)(2,1)S(1)}, u32[]{:S(2)}, u32[]{:S(2)}) async-start(bf16[8,2,128]{2,1,0:T(2,128)(2,1)} %reshape.334), calls=%async_computation.1 | async-start | bytes 8192 | tf_op jit(solution)/shard_map/all_to_all | solution.py:61
  45.5 2.0 %gather_fusion.4 = bf16[256,1024]{1,0:T(8,128)(2,1)} fusion(bf16[128,1024]{1,0:T(8,128)(2,1)S(1)} %convolution_convert_fusion, s32[1024]{0:T(1024)S(1)} %pad_clamp_fusion.3), kind=kCustom, calls=%fused_computation.4 | custom fusion | bytes 1049600 | tf_op jit(solution)/shard_map/gather | solution.py:56
  47.5 4.5 %all-to-all-done.1 = bf16[8,2,128]{2,1,0:T(2,128)(2,1)S(1)} async-done(((bf16[8,2,128]{2,1,0:T(2,128)(2,1)}), bf16[8,2,128]{2,1,0:T(2,128)(2,1)S(1)}, u32[]{:S(2)}, u32[]{:S(2)}) %all-to-all-start.1) | async-done | bytes 4128 | tf_op jit(solution)/shard_map/all_to_all | solution.py:61
  51.9 3.5 %all-to-all-start.2 = ((bf16[8,32,1024]{2,1,0:T(8,128)(2,1)}), bf16[8,32,1024]{2,1,0:T(8,128)(2,1)S(1)}, u32[]{:S(2)}, u32[]{:S(2)}) async-start(bf16[8,32,1024]{2,1,0:T(8,128)(2,1)} %bitcast.17), calls=%async_computation.2 | async-start | bytes 1048576 | tf_op jit(solution)/shard_map/all_to_all | solution.py:60
  57.3 11.8 %all-to-all-done.2 = bf16[8,32,1024]{2,1,0:T(8,128)(2,1)S(1)} async-done(((bf16[8,32,1024]{2,1,0:T(8,128)(2,1)}), bf16[8,32,1024]{2,1,0:T(8,128)(2,1)S(1)}, u32[]{:S(2)}, u32[]{:S(2)}) %all-to-all-start.2) | async-done | bytes 524320 | tf_op jit(solution)/shard_map/all_to_all | solution.py:60
  69.2 39.5 %while.10 = (s32[]{:T(128)}, bf16[2,64,1024]{2,1,0:T(8,128)(2,1)}, s32[2]{0:T(128)S(1)}, s32[128]{0:T(128)S(1)}, s32[128,16]{0,1:T(8,128)S(1)}, /*index=5*/pred[...) while((s32[]{:T(128)}, bf16[2,64,1024]{2,1,0:T(8,128)(2,1)}, ...), condition=%wide.region_3.4_spmd, body=%wide.region_0.3_spmd.sunk | while | flops 2736134 | bytes 15340083 | solution.py:103
  70.8 6.5 %gather_fusion.1 = pred[1024]{0:T(1024)(128)(4,1)S(1)} fusion(pred[384]{0:T(512)(128)(4,1)S(1)} %get-tuple-element.254, s32[1024]{0:T(1024)S(1)} %broadcast_clamp_fusion.2), kind=kCustom, calls=%fused_computation.clone.1 | custom fusion | bytes 6144 | tf_op jit(solution)/shard_map/while/body/eval_jaxpr/gather | solution.py:82
  77.5 2.8 %gather_fusion = f32[1024,8]{1,0:T(8,128)S(1)} fusion(f32[384,8]{1,0:T(8,128)S(1)} %get-tuple-element.256, s32[1024]{0:T(1024)S(1)} %broadcast_clamp_fusion.2), kind=kCustom, calls=%fused_computation.1.clone.1 | custom fusion | bytes 69632 | tf_op jit(solution)/shard_map/while/body/eval_jaxpr/gather | solution.py:85
  81.3 1.0 copy.105
  82.2 4.1 %gather_fusion.2 = bf16[1024,1024]{1,0:T(8,128)(2,1)S(1)} fusion(bf16[384,1024]{1,0:T(8,128)(2,1)S(1)} %get-tuple-element.258, s32[1024]{0:T(1024)S(1)} %broadcast_clamp_fusion.2), kind=kCustom, calls=%fused_computation.2.clone.1 | custom fusion | bytes 4198400 | tf_op jit(solution)/shard_map/while/body/eval_jaxpr/gather | solution.py:94
  90.5 6.5 %gather_fusion.1 = pred[1024]{0:T(1024)(128)(4,1)S(1)} fusion(pred[384]{0:T(512)(128)(4,1)S(1)} %get-tuple-element.254, s32[1024]{0:T(1024)S(1)} %broadcast_clamp_fusion.2), kind=kCustom, calls=%fused_computation.clone.1 | custom fusion | bytes 6144 | tf_op jit(solution)/shard_map/while/body/eval_jaxpr/gather | solution.py:82
  97.3 2.8 %gather_fusion = f32[1024,8]{1,0:T(8,128)S(1)} fusion(f32[384,8]{1,0:T(8,128)S(1)} %get-tuple-element.256, s32[1024]{0:T(1024)S(1)} %broadcast_clamp_fusion.2), kind=kCustom, calls=%fused_computation.1.clone.1 | custom fusion | bytes 69632 | tf_op jit(solution)/shard_map/while/body/eval_jaxpr/gather | solution.py:85
  101.0 1.0 copy.105
  102.0 4.1 %gather_fusion.2 = bf16[1024,1024]{1,0:T(8,128)(2,1)S(1)} fusion(bf16[384,1024]{1,0:T(8,128)(2,1)S(1)} %get-tuple-element.258, s32[1024]{0:T(1024)S(1)} %broadcast_clamp_fusion.2), kind=kCustom, calls=%fused_computation.2.clone.1 | custom fusion | bytes 4198400 | tf_op jit(solution)/shard_map/while/body/eval_jaxpr/gather | solution.py:94
  108.7 1.8 %gather_fusion.5 = bf16[64,1024]{1,0:T(8,128)(2,1)S(1)} fusion(bf16[128,1024]{1,0:T(8,128)(2,1)} %bitcast.19, s32[1024]{0:T(1024)S(1)} %pad_clamp_fusion.2), kind=kCustom, calls=%fused_computation.5 | custom fusion | bytes 262400 | tf_op jit(solution)/shard_map/gather | solution.py:116
  111.2 3.6 %all-to-all-start.3 = ((bf16[8,4,2,1024]{3,2,1,0:T(2,128)(2,1)}), bf16[8,4,2,1024]{3,2,1,0:T(2,128)(2,1)S(1)}, u32[]{:S(2)}, u32[]{:S(2)}) async-start(bf16[8,4,2,1024]{3,2,1,0:T(2,128)(2,1)} %reshape.259), calls=%async_computation.3 | async-start | bytes 262144 | tf_op jit(solution)/shard_map/all_to_all | solution.py:107
  115.5 6.7 %all-to-all-done.3 = bf16[8,4,2,1024]{3,2,1,0:T(2,128)(2,1)S(1)} async-done(((bf16[8,4,2,1024]{3,2,1,0:T(2,128)(2,1)}), bf16[8,4,2,1024]{3,2,1,0:T(2,128)(2,1)S(1)}, u32[]{:S(2)}, u32[]{:S(2)}) %all-to-all-start.3) | async-done | bytes 131104 | tf_op jit(solution)/shard_map/all_to_all | solution.py:107
  122.9 3.5 %all-to-all-start.4 = ((bf16[8,4,2,1024]{3,2,0,1:T(2,128)(2,1)}), bf16[8,4,2,1024]{3,2,0,1:T(2,128)(2,1)S(1)}, u32[]{:S(2)}, u32[]{:S(2)}) async-start(bf16[8,4,2,1024]{3,2,0,1:T(2,128)(2,1)} %copy.68), calls=%async_computation.4 | async-start | bytes 262144 | tf_op jit(solution)/shard_map/all_to_all | solution.py:106
  126.4 4.4 %all-to-all-done.4 = bf16[8,4,2,1024]{3,2,0,1:T(2,128)(2,1)S(1)} async-done(((bf16[8,4,2,1024]{3,2,0,1:T(2,128)(2,1)}), bf16[8,4,2,1024]{3,2,0,1:T(2,128)(2,1)S(1)}, u32[]{:S(2)}, u32[]{:S(2)}) %all-to-all-start.4) | async-done | bytes 131104 | tf_op jit(solution)/shard_map/all_to_all | solution.py:106
  131.0 1.2 gather_fusion.6
  132.2 1.2 gather_fusion.7
  133.4 2.3 %fusion.14 = f32[256,512]{1,0:T(8,128)S(1)} fusion(bf16[2048,512]{1,0:T(8,128)(2,1)} %all-gather.5.cloned.1.call-done, bf16[256,1024]{1,0:T(8,128)(2,1)S(1)} %gather_fusion.7, bf16[256,1024]{1,0:T(8,128)(2,1)S(1)} %gather_fusion.6), kind=kOutput, calls=%fused_computation.43 | convolution fusion | flops 538968064 | bytes 3670016 | tf_op jit(solution)/shard_map/dot_general | solution.py:120
  138.1 2.8 %scatter_custom_fusion.1 = f32[64,1024]{1,0:T(8,128)S(1)} fusion(s32[256]{0:T(256)S(1)} %bitcast.126, f32[256,2048]{1,0:T(8,128)S(1)} %fusion.20, f32[]{:T(128)} %constant.5.clone.1), kind=kCustom, calls=%fused_computation.39 | custom fusion | flops 262144 | bytes 1310724 | tf_op jit(solution)/shard_map/scatter-add | solution.py:136
  140.9 2.8 %scatter_custom_fusion = f32[64,1024]{1,0:T(8,128)S(1)} fusion(s32[256]{0:T(256)S(1)} %bitcast.125, f32[256,2048]{1,0:T(8,128)S(1)} %fusion.20, f32[]{:T(128)} %constant.5.clone.1), kind=kCustom, calls=%fused_computation.41 | custom fusion | flops 262144 | bytes 1310724 | tf_op jit(solution)/shard_map/scatter-add | solution.py:131
  143.8 9.7 %all_to_all.39 = bf16[8,4,2,1024]{3,2,1,0:T(2,128)(2,1)S(1)} all-to-all(bf16[8,4,2,1024]{3,2,1,0:T(2,128)(2,1)S(1)} %reshape.215), channel_id=1, replica_groups=mesh['dom'=8,'edge'=4] {'dom'}, dimensions={0} | all-to-all | bytes 262144 | tf_op jit(solution)/shard_map/all_to_all | solution.py:107
  154.3 3.3 %all-to-all-start.6 = ((bf16[8,4,2,1024]{3,2,0,1:T(2,128)(2,1)}), bf16[8,4,2,1024]{3,2,0,1:T(2,128)(2,1)S(1)}, u32[]{:S(2)}, u32[]{:S(2)}) async-start(bf16[8,4,2,1024]{3,2,0,1:T(2,128)(2,1)} %copy.71), calls=%async_computation.6 | async-start | bytes 262144 | tf_op jit(solution)/shard_map/all_to_all | solution.py:106
  157.8 4.4 %all-to-all-done.6 = bf16[8,4,2,1024]{3,2,0,1:T(2,128)(2,1)S(1)} async-done(((bf16[8,4,2,1024]{3,2,0,1:T(2,128)(2,1)}), bf16[8,4,2,1024]{3,2,0,1:T(2,128)(2,1)S(1)}, u32[]{:S(2)}, u32[]{:S(2)}) %all-to-all-start.6) | async-done | bytes 131104 | tf_op jit(solution)/shard_map/all_to_all | solution.py:106
  162.6 1.9 %scatter_custom_fusion.2 = f32[128,1024]{1,0:T(8,128)} fusion(s32[64]{0:T(128)S(1)} %reshape.300, f32[64,1024]{1,0:T(8,128)S(1)} %reshape.302, f32[]{:T(128)} %constant.5.clone.1), kind=kCustom, calls=%fused_computation.60 | custom fusion | flops 65536 | bytes 524292 | tf_op jit(solution)/shard_map/scatter-add | solution.py:139
  (130 shorter events, 21.0 us)
Async XLA Ops:
  7.2 27.8 %copy-start = (bf16[128,1024]{1,0:T(8,128)(2,1)S(1)}, bf16[128,1024]{1,0:T(8,128)(2,1)}, u32[]{:S(2)}) copy-start(bf16[128,1024]{1,0:T(8,128)(2,1)} %param.16) | copy-start | bytes 786436
  7.2 29.8 %copy-start.9 = (f32[8,128]{1,0:T(8,128)S(1)}, f32[8,128]{1,0:T(8,128)}, u32[]{:S(2)}) copy-start(f32[8,128]{1,0:T(8,128)} %param.19) | copy-start | bytes 12292
  7.2 30.4 %copy-start.10 = (f32[8,128]{1,0:T(8,128)S(1)}, f32[8,128]{1,0:T(8,128)}, u32[]{:S(2)}) copy-start(f32[8,128]{1,0:T(8,128)} %param.18) | copy-start | bytes 12292
  7.2 27.7 %all-gather.3.cloned.1.call-start = ((), (), s32[]{:S(2)}) async-start(), calls=%async_computation.7 | async-start | bytes 2621440 | tf_op jit(solution)/shard_map/all_gather | solution.py:50
  9.3 30.7 %all-to-all-start = ((s32[8,1,1]{2,1,0:T(1,128)}), s32[8,1,1]{2,1,0:T(1,128)S(1)}, u32[]{:S(2)}, u32[]{:S(2)}) async-start(s32[8,1,1]{2,1,0:T(1,128)} %copy.60), calls=%async_computation | async-start | bytes 8192 | tf_op jit(solution)/shard_map/all_to_all | solution.py:62
  39.9 12.0 %all-to-all-start.1 = ((bf16[8,2,128]{2,1,0:T(2,128)(2,1)}), bf16[8,2,128]{2,1,0:T(2,128)(2,1)S(1)}, u32[]{:S(2)}, u32[]{:S(2)}) async-start(bf16[8,2,128]{2,1,0:T(2,128)(2,1)} %reshape.334), calls=%async_computation.1 | async-start | bytes 8192 | tf_op jit(solution)/shard_map/all_to_all | solution.py:61
  45.5 10.7 %copy-start.5 = (s32[1,1,8,4,2]{2,4,3,1,0:T(2,128)S(1)}, s32[1,1,8,4,2]{2,4,3,1,0:T(2,128)}, u32[]{:S(2)}) copy-start(s32[1,1,8,4,2]{2,4,3,1,0:T(2,128)} %param.24) | copy-start | bytes 772
  45.5 11.0 %copy-start.6 = (s32[1,1,2,256]{3,2,1,0:T(2,128)S(1)}, s32[1,1,2,256]{3,2,1,0:T(2,128)}, u32[]{:S(2)}) copy-start(s32[1,1,2,256]{3,2,1,0:T(2,128)} %param.25) | copy-start | bytes 6148
  47.5 21.8 %copy-start.4 = (s32[128,16]{0,1:T(8,128)S(1)}, s32[128,16]{0,1:T(8,128)}, u32[]{:S(2)}) copy-start(s32[128,16]{0,1:T(8,128)} %param.20) | copy-start | bytes 24580
  47.5 21.8 %copy-start.12 = (s32[128]{0:T(128)S(1)}, s32[128]{0:T(128)}, u32[]{:S(2)}) copy-start(s32[128]{0:T(128)} %param.21) | copy-start | bytes 1540
  51.9 17.2 %all-to-all-start.2 = ((bf16[8,32,1024]{2,1,0:T(8,128)(2,1)}), bf16[8,32,1024]{2,1,0:T(8,128)(2,1)S(1)}, u32[]{:S(2)}, u32[]{:S(2)}) async-start(bf16[8,32,1024]{2,1,0:T(8,128)(2,1)} %bitcast.17), calls=%async_computation.2 | async-start | bytes 1048576 | tf_op jit(solution)/shard_map/all_to_all | solution.py:60
  55.4 77.9 %all-gather.5.cloned.1.call-start = ((), (), s32[]{:S(2)}) async-start(), calls=%async_computation.8 | async-start | bytes 2621440 | tf_op jit(solution)/shard_map/all_gather | solution.py:119
  69.2 45.6 %copy-start.7 = (s32[1,1,256]{2,1,0:T(1,128)S(1)}, s32[1,1,256]{2,1,0:T(1,128)}, u32[]{:S(2)}) copy-start(s32[1,1,256]{2,1,0:T(1,128)} %param.27) | copy-start | bytes 3076
  69.2 8.0 %copy-start.1 = (bf16[128,1024]{1,0:T(8,128)(2,1)}, bf16[128,1024]{1,0:T(8,128)(2,1)S(1)}, u32[]{:S(2)}) copy-start(bf16[128,1024]{1,0:T(8,128)(2,1)S(1)} %get-tuple-element.259) | copy-start | bytes 786436 | tf_op jit(solution)/shard_map/while
  86.3 1.0 copy-start.3
  86.9 1.0 copy-start.2
  89.0 8.0 %copy-start.1 = (bf16[128,1024]{1,0:T(8,128)(2,1)}, bf16[128,1024]{1,0:T(8,128)(2,1)S(1)}, u32[]{:S(2)}) copy-start(bf16[128,1024]{1,0:T(8,128)(2,1)S(1)} %get-tuple-element.259) | copy-start | bytes 786436 | tf_op jit(solution)/shard_map/while
  106.0 1.0 copy-start.3
  106.7 1.0 copy-start.2
  111.2 11.0 %all-to-all-start.3 = ((bf16[8,4,2,1024]{3,2,1,0:T(2,128)(2,1)}), bf16[8,4,2,1024]{3,2,1,0:T(2,128)(2,1)S(1)}, u32[]{:S(2)}, u32[]{:S(2)}) async-start(bf16[8,4,2,1024]{3,2,1,0:T(2,128)(2,1)} %reshape.259), calls=%async_computation.3 | async-start | bytes 262144 | tf_op jit(solution)/shard_map/all_to_all | solution.py:107
  122.9 7.9 %all-to-all-start.4 = ((bf16[8,4,2,1024]{3,2,0,1:T(2,128)(2,1)}), bf16[8,4,2,1024]{3,2,0,1:T(2,128)(2,1)S(1)}, u32[]{:S(2)}, u32[]{:S(2)}) async-start(bf16[8,4,2,1024]{3,2,0,1:T(2,128)(2,1)} %copy.68), calls=%async_computation.4 | async-start | bytes 262144 | tf_op jit(solution)/shard_map/all_to_all | solution.py:106
  133.3 2.3 %copy-start.11 = (f32[512]{0:T(512)S(1)}, f32[512]{0:T(512)}, u32[]{:S(2)}) copy-start(f32[512]{0:T(512)} %param.29) | copy-start | bytes 6148
  135.7 1.6 copy-start.8
  154.3 7.9 %all-to-all-start.6 = ((bf16[8,4,2,1024]{3,2,0,1:T(2,128)(2,1)}), bf16[8,4,2,1024]{3,2,0,1:T(2,128)(2,1)S(1)}, u32[]{:S(2)}, u32[]{:S(2)}) async-start(bf16[8,4,2,1024]{3,2,0,1:T(2,128)(2,1)} %copy.71), calls=%async_computation.6 | async-start | bytes 262144 | tf_op jit(solution)/shard_map/all_to_all | solution.py:106
Sparse Core Ops, SparseCore 0:
  9.6 25.2 all-gather.2
  57.8 22.9 all-gather.4
where the time goes:
time: 172 us; the launch traced here: 171 us
  waiting for transfers between devices  50.8 us (30%)
  local copies, waits for them, and re-layouts  47.7 us (28%)
  starting transfers between devices  26.8 us (16%)
  between operations  15.1 us (9%)
  other arithmetic  11.5 us (7%)
  blocking collectives  9.74 us (6%)
  matrix products  8.13 us (5%)
    all_gather x1, waiting for transfers between devices, local(): lax.all_gather(gat_weight, 'edge', axis=0, tiled=True)  17.6 us
    gather x4, local copies, waits for them, and re-layouts, attend(): table_live[neighbour_ids]  13.2 us
    all_to_all x1, waiting for transfers between devices, local(): lax.all_to_all(send_rows, 'dom', split_axis=0, concat_axis=0, tiled=True)  11.8 us
    all_to_all x1, blocking collectives, route(): lax.all_to_all(payload, 'dom', split_axis=0, concat_axis=0, tiled=True)  9.74 us
    all_to_all x2, waiting for transfers between devices, route(): lax.all_to_all(lax.all_to_all(payload, 'dom', split_axis=0, concat_axis=0...  8.78 us
    gather x2, local copies, waits for them, and re-layouts, attend(): key_table[neighbour_ids]  8.11 us
    all_to_all x1, starting transfers between devices, local(): lax.all_to_all(send_count, 'dom', split_axis=0, concat_axis=0, tiled=True)  7.25 us
    all_to_all x2, starting transfers between devices, route(): lax.all_to_all(lax.all_to_all(payload, 'dom', split_axis=0, concat_axis=0...  6.83 us
  transfers between devices with their start and end apart: 8, of which 6 were waited for; matrix products, arithmetic and copies ran while one was open for 31% of the time, Pallas kernels for 0%

commit v1 on v0

v1 whole, which is shorter than its diff:
```python
import functools

import jax
import jax.numpy as jnp
from jax import lax
from jax.experimental import pallas as pl
from jax.experimental.pallas import tpu as pltpu
from jax.sharding import PartitionSpec as P

F32 = jnp.float32
BF16 = jnp.bfloat16
DEAD = 64.0
VMEM = pl.BlockSpec(memory_space=pltpu.VMEM)
SPACES = {
    "v": VMEM,
    "s": pl.BlockSpec(memory_space=pltpu.SMEM),
    "any": pl.BlockSpec(memory_space=pl.ANY),
}


def dot(a, b, dims=((1,), (0,))):
    return lax.dot_general(a, b, (dims, ((), ())), preferred_element_type=F32)


def call(kernel, outs, ins, scratch=()):
    specs = [SPACES[space] for space, _ in ins]
    return pl.pallas_call(
        kernel,
        out_shape=outs,
        in_specs=specs,
        out_specs=jax.tree.map(lambda _: VMEM, outs),
        scratch_shapes=list(scratch),
        compiler_params=pltpu.CompilerParams(vmem_limit_bytes=48 * 1024 * 1024),
    )(*[array for _, array in ins])


def halo_kernel(count_ref, rows_ref, feats_ref, out_ref):
    doms, block = rows_ref.shape
    at = lax.broadcasted_iota(jnp.int32, (1, block), 1)
    pieces = [
        jnp.where(at < count_ref[0, s], rows_ref[s : s + 1, :], -1) for s in range(doms)
    ]
    flat = jnp.concatenate(pieces, axis=1)
    total = doms * block
    nodes = feats_ref.shape[0]
    pick = (lax.broadcasted_iota(jnp.int32, (nodes, total), 0) == flat).astype(F32).astype(BF16)
    rows = dot(pick, feats_ref[...], ((0,), (0,)))
    first = lax.broadcasted_iota(jnp.int32, (16, total), 0) == 0
    dead = jnp.where(first & (flat < 0), 1.0, 0.0).astype(BF16)
    mark_at = (lax.broadcasted_iota(jnp.int32, (16, 128), 0) == 0) & (
        lax.broadcasted_iota(jnp.int32, (16, 128), 1) == 0
    )
    mark = jnp.where(mark_at, DEAD, 0.0).astype(BF16)
    out_ref[:, :128] = (rows[:, :128] + dot(dead, mark, ((0,), (0,)))).astype(BF16)
    out_ref[:, 128:] = rows[:, 128:].astype(BF16)


def count_kernel(neigh_ref, degree_ref, out_ref):
    nodes, table = out_ref.shape
    slots = neigh_ref.shape[0]
    degree = degree_ref[...]
    for base in range(0, table, nodes):
        at = base + lax.broadcasted_iota(jnp.int32, (nodes, nodes), 0)
        total = jnp.zeros((nodes, nodes), F32)
        if base == 0:
            total = (at == lax.broadcasted_iota(jnp.int32, (nodes, nodes), 1)).astype(F32)
        for j in range(slots):
            ids = jnp.where(j < degree, neigh_ref[j : j + 1, :], -1)
            total = total + (at == ids).astype(F32)
        out_ref[:, base : base + nodes] = total.T


def block_diagonal(vectors):
    heads, size = vectors.shape
    wide = jnp.concatenate([vectors] * heads, axis=1)
    lane_head = lax.broadcasted_iota(jnp.int32, wide.shape, 1) // size
    wide = jnp.where(lane_head == lax.broadcasted_iota(jnp.int32, wide.shape, 0), wide, 0.0)
    high = wide.astype(BF16).astype(F32)
    middle = (wide - high).astype(BF16).astype(F32)
    low = (wide - high - middle).astype(BF16).astype(F32)
    return jnp.concatenate([high, middle, low, jnp.zeros_like(wide)], axis=0).astype(BF16)


def load_shards(at_ref, shards, weight_ref, sems):
    depth = shards[0].shape[0]
    copies = []
    for i, shard in enumerate(shards):
        rows = pl.ds(pl.multiple_of(at_ref[i] * depth, depth), depth)
        copies.append(pltpu.make_async_copy(shard, weight_ref.at[rows, :], sems.at[i]))
        copies[-1].start()
    return copies


def attend_kernel(
    shard_count, at_ref, own_ref, got_ref, count_ref, src_ref, dst_ref, ends_ref, *rest
):
    shards = rest[:shard_count]
    out_ref, send_ref, proj_ref, stage_ref, weight_ref, sems = rest[shard_count:]
    copies = load_shards(at_ref, shards, weight_ref, sems)
    nodes, width = own_ref.shape
    heads, size = src_ref.shape
    for copy in copies:
        copy.wait()
    for first, ref in ((0, own_ref), (nodes, got_ref)):
        proj_ref[first : first + ref.shape[0], :] = dot(ref[...], weight_ref[...]).astype(BF16)
    parts = dot(block_diagonal(src_ref[...]), proj_ref[...], ((1,), (1,)))
    src = parts[:heads] + parts[heads : 2 * heads] + parts[2 * heads : 3 * heads]
    src = src.astype(BF16).astype(F32)
    parts = dot(proj_ref[:nodes, :], block_diagonal(dst_ref[...]), ((1,), (1,)))
    dst = parts[:, :heads] + parts[:, heads : 2 * heads] + parts[:, 2 * heads : 3 * heads]
    first_lane = (lax.broadcasted_iota(jnp.int32, (16, 128), 1) == 0).astype(F32).astype(BF16)
    mark = dot(first_lane, got_ref[:, :128], ((1,), (1,)))[:1]
    live = jnp.concatenate([jnp.ones((1, nodes), F32), jnp.where(mark < DEAD / 2, 1.0, 0.0)], axis=1)
    count = count_ref[...] * live
    seen = count > 0
    for h in range(heads):
        logit = dst[:, h : h + 1] + src[h : h + 1, :]
        logit = jnp.where(seen, jnp.maximum(logit, 0.2 * logit), -jnp.inf)
        peak = jnp.max(logit, axis=1, keepdims=True)
        terms = jnp.exp(logit - peak)
        running = jnp.sum(count * terms, axis=1, keepdims=True)
        weight = (terms * (1.0 / running)).astype(BF16).astype(F32) * count
        high = weight.astype(BF16)
        low = (weight - high.astype(F32)).astype(BF16)
        rows = proj_ref[:, h * size : (h + 1) * size]
        total = dot(high, rows) + dot(low, rows)
        total = jnp.where(total > 0, total, jnp.exp(jnp.minimum(total, 0.0)) - 1.0)
        out_ref[:, h * size : (h + 1) * size] = total.astype(BF16)
    slots = ends_ref.shape[1]
    pick = (lax.broadcasted_iota(jnp.int32, (nodes, slots), 0) == ends_ref[...]).astype(F32)
    pack_rows(dot(pick.astype(BF16), out_ref[...], ((0,), (0,))), stage_ref, send_ref)


def pack_rows(rows, stage_ref, out_ref):
    slots, width = rows.shape
    pieces = width // 128
    for c in range(pieces):
        stage_ref[pl.ds(c, slots, stride=pieces), :] = rows[:, c * 128 : (c + 1) * 128]
    out_ref[...] = stage_ref[...].astype(BF16)


def unpack_rows(ref, stage_ref, pieces):
    stage_ref[...] = ref[...].astype(F32)
    slots = ref.shape[0] // pieces
    parts = [stage_ref[pl.ds(c, slots, stride=pieces), :] for c in range(pieces)]
    return jnp.concatenate(parts, axis=1).astype(BF16)


def score_kernel(shard_count, at_ref, live_ref, got_ref, ends_ref, labels_ref, out_w_ref, *rest):
    shards = rest[:shard_count]
    scores_ref, back_ref, pair_ref, stage_ref, weight_ref, sems = rest[shard_count:]
    copies = load_shards(at_ref, shards, weight_ref, sems)
    cands = ends_ref.shape[1]
    width = weight_ref.shape[0] // 2
    slots = got_ref.shape[0] * 128 // width
    rows = unpack_rows(got_ref, stage_ref, width // 128)
    slot_at = lax.broadcasted_iota(jnp.int32, (slots, cands), 0)
    picks = [(slot_at == ends_ref[i : i + 1, :]).astype(F32).astype(BF16) for i in range(2)]
    for i in range(2):
        pair_ref[:, i * width : (i + 1) * width] = dot(picks[i], rows, ((0,), (0,))).astype(BF16)
    for copy in copies:
        copy.wait()
    pre_act = dot(pair_ref[...], weight_ref[...])
    out_w = out_w_ref[...]
    gate = jax.nn.sigmoid(pre_act)
    score = jnp.sum(pre_act * gate * out_w, axis=1, keepdims=True)
    live = lax.broadcasted_iota(jnp.int32, (cands, 1), 0) < live_ref[0, 0]
    score = jnp.where(live, score, 0.0)
    scores_ref[...] = jnp.broadcast_to(score, (cands, 128)).T[:1]
    labels = jnp.broadcast_to(labels_ref[...].astype(F32), (8, cands)).T[:, :1]
    grad_score = jnp.where(live, jax.nn.sigmoid(score) - labels, 0.0)
    grad_pre = (grad_score * out_w * (gate * (1.0 + pre_act * (1.0 - gate)))).astype(BF16)
    slot_grad = jnp.zeros((2 * slots, width), F32)
    for i in range(2):
        total = dot(picks[i], grad_pre)
        high = total.astype(BF16)
        low = (total - high.astype(F32)).astype(BF16)
        both = jnp.concatenate([high, low], axis=0)
        slot_grad = slot_grad + dot(both, weight_ref[i * width : (i + 1) * width, :], ((1,), (1,)))
    pack_rows(slot_grad[:slots] + slot_grad[slots:], stage_ref, back_ref)


def scatter_kernel(ends_ref, got_ref, out_ref, stage_ref):
    nodes, width = out_ref.shape
    slots = ends_ref.shape[1]
    rows = unpack_rows(got_ref, stage_ref, width // 128)
    pick = (lax.broadcasted_iota(jnp.int32, (nodes, slots), 0) == ends_ref[...]).astype(F32)
    out_ref[...] = dot(pick.astype(BF16), rows)


def gather_edge(shard, me, edge_count):
    ys = edge_count // 2
    swap = [(e, e ^ 1) for e in range(edge_count)]
    found, at = [], []
    for k in range(ys):
        here = shard
        if k:
            here = lax.ppermute(
                shard, "edge", [(e, (e + 2 * k) % edge_count) for e in range(edge_count)]
            )
        source = (me - 2 * k) % edge_count
        found += [here, lax.ppermute(here, "edge", swap)]
        at += [source, source ^ 1]
    return found, jnp.stack(at).astype(jnp.int32)


def local(
    node_feats,
    gat_weight,
    attn_src,
    attn_dst,
    neighbours,
    degree,
    halo_rows,
    halo_count,
    endpoint_rows,
    cand_ends,
    cand_count,
    labels,
    mlp_weight,
    out_weight,
):
    nodes, width = node_feats.shape
    dom_count = lax.axis_size("dom")
    edge_count = lax.axis_size("edge")
    me = lax.axis_index("edge")
    block = halo_rows.shape[-1]
    cands = labels.shape[-1]
    hidden = out_weight.shape[0]
    halo = dom_count * block
    table = nodes + halo
    slots = dom_count * edge_count * endpoint_rows.shape[-1]
    pieces = width // 128
    everyone = ("dom", "edge")
    shape = jax.ShapeDtypeStruct

    send_rows = call(
        halo_kernel,
        shape((halo, width), BF16),
        [("s", halo_count[0]), ("v", halo_rows[0, 0]), ("v", node_feats)],
    )
    gat_shards, shard_at = gather_edge(gat_weight, me, edge_count)
    got_rows = lax.all_to_all(send_rows, "dom", split_axis=0, concat_axis=0, tiled=True)
    counts = call(
        count_kernel,
        shape((nodes, table), F32),
        [("v", neighbours.T), ("v", degree.reshape(1, nodes))],
    )
    ends_flat = endpoint_rows.reshape(1, slots)
    mlp_shards, _ = gather_edge(mlp_weight, me, edge_count)
    node_out, send_ends = call(
        functools.partial(attend_kernel, len(gat_shards)),
        (shape((nodes, width), BF16), shape((slots * pieces, 128), BF16)),
        [
            ("s", shard_at),
            ("v", node_feats),
            ("v", got_rows),
            ("v", counts),
            ("v", attn_src),
            ("v", attn_dst),
            ("v", ends_flat),
        ]
        + [("any", w) for w in gat_shards],
        [
            pltpu.VMEM((table, width), BF16),
            pltpu.VMEM((slots * pieces, 128), F32),
            pltpu.VMEM((width, width), BF16),
            pltpu.SemaphoreType.DMA((edge_count,)),
        ],
    )
    got_ends = lax.all_to_all(send_ends, everyone, split_axis=0, concat_axis=0, tiled=True)
    scores, send_back = call(
        functools.partial(score_kernel, len(mlp_shards)),
        (shape((1, cands), F32), shape((slots * pieces, 128), BF16)),
        [
            ("s", shard_at),
            ("s", cand_count),
            ("v", got_ends),
            ("v", cand_ends[0, 0]),
            ("v", labels[0]),
            ("v", out_weight.reshape(1, hidden)),
        ]
        + [("any", w) for w in mlp_shards],
        [
            pltpu.VMEM((cands, 2 * width), BF16),
            pltpu.VMEM((slots * pieces, 128), F32),
            pltpu.VMEM((2 * width, hidden), BF16),
            pltpu.SemaphoreType.DMA((edge_count,)),
        ],
    )
    got_back = lax.all_to_all(send_back, everyone, split_axis=0, concat_axis=0, tiled=True)
    node_grad = call(
        scatter_kernel,
        shape((nodes, width), F32),
        [("v", ends_flat), ("v", got_back)],
        [pltpu.VMEM((slots * pieces, 128), F32)],
    )
    return (node_out, scores.reshape(1, 1, cands), node_grad)


def solution(mesh):
    in_specs = (
        P(("dom", "edge"), None),
        P("edge", None),
        P(),
        P(),
        P(("dom", "edge"), None),
        P(("dom", "edge")),
        P("dom", "edge", None, None),
        P("dom", "edge", None),
        P("dom", "edge", None, None, None),
        P("dom", "edge", None, None),
        P("dom", "edge"),
        P("dom", "edge", None),
        P("edge", None),
        P(),
    )
    out_specs = (P(("dom", "edge"), None), P("dom", "edge", None), P(("dom", "edge"), None))
    return jax.shard_map(local, mesh=mesh, in_specs=in_specs, out_specs=out_specs, check_vma=False)
```

time: 172 us -> 64.3 us (0.37)
  local copies, waits for them, and re-layouts: 47.7 us -> 3.69 us
  waiting for transfers between devices: 50.8 us -> 20 us
  between operations: 15.1 us -> 1.39 us
  Pallas kernels: 0 us -> 12.4 us
  other arithmetic: 11.5 us -> 0.08 us
  starting transfers between devices: 26.8 us -> 16.3 us
  matrix products: 8.13 us -> 0 us
    gather x15 -> x0, local copies, waits for them, and re-layouts: 34.6 us -> none  [the longest x4 13.2 us: attend(): table_live[neighbour_ids]]
    all_gather x2 -> x0, waiting for transfers between devices: 17.6 us -> none  [the longest x1 17.6 us: local(): lax.all_gather(gat_weight, 'edge', axis=0, tiled=True)]
    all_to_all x5 -> x1, starting transfers between devices: 23.3 us -> 6.19 us  [local(): lax.all_to_all(send_ends, everyone, split_axis=0, concat_axis=0, tiled=True)]
    pallas_call x0 -> x5, Pallas kernels: none -> 12.4 us  [call(): pl.pallas_call(kernel, out_shape=outs, in_specs=specs, out_specs=jax.tree...]
    all_to_all x5 -> x1, waiting for transfers between devices: 19.9 us -> 7.56 us  [local(): lax.all_to_all(send_ends, everyone, split_axis=0, concat_axis=0, tiled=True)]
    ppermute x0 -> x6, waiting for transfers between devices: none -> 12.3 us  [the longest x2 12.3 us: gather_edge(): lax.ppermute(shard, 'edge', [(e, (e + 2 * k) % edge_count) for e in range...]
    all_to_all x1, waiting for transfers between devices: 11.8 us -> 0.15 us  [local(): lax.all_to_all(send_rows, 'dom', split_axis=0, concat_axis=0, tiled=True)]
    dot_general x8 -> x0, matrix products: 8.13 us -> none  [the longest x1 2.29 us: local(): pre_act = jnp.dot(pair_rows, mlp_full, preferred_element_type=jnp.float32)]
  transfers between devices with their start and end apart: 8 -> 8, of which waited for: 6 -> 4; matrix products, arithmetic and copies ran while one was open for 31% -> 0% of each run, Pallas kernels for 0% -> 12%
where the time goes in v1:
time: 64.3 us; the launch traced here: 63.8 us
  waiting for transfers between devices  20 us (31%)
  starting transfers between devices  16.3 us (25%)
  Pallas kernels  12.4 us (19%)
  blocking collectives  10 us (16%)
  local copies, waits for them, and re-layouts  3.69 us (6%)
  between operations  1.39 us (2%)
    pallas_call x5, Pallas kernels, call(): pl.pallas_call(kernel, out_shape=outs, in_specs=specs, out_specs=jax.tree...  12.4 us
    ppermute x2, waiting for transfers between devices, gather_edge(): lax.ppermute(shard, 'edge', [(e, (e + 2 * k) % edge_count) for e in range...  12.3 us
    all_to_all x1, blocking collectives, local(): lax.all_to_all(send_back, everyone, split_axis=0, concat_axis=0, tiled=True)  10 us
    all_to_all x1, waiting for transfers between devices, local(): lax.all_to_all(send_ends, everyone, split_axis=0, concat_axis=0, tiled=True)  7.56 us
    all_to_all x1, starting transfers between devices, local(): lax.all_to_all(send_ends, everyone, split_axis=0, concat_axis=0, tiled=True)  6.19 us
    all_to_all x1, starting transfers between devices, local(): lax.all_to_all(send_rows, 'dom', split_axis=0, concat_axis=0, tiled=True)  5.95 us
    ppermute x2, starting transfers between devices, gather_edge(): lax.ppermute(shard, 'edge', [(e, (e + 2 * k) % edge_count) for e in range...  3.6 us
    unnamed x27, local copies, waits for them, and re-layouts  3.58 us
  transfers between devices with their start and end apart: 8, of which 4 were waited for; matrix products, arithmetic and copies ran while one was open for 0% of the time, Pallas kernels for 12%

profile of v1, /device:TPU:0, one launch (start us, length us, event | category | flops | bytes accessed | tf_op | source)
XLA Modules:
  0.0 63.8 jit_solution(3558484837614518903)
XLA Ops:
  0.6 3.0 %collective-permute-start.1 = (bf16[256,1024]{1,0:T(8,128)(2,1)}, bf16[256,1024]{1,0:T(8,128)(2,1)}, u32[]{:S(2)}, u32[]{:S(2)}) collective-permute-start(bf16[256,1024]{1,0:T(8,128)(2,1)} %rest_0_.2), channel_id=1, source_target_pairs={{0,2},{1,3},{2,0},{3,1},{4,6},{5,7},{6,4},{7,5},{8,10},{9,11},{10,... | collective-permute-start | bytes 1572872 | tf_op jit(solution)/shard_map/ppermute | solution.py:198
  3.7 0.7 %copy-done.11 = s32[1,1,8]{2,1,0:T(1,128)S(1)} copy-done((s32[1,1,8]{2,1,0:T(1,128)S(1)}, s32[1,1,8]{2,1,0:T(1,128)}, u32[]{:S(2)}) %copy-start.11) | copy-done | bytes 56
  4.3 0.9 %copy-done = bf16[128,1024]{1,0:T(8,128)(2,1)S(1)} copy-done((bf16[128,1024]{1,0:T(8,128)(2,1)S(1)}, bf16[128,1024]{1,0:T(8,128)(2,1)}, u32[]{:S(2)}) %copy-start) | copy-done | bytes 262168
  5.3 0.7 %copy-done.4 = s32[1,1,8,32]{3,2,1,0:T(8,128)S(1)} copy-done((s32[1,1,8,32]{3,2,1,0:T(8,128)S(1)}, s32[1,1,8,32]{3,2,1,0:T(8,128)}, u32[]{:S(2)}) %copy-start.4) | copy-done | bytes 1048
  6.0 1.8 %shard_map.157 = bf16[256,1024]{1,0:T(8,128)(2,1)} custom-call(s32[1,8]{1,0:T(1,128)S(1)} %bitcast.28, s32[8,32]{1,0:T(8,128)S(1)} %bitcast.23, bf16[128,1024]{1,0:T(8,128)(2,1)S(1)} %copy-done), custom_call_target="tpu_custom_call" | custom-call | tf_op jit(solution)/shard_map/pallas_call | solution.py:27
  7.7 5.9 %all-to-all-start = ((bf16[8,32,1024]{2,1,0:T(8,128)(2,1)}), bf16[8,32,1024]{2,1,0:T(8,128)(2,1)S(1)}, u32[]{:S(2)}, u32[]{:S(2)}) async-start(bf16[8,32,1024]{2,1,0:T(8,128)(2,1)} %bitcast.6), calls=%async_computation | async-start | bytes 1048576 | tf_op jit(solution)/shard_map/all_to_all | solution.py:243
  13.7 0.0 copy-start.1
  13.7 0.6 collective-permute-start.4
  14.3 0.0 collective-permute-start
  14.3 2.0 %collective-permute-done.1.rest_2_ = bf16[256,1024]{1,0:T(8,128)(2,1)} collective-permute-done((bf16[256,1024]{1,0:T(8,128)(2,1)}, bf16[256,1024]{1,0:T(8,128)(2,1)}, u32[]{:S(2)}, u32[]{:S(2)}) %collective-permute-start.1) | collective-permute-done | bytes 524320 | tf_op jit(solution)/shard_map/ppermute | solution.py:198
  16.3 0.5 collective-permute-start.3
  16.8 10.2 %collective-permute-done.4.rest_2_ = bf16[512,512]{1,0:T(8,128)(2,1)S(1)} collective-permute-done((bf16[512,512]{1,0:T(8,128)(2,1)S(1)}, bf16[512,512]{1,0:T(8,128)(2,1)S(1)}, u32[]{:S(2)}, u32[]{:S(2)}) %collective-permute-start.4) | collective-permute-done | bytes 524320 | tf_op jit(solution)/shard_map/ppermute | solution.py:198
  27.0 0.0 collective-permute-start.5
  27.0 0.1 copy.18
  27.1 0.1 reshape.25.ends_ref
  27.3 0.4 shard_map.158.count_ref
  27.7 0.0 copy-start.5
  27.7 0.0 copy-start.6
  27.7 0.1 pad_add_fusion.at_ref
  27.8 0.0 collective-permute-done.rest_1_
  27.8 0.1 all-to-all-done
  27.9 0.4 copy-done.5
  28.4 0.0 copy-done.6
  28.4 5.6 %shard_map.159 = (bf16[128,1024]{1,0:T(8,128)(2,1)}, bf16[512,128]{1,0:T(8,128)(2,1)}) custom-call(s32[4]{0:T(128)S(1)} %pad_add_fusion.at_ref, bf16[128,1024]{1,0:T(8,128)(2,1)S(1)} %copy-done.1, bf16[256,1024]{1,0:T(8,128)(2,1)S(1)} %bitcast.18, f32[128,384]{1,0:T(8,128)S(1)} %shard_map.158.count_ref, f32[8,128]{1,0:T(8,128)S(1)} %copy-done.5, ...), custom_call_target="tpu_custom_call" | custom-call | tf_op jit(solution)/shard_map/pallas_call | solution.py:27
  34.0 6.2 %all-to-all-start.1 = ((bf16[32,16,128]{2,1,0:T(8,128)(2,1)}), bf16[32,16,128]{2,1,0:T(8,128)(2,1)S(1)}, u32[]{:S(2)}, u32[]{:S(2)}) async-start(bf16[32,16,128]{2,1,0:T(8,128)(2,1)} %bitcast.10), calls=%async_computation.1 | async-start | bytes 262144 | tf_op jit(solution)/shard_map/all_to_all | solution.py:271
  40.9 7.6 %all-to-all-done.1 = bf16[32,16,128]{2,1,0:T(8,128)(2,1)S(1)} async-done(((bf16[32,16,128]{2,1,0:T(8,128)(2,1)}), bf16[32,16,128]{2,1,0:T(8,128)(2,1)S(1)}, u32[]{:S(2)}, u32[]{:S(2)}) %all-to-all-start.1) | async-done | bytes 131104 | tf_op jit(solution)/shard_map/all_to_all | solution.py:271
  48.4 0.7 %copy-done.8 = f32[512]{0:T(512)S(1)} copy-done((f32[512]{0:T(512)S(1)}, f32[512]{0:T(512)}, u32[]{:S(2)}) %copy-start.8) | copy-done | bytes 2072
  49.1 0.0 copy-done.7
  49.1 0.0 copy-done.9
  49.2 3.6 %shard_map.160 = (f32[1,256]{1,0:T(1,128)}, bf16[512,128]{1,0:T(8,128)(2,1)S(1)}) custom-call(s32[4]{0:T(128)S(1)} %pad_add_fusion.at_ref, s32[1,1]{1,0:T(1,128)S(6)} %copy.19.live_ref, bf16[512,128]{1,0:T(8,128)(2,1)S(1)} %bitcast.19, s32[2,256]{1,0:T(2,128)S(1)} %bitcast.24, s32[1,256]{1,0:T(1,128)S(1)} %bitcast.26, f32[1,512]{1,0:T(1,128)S(1)} %bitcast.25, ...), custom_call_target="tpu_custom_call" | custom-call | tf_op jit(solution)/shard_map/pallas_call | solution.py:27
  52.8 10.0 %all_to_all.33 = bf16[32,16,128]{2,1,0:T(8,128)(2,1)S(1)} all-to-all(bf16[32,16,128]{2,1,0:T(8,128)(2,1)S(1)} %bitcast.21), channel_id=1, replica_groups=mesh['dom'=8,'edge'=4] {'dom','edge'}, dimensions={0} | all-to-all | bytes 262144 | tf_op jit(solution)/shard_map/all_to_all | solution.py:291
  62.8 1.0 %shard_map.161 = f32[128,1024]{1,0:T(8,128)} custom-call(s32[1,64]{1,0:T(1,128)S(1)} %reshape.25.ends_ref, bf16[512,128]{1,0:T(8,128)(2,1)S(1)} %bitcast.20), custom_call_target="tpu_custom_call" | custom-call | tf_op jit(solution)/shard_map/pallas_call | solution.py:27
  (19 shorter events, 0.0 us)
Async XLA Ops:
  0.6 15.7 %collective-permute-start.1 = (bf16[256,1024]{1,0:T(8,128)(2,1)}, bf16[256,1024]{1,0:T(8,128)(2,1)}, u32[]{:S(2)}, u32[]{:S(2)}) collective-permute-start(bf16[256,1024]{1,0:T(8,128)(2,1)} %rest_0_.2), channel_id=1, source_target_pairs={{0,2},{1,3},{2,0},{3,1},{4,6},{5,7},{6,4},{7,5},{8,10},{9,11},{10,... | collective-permute-start | bytes 1572872 | tf_op jit(solution)/shard_map/ppermute | solution.py:198
  3.7 0.7 %copy-start.11 = (s32[1,1,8]{2,1,0:T(1,128)S(1)}, s32[1,1,8]{2,1,0:T(1,128)}, u32[]{:S(2)}) copy-start(s32[1,1,8]{2,1,0:T(1,128)} %param.21) | copy-start | bytes 100
  4.3 0.9 %copy-start = (bf16[128,1024]{1,0:T(8,128)(2,1)S(1)}, bf16[128,1024]{1,0:T(8,128)(2,1)}, u32[]{:S(2)}) copy-start(bf16[128,1024]{1,0:T(8,128)(2,1)} %own_ref.1) | copy-start | bytes 786436
  5.3 0.7 %copy-start.4 = (s32[1,1,8,32]{3,2,1,0:T(8,128)S(1)}, s32[1,1,8,32]{3,2,1,0:T(8,128)}, u32[]{:S(2)}) copy-start(s32[1,1,8,32]{3,2,1,0:T(8,128)} %param.20) | copy-start | bytes 3076
  7.7 6.0 %copy-start.2 = (bf16[512,512]{1,0:T(8,128)(2,1)S(1)}, bf16[512,512]{1,0:T(8,128)(2,1)}, u32[]{:S(2)}) copy-start(bf16[512,512]{1,0:T(8,128)(2,1)} %rest_0_.3) | copy-start | bytes 1572868
  7.7 19.3 %copy-start.12 = (s32[1,1,8,4,2]{2,4,3,1,0:T(2,128)S(1)}, s32[1,1,8,4,2]{2,4,3,1,0:T(2,128)}, u32[]{:S(2)}) copy-start(s32[1,1,8,4,2]{2,4,3,1,0:T(2,128)} %param.22) | copy-start | bytes 772
  7.7 19.5 %copy-start.3 = (s32[128,16]{0,1:T(8,128)S(1)}, s32[128,16]{0,1:T(8,128)}, u32[]{:S(2)}) copy-start(s32[128,16]{0,1:T(8,128)} %param.18) | copy-start | bytes 24580
  7.7 19.6 %copy-start.10 = (s32[128]{0:T(128)S(1)}, s32[128]{0:T(128)}, u32[]{:S(2)}) copy-start(s32[128]{0:T(128)} %param.19) | copy-start | bytes 1540
  7.7 20.2 %all-to-all-start = ((bf16[8,32,1024]{2,1,0:T(8,128)(2,1)}), bf16[8,32,1024]{2,1,0:T(8,128)(2,1)S(1)}, u32[]{:S(2)}, u32[]{:S(2)}) async-start(bf16[8,32,1024]{2,1,0:T(8,128)(2,1)} %bitcast.6), calls=%async_computation | async-start | bytes 1048576 | tf_op jit(solution)/shard_map/all_to_all | solution.py:243
  13.7 14.3 %copy-start.1 = (bf16[128,1024]{1,0:T(8,128)(2,1)S(1)}, bf16[128,1024]{1,0:T(8,128)(2,1)}, u32[]{:S(2)}) copy-start(bf16[128,1024]{1,0:T(8,128)(2,1)} %own_ref.1) | copy-start | bytes 786436
  13.7 13.3 %collective-permute-start.4 = (bf16[512,512]{1,0:T(8,128)(2,1)S(1)}, bf16[512,512]{1,0:T(8,128)(2,1)S(1)}, u32[]{:S(2)}, u32[]{:S(2)}) collective-permute-start(bf16[512,512]{1,0:T(8,128)(2,1)S(1)} %copy-done.2), channel_id=1, source_target_pairs={{0,2},{1,3},{2,0},{3,1},{4,6},{5,7},{6,4},{7,5},{8,10},{9,11},{10,... | collective-permute-start | bytes 1572872 | tf_op jit(solution)/shard_map/ppermute | solution.py:198
  14.3 13.5 %collective-permute-start = (bf16[256,1024]{1,0:T(8,128)(2,1)}, bf16[256,1024]{1,0:T(8,128)(2,1)}, u32[]{:S(2)}, u32[]{:S(2)}) collective-permute-start(bf16[256,1024]{1,0:T(8,128)(2,1)} %rest_0_.2), channel_id=1, source_target_pairs={{0,1},{1,0},{2,3},{3,2},{4,5},{5,4},{6,7},{7,6},{8,9},{9,8},{10,11... | collective-permute-start | bytes 1572872 | tf_op jit(solution)/shard_map/ppermute | solution.py:202
  16.3 11.6 %collective-permute-start.2 = (bf16[256,1024]{1,0:T(8,128)(2,1)}, bf16[256,1024]{1,0:T(8,128)(2,1)}, u32[]{:S(2)}, u32[]{:S(2)}) collective-permute-start(bf16[256,1024]{1,0:T(8,128)(2,1)} %collective-permute-done.1.rest_2_), channel_id=1, source_target_pairs={{0,1},{1,0},{2,3},{3,2},{4,5},{5,4},{6,7},{7,6},{8,9},{9,8},{10,11... | collective-permute-start | bytes 1572872 | tf_op jit(solution)/shard_map/ppermute | solution.py:202
  16.3 24.6 %collective-permute-start.3 = (bf16[512,512]{1,0:T(8,128)(2,1)S(1)}, bf16[512,512]{1,0:T(8,128)(2,1)S(1)}, u32[]{:S(2)}, u32[]{:S(2)}) collective-permute-start(bf16[512,512]{1,0:T(8,128)(2,1)S(1)} %copy-done.2), channel_id=1, source_target_pairs={{0,1},{1,0},{2,3},{3,2},{4,5},{5,4},{6,7},{7,6},{8,9},{9,8},{10,11... | collective-permute-start | bytes 1572872 | tf_op jit(solution)/shard_map/ppermute | solution.py:202
  27.0 13.8 %collective-permute-start.5 = (bf16[512,512]{1,0:T(8,128)(2,1)S(1)}, bf16[512,512]{1,0:T(8,128)(2,1)S(1)}, u32[]{:S(2)}, u32[]{:S(2)}) collective-permute-start(bf16[512,512]{1,0:T(8,128)(2,1)S(1)} %collective-permute-done.4.rest_2_), channel_id=1, source_target_pairs={{0,1},{1,0},{2,3},{3,2},{4,5},{5,4},{6,7},{7,6},{8,9},{9,8},{10,11... | collective-permute-start | bytes 1572872 | tf_op jit(solution)/shard_map/ppermute | solution.py:202
  27.7 0.7 %copy-start.5 = (f32[8,128]{1,0:T(8,128)S(1)}, f32[8,128]{1,0:T(8,128)}, u32[]{:S(2)}) copy-start(f32[8,128]{1,0:T(8,128)} %src_ref.1) | copy-start | bytes 12292
  27.7 0.7 %copy-start.6 = (f32[8,128]{1,0:T(8,128)S(1)}, f32[8,128]{1,0:T(8,128)}, u32[]{:S(2)}) copy-start(f32[8,128]{1,0:T(8,128)} %dst_ref.1) | copy-start | bytes 12292
  34.0 14.4 %all-to-all-start.1 = ((bf16[32,16,128]{2,1,0:T(8,128)(2,1)}), bf16[32,16,128]{2,1,0:T(8,128)(2,1)S(1)}, u32[]{:S(2)}, u32[]{:S(2)}) async-start(bf16[32,16,128]{2,1,0:T(8,128)(2,1)} %bitcast.10), calls=%async_computation.1 | async-start | bytes 262144 | tf_op jit(solution)/shard_map/all_to_all | solution.py:271
  48.4 0.7 %copy-start.8 = (f32[512]{0:T(512)S(1)}, f32[512]{0:T(512)}, u32[]{:S(2)}) copy-start(f32[512]{0:T(512)} %param.27) | copy-start | bytes 6148
  48.4 0.7 %copy-start.7 = (s32[1,1,2,256]{3,2,1,0:T(2,128)S(1)}, s32[1,1,2,256]{3,2,1,0:T(2,128)}, u32[]{:S(2)}) copy-start(s32[1,1,2,256]{3,2,1,0:T(2,128)} %param.23) | copy-start | bytes 6148
  48.4 0.7 %copy-start.9 = (s32[1,1,256]{2,1,0:T(1,128)S(1)}, s32[1,1,256]{2,1,0:T(1,128)}, u32[]{:S(2)}) copy-start(s32[1,1,256]{2,1,0:T(1,128)} %param.25) | copy-start | bytes 3076

commit v2 on v1

--- a/solution.py
+++ b/solution.py
@@ -23,23 +23,44 @@
 
 
 def call(kernel, outs, ins, scratch=()):
-    specs = [SPACES[space] for space, _ in ins]
+    fetched = [i for i, (space, _) in enumerate(ins) if space == "f"]
+
+    def body(*refs):
+        refs = list(refs)
+        local_count = len(fetched) + 1
+        own, (held, sems) = refs[:-local_count], (refs[-local_count:-1], refs[-1])
+        copies = []
+        for n, i in enumerate(fetched):
+            copies.append(pltpu.make_async_copy(own[i], held[n], sems.at[n]))
+            copies[-1].start()
+            own[i] = held[n]
+
+        def ready():
+            for copy in copies:
+                copy.wait()
+
+        kernel(ready, *own)
+
     return pl.pallas_call(
-        kernel,
+        body,
         out_shape=outs,
-        in_specs=specs,
+        in_specs=[SPACES["any" if space == "f" else space] for space, _ in ins],
         out_specs=jax.tree.map(lambda _: VMEM, outs),
-        scratch_shapes=list(scratch),
+        scratch_shapes=list(scratch)
+        + [pltpu.VMEM(ins[i][1].shape, ins[i][1].dtype) for i in fetched]
+        + [pltpu.SemaphoreType.DMA((max(1, len(fetched)),))],
         compiler_params=pltpu.CompilerParams(vmem_limit_bytes=48 * 1024 * 1024),
     )(*[array for _, array in ins])
 
 
-def halo_kernel(count_ref, rows_ref, feats_ref, out_ref):
+def halo_kernel(ready, me_ref, count_ref, rows_ref, feats_ref, *out_refs):
     doms, block = rows_ref.shape
     at = lax.broadcasted_iota(jnp.int32, (1, block), 1)
-    pieces = [
-        jnp.where(at < count_ref[0, s], rows_ref[s : s + 1, :], -1) for s in range(doms)
-    ]
+    ready()
+    pieces = []
+    for k in range(doms):
+        s = me_ref[0] ^ k
+        pieces.append(jnp.where(at < count_ref[0, s], rows_ref[pl.ds(s, 1), :], -1))
     flat = jnp.concatenate(pieces, axis=1)
     total = doms * block
     nodes = feats_ref.shape[0]
@@ -51,11 +72,15 @@
         lax.broadcasted_iota(jnp.int32, (16, 128), 1) == 0
     )
     mark = jnp.where(mark_at, DEAD, 0.0).astype(BF16)
-    out_ref[:, :128] = (rows[:, :128] + dot(dead, mark, ((0,), (0,)))).astype(BF16)
-    out_ref[:, 128:] = rows[:, 128:].astype(BF16)
-
-
-def count_kernel(neigh_ref, degree_ref, out_ref):
+    head = (rows[:, :128] + dot(dead, mark, ((0,), (0,)))).astype(BF16)
+    tail = rows[:, 128:].astype(BF16)
+    for k, out_ref in enumerate(out_refs):
+        out_ref[:, :128] = head[k * block : (k + 1) * block, :]
+        out_ref[:, 128:] = tail[k * block : (k + 1) * block, :]
+
+
+def count_kernel(ready, neigh_ref, degree_ref, out_ref):
+    ready()
     nodes, table = out_ref.shape
     slots = neigh_ref.shape[0]
     degree = degree_ref[...]
@@ -92,11 +117,13 @@
 
 
 def attend_kernel(
-    shard_count, at_ref, own_ref, got_ref, count_ref, src_ref, dst_ref, ends_ref, *rest
+    shard_count, ready, at_ref, block_at_ref, own_ref, count_ref, src_ref, dst_ref, ends_ref, *rest
 ):
-    shards = rest[:shard_count]
-    out_ref, send_ref, proj_ref, stage_ref, weight_ref, sems = rest[shard_count:]
+    shards, blocks = rest[:shard_count], rest[shard_count:-8]
+    out_ref, send_ref, proj_ref, stage_ref, weight_ref, sems, got_ref, block_sems = rest[-8:]
     copies = load_shards(at_ref, shards, weight_ref, sems)
+    copies += load_shards(block_at_ref, blocks, got_ref, block_sems)
+    ready()
     nodes, width = own_ref.shape
     heads, size = src_ref.shape
     for copy in copies:
@@ -146,12 +173,15 @@
     return jnp.concatenate(parts, axis=1).astype(BF16)
 
 
-def score_kernel(shard_count, at_ref, live_ref, got_ref, ends_ref, labels_ref, out_w_ref, *rest):
+def score_kernel(
+    shard_count, ready, at_ref, live_ref, got_ref, ends_ref, labels_ref, out_w_ref, *rest
+):
     shards = rest[:shard_count]
     scores_ref, back_ref, pair_ref, stage_ref, weight_ref, sems = rest[shard_count:]
     copies = load_shards(at_ref, shards, weight_ref, sems)
     cands = ends_ref.shape[1]
     width = weight_ref.shape[0] // 2
+    ready()
     slots = got_ref.shape[0] * 128 // width
     rows = unpack_rows(got_ref, stage_ref, width // 128)
     slot_at = lax.broadcasted_iota(jnp.int32, (slots, cands), 0)
@@ -180,7 +210,8 @@
     pack_rows(slot_grad[:slots] + slot_grad[slots:], stage_ref, back_ref)
 
 
-def scatter_kernel(ends_ref, got_ref, out_ref, stage_ref):
+def scatter_kernel(ready, ends_ref, got_ref, out_ref, stage_ref):
+    ready()
     nodes, width = out_ref.shape
     slots = ends_ref.shape[1]
     rows = unpack_rows(got_ref, stage_ref, width // 128)
@@ -188,20 +219,17 @@
     out_ref[...] = dot(pick.astype(BF16), rows)
 
 
-def gather_edge(shard, me, edge_count):
-    ys = edge_count // 2
-    swap = [(e, e ^ 1) for e in range(edge_count)]
-    found, at = [], []
-    for k in range(ys):
-        here = shard
-        if k:
-            here = lax.ppermute(
-                shard, "edge", [(e, (e + 2 * k) % edge_count) for e in range(edge_count)]
-            )
-        source = (me - 2 * k) % edge_count
-        found += [here, lax.ppermute(here, "edge", swap)]
-        at += [source, source ^ 1]
-    return found, jnp.stack(at).astype(jnp.int32)
+def swap(array, axis, k):
+    count = lax.axis_size(axis)
+    return lax.ppermute(array, axis, [(i, i ^ k) for i in range(count)])
+
+
+def across(shard, edge_count):
+    return [shard] + [swap(shard, "edge", 2 * k) for k in range(1, edge_count // 2)]
+
+
+def from_core(shards):
+    return [one for shard in shards for one in (shard, swap(shard, "edge", 1))]
 
 
 def local(
@@ -223,7 +251,6 @@
     nodes, width = node_feats.shape
     dom_count = lax.axis_size("dom")
     edge_count = lax.axis_size("edge")
-    me = lax.axis_index("edge")
     block = halo_rows.shape[-1]
     cands = labels.shape[-1]
     hidden = out_weight.shape[0]
@@ -234,51 +261,59 @@
     everyone = ("dom", "edge")
     shape = jax.ShapeDtypeStruct
 
-    send_rows = call(
+    dom_at = (lax.axis_index("dom") ^ jnp.arange(dom_count)).astype(jnp.int32)
+    shard_at = (lax.axis_index("edge") ^ jnp.arange(edge_count)).astype(jnp.int32)
+    gat_across = across(gat_weight, edge_count)
+    blocks = call(
         halo_kernel,
-        shape((halo, width), BF16),
-        [("s", halo_count[0]), ("v", halo_rows[0, 0]), ("v", node_feats)],
-    )
-    gat_shards, shard_at = gather_edge(gat_weight, me, edge_count)
-    got_rows = lax.all_to_all(send_rows, "dom", split_axis=0, concat_axis=0, tiled=True)
+        [shape((block, width), BF16)] * dom_count,
+        [("s", dom_at), ("s", halo_count[0]), ("f", halo_rows[0, 0]), ("f", node_feats)],
+    )
+    blocks = [blocks[0]] + [swap(blocks[k], "dom", k) for k in range(1, dom_count)]
+    gat_shards = from_core(gat_across)
     counts = call(
         count_kernel,
         shape((nodes, table), F32),
-        [("v", neighbours.T), ("v", degree.reshape(1, nodes))],
+        [("f", neighbours.T), ("f", degree.reshape(1, nodes))],
     )
     ends_flat = endpoint_rows.reshape(1, slots)
-    mlp_shards, _ = gather_edge(mlp_weight, me, edge_count)
+    mlp_weight, *gat_shards = lax.optimization_barrier((mlp_weight, *gat_shards))
+    mlp_across = across(mlp_weight, edge_count)
     node_out, send_ends = call(
-        functools.partial(attend_kernel, len(gat_shards)),
+        functools.partial(attend_kernel, edge_count),
         (shape((nodes, width), BF16), shape((slots * pieces, 128), BF16)),
         [
             ("s", shard_at),
-            ("v", node_feats),
-            ("v", got_rows),
+            ("s", dom_at),
+            ("f", node_feats),
             ("v", counts),
-            ("v", attn_src),
-            ("v", attn_dst),
+            ("f", attn_src),
+            ("f", attn_dst),
             ("v", ends_flat),
         ]
-        + [("any", w) for w in gat_shards],
+        + [("any", w) for w in gat_shards + list(blocks)],
         [
             pltpu.VMEM((table, width), BF16),
             pltpu.VMEM((slots * pieces, 128), F32),
             pltpu.VMEM((width, width), BF16),
             pltpu.SemaphoreType.DMA((edge_count,)),
+            pltpu.VMEM((halo, width), BF16),
+            pltpu.SemaphoreType.DMA((dom_count,)),
         ],
     )
+    send_ends, *mlp_across = lax.optimization_barrier((send_ends, *mlp_across))
+    mlp_shards = from_core(mlp_across)
     got_ends = lax.all_to_all(send_ends, everyone, split_axis=0, concat_axis=0, tiled=True)
     scores, send_back = call(
-        functools.partial(score_kernel, len(mlp_shards)),
+        functools.partial(score_kernel, edge_count),
         (shape((1, cands), F32), shape((slots * pieces, 128), BF16)),
         [
             ("s", shard_at),
             ("s", cand_count),
             ("v", got_ends),
-            ("v", cand_ends[0, 0]),
-            ("v", labels[0]),
-            ("v", out_weight.reshape(1, hidden)),
+            ("f", cand_ends[0, 0]),
+            ("f", labels[0]),
+            ("f", out_weight.reshape(1, hidden)),
         ]
         + [("any", w) for w in mlp_shards],
         [

time: 64.3 us -> 74.9 us (1.16)
  waiting for transfers between devices: 20 us -> 28.5 us
  starting transfers between devices: 16.3 us -> 19.2 us
  Pallas kernels: 12.4 us -> 11.3 us
    ppermute x6 -> x13, starting transfers between devices: 4.12 us -> 16.6 us  [swap(): return lax.ppermute(array, axis, [(i, i ^ k) for i in range(count)])]
    ppermute x6 -> x13, waiting for transfers between devices: 12.3 us -> 20.9 us  [swap(): return lax.ppermute(array, axis, [(i, i ^ k) for i in range(count)])]
    all_to_all x1 -> x0, starting transfers between devices: 5.95 us -> none  [local(): lax.all_to_all(send_rows, 'dom', split_axis=0, concat_axis=0, tiled=True)]
    all_to_all x1, starting transfers between devices: 6.19 us -> 2.58 us  [local(): lax.all_to_all(send_ends, everyone, split_axis=0, concat_axis=0, tiled=True)]
    pallas_call x5, Pallas kernels: 12.4 us -> 11.3 us  [call(): pl.pallas_call(body, out_shape=outs, in_specs=[SPACES['any' if space == '...]
    unnamed x27 -> x29, local copies, waits for them, and re-layouts: 3.58 us -> 4.15 us
  transfers between devices with their start and end apart: 8 -> 14, of which waited for: 4 -> 5; matrix products, arithmetic and copies ran while one was open for 0% -> 0% of each run, Pallas kernels for 12% -> 9%
where the time goes in v2:
time: 74.9 us; the launch traced here: 74.5 us
  waiting for transfers between devices  28.5 us (38%)
  starting transfers between devices  19.2 us (26%)
  Pallas kernels  11.3 us (15%)
  blocking collectives  9.93 us (13%)
  local copies, waits for them, and re-layouts  4.25 us (6%)
  between operations  1.43 us (2%)
    ppermute x13, waiting for transfers between devices, swap(): return lax.ppermute(array, axis, [(i, i ^ k) for i in range(count)])  20.9 us
    ppermute x13, starting transfers between devices, swap(): return lax.ppermute(array, axis, [(i, i ^ k) for i in range(count)])  16.6 us
    pallas_call x5, Pallas kernels, call(): pl.pallas_call(body, out_shape=outs, in_specs=[SPACES['any' if space == '...  11.3 us
    all_to_all x1, blocking collectives, local(): lax.all_to_all(send_back, everyone, split_axis=0, concat_axis=0, tiled=True)  9.93 us
    all_to_all x1, waiting for transfers between devices, local(): lax.all_to_all(send_ends, everyone, split_axis=0, concat_axis=0, tiled=True)  7.58 us
    unnamed x29, local copies, waits for them, and re-layouts  4.15 us
    all_to_all x1, starting transfers between devices, local(): lax.all_to_all(send_ends, everyone, split_axis=0, concat_axis=0, tiled=True)  2.58 us
  transfers between devices with their start and end apart: 14, of which 5 were waited for; matrix products, arithmetic and copies ran while one was open for 0% of the time, Pallas kernels for 9%

profile of v2, /device:TPU:0, one launch (start us, length us, event | category | flops | bytes accessed | tf_op | source)
XLA Modules:
  0.0 74.5 jit_solution(10827265462690096330)
XLA Ops:
  0.6 3.0 %collective-permute-start.1 = (bf16[256,1024]{1,0:T(8,128)(2,1)}, bf16[256,1024]{1,0:T(8,128)(2,1)S(1)}, u32[]{:S(2)}, u32[]{:S(2)}) collective-permute-start(bf16[256,1024]{1,0:T(8,128)(2,1)} %refs_7_), channel_id=1, source_target_pairs={{0,2},{1,3},{2,0},{3,1},{4,6},{5,7},{6,4},{7,5},{8,10},{9,11},{10,... | collective-permute-start | bytes 1572872 | tf_op jit(solution)/shard_map/ppermute | solution.py:224
  3.7 12.1 %collective-permute-done.1.refs_9_ = bf16[256,1024]{1,0:T(8,128)(2,1)S(1)} collective-permute-done((bf16[256,1024]{1,0:T(8,128)(2,1)}, bf16[256,1024]{1,0:T(8,128)(2,1)S(1)}, u32[]{:S(2)}, u32[]{:S(2)}) %collective-permute-start.1) | collective-permute-done | bytes 524320 | tf_op jit(solution)/shard_map/ppermute | solution.py:224
  15.8 1.9 %collective-permute-done.2.refs_10_ = bf16[256,1024]{1,0:T(8,128)(2,1)S(1)} collective-permute-done((bf16[256,1024]{1,0:T(8,128)(2,1)S(1)}, bf16[256,1024]{1,0:T(8,128)(2,1)S(1)}, u32[]{:S(2)}, u32[]{:S(2)}) %collective-permute-start.2) | collective-permute-done | bytes 524320 | tf_op jit(solution)/shard_map/ppermute | solution.py:224
  17.7 1.7 %collective-permute-start.10 = (bf16[512,512]{1,0:T(8,128)(2,1)}, bf16[512,512]{1,0:T(8,128)(2,1)S(1)}, u32[]{:S(2)}, u32[]{:S(2)}) collective-permute-start(bf16[512,512]{1,0:T(8,128)(2,1)} %refs_6_), channel_id=1, source_target_pairs={{0,2},{1,3},{2,0},{3,1},{4,6},{5,7},{6,4},{7,5},{8,10},{9,11},{10,... | collective-permute-start | bytes 1572872 | tf_op jit(solution)/shard_map/ppermute | solution.py:224
  19.5 0.7 copy-done.5
  20.1 0.9 %copy-done = bf16[128,1024]{1,0:T(8,128)(2,1)S(1)} copy-done((bf16[128,1024]{1,0:T(8,128)(2,1)S(1)}, bf16[128,1024]{1,0:T(8,128)(2,1)}, u32[]{:S(2)}) %copy-start) | copy-done | bytes 262168
  21.1 1.0 %shard_map.158 = (bf16[32,1024]{1,0:T(8,128)(2,1)S(1)}, bf16[32,1024]{1,0:T(8,128)(2,1)S(1)}, bf16[32,1024]{1,0:T(8,128)(2,1)S(1)}, bf16[32,1024]{1,0:T(8,128)(2...) custom-call(s32[8]{0:T(128)S(1)} %iota_xor_fusion.refs_0_.refs_1_, ...), custom_call_target="tpu_custom_call" | custom-call | tf_op jit(solution)/shard_map/pallas_call | solution.py:44
  22.1 1.6 %collective-permute-start.3 = (bf16[32,1024]{1,0:T(8,128)(2,1)S(1)}, bf16[32,1024]{1,0:T(8,128)(2,1)S(1)}, u32[]{:S(2)}, u32[]{:S(2)}) collective-permute-start(bf16[32,1024]{1,0:T(8,128)(2,1)S(1)} %get-tuple-element.28), channel_id=1, source_target_pairs={{0,4},{4,0},{8,12},{12,8},{16,20},{20,16},{24,28},{28,24},{1,5},{5... | collective-permute-start | bytes 196616 | tf_op jit(solution)/shard_map/ppermute | solution.py:224
  23.7 1.6 %collective-permute-start.4 = (bf16[32,1024]{1,0:T(8,128)(2,1)S(1)}, bf16[32,1024]{1,0:T(8,128)(2,1)S(1)}, u32[]{:S(2)}, u32[]{:S(2)}) collective-permute-start(bf16[32,1024]{1,0:T(8,128)(2,1)S(1)} %get-tuple-element.29), channel_id=1, source_target_pairs={{0,8},{4,12},{8,0},{12,4},{16,24},{20,28},{24,16},{28,20},{1,9},{5... | collective-permute-start | bytes 196616 | tf_op jit(solution)/shard_map/ppermute | solution.py:224
  25.3 0.4 collective-permute-start.5
  25.7 2.6 %collective-permute-start.6 = (bf16[32,1024]{1,0:T(8,128)(2,1)S(1)}, bf16[32,1024]{1,0:T(8,128)(2,1)S(1)}, u32[]{:S(2)}, u32[]{:S(2)}) collective-permute-start(bf16[32,1024]{1,0:T(8,128)(2,1)S(1)} %get-tuple-element.31), channel_id=1, source_target_pairs={{0,16},{4,20},{8,24},{12,28},{16,0},{20,4},{24,8},{28,12},{1,17},{... | collective-permute-start | bytes 196616 | tf_op jit(solution)/shard_map/ppermute | solution.py:224
  28.3 0.1 copy.18
  28.4 0.1 reshape.23.refs_6_.refs_0_
  28.5 0.6 copy-done.4
  29.1 0.1 copy-done.12
  29.1 0.4 shard_map.157.refs_3_
  29.6 1.3 %collective-permute-start.7 = (bf16[32,1024]{1,0:T(8,128)(2,1)S(1)}, bf16[32,1024]{1,0:T(8,128)(2,1)S(1)}, u32[]{:S(2)}, u32[]{:S(2)}) collective-permute-start(bf16[32,1024]{1,0:T(8,128)(2,1)S(1)} %get-tuple-element.32), channel_id=1, source_target_pairs={{0,20},{4,16},{8,28},{12,24},{16,4},{20,0},{24,12},{28,8},{1,21},{... | collective-permute-start | bytes 196616 | tf_op jit(solution)/shard_map/ppermute | solution.py:224
  31.0 3.6 %collective-permute-start.8 = (bf16[32,1024]{1,0:T(8,128)(2,1)S(1)}, bf16[32,1024]{1,0:T(8,128)(2,1)S(1)}, u32[]{:S(2)}, u32[]{:S(2)}) collective-permute-start(bf16[32,1024]{1,0:T(8,128)(2,1)S(1)} %get-tuple-element.33), channel_id=1, source_target_pairs={{0,24},{4,28},{8,16},{12,20},{16,8},{20,12},{24,0},{28,4},{1,25},{... | collective-permute-start | bytes 196616 | tf_op jit(solution)/shard_map/ppermute | solution.py:224
  34.6 0.2 collective-permute-start.9
  34.8 4.1 %collective-permute-done.7.refs_16_ = bf16[32,1024]{1,0:T(8,128)(2,1)S(1)} collective-permute-done((bf16[32,1024]{1,0:T(8,128)(2,1)S(1)}, bf16[32,1024]{1,0:T(8,128)(2,1)S(1)}, u32[]{:S(2)}, u32[]{:S(2)}) %collective-permute-start.7) | collective-permute-done | bytes 65568 | tf_op jit(solution)/shard_map/ppermute | solution.py:224
  38.9 2.7 %collective-permute-done.9.refs_18_ = bf16[32,1024]{1,0:T(8,128)(2,1)S(1)} collective-permute-done((bf16[32,1024]{1,0:T(8,128)(2,1)S(1)}, bf16[32,1024]{1,0:T(8,128)(2,1)S(1)}, u32[]{:S(2)}, u32[]{:S(2)}) %collective-permute-start.9) | collective-permute-done | bytes 65568 | tf_op jit(solution)/shard_map/ppermute | solution.py:224
  41.6 1.0 %copy-done.2 = bf16[256,1024]{1,0:T(8,128)(2,1)S(1)} copy-done((bf16[256,1024]{1,0:T(8,128)(2,1)S(1)}, bf16[256,1024]{1,0:T(8,128)(2,1)}, u32[]{:S(2)}) %copy-start.2) | copy-done | bytes 524312
  42.6 5.1 %shard_map.159 = (bf16[128,1024]{1,0:T(8,128)(2,1)}, bf16[512,128]{1,0:T(8,128)(2,1)}) custom-call(s32[4]{0:T(128)S(1)} %iota_xor_fusion.1.refs_0_, s32[8]{0:T(128)S(1)} %iota_xor_fusion.refs_0_.refs_1_, bf16[128,1024]{1,0:T(8,128)(2,1)S(1)} %copy-done.1, f32[128,384]{1,0:T(8,128)S(1)} %shard_map.157.refs_3_, f32[8,128]{1,0:T(8,128)S(1)} %copy-done.6, ...), custom_call_target="tpu_custom_call" | custom-call | tf_op jit(solution)/shard_map/pallas_call | solution.py:44
  47.8 0.1 collective-permute-start.11
  47.9 0.5 collective-permute-start.12
  48.4 2.6 %all-to-all-start = ((bf16[32,16,128]{2,1,0:T(8,128)(2,1)}), bf16[32,16,128]{2,1,0:T(8,128)(2,1)S(1)}, u32[]{:S(2)}, u32[]{:S(2)}) async-start(bf16[32,16,128]{2,1,0:T(8,128)(2,1)} %bitcast.4), calls=%async_computation | async-start | bytes 262144 | tf_op jit(solution)/shard_map/all_to_all | solution.py:306
  51.6 7.6 %all-to-all-done = bf16[32,16,128]{2,1,0:T(8,128)(2,1)S(1)} async-done(((bf16[32,16,128]{2,1,0:T(8,128)(2,1)}), bf16[32,16,128]{2,1,0:T(8,128)(2,1)S(1)}, u32[]{:S(2)}, u32[]{:S(2)}) %all-to-all-start) | async-done | bytes 131104 | tf_op jit(solution)/shard_map/all_to_all | solution.py:306
  59.2 0.7 copy-done.9
  59.9 0.0 copy-done.8
  59.9 3.7 %shard_map.160 = (f32[1,256]{1,0:T(1,128)}, bf16[512,128]{1,0:T(8,128)(2,1)S(1)}) custom-call(s32[4]{0:T(128)S(1)} %iota_xor_fusion.1.refs_0_, s32[1,1]{1,0:T(1,128)S(6)} %copy.19.refs_1_, bf16[512,128]{1,0:T(8,128)(2,1)S(1)} %bitcast.12, s32[2,256]{1,0:T(2,128)S(1)} %bitcast.17, s32[1,256]{1,0:T(1,128)S(1)} %bitcast.19, f32[1,512]{1,0:T(1,128)S(1)} %bitcast.18, ...), custom_call_target="tpu_custom_call" | custom-call | tf_op jit(solution)/shard_map/pallas_call | solution.py:44
  63.6 9.9 %all_to_all.22 = bf16[32,16,128]{2,1,0:T(8,128)(2,1)S(1)} all-to-all(bf16[32,16,128]{2,1,0:T(8,128)(2,1)S(1)} %bitcast.14), channel_id=1, replica_groups=mesh['dom'=8,'edge'=4] {'dom','edge'}, dimensions={0} | all-to-all | bytes 262144 | tf_op jit(solution)/shard_map/all_to_all | solution.py:326
  73.5 1.0 %shard_map.161 = f32[128,1024]{1,0:T(8,128)} custom-call(s32[1,64]{1,0:T(1,128)S(1)} %reshape.23.refs_6_.refs_0_, bf16[512,128]{1,0:T(8,128)(2,1)S(1)} %bitcast.13), custom_call_target="tpu_custom_call" | custom-call | tf_op jit(solution)/shard_map/pallas_call | solution.py:44
  (34 shorter events, 0.1 us)
Async XLA Ops:
  0.6 15.2 %collective-permute-start.1 = (bf16[256,1024]{1,0:T(8,128)(2,1)}, bf16[256,1024]{1,0:T(8,128)(2,1)S(1)}, u32[]{:S(2)}, u32[]{:S(2)}) collective-permute-start(bf16[256,1024]{1,0:T(8,128)(2,1)} %refs_7_), channel_id=1, source_target_pairs={{0,2},{1,3},{2,0},{3,1},{4,6},{5,7},{6,4},{7,5},{8,10},{9,11},{10,... | collective-permute-start | bytes 1572872 | tf_op jit(solution)/shard_map/ppermute | solution.py:224
  3.7 12.1 %collective-permute-start = (bf16[256,1024]{1,0:T(8,128)(2,1)}, bf16[256,1024]{1,0:T(8,128)(2,1)S(1)}, u32[]{:S(2)}, u32[]{:S(2)}) collective-permute-start(bf16[256,1024]{1,0:T(8,128)(2,1)} %refs_7_), channel_id=1, source_target_pairs={{0,1},{1,0},{2,3},{3,2},{4,5},{5,4},{6,7},{7,6},{8,9},{9,8},{10,11... | collective-permute-start | bytes 1572872 | tf_op jit(solution)/shard_map/ppermute | solution.py:224
  15.8 1.9 %collective-permute-start.2 = (bf16[256,1024]{1,0:T(8,128)(2,1)S(1)}, bf16[256,1024]{1,0:T(8,128)(2,1)S(1)}, u32[]{:S(2)}, u32[]{:S(2)}) collective-permute-start(bf16[256,1024]{1,0:T(8,128)(2,1)S(1)} %collective-permute-done.1.refs_9_), channel_id=1, source_target_pairs={{0,1},{1,0},{2,3},{3,2},{4,5},{5,4},{6,7},{7,6},{8,9},{9,8},{10,11... | collective-permute-start | bytes 1572872 | tf_op jit(solution)/shard_map/ppermute | solution.py:224
  17.7 30.1 %collective-permute-start.10 = (bf16[512,512]{1,0:T(8,128)(2,1)}, bf16[512,512]{1,0:T(8,128)(2,1)S(1)}, u32[]{:S(2)}, u32[]{:S(2)}) collective-permute-start(bf16[512,512]{1,0:T(8,128)(2,1)} %refs_6_), channel_id=1, source_target_pairs={{0,2},{1,3},{2,0},{3,1},{4,6},{5,7},{6,4},{7,5},{8,10},{9,11},{10,... | collective-permute-start | bytes 1572872 | tf_op jit(solution)/shard_map/ppermute | solution.py:224
  19.4 0.7 copy-start.5
  19.5 0.7 copy-start.11
  20.1 1.0 %copy-start = (bf16[128,1024]{1,0:T(8,128)(2,1)S(1)}, bf16[128,1024]{1,0:T(8,128)(2,1)}, u32[]{:S(2)}) copy-start(bf16[128,1024]{1,0:T(8,128)(2,1)} %refs_2_.1) | copy-start | bytes 786436
  21.1 20.5 %copy-start.1 = (bf16[128,1024]{1,0:T(8,128)(2,1)S(1)}, bf16[128,1024]{1,0:T(8,128)(2,1)}, u32[]{:S(2)}) copy-start(bf16[128,1024]{1,0:T(8,128)(2,1)} %refs_2_.1) | copy-start | bytes 786436
  22.1 7.5 %collective-permute-start.3 = (bf16[32,1024]{1,0:T(8,128)(2,1)S(1)}, bf16[32,1024]{1,0:T(8,128)(2,1)S(1)}, u32[]{:S(2)}, u32[]{:S(2)}) collective-permute-start(bf16[32,1024]{1,0:T(8,128)(2,1)S(1)} %get-tuple-element.28), channel_id=1, source_target_pairs={{0,4},{4,0},{8,12},{12,8},{16,20},{20,16},{24,28},{28,24},{1,5},{5... | collective-permute-start | bytes 196616 | tf_op jit(solution)/shard_map/ppermute | solution.py:224
  23.7 4.6 %copy-start.13 = (s32[1,1,8,4,2]{2,4,3,1,0:T(2,128)S(1)}, s32[1,1,8,4,2]{2,4,3,1,0:T(2,128)}, u32[]{:S(2)}) copy-start(s32[1,1,8,4,2]{2,4,3,1,0:T(2,128)} %param.22) | copy-start | bytes 772
  23.7 7.3 %collective-permute-start.4 = (bf16[32,1024]{1,0:T(8,128)(2,1)S(1)}, bf16[32,1024]{1,0:T(8,128)(2,1)S(1)}, u32[]{:S(2)}, u32[]{:S(2)}) collective-permute-start(bf16[32,1024]{1,0:T(8,128)(2,1)S(1)} %get-tuple-element.29), channel_id=1, source_target_pairs={{0,8},{4,12},{8,0},{12,4},{16,24},{20,28},{24,16},{28,20},{1,9},{5... | collective-permute-start | bytes 196616 | tf_op jit(solution)/shard_map/ppermute | solution.py:224
  25.3 9.3 %collective-permute-start.5 = (bf16[32,1024]{1,0:T(8,128)(2,1)S(1)}, bf16[32,1024]{1,0:T(8,128)(2,1)S(1)}, u32[]{:S(2)}, u32[]{:S(2)}) collective-permute-start(bf16[32,1024]{1,0:T(8,128)(2,1)S(1)} %get-tuple-element.30), channel_id=1, source_target_pairs={{0,12},{4,8},{8,4},{12,0},{16,28},{20,24},{24,20},{28,16},{1,13},{... | collective-permute-start | bytes 196616 | tf_op jit(solution)/shard_map/ppermute | solution.py:224
  25.7 9.1 %collective-permute-start.6 = (bf16[32,1024]{1,0:T(8,128)(2,1)S(1)}, bf16[32,1024]{1,0:T(8,128)(2,1)S(1)}, u32[]{:S(2)}, u32[]{:S(2)}) collective-permute-start(bf16[32,1024]{1,0:T(8,128)(2,1)S(1)} %get-tuple-element.31), channel_id=1, source_target_pairs={{0,16},{4,20},{8,24},{12,28},{16,0},{20,4},{24,8},{28,12},{1,17},{... | collective-permute-start | bytes 196616 | tf_op jit(solution)/shard_map/ppermute | solution.py:224
  28.4 0.7 copy-start.4
  28.5 0.7 copy-start.12
  29.6 12.0 %copy-start.7 = (f32[8,128]{1,0:T(8,128)S(1)}, f32[8,128]{1,0:T(8,128)}, u32[]{:S(2)}) copy-start(f32[8,128]{1,0:T(8,128)} %refs_5_.1) | copy-start | bytes 12292
  29.6 12.0 %copy-start.6 = (f32[8,128]{1,0:T(8,128)S(1)}, f32[8,128]{1,0:T(8,128)}, u32[]{:S(2)}) copy-start(f32[8,128]{1,0:T(8,128)} %refs_4_.1) | copy-start | bytes 12292
  29.6 9.3 %collective-permute-start.7 = (bf16[32,1024]{1,0:T(8,128)(2,1)S(1)}, bf16[32,1024]{1,0:T(8,128)(2,1)S(1)}, u32[]{:S(2)}, u32[]{:S(2)}) collective-permute-start(bf16[32,1024]{1,0:T(8,128)(2,1)S(1)} %get-tuple-element.32), channel_id=1, source_target_pairs={{0,20},{4,16},{8,28},{12,24},{16,4},{20,0},{24,12},{28,8},{1,21},{... | collective-permute-start | bytes 196616 | tf_op jit(solution)/shard_map/ppermute | solution.py:224
  31.0 8.0 %collective-permute-start.8 = (bf16[32,1024]{1,0:T(8,128)(2,1)S(1)}, bf16[32,1024]{1,0:T(8,128)(2,1)S(1)}, u32[]{:S(2)}, u32[]{:S(2)}) collective-permute-start(bf16[32,1024]{1,0:T(8,128)(2,1)S(1)} %get-tuple-element.33), channel_id=1, source_target_pairs={{0,24},{4,28},{8,16},{12,20},{16,8},{20,12},{24,0},{28,4},{1,25},{... | collective-permute-start | bytes 196616 | tf_op jit(solution)/shard_map/ppermute | solution.py:224
  34.6 7.0 %collective-permute-start.9 = (bf16[32,1024]{1,0:T(8,128)(2,1)S(1)}, bf16[32,1024]{1,0:T(8,128)(2,1)S(1)}, u32[]{:S(2)}, u32[]{:S(2)}) collective-permute-start(bf16[32,1024]{1,0:T(8,128)(2,1)S(1)} %get-tuple-element.34), channel_id=1, source_target_pairs={{0,28},{4,24},{8,20},{12,16},{16,12},{20,8},{24,4},{28,0},{1,29},{... | collective-permute-start | bytes 196616 | tf_op jit(solution)/shard_map/ppermute | solution.py:224
  41.6 1.0 %copy-start.2 = (bf16[256,1024]{1,0:T(8,128)(2,1)S(1)}, bf16[256,1024]{1,0:T(8,128)(2,1)}, u32[]{:S(2)}) copy-start(bf16[256,1024]{1,0:T(8,128)(2,1)} %refs_7_) | copy-start | bytes 1572868
  42.6 5.2 %copy-start.3 = (bf16[512,512]{1,0:T(8,128)(2,1)S(1)}, bf16[512,512]{1,0:T(8,128)(2,1)}, u32[]{:S(2)}) copy-start(bf16[512,512]{1,0:T(8,128)(2,1)} %refs_6_) | copy-start | bytes 1572868
  47.8 11.4 %collective-permute-start.11 = (bf16[512,512]{1,0:T(8,128)(2,1)S(1)}, bf16[512,512]{1,0:T(8,128)(2,1)S(1)}, u32[]{:S(2)}, u32[]{:S(2)}) collective-permute-start(bf16[512,512]{1,0:T(8,128)(2,1)S(1)} %copy-done.3), channel_id=1, source_target_pairs={{0,1},{1,0},{2,3},{3,2},{4,5},{5,4},{6,7},{7,6},{8,9},{9,8},{10,11... | collective-permute-start | bytes 1572872 | tf_op jit(solution)/shard_map/ppermute | solution.py:224
  47.9 11.3 %collective-permute-start.12 = (bf16[512,512]{1,0:T(8,128)(2,1)S(1)}, bf16[512,512]{1,0:T(8,128)(2,1)S(1)}, u32[]{:S(2)}, u32[]{:S(2)}) collective-permute-start(bf16[512,512]{1,0:T(8,128)(2,1)S(1)} %collective-permute-done.10.refs_8_), channel_id=1, source_target_pairs={{0,1},{1,0},{2,3},{3,2},{4,5},{5,4},{6,7},{7,6},{8,9},{9,8},{10,11... | collective-permute-start | bytes 1572872 | tf_op jit(solution)/shard_map/ppermute | solution.py:224
  48.4 10.8 %all-to-all-start = ((bf16[32,16,128]{2,1,0:T(8,128)(2,1)}), bf16[32,16,128]{2,1,0:T(8,128)(2,1)S(1)}, u32[]{:S(2)}, u32[]{:S(2)}) async-start(bf16[32,16,128]{2,1,0:T(8,128)(2,1)} %bitcast.4), calls=%async_computation | async-start | bytes 262144 | tf_op jit(solution)/shard_map/all_to_all | solution.py:306
  59.2 0.7 copy-start.9
  59.2 0.7 copy-start.8
  59.2 0.7 copy-start.10

commit v3 on v2

--- a/solution.py
+++ b/solution.py
@@ -22,7 +22,7 @@
     return lax.dot_general(a, b, (dims, ((), ())), preferred_element_type=F32)
 
 
-def call(kernel, outs, ins, scratch=()):
+def call(kernel, outs, ins, scratch=(), vmem_mib=48):
     fetched = [i for i, (space, _) in enumerate(ins) if space == "f"]
 
     def body(*refs):
@@ -49,18 +49,17 @@
         scratch_shapes=list(scratch)
         + [pltpu.VMEM(ins[i][1].shape, ins[i][1].dtype) for i in fetched]
         + [pltpu.SemaphoreType.DMA((max(1, len(fetched)),))],
-        compiler_params=pltpu.CompilerParams(vmem_limit_bytes=48 * 1024 * 1024),
+        compiler_params=pltpu.CompilerParams(vmem_limit_bytes=vmem_mib * 1024 * 1024),
     )(*[array for _, array in ins])
 
 
-def halo_kernel(ready, me_ref, count_ref, rows_ref, feats_ref, *out_refs):
+def halo_kernel(ready, count_ref, rows_ref, feats_ref, out_ref):
     doms, block = rows_ref.shape
     at = lax.broadcasted_iota(jnp.int32, (1, block), 1)
     ready()
-    pieces = []
-    for k in range(doms):
-        s = me_ref[0] ^ k
-        pieces.append(jnp.where(at < count_ref[0, s], rows_ref[pl.ds(s, 1), :], -1))
+    pieces = [
+        jnp.where(at < count_ref[:, s : s + 1], rows_ref[s : s + 1, :], -1) for s in range(doms)
+    ]
     flat = jnp.concatenate(pieces, axis=1)
     total = doms * block
     nodes = feats_ref.shape[0]
@@ -72,11 +71,8 @@
         lax.broadcasted_iota(jnp.int32, (16, 128), 1) == 0
     )
     mark = jnp.where(mark_at, DEAD, 0.0).astype(BF16)
-    head = (rows[:, :128] + dot(dead, mark, ((0,), (0,)))).astype(BF16)
-    tail = rows[:, 128:].astype(BF16)
-    for k, out_ref in enumerate(out_refs):
-        out_ref[:, :128] = head[k * block : (k + 1) * block, :]
-        out_ref[:, 128:] = tail[k * block : (k + 1) * block, :]
+    out_ref[:, :128] = (rows[:, :128] + dot(dead, mark, ((0,), (0,)))).astype(BF16)
+    out_ref[:, 128:] = rows[:, 128:].astype(BF16)
 
 
 def count_kernel(ready, neigh_ref, degree_ref, out_ref):
@@ -117,12 +113,11 @@
 
 
 def attend_kernel(
-    shard_count, ready, at_ref, block_at_ref, own_ref, count_ref, src_ref, dst_ref, ends_ref, *rest
+    shard_count, ready, at_ref, own_ref, got_ref, count_ref, src_ref, dst_ref, ends_ref, *rest
 ):
-    shards, blocks = rest[:shard_count], rest[shard_count:-8]
-    out_ref, send_ref, proj_ref, stage_ref, weight_ref, sems, got_ref, block_sems = rest[-8:]
+    shards = rest[:shard_count]
+    out_ref, send_ref, proj_ref, stage_ref, weight_ref, sems = rest[shard_count:]
     copies = load_shards(at_ref, shards, weight_ref, sems)
-    copies += load_shards(block_at_ref, blocks, got_ref, block_sems)
     ready()
     nodes, width = own_ref.shape
     heads, size = src_ref.shape
@@ -261,15 +256,17 @@
     everyone = ("dom", "edge")
     shape = jax.ShapeDtypeStruct
 
-    dom_at = (lax.axis_index("dom") ^ jnp.arange(dom_count)).astype(jnp.int32)
     shard_at = (lax.axis_index("edge") ^ jnp.arange(edge_count)).astype(jnp.int32)
     gat_across = across(gat_weight, edge_count)
-    blocks = call(
+    send_rows = call(
         halo_kernel,
-        [shape((block, width), BF16)] * dom_count,
-        [("s", dom_at), ("s", halo_count[0]), ("f", halo_rows[0, 0]), ("f", node_feats)],
-    )
-    blocks = [blocks[0]] + [swap(blocks[k], "dom", k) for k in range(1, dom_count)]
+        shape((halo, width), BF16),
+        [("f", halo_count[0]), ("f", halo_rows[0, 0]), ("f", node_feats)],
+        vmem_mib=60,
+    )
+    send_rows, *gat_across = lax.optimization_barrier((send_rows, *gat_across))
+    got_rows = lax.all_to_all(send_rows, "dom", split_axis=0, concat_axis=0, tiled=True)
+    mlp_weight, *gat_across = lax.optimization_barrier((mlp_weight, *gat_across))
     gat_shards = from_core(gat_across)
     counts = call(
         count_kernel,
@@ -277,28 +274,25 @@
         [("f", neighbours.T), ("f", degree.reshape(1, nodes))],
     )
     ends_flat = endpoint_rows.reshape(1, slots)
-    mlp_weight, *gat_shards = lax.optimization_barrier((mlp_weight, *gat_shards))
     mlp_across = across(mlp_weight, edge_count)
     node_out, send_ends = call(
         functools.partial(attend_kernel, edge_count),
         (shape((nodes, width), BF16), shape((slots * pieces, 128), BF16)),
         [
             ("s", shard_at),
-            ("s", dom_at),
             ("f", node_feats),
-            ("v", counts),
+            ("f", got_rows),
+            ("f", counts),
             ("f", attn_src),
             ("f", attn_dst),
-            ("v", ends_flat),
+            ("f", ends_flat),
         ]
-        + [("any", w) for w in gat_shards + list(blocks)],
+        + [("any", w) for w in gat_shards],
         [
             pltpu.VMEM((table, width), BF16),
             pltpu.VMEM((slots * pieces, 128), F32),
             pltpu.VMEM((width, width), BF16),
             pltpu.SemaphoreType.DMA((edge_count,)),
-            pltpu.VMEM((halo, width), BF16),
-            pltpu.SemaphoreType.DMA((dom_count,)),
         ],
     )
     send_ends, *mlp_across = lax.optimization_barrier((send_ends, *mlp_across))
@@ -310,7 +304,7 @@
         [
             ("s", shard_at),
             ("s", cand_count),
-            ("v", got_ends),
+            ("f", got_ends),
             ("f", cand_ends[0, 0]),
             ("f", labels[0]),
             ("f", out_weight.reshape(1, hidden)),
@@ -327,7 +321,7 @@
     node_grad = call(
         scatter_kernel,
         shape((nodes, width), F32),
-        [("v", ends_flat), ("v", got_back)],
+        [("f", ends_flat), ("f", got_back)],
         [pltpu.VMEM((slots * pieces, 128), F32)],
     )
     return (node_out, scores.reshape(1, 1, cands), node_grad)

time: 74.9 us -> 70 us (0.935)
  starting transfers between devices: 19.2 us -> 15.5 us
  local copies, waits for them, and re-layouts: 4.25 us -> 1.58 us
  Pallas kernels: 11.3 us -> 13.5 us
  waiting for transfers between devices: 28.5 us -> 27.6 us
    ppermute x13 -> x6, waiting for transfers between devices: 20.9 us -> 9.78 us  [swap(): return lax.ppermute(array, axis, [(i, i ^ k) for i in range(count)])]
    ppermute x13 -> x6, starting transfers between devices: 16.6 us -> 5.69 us  [swap(): return lax.ppermute(array, axis, [(i, i ^ k) for i in range(count)])]
    all_to_all x0 -> x1, waiting for transfers between devices: none -> 10.2 us  [local(): lax.all_to_all(send_rows, 'dom', split_axis=0, concat_axis=0, tiled=True)]
    all_to_all x0 -> x1, starting transfers between devices: none -> 6.16 us  [local(): lax.all_to_all(send_rows, 'dom', split_axis=0, concat_axis=0, tiled=True)]
    unnamed x29 -> x23, local copies, waits for them, and re-layouts: 4.15 us -> 1.47 us
    pallas_call x5, Pallas kernels: 11.3 us -> 13.5 us  [call(): pl.pallas_call(body, out_shape=outs, in_specs=[SPACES['any' if space == '...]
    all_to_all x1, starting transfers between devices: 2.58 us -> 3.67 us  [local(): lax.all_to_all(send_ends, everyone, split_axis=0, concat_axis=0, tiled=True)]
  transfers between devices with their start and end apart: 14 -> 8, of which waited for: 5 -> 3; matrix products, arithmetic and copies ran while one was open for 0% -> 0% of each run, Pallas kernels for 9% -> 12%
where the time goes in v3:
time: 70 us; the launch traced here: 69.6 us
  waiting for transfers between devices  27.6 us (39%)
  starting transfers between devices  15.5 us (22%)
  Pallas kernels  13.5 us (19%)
  blocking collectives  10 us (14%)
  local copies, waits for them, and re-layouts  1.58 us (2%)
  between operations  1.41 us (2%)
    pallas_call x5, Pallas kernels, call(): pl.pallas_call(body, out_shape=outs, in_specs=[SPACES['any' if space == '...  13.5 us
    all_to_all x1, waiting for transfers between devices, local(): lax.all_to_all(send_rows, 'dom', split_axis=0, concat_axis=0, tiled=True)  10.2 us
    all_to_all x1, blocking collectives, local(): lax.all_to_all(send_back, everyone, split_axis=0, concat_axis=0, tiled=True)  10 us
    ppermute x6, waiting for transfers between devices, swap(): return lax.ppermute(array, axis, [(i, i ^ k) for i in range(count)])  9.78 us
    all_to_all x1, waiting for transfers between devices, local(): lax.all_to_all(send_ends, everyone, split_axis=0, concat_axis=0, tiled=True)  7.58 us
    all_to_all x1, starting transfers between devices, local(): lax.all_to_all(send_rows, 'dom', split_axis=0, concat_axis=0, tiled=True)  6.16 us
    ppermute x6, starting transfers between devices, swap(): return lax.ppermute(array, axis, [(i, i ^ k) for i in range(count)])  5.69 us
    all_to_all x1, starting transfers between devices, local(): lax.all_to_all(send_ends, everyone, split_axis=0, concat_axis=0, tiled=True)  3.67 us
  transfers between devices with their start and end apart: 8, of which 3 were waited for; matrix products, arithmetic and copies ran while one was open for 0% of the time, Pallas kernels for 12%

profile of v3, /device:TPU:0, one launch (start us, length us, event | category | flops | bytes accessed | tf_op | source)
XLA Modules:
  0.0 69.6 jit_solution(7646392220554326078)
XLA Ops:
  0.6 3.0 %collective-permute-start = (bf16[256,1024]{1,0:T(8,128)(2,1)}, bf16[256,1024]{1,0:T(8,128)(2,1)S(1)}, u32[]{:S(2)}, u32[]{:S(2)}) collective-permute-start(bf16[256,1024]{1,0:T(8,128)(2,1)} %refs_7_), channel_id=1, source_target_pairs={{0,2},{1,3},{2,0},{3,1},{4,6},{5,7},{6,4},{7,5},{8,10},{9,11},{10,... | collective-permute-start | bytes 1572872 | tf_op jit(solution)/shard_map/ppermute | solution.py:219
  3.7 2.4 %shard_map.157 = bf16[256,1024]{1,0:T(8,128)(2,1)} custom-call(s32[1,8]{1,0:T(1,128)} %bitcast.25, s32[8,32]{1,0:T(8,128)} %bitcast.24, bf16[128,1024]{1,0:T(8,128)(2,1)} %refs_1_.2), custom_call_target="tpu_custom_call" | custom-call | tf_op jit(solution)/shard_map/pallas_call | solution.py:44
  6.0 9.8 %collective-permute-done.refs_9_ = bf16[256,1024]{1,0:T(8,128)(2,1)S(1)} collective-permute-done((bf16[256,1024]{1,0:T(8,128)(2,1)}, bf16[256,1024]{1,0:T(8,128)(2,1)S(1)}, u32[]{:S(2)}, u32[]{:S(2)}) %collective-permute-start) | collective-permute-done | bytes 524320 | tf_op jit(solution)/shard_map/ppermute | solution.py:219
  15.8 6.2 %all-to-all-start = ((bf16[8,32,1024]{2,1,0:T(8,128)(2,1)}), bf16[8,32,1024]{2,1,0:T(8,128)(2,1)S(1)}, u32[]{:S(2)}, u32[]{:S(2)}) async-start(bf16[8,32,1024]{2,1,0:T(8,128)(2,1)} %bitcast.23), calls=%async_computation | async-start | bytes 1048576 | tf_op jit(solution)/shard_map/all_to_all | solution.py:268
  22.0 0.1 collective-permute-start.1
  22.0 0.5 collective-permute-start.2
  22.5 1.5 %collective-permute-start.3 = (bf16[512,512]{1,0:T(8,128)(2,1)S(1)}, bf16[512,512]{1,0:T(8,128)(2,1)S(1)}, u32[]{:S(2)}, u32[]{:S(2)}) collective-permute-start(bf16[512,512]{1,0:T(8,128)(2,1)S(1)} %copy-done.1), channel_id=1, source_target_pairs={{0,2},{1,3},{2,0},{3,1},{4,6},{5,7},{6,4},{7,5},{8,10},{9,11},{10,... | collective-permute-start | bytes 1572872 | tf_op jit(solution)/shard_map/ppermute | solution.py:219
  24.1 0.1 copy.18
  24.2 0.1 reshape.25.refs_6_.refs_0_
  24.3 0.0 copy-start.9
  24.3 0.6 copy-done.3
  24.9 0.1 copy-done.9
  25.0 0.4 shard_map.158.refs_3_
  25.4 0.0 collective-permute-done.1.refs_8_
  25.4 0.0 collective-permute-done.2.refs_10_
  25.4 10.2 %all-to-all-done = bf16[8,32,1024]{2,1,0:T(8,128)(2,1)S(1)} async-done(((bf16[8,32,1024]{2,1,0:T(8,128)(2,1)}), bf16[8,32,1024]{2,1,0:T(8,128)(2,1)S(1)}, u32[]{:S(2)}, u32[]{:S(2)}) %all-to-all-start) | async-done | bytes 524320 | tf_op jit(solution)/shard_map/all_to_all | solution.py:268
  35.6 5.7 %shard_map.159 = (bf16[128,1024]{1,0:T(8,128)(2,1)}, bf16[512,128]{1,0:T(8,128)(2,1)}) custom-call(s32[4]{0:T(128)S(1)} %iota_xor_fusion.refs_0_, bf16[128,1024]{1,0:T(8,128)(2,1)S(1)} %copy-done, bf16[256,1024]{1,0:T(8,128)(2,1)S(1)} %bitcast.14, f32[128,384]{1,0:T(8,128)S(1)} %shard_map.158.refs_3_, f32[8,128]{1,0:T(8,128)S(1)} %copy-done.4, ...), custom_call_target="tpu_custom_call" | custom-call | tf_op jit(solution)/shard_map/pallas_call | solution.py:44
  41.4 0.0 collective-permute-done.3.refs_8_
  41.4 0.1 collective-permute-start.4
  41.5 0.5 collective-permute-start.5
  42.0 3.7 %all-to-all-start.1 = ((bf16[32,16,128]{2,1,0:T(8,128)(2,1)}), bf16[32,16,128]{2,1,0:T(8,128)(2,1)S(1)}, u32[]{:S(2)}, u32[]{:S(2)}) async-start(bf16[32,16,128]{2,1,0:T(8,128)(2,1)} %bitcast.6), calls=%async_computation.1 | async-start | bytes 262144 | tf_op jit(solution)/shard_map/all_to_all | solution.py:300
  46.3 7.6 %all-to-all-done.1 = bf16[32,16,128]{2,1,0:T(8,128)(2,1)S(1)} async-done(((bf16[32,16,128]{2,1,0:T(8,128)(2,1)}), bf16[32,16,128]{2,1,0:T(8,128)(2,1)S(1)}, u32[]{:S(2)}, u32[]{:S(2)}) %all-to-all-start.1) | async-done | bytes 131104 | tf_op jit(solution)/shard_map/all_to_all | solution.py:300
  53.9 0.0 collective-permute-done.4.refs_7_
  53.9 0.0 collective-permute-done.5.refs_9_
  53.9 0.0 copy-start.6
  53.9 0.0 copy-start.8
  53.9 0.7 copy-done.7
  54.6 0.0 copy-done.6
  54.6 0.0 copy-done.8
  54.6 3.8 %shard_map.160 = (f32[1,256]{1,0:T(1,128)}, bf16[512,128]{1,0:T(8,128)(2,1)S(1)}) custom-call(s32[4]{0:T(128)S(1)} %iota_xor_fusion.refs_0_, s32[1,1]{1,0:T(1,128)S(6)} %copy.19.refs_1_, bf16[512,128]{1,0:T(8,128)(2,1)S(1)} %bitcast.15, s32[2,256]{1,0:T(2,128)S(1)} %bitcast.19, s32[1,256]{1,0:T(1,128)S(1)} %bitcast.21, f32[1,512]{1,0:T(1,128)S(1)} %bitcast.20, ...), custom_call_target="tpu_custom_call" | custom-call | tf_op jit(solution)/shard_map/pallas_call | solution.py:44
  58.4 10.0 %all_to_all.33 = bf16[32,16,128]{2,1,0:T(8,128)(2,1)S(1)} all-to-all(bf16[32,16,128]{2,1,0:T(8,128)(2,1)S(1)} %bitcast.17), channel_id=1, replica_groups=mesh['dom'=8,'edge'=4] {'dom','edge'}, dimensions={0} | all-to-all | bytes 262144 | tf_op jit(solution)/shard_map/all_to_all | solution.py:320
  68.4 1.2 %shard_map.161 = f32[128,1024]{1,0:T(8,128)} custom-call(s32[1,64]{1,0:T(1,128)S(1)} %reshape.25.refs_6_.refs_0_, bf16[512,128]{1,0:T(8,128)(2,1)S(1)} %bitcast.16), custom_call_target="tpu_custom_call" | custom-call | tf_op jit(solution)/shard_map/pallas_call | solution.py:44
  (15 shorter events, 0.0 us)
Async XLA Ops:
  0.6 15.2 %collective-permute-start = (bf16[256,1024]{1,0:T(8,128)(2,1)}, bf16[256,1024]{1,0:T(8,128)(2,1)S(1)}, u32[]{:S(2)}, u32[]{:S(2)}) collective-permute-start(bf16[256,1024]{1,0:T(8,128)(2,1)} %refs_7_), channel_id=1, source_target_pairs={{0,2},{1,3},{2,0},{3,1},{4,6},{5,7},{6,4},{7,5},{8,10},{9,11},{10,... | collective-permute-start | bytes 1572872 | tf_op jit(solution)/shard_map/ppermute | solution.py:219
  3.7 18.3 %copy-start.2 = (bf16[256,1024]{1,0:T(8,128)(2,1)S(1)}, bf16[256,1024]{1,0:T(8,128)(2,1)}, u32[]{:S(2)}) copy-start(bf16[256,1024]{1,0:T(8,128)(2,1)} %refs_7_) | copy-start | bytes 1572868
  15.8 6.7 %copy-start.1 = (bf16[512,512]{1,0:T(8,128)(2,1)S(1)}, bf16[512,512]{1,0:T(8,128)(2,1)}, u32[]{:S(2)}) copy-start(bf16[512,512]{1,0:T(8,128)(2,1)} %refs_6_) | copy-start | bytes 1572868
  15.8 8.3 %copy-start.10 = (s32[1,1,8,4,2]{2,4,3,1,0:T(2,128)S(1)}, s32[1,1,8,4,2]{2,4,3,1,0:T(2,128)}, u32[]{:S(2)}) copy-start(s32[1,1,8,4,2]{2,4,3,1,0:T(2,128)} %param.22) | copy-start | bytes 772
  15.8 19.8 %copy-start = (bf16[128,1024]{1,0:T(8,128)(2,1)S(1)}, bf16[128,1024]{1,0:T(8,128)(2,1)}, u32[]{:S(2)}) copy-start(bf16[128,1024]{1,0:T(8,128)(2,1)} %refs_1_.2) | copy-start | bytes 786436
  15.8 19.8 %all-to-all-start = ((bf16[8,32,1024]{2,1,0:T(8,128)(2,1)}), bf16[8,32,1024]{2,1,0:T(8,128)(2,1)S(1)}, u32[]{:S(2)}, u32[]{:S(2)}) async-start(bf16[8,32,1024]{2,1,0:T(8,128)(2,1)} %bitcast.23), calls=%async_computation | async-start | bytes 1048576 | tf_op jit(solution)/shard_map/all_to_all | solution.py:268
  22.0 3.4 %collective-permute-start.1 = (bf16[256,1024]{1,0:T(8,128)(2,1)S(1)}, bf16[256,1024]{1,0:T(8,128)(2,1)}, u32[]{:S(2)}, u32[]{:S(2)}) collective-permute-start(bf16[256,1024]{1,0:T(8,128)(2,1)S(1)} %copy-done.2), channel_id=1, source_target_pairs={{0,1},{1,0},{2,3},{3,2},{4,5},{5,4},{6,7},{7,6},{8,9},{9,8},{10,11... | collective-permute-start | bytes 1572872 | tf_op jit(solution)/shard_map/ppermute | solution.py:219
  22.0 3.4 %collective-permute-start.2 = (bf16[256,1024]{1,0:T(8,128)(2,1)S(1)}, bf16[256,1024]{1,0:T(8,128)(2,1)}, u32[]{:S(2)}, u32[]{:S(2)}) collective-permute-start(bf16[256,1024]{1,0:T(8,128)(2,1)S(1)} %collective-permute-done.refs_9_), channel_id=1, source_target_pairs={{0,1},{1,0},{2,3},{3,2},{4,5},{5,4},{6,7},{7,6},{8,9},{9,8},{10,11... | collective-permute-start | bytes 1572872 | tf_op jit(solution)/shard_map/ppermute | solution.py:219
  22.5 18.8 %collective-permute-start.3 = (bf16[512,512]{1,0:T(8,128)(2,1)S(1)}, bf16[512,512]{1,0:T(8,128)(2,1)S(1)}, u32[]{:S(2)}, u32[]{:S(2)}) collective-permute-start(bf16[512,512]{1,0:T(8,128)(2,1)S(1)} %copy-done.1), channel_id=1, source_target_pairs={{0,2},{1,3},{2,0},{3,1},{4,6},{5,7},{6,4},{7,5},{8,10},{9,11},{10,... | collective-permute-start | bytes 1572872 | tf_op jit(solution)/shard_map/ppermute | solution.py:219
  24.2 0.7 %copy-start.3 = (s32[128,16]{0,1:T(8,128)S(1)}, s32[128,16]{0,1:T(8,128)}, u32[]{:S(2)}) copy-start(s32[128,16]{0,1:T(8,128)} %param.18) | copy-start | bytes 24580
  24.3 0.7 copy-start.9
  24.9 10.7 %copy-start.4 = (f32[8,128]{1,0:T(8,128)S(1)}, f32[8,128]{1,0:T(8,128)}, u32[]{:S(2)}) copy-start(f32[8,128]{1,0:T(8,128)} %refs_4_.1) | copy-start | bytes 12292
  24.9 10.7 %copy-start.5 = (f32[8,128]{1,0:T(8,128)S(1)}, f32[8,128]{1,0:T(8,128)}, u32[]{:S(2)}) copy-start(f32[8,128]{1,0:T(8,128)} %refs_5_.1) | copy-start | bytes 12292
  41.4 12.5 %collective-permute-start.4 = (bf16[512,512]{1,0:T(8,128)(2,1)S(1)}, bf16[512,512]{1,0:T(8,128)(2,1)S(1)}, u32[]{:S(2)}, u32[]{:S(2)}) collective-permute-start(bf16[512,512]{1,0:T(8,128)(2,1)S(1)} %copy-done.1), channel_id=1, source_target_pairs={{0,1},{1,0},{2,3},{3,2},{4,5},{5,4},{6,7},{7,6},{8,9},{9,8},{10,11... | collective-permute-start | bytes 1572872 | tf_op jit(solution)/shard_map/ppermute | solution.py:219
  41.5 12.4 %collective-permute-start.5 = (bf16[512,512]{1,0:T(8,128)(2,1)S(1)}, bf16[512,512]{1,0:T(8,128)(2,1)S(1)}, u32[]{:S(2)}, u32[]{:S(2)}) collective-permute-start(bf16[512,512]{1,0:T(8,128)(2,1)S(1)} %collective-permute-done.3.refs_8_), channel_id=1, source_target_pairs={{0,1},{1,0},{2,3},{3,2},{4,5},{5,4},{6,7},{7,6},{8,9},{9,8},{10,11... | collective-permute-start | bytes 1572872 | tf_op jit(solution)/shard_map/ppermute | solution.py:219
  42.0 11.9 %all-to-all-start.1 = ((bf16[32,16,128]{2,1,0:T(8,128)(2,1)}), bf16[32,16,128]{2,1,0:T(8,128)(2,1)S(1)}, u32[]{:S(2)}, u32[]{:S(2)}) async-start(bf16[32,16,128]{2,1,0:T(8,128)(2,1)} %bitcast.6), calls=%async_computation.1 | async-start | bytes 262144 | tf_op jit(solution)/shard_map/all_to_all | solution.py:300
  53.9 0.7 copy-start.7
  53.9 0.7 copy-start.6
  53.9 0.7 copy-start.8

commit v4 on v3

--- a/solution.py
+++ b/solution.py
@@ -264,9 +264,9 @@
         [("f", halo_count[0]), ("f", halo_rows[0, 0]), ("f", node_feats)],
         vmem_mib=60,
     )
-    send_rows, *gat_across = lax.optimization_barrier((send_rows, *gat_across))
+    gat_across = lax.optimization_barrier((send_rows, *gat_across))[1:]
     got_rows = lax.all_to_all(send_rows, "dom", split_axis=0, concat_axis=0, tiled=True)
-    mlp_weight, *gat_across = lax.optimization_barrier((mlp_weight, *gat_across))
+    mlp_weight = lax.optimization_barrier((mlp_weight, *gat_across))[0]
     gat_shards = from_core(gat_across)
     counts = call(
         count_kernel,
@@ -295,7 +295,7 @@
             pltpu.SemaphoreType.DMA((edge_count,)),
         ],
     )
-    send_ends, *mlp_across = lax.optimization_barrier((send_ends, *mlp_across))
+    mlp_across = lax.optimization_barrier((send_ends, *mlp_across))[1:]
     mlp_shards = from_core(mlp_across)
     got_ends = lax.all_to_all(send_ends, everyone, split_axis=0, concat_axis=0, tiled=True)
     scores, send_back = call(

time: 70 us -> 61.1 us (0.87)
  waiting for transfers between devices: 27.6 us -> 18.2 us
    ppermute x6, waiting for transfers between devices: 9.78 us -> 3.8 us  [swap(): return lax.ppermute(array, axis, [(i, i ^ k) for i in range(count)])]
    all_to_all x1, waiting for transfers between devices: 10.2 us -> 6.87 us  [local(): lax.all_to_all(send_rows, 'dom', split_axis=0, concat_axis=0, tiled=True)]
  transfers between devices with their start and end apart: 8 -> 8, of which waited for: 3 -> 3; matrix products, arithmetic and copies ran while one was open for 0% -> 0% of each run, Pallas kernels for 12% -> 14%
where the time goes in v4:
time: 61.1 us; the launch traced here: 60.7 us
  waiting for transfers between devices  18.2 us (30%)
  starting transfers between devices  15.9 us (26%)
  Pallas kernels  13.5 us (22%)
  blocking collectives  9.99 us (16%)
  local copies, waits for them, and re-layouts  1.59 us (3%)
  between operations  1.43 us (2%)
    pallas_call x5, Pallas kernels, call(): pl.pallas_call(body, out_shape=outs, in_specs=[SPACES['any' if space == '...  13.5 us
    all_to_all x1, blocking collectives, local(): lax.all_to_all(send_back, everyone, split_axis=0, concat_axis=0, tiled=True)  9.99 us
    all_to_all x1, waiting for transfers between devices, local(): lax.all_to_all(send_ends, everyone, split_axis=0, concat_axis=0, tiled=True)  7.58 us
    all_to_all x1, waiting for transfers between devices, local(): lax.all_to_all(send_rows, 'dom', split_axis=0, concat_axis=0, tiled=True)  6.87 us
    all_to_all x1, starting transfers between devices, local(): lax.all_to_all(send_rows, 'dom', split_axis=0, concat_axis=0, tiled=True)  5.95 us
    ppermute x6, starting transfers between devices, swap(): return lax.ppermute(array, axis, [(i, i ^ k) for i in range(count)])  5.85 us
    all_to_all x1, starting transfers between devices, local(): lax.all_to_all(send_ends, everyone, split_axis=0, concat_axis=0, tiled=True)  4.1 us
    ppermute x6, waiting for transfers between devices, swap(): return lax.ppermute(array, axis, [(i, i ^ k) for i in range(count)])  3.8 us
  transfers between devices with their start and end apart: 8, of which 3 were waited for; matrix products, arithmetic and copies ran while one was open for 0% of the time, Pallas kernels for 14%

profile of v4, /device:TPU:0, one launch (start us, length us, event | category | flops | bytes accessed | tf_op | source)
XLA Modules:
  0.0 60.7 jit_solution(5236197863218475847)
XLA Ops:
  0.6 3.0 %collective-permute-start = (bf16[256,1024]{1,0:T(8,128)(2,1)}, bf16[256,1024]{1,0:T(8,128)(2,1)S(1)}, u32[]{:S(2)}, u32[]{:S(2)}) collective-permute-start(bf16[256,1024]{1,0:T(8,128)(2,1)} %refs_7_), channel_id=1, source_target_pairs={{0,2},{1,3},{2,0},{3,1},{4,6},{5,7},{6,4},{7,5},{8,10},{9,11},{10,... | collective-permute-start | bytes 1572872 | tf_op jit(solution)/shard_map/ppermute | solution.py:219
  3.7 2.4 %shard_map.157 = bf16[256,1024]{1,0:T(8,128)(2,1)} custom-call(s32[1,8]{1,0:T(1,128)} %bitcast.25, s32[8,32]{1,0:T(8,128)} %bitcast.24, bf16[128,1024]{1,0:T(8,128)(2,1)} %refs_1_.2), custom_call_target="tpu_custom_call" | custom-call | tf_op jit(solution)/shard_map/pallas_call | solution.py:44
  6.0 0.0 copy-start.1
  6.0 0.0 copy-start.10
  6.0 0.0 copy-start
  6.1 5.9 %all-to-all-start = ((bf16[8,32,1024]{2,1,0:T(8,128)(2,1)}), bf16[8,32,1024]{2,1,0:T(8,128)(2,1)S(1)}, u32[]{:S(2)}, u32[]{:S(2)}) async-start(bf16[8,32,1024]{2,1,0:T(8,128)(2,1)} %bitcast.23), calls=%async_computation | async-start | bytes 1048576 | tf_op jit(solution)/shard_map/all_to_all | solution.py:268
  12.0 3.8 %collective-permute-done.refs_9_ = bf16[256,1024]{1,0:T(8,128)(2,1)S(1)} collective-permute-done((bf16[256,1024]{1,0:T(8,128)(2,1)}, bf16[256,1024]{1,0:T(8,128)(2,1)S(1)}, u32[]{:S(2)}, u32[]{:S(2)}) %collective-permute-start) | collective-permute-done | bytes 524320 | tf_op jit(solution)/shard_map/ppermute | solution.py:219
  15.8 0.0 collective-permute-start.1
  15.8 0.5 collective-permute-start.2
  16.3 1.7 %collective-permute-start.3 = (bf16[512,512]{1,0:T(8,128)(2,1)S(1)}, bf16[512,512]{1,0:T(8,128)(2,1)S(1)}, u32[]{:S(2)}, u32[]{:S(2)}) collective-permute-start(bf16[512,512]{1,0:T(8,128)(2,1)S(1)} %copy-done.1), channel_id=1, source_target_pairs={{0,2},{1,3},{2,0},{3,1},{4,6},{5,7},{6,4},{7,5},{8,10},{9,11},{10,... | collective-permute-start | bytes 1572872 | tf_op jit(solution)/shard_map/ppermute | solution.py:219
  18.1 0.1 copy.18
  18.2 0.1 reshape.25.refs_6_.refs_0_
  18.3 0.0 copy-start.9
  18.3 0.6 copy-done.3
  18.9 0.1 copy-done.9
  18.9 0.4 shard_map.158.refs_3_
  19.4 6.9 %all-to-all-done = bf16[8,32,1024]{2,1,0:T(8,128)(2,1)S(1)} async-done(((bf16[8,32,1024]{2,1,0:T(8,128)(2,1)}), bf16[8,32,1024]{2,1,0:T(8,128)(2,1)S(1)}, u32[]{:S(2)}, u32[]{:S(2)}) %all-to-all-start) | async-done | bytes 524320 | tf_op jit(solution)/shard_map/all_to_all | solution.py:268
  26.3 0.0 collective-permute-done.1.refs_8_
  26.3 5.7 %shard_map.159 = (bf16[128,1024]{1,0:T(8,128)(2,1)}, bf16[512,128]{1,0:T(8,128)(2,1)}) custom-call(s32[4]{0:T(128)S(1)} %iota_xor_fusion.refs_0_, bf16[128,1024]{1,0:T(8,128)(2,1)S(1)} %copy-done, bf16[256,1024]{1,0:T(8,128)(2,1)S(1)} %bitcast.14, f32[128,384]{1,0:T(8,128)S(1)} %shard_map.158.refs_3_, f32[8,128]{1,0:T(8,128)S(1)} %copy-done.4, ...), custom_call_target="tpu_custom_call" | custom-call | tf_op jit(solution)/shard_map/pallas_call | solution.py:44
  32.0 0.0 collective-permute-done.3.refs_8_
  32.0 0.1 collective-permute-start.4
  32.1 0.5 collective-permute-start.5
  32.6 4.1 %all-to-all-start.1 = ((bf16[32,16,128]{2,1,0:T(8,128)(2,1)}), bf16[32,16,128]{2,1,0:T(8,128)(2,1)S(1)}, u32[]{:S(2)}, u32[]{:S(2)}) async-start(bf16[32,16,128]{2,1,0:T(8,128)(2,1)} %bitcast.6), calls=%async_computation.1 | async-start | bytes 262144 | tf_op jit(solution)/shard_map/all_to_all | solution.py:300
  37.4 7.6 %all-to-all-done.1 = bf16[32,16,128]{2,1,0:T(8,128)(2,1)S(1)} async-done(((bf16[32,16,128]{2,1,0:T(8,128)(2,1)}), bf16[32,16,128]{2,1,0:T(8,128)(2,1)S(1)}, u32[]{:S(2)}, u32[]{:S(2)}) %all-to-all-start.1) | async-done | bytes 131104 | tf_op jit(solution)/shard_map/all_to_all | solution.py:300
  45.0 0.0 copy-start.6
  45.0 0.0 copy-start.8
  45.0 0.7 %copy-done.7 = f32[512]{0:T(512)S(1)} copy-done((f32[512]{0:T(512)S(1)}, f32[512]{0:T(512)}, u32[]{:S(2)}) %copy-start.7) | copy-done | bytes 2072
  45.7 0.0 copy-done.6
  45.7 0.0 copy-done.8
  45.7 3.8 %shard_map.160 = (f32[1,256]{1,0:T(1,128)}, bf16[512,128]{1,0:T(8,128)(2,1)S(1)}) custom-call(s32[4]{0:T(128)S(1)} %iota_xor_fusion.refs_0_, s32[1,1]{1,0:T(1,128)S(6)} %copy.19.refs_1_, bf16[512,128]{1,0:T(8,128)(2,1)S(1)} %bitcast.15, s32[2,256]{1,0:T(2,128)S(1)} %bitcast.19, s32[1,256]{1,0:T(1,128)S(1)} %bitcast.21, f32[1,512]{1,0:T(1,128)S(1)} %bitcast.20, ...), custom_call_target="tpu_custom_call" | custom-call | tf_op jit(solution)/shard_map/pallas_call | solution.py:44
  49.5 10.0 %all_to_all.33 = bf16[32,16,128]{2,1,0:T(8,128)(2,1)S(1)} all-to-all(bf16[32,16,128]{2,1,0:T(8,128)(2,1)S(1)} %bitcast.17), channel_id=1, replica_groups=mesh['dom'=8,'edge'=4] {'dom','edge'}, dimensions={0} | all-to-all | bytes 262144 | tf_op jit(solution)/shard_map/all_to_all | solution.py:320
  59.5 1.2 %shard_map.161 = f32[128,1024]{1,0:T(8,128)} custom-call(s32[1,64]{1,0:T(1,128)S(1)} %reshape.25.refs_6_.refs_0_, bf16[512,128]{1,0:T(8,128)(2,1)S(1)} %bitcast.16), custom_call_target="tpu_custom_call" | custom-call | tf_op jit(solution)/shard_map/pallas_call | solution.py:44
  (15 shorter events, 0.0 us)
Async XLA Ops:
  0.6 15.2 %collective-permute-start = (bf16[256,1024]{1,0:T(8,128)(2,1)}, bf16[256,1024]{1,0:T(8,128)(2,1)S(1)}, u32[]{:S(2)}, u32[]{:S(2)}) collective-permute-start(bf16[256,1024]{1,0:T(8,128)(2,1)} %refs_7_), channel_id=1, source_target_pairs={{0,2},{1,3},{2,0},{3,1},{4,6},{5,7},{6,4},{7,5},{8,10},{9,11},{10,... | collective-permute-start | bytes 1572872 | tf_op jit(solution)/shard_map/ppermute | solution.py:219
  3.7 12.1 %copy-start.2 = (bf16[256,1024]{1,0:T(8,128)(2,1)S(1)}, bf16[256,1024]{1,0:T(8,128)(2,1)}, u32[]{:S(2)}) copy-start(bf16[256,1024]{1,0:T(8,128)(2,1)} %refs_7_) | copy-start | bytes 1572868
  6.0 10.3 %copy-start.1 = (bf16[512,512]{1,0:T(8,128)(2,1)S(1)}, bf16[512,512]{1,0:T(8,128)(2,1)}, u32[]{:S(2)}) copy-start(bf16[512,512]{1,0:T(8,128)(2,1)} %refs_6_) | copy-start | bytes 1572868
  6.0 12.0 %copy-start.10 = (s32[1,1,8,4,2]{2,4,3,1,0:T(2,128)S(1)}, s32[1,1,8,4,2]{2,4,3,1,0:T(2,128)}, u32[]{:S(2)}) copy-start(s32[1,1,8,4,2]{2,4,3,1,0:T(2,128)} %param.22) | copy-start | bytes 772
  6.0 20.2 %copy-start = (bf16[128,1024]{1,0:T(8,128)(2,1)S(1)}, bf16[128,1024]{1,0:T(8,128)(2,1)}, u32[]{:S(2)}) copy-start(bf16[128,1024]{1,0:T(8,128)(2,1)} %refs_1_.2) | copy-start | bytes 786436
  6.1 20.2 %all-to-all-start = ((bf16[8,32,1024]{2,1,0:T(8,128)(2,1)}), bf16[8,32,1024]{2,1,0:T(8,128)(2,1)S(1)}, u32[]{:S(2)}, u32[]{:S(2)}) async-start(bf16[8,32,1024]{2,1,0:T(8,128)(2,1)} %bitcast.23), calls=%async_computation | async-start | bytes 1048576 | tf_op jit(solution)/shard_map/all_to_all | solution.py:268
  15.8 10.5 %collective-permute-start.1 = (bf16[256,1024]{1,0:T(8,128)(2,1)S(1)}, bf16[256,1024]{1,0:T(8,128)(2,1)}, u32[]{:S(2)}, u32[]{:S(2)}) collective-permute-start(bf16[256,1024]{1,0:T(8,128)(2,1)S(1)} %copy-done.2), channel_id=1, source_target_pairs={{0,1},{1,0},{2,3},{3,2},{4,5},{5,4},{6,7},{7,6},{8,9},{9,8},{10,11... | collective-permute-start | bytes 1572872 | tf_op jit(solution)/shard_map/ppermute | solution.py:219
  15.8 10.5 %collective-permute-start.2 = (bf16[256,1024]{1,0:T(8,128)(2,1)S(1)}, bf16[256,1024]{1,0:T(8,128)(2,1)}, u32[]{:S(2)}, u32[]{:S(2)}) collective-permute-start(bf16[256,1024]{1,0:T(8,128)(2,1)S(1)} %collective-permute-done.refs_9_), channel_id=1, source_target_pairs={{0,1},{1,0},{2,3},{3,2},{4,5},{5,4},{6,7},{7,6},{8,9},{9,8},{10,11... | collective-permute-start | bytes 1572872 | tf_op jit(solution)/shard_map/ppermute | solution.py:219
  16.3 15.7 %collective-permute-start.3 = (bf16[512,512]{1,0:T(8,128)(2,1)S(1)}, bf16[512,512]{1,0:T(8,128)(2,1)S(1)}, u32[]{:S(2)}, u32[]{:S(2)}) collective-permute-start(bf16[512,512]{1,0:T(8,128)(2,1)S(1)} %copy-done.1), channel_id=1, source_target_pairs={{0,2},{1,3},{2,0},{3,1},{4,6},{5,7},{6,4},{7,5},{8,10},{9,11},{10,... | collective-permute-start | bytes 1572872 | tf_op jit(solution)/shard_map/ppermute | solution.py:219
  18.2 0.7 %copy-start.3 = (s32[128,16]{0,1:T(8,128)S(1)}, s32[128,16]{0,1:T(8,128)}, u32[]{:S(2)}) copy-start(s32[128,16]{0,1:T(8,128)} %param.18) | copy-start | bytes 24580
  18.3 0.7 %copy-start.9 = (s32[128]{0:T(128)S(1)}, s32[128]{0:T(128)}, u32[]{:S(2)}) copy-start(s32[128]{0:T(128)} %param.19) | copy-start | bytes 1540
  18.9 7.3 %copy-start.4 = (f32[8,128]{1,0:T(8,128)S(1)}, f32[8,128]{1,0:T(8,128)}, u32[]{:S(2)}) copy-start(f32[8,128]{1,0:T(8,128)} %refs_4_.1) | copy-start | bytes 12292
  18.9 7.3 %copy-start.5 = (f32[8,128]{1,0:T(8,128)S(1)}, f32[8,128]{1,0:T(8,128)}, u32[]{:S(2)}) copy-start(f32[8,128]{1,0:T(8,128)} %refs_5_.1) | copy-start | bytes 12292
  32.0 12.9 %collective-permute-start.4 = (bf16[512,512]{1,0:T(8,128)(2,1)S(1)}, bf16[512,512]{1,0:T(8,128)(2,1)S(1)}, u32[]{:S(2)}, u32[]{:S(2)}) collective-permute-start(bf16[512,512]{1,0:T(8,128)(2,1)S(1)} %copy-done.1), channel_id=1, source_target_pairs={{0,1},{1,0},{2,3},{3,2},{4,5},{5,4},{6,7},{7,6},{8,9},{9,8},{10,11... | collective-permute-start | bytes 1572872 | tf_op jit(solution)/shard_map/ppermute | solution.py:219
  32.1 12.8 %collective-permute-start.5 = (bf16[512,512]{1,0:T(8,128)(2,1)S(1)}, bf16[512,512]{1,0:T(8,128)(2,1)S(1)}, u32[]{:S(2)}, u32[]{:S(2)}) collective-permute-start(bf16[512,512]{1,0:T(8,128)(2,1)S(1)} %collective-permute-done.3.refs_8_), channel_id=1, source_target_pairs={{0,1},{1,0},{2,3},{3,2},{4,5},{5,4},{6,7},{7,6},{8,9},{9,8},{10,11... | collective-permute-start | bytes 1572872 | tf_op jit(solution)/shard_map/ppermute | solution.py:219
  32.6 12.3 %all-to-all-start.1 = ((bf16[32,16,128]{2,1,0:T(8,128)(2,1)}), bf16[32,16,128]{2,1,0:T(8,128)(2,1)S(1)}, u32[]{:S(2)}, u32[]{:S(2)}) async-start(bf16[32,16,128]{2,1,0:T(8,128)(2,1)} %bitcast.6), calls=%async_computation.1 | async-start | bytes 262144 | tf_op jit(solution)/shard_map/all_to_all | solution.py:300
  45.0 0.7 %copy-start.7 = (f32[512]{0:T(512)S(1)}, f32[512]{0:T(512)}, u32[]{:S(2)}) copy-start(f32[512]{0:T(512)} %param.27) | copy-start | bytes 6148
  45.0 0.7 %copy-start.6 = (s32[1,1,2,256]{3,2,1,0:T(2,128)S(1)}, s32[1,1,2,256]{3,2,1,0:T(2,128)}, u32[]{:S(2)}) copy-start(s32[1,1,2,256]{3,2,1,0:T(2,128)} %param.23) | copy-start | bytes 6148
  45.0 0.7 %copy-start.8 = (s32[1,1,256]{2,1,0:T(1,128)S(1)}, s32[1,1,256]{2,1,0:T(1,128)}, u32[]{:S(2)}) copy-start(s32[1,1,256]{2,1,0:T(1,128)} %param.25) | copy-start | bytes 3076

commit v5 on v2

v5 whole, which is shorter than its diff:
```python
import functools

import jax
import jax.numpy as jnp
from jax import lax
from jax.experimental import pallas as pl
from jax.experimental.pallas import tpu as pltpu
from jax.sharding import PartitionSpec as P

F32 = jnp.float32
BF16 = jnp.bfloat16
LOG2_E = 1.4426950408889634
DEAD = 64.0
VMEM = pl.BlockSpec(memory_space=pltpu.VMEM)
SPACES = {
    "v": VMEM,
    "s": pl.BlockSpec(memory_space=pltpu.SMEM),
    "f": pl.BlockSpec(memory_space=pl.ANY),
}


def dot(a, b, dims=((1,), (0,))):
    return lax.dot_general(a, b, (dims, ((), ())), preferred_element_type=F32)


def call(kernel, outs, ins, scratch=(), vmem_mib=48):
    fetched = [i for i, (space, _) in enumerate(ins) if space == "f"]

    def body(*refs):
        refs = list(refs)
        local_count = len(fetched) + 1
        own, (held, sems) = refs[:-local_count], (refs[-local_count:-1], refs[-1])
        copies = []
        for n, i in enumerate(fetched):
            copies.append(pltpu.make_async_copy(own[i], held[n], sems.at[n]))
            copies[-1].start()
            own[i] = held[n]

        def ready():
            for copy in copies:
                copy.wait()

        kernel(ready, *own)

    return pl.pallas_call(
        body,
        out_shape=outs,
        in_specs=[SPACES[space] for space, _ in ins],
        out_specs=jax.tree.map(lambda _: VMEM, outs),
        scratch_shapes=list(scratch)
        + [pltpu.VMEM(ins[i][1].shape, ins[i][1].dtype) for i in fetched]
        + [pltpu.SemaphoreType.DMA((max(1, len(fetched)),))],
        compiler_params=pltpu.CompilerParams(vmem_limit_bytes=vmem_mib * 1024 * 1024),
    )(*[array for _, array in ins])


def halo_kernel(ready, count_ref, rows_ref, feats_ref, *out_refs):
    doms, block = rows_ref.shape
    at = lax.broadcasted_iota(jnp.int32, (1, block), 1)
    me = lax.axis_index("dom")
    ready()
    pieces = []
    for k in range(doms):
        s = me ^ k
        pieces.append(jnp.where(at < count_ref[0, s], rows_ref[pl.ds(s, 1), :], -1))
    flat = jnp.concatenate(pieces, axis=1)
    total = doms * block
    nodes = feats_ref.shape[0]
    pick = (lax.broadcasted_iota(jnp.int32, (nodes, total), 0) == flat).astype(F32).astype(BF16)
    rows = dot(pick, feats_ref[...], ((0,), (0,)))
    first = lax.broadcasted_iota(jnp.int32, (16, total), 0) == 0
    dead = jnp.where(first & (flat < 0), 1.0, 0.0).astype(BF16)
    mark_at = (lax.broadcasted_iota(jnp.int32, (16, 128), 0) == 0) & (
        lax.broadcasted_iota(jnp.int32, (16, 128), 1) == 0
    )
    mark = jnp.where(mark_at, DEAD, 0.0).astype(BF16)
    head = (rows[:, :128] + dot(dead, mark, ((0,), (0,)))).astype(BF16)
    tail = rows[:, 128:].astype(BF16)
    for k, out_ref in enumerate(out_refs):
        out_ref[:, :128] = head[k * block : (k + 1) * block, :]
        out_ref[:, 128:] = tail[k * block : (k + 1) * block, :]


def block_diagonal(vectors):
    heads, size = vectors.shape
    wide = jnp.concatenate([vectors] * heads, axis=1)
    lane_head = lax.broadcasted_iota(jnp.int32, wide.shape, 1) // size
    wide = jnp.where(lane_head == lax.broadcasted_iota(jnp.int32, wide.shape, 0), wide, 0.0)
    high = wide.astype(BF16).astype(F32)
    middle = (wide - high).astype(BF16).astype(F32)
    low = (wide - high - middle).astype(BF16).astype(F32)
    return jnp.concatenate([high, middle, low, jnp.zeros_like(wide)], axis=0).astype(BF16)


def prepare_kernel(
    block,
    ready,
    live_ref,
    neigh_ref,
    degree_ref,
    src_ref,
    dst_ref,
    ends_ref,
    cand_ref,
    labels_ref,
    out_w_ref,
    gat_ref,
    mlp_ref,
    count_ref,
    factor_ref,
    diag_src_ref,
    diag_dst_ref,
    pick_ref,
    gather_ref,
    scatter_ref,
    known_ref,
    weight_ref,
    gat_own_ref,
    mlp_own_ref,
):
    ready()
    nodes, table = count_ref.shape
    slots = neigh_ref.shape[0]
    ids = neigh_ref[...]
    past = ids - nodes
    moved = nodes + ((past // block) ^ lax.axis_index("dom")) * block + past % block
    ids = jnp.where(ids < nodes, ids, moved)
    ids = jnp.where(lax.broadcasted_iota(jnp.int32, ids.shape, 0) < degree_ref[...], ids, -1)
    for base in range(0, table, nodes):
        at = base + lax.broadcasted_iota(jnp.int32, (nodes, nodes), 0)
        total = jnp.zeros((nodes, nodes), F32)
        if base == 0:
            total = (at == lax.broadcasted_iota(jnp.int32, (nodes, nodes), 1)).astype(F32)
        for j in range(slots):
            total = total + (at == ids[j : j + 1, :]).astype(F32)
        total = total.T
        power = jnp.where(total > 1, 2.0, total)
        power = jnp.where(total > 2, 4.0, power)
        power = jnp.where(total > 5, 8.0, power)
        power = jnp.where(total > 13, 16.0, power)
        count_ref[:, base : base + nodes] = total
        factor_ref[0, :, base : base + nodes] = power.astype(BF16)
        factor_ref[1, :, base : base + nodes] = (total - power).astype(BF16)
    diag_src_ref[...] = block_diagonal(src_ref[...])
    diag_dst_ref[...] = block_diagonal(dst_ref[...])
    ends = ends_ref.shape[1]
    node_at = lax.broadcasted_iota(jnp.int32, (nodes, ends), 0)
    pick_ref[...] = (node_at == ends_ref[...]).astype(F32).astype(BF16)
    cands = cand_ref.shape[1]
    slot_at = lax.broadcasted_iota(jnp.int32, (ends, cands), 0)
    for i in range(2):
        one_hot = (slot_at == cand_ref[i : i + 1, :]).astype(F32)
        scatter_ref[i] = one_hot.astype(BF16)
        gather_ref[i] = one_hot.T.astype(BF16)
    live = (lax.broadcasted_iota(jnp.int32, (1, cands), 1) < live_ref[0, 0]).astype(F32)
    known = jnp.concatenate([live, labels_ref[...].astype(F32), jnp.zeros((126, cands), F32)], axis=0)
    known_ref[...] = known.T
    weight_ref[...] = out_w_ref[...]
    gat_own_ref[...] = gat_ref[...]
    mlp_own_ref[...] = mlp_ref[...]


def shard_dots(rows_ref, shards, whole_ref=None):
    me = lax.axis_index("edge")
    depth = shards[0].shape[0]
    if depth % 128:
        for i, shard in enumerate(shards):
            whole_ref[pl.ds(pl.multiple_of((me ^ i) * depth, depth), depth), :] = shard[...]
        return dot(rows_ref[...], whole_ref[...])
    total = None
    for i, shard in enumerate(shards):
        cols = pl.ds(pl.multiple_of((me ^ i) * depth, depth), depth)
        part = dot(rows_ref[:, cols], shard[...])
        total = part if total is None else total + part
    return total


def attend_kernel(
    shard_count,
    ready,
    own_ref,
    count_ref,
    factor_ref,
    diag_src_ref,
    diag_dst_ref,
    pick_ref,
    *rest,
):
    shards, blocks = rest[:shard_count], rest[shard_count:-8]
    out_ref, send_ref, proj_ref, stage_ref, rows_ref, bias_ref, mix_ref, whole_ref = rest[-8:]
    ready()
    nodes, width = own_ref.shape
    table = proj_ref.shape[0]
    block = blocks[0].shape[0]
    heads = diag_src_ref.shape[0] // 4
    size = width // heads
    rows_ref[:nodes, :] = own_ref[...]
    for k, ref in enumerate(blocks):
        rows_ref[nodes + k * block : nodes + (k + 1) * block, :] = ref[...]
    proj_ref[...] = shard_dots(rows_ref, shards, whole_ref).astype(BF16)
    parts = dot(diag_src_ref[...], proj_ref[...], ((1,), (1,)))
    src = parts[:heads] + parts[heads : 2 * heads] + parts[2 * heads : 3 * heads]
    src = src.astype(BF16).astype(F32) * LOG2_E
    parts = dot(proj_ref[:nodes, :], diag_dst_ref[...], ((1,), (1,)))
    dst = parts[:, :heads] + parts[:, heads : 2 * heads] + parts[:, 2 * heads : 3 * heads]
    dst = dst * LOG2_E
    first_lane = (lax.broadcasted_iota(jnp.int32, (16, 128), 1) == 0).astype(F32).astype(BF16)
    mark = dot(first_lane, rows_ref[nodes:, :128], ((1,), (1,)))[:1]
    hide = jnp.where(mark < DEAD / 2, 0.0, -jnp.inf)
    hide = jnp.concatenate([jnp.zeros((1, nodes), F32), hide], axis=1)
    bias_ref[...] = jnp.where(count_ref[...] > 0, hide, -jnp.inf)
    chunk = 32
    for h in range(heads):
        for r in range(0, nodes, chunk):
            here = slice(r, r + chunk)
            logit = dst[here, h : h + 1] + src[h : h + 1, :]
            logit = jnp.maximum(logit, 0.2 * logit) + bias_ref[here, :]
            terms = jnp.exp2(logit - jnp.max(logit, axis=1, keepdims=True))
            running = jnp.sum(count_ref[here, :] * terms, axis=1, keepdims=True)
            weight = (terms * (1.0 / running)).astype(BF16)
            mix_ref[h % 2, here, :] = weight * factor_ref[0, here, :]
            mix_ref[h % 2, nodes + r : nodes + r + chunk, :] = weight * factor_ref[1, here, :]
        both = dot(mix_ref[h % 2], proj_ref[:, h * size : (h + 1) * size])
        total = both[:nodes] + both[nodes:]
        total = jnp.where(total > 0, total, jnp.exp(jnp.minimum(total, 0.0)) - 1.0)
        out_ref[:, h * size : (h + 1) * size] = total.astype(BF16)
    pack_rows(dot(pick_ref[...], out_ref[...], ((0,), (0,))), stage_ref, send_ref)


def pack_rows(rows, stage_ref, out_ref):
    slots, width = rows.shape
    pieces = width // 128
    for c in range(pieces):
        stage_ref[pl.ds(c, slots, stride=pieces), :] = rows[:, c * 128 : (c + 1) * 128]
    out_ref[...] = stage_ref[...].astype(BF16)


def unpack_rows(ref, stage_ref, pieces):
    stage_ref[...] = ref[...].astype(F32)
    slots = ref.shape[0] // pieces
    parts = [stage_ref[pl.ds(c, slots, stride=pieces), :] for c in range(pieces)]
    return jnp.concatenate(parts, axis=1).astype(BF16)


def score_kernel(
    shard_count, ready, got_ref, gather_ref, scatter_ref, known_ref, out_w_ref, *rest
):
    shards = rest[:shard_count]
    scores_ref, back_ref, pair_ref, stage_ref, sum_ref, grad_ref = rest[shard_count:]
    ready()
    cands = known_ref.shape[0]
    depth = shards[0].shape[0]
    slots, width = grad_ref.shape[1:]
    rows = unpack_rows(got_ref, stage_ref, width // 128)
    for i in range(2):
        pair_ref[:, i * width : (i + 1) * width] = dot(gather_ref[i], rows).astype(BF16)
    pre_act = shard_dots(pair_ref, shards)
    out_w = out_w_ref[...]
    live = known_ref[:, :1]
    gate = jax.nn.sigmoid(pre_act)
    score = jnp.sum(pre_act * gate * out_w, axis=1, keepdims=True) * live
    scores_ref[...] = jnp.broadcast_to(score, (cands, 128)).T[:1]
    grad_score = (jax.nn.sigmoid(score) - known_ref[:, 1:2]) * live
    grad_pre = (grad_score * out_w * (gate * (1.0 + pre_act * (1.0 - gate)))).astype(BF16)
    for i in range(2):
        total = dot(scatter_ref[i], grad_pre)
        high = total.astype(BF16)
        sum_ref[i, :slots, :] = high
        sum_ref[i, slots:, :] = (total - high.astype(F32)).astype(BF16)
    per_half = width // depth
    for i, shard in enumerate(shards):
        at = lax.axis_index("edge") ^ i
        half = at // per_half
        col = pl.multiple_of((at % per_half) * depth, depth)
        both = dot(sum_ref[half], shard[...], ((1,), (1,)))
        grad_ref[half, :, pl.ds(col, depth)] = both[:slots] + both[slots:]
    pack_rows(grad_ref[0] + grad_ref[1], stage_ref, back_ref)


def scatter_kernel(ready, pick_ref, got_ref, out_ref, stage_ref):
    ready()
    rows = unpack_rows(got_ref, stage_ref, out_ref.shape[1] // 128)
    out_ref[...] = dot(pick_ref[...], rows)


def swap(array, axis, k):
    count = lax.axis_size(axis)
    return lax.ppermute(array, axis, [(i, i ^ k) for i in range(count)])


def across(shard, edge_count):
    return [shard] + [swap(shard, "edge", 2 * k) for k in range(1, edge_count // 2)]


def from_core(shards):
    return [one for shard in shards for one in (shard, swap(shard, "edge", 1))]


def local(
    node_feats,
    gat_weight,
    attn_src,
    attn_dst,
    neighbours,
    degree,
    halo_rows,
    halo_count,
    endpoint_rows,
    cand_ends,
    cand_count,
    labels,
    mlp_weight,
    out_weight,
):
    nodes, width = node_feats.shape
    dom_count = lax.axis_size("dom")
    edge_count = lax.axis_size("edge")
    block = halo_rows.shape[-1]
    cands = labels.shape[-1]
    hidden = out_weight.shape[0]
    halo = dom_count * block
    table = nodes + halo
    slots = dom_count * edge_count * endpoint_rows.shape[-1]
    pieces = width // 128
    everyone = ("dom", "edge")
    shape = jax.ShapeDtypeStruct

    heads = attn_src.shape[0]
    gat_across = across(gat_weight, edge_count)
    blocks = call(
        halo_kernel,
        [shape((block, width), BF16)] * dom_count,
        [("s", halo_count[0]), ("f", halo_rows[0, 0]), ("f", node_feats)],
        vmem_mib=60,
    )
    far = range(dom_count // 2, dom_count)
    moved = {0: blocks[0]}
    for k in [*far, *range(1, dom_count // 2)]:
        moved[k] = swap(blocks[k], "dom", k)
    gat_across = lax.optimization_barrier((*gat_across, *[moved[k] for k in far]))[: len(gat_across)]
    held_mlp = lax.optimization_barrier((mlp_weight, *gat_across))[0]
    gat_shards = from_core(gat_across)
    prepared = call(
        functools.partial(prepare_kernel, block),
        (
            shape((nodes, table), F32),
            shape((2, nodes, table), BF16),
            shape((4 * heads, width), BF16),
            shape((4 * heads, width), BF16),
            shape((nodes, slots), BF16),
            shape((2, cands, slots), BF16),
            shape((2, slots, cands), BF16),
            shape((cands, 128), F32),
            shape((1, hidden), F32),
            shape(gat_weight.shape, BF16),
            shape(mlp_weight.shape, BF16),
        ),
        [
            ("s", cand_count),
            ("f", neighbours.T),
            ("f", degree.reshape(1, nodes)),
            ("f", attn_src),
            ("f", attn_dst),
            ("f", endpoint_rows.reshape(1, slots)),
            ("f", cand_ends[0, 0]),
            ("f", labels[0]),
            ("f", out_weight.reshape(1, hidden)),
            ("f", gat_weight),
            ("f", mlp_weight),
        ],
    )
    counts, factors, diag_src, diag_dst, pick, gather, scatter, known, out_row, *own = prepared
    gat_shards[0] = own[0]
    mlp_across = across(held_mlp, edge_count)
    packed = pltpu.VMEM((slots * pieces, 128), F32)
    node_out, send_ends = call(
        functools.partial(attend_kernel, edge_count),
        (shape((nodes, width), BF16), shape((slots * pieces, 128), BF16)),
        [
            ("v", node_feats),
            ("v", counts),
            ("v", factors),
            ("v", diag_src),
            ("v", diag_dst),
            ("v", pick),
        ]
        + [("v", w) for w in gat_shards]
        + [("v", moved[k]) for k in range(dom_count)],
        [
            pltpu.VMEM((table, width), BF16),
            packed,
            pltpu.VMEM((table, width), BF16),
            pltpu.VMEM((nodes, table), F32),
            pltpu.VMEM((2, 2 * nodes, table), BF16),
            pltpu.VMEM((width if width // edge_count % 128 else 16, width), BF16),
        ],
    )
    mlp_across = lax.optimization_barrier((send_ends, *mlp_across))[1:]
    mlp_shards = from_core(mlp_across)
    mlp_shards[0] = own[1]
    got_ends = lax.all_to_all(send_ends, everyone, split_axis=0, concat_axis=0, tiled=True)
    scores, send_back = call(
        functools.partial(score_kernel, edge_count),
        (shape((1, cands), F32), shape((slots * pieces, 128), BF16)),
        [
            ("v", got_ends),
            ("v", gather),
            ("v", scatter),
            ("v", known),
            ("v", out_row),
        ]
        + [("v", w) for w in mlp_shards],
        [
            pltpu.VMEM((cands, 2 * width), BF16),
            packed,
            pltpu.VMEM((2, 2 * slots, hidden), BF16),
            pltpu.VMEM((2, slots, width), F32),
        ],
    )
    got_back = lax.all_to_all(send_back, everyone, split_axis=0, concat_axis=0, tiled=True)
    node_grad = call(
        scatter_kernel, shape((nodes, width), F32), [("v", pick), ("v", got_back)], [packed]
    )
    return (node_out, scores.reshape(1, 1, cands), node_grad)


def solution(mesh):
    in_specs = (
        P(("dom", "edge"), None),
        P("edge", None),
        P(),
        P(),
        P(("dom", "edge"), None),
        P(("dom", "edge")),
        P("dom", "edge", None, None),
        P("dom", "edge", None),
        P("dom", "edge", None, None, None),
        P("dom", "edge", None, None),
        P("dom", "edge"),
        P("dom", "edge", None),
        P("edge", None),
        P(),
    )
    out_specs = (P(("dom", "edge"), None), P("dom", "edge", None), P(("dom", "edge"), None))
    return jax.shard_map(local, mesh=mesh, in_specs=in_specs, out_specs=out_specs, check_vma=False)
```

time: 74.9 us -> 64.8 us (0.87)
  waiting for transfers between devices: 28.5 us -> 9.36 us
  blocking collectives: 9.93 us -> 23.3 us
  starting transfers between devices: 19.2 us -> 16.2 us
  local copies, waits for them, and re-layouts: 4.25 us -> 3.1 us
    all_to_all x0 -> x1, blocking collectives: none -> 13.3 us  [local(): lax.all_to_all(send_ends, everyone, split_axis=0, concat_axis=0, tiled=True)]
    ppermute x13, waiting for transfers between devices: 20.9 us -> 9.36 us  [swap(): return lax.ppermute(array, axis, [(i, i ^ k) for i in range(count)])]
    all_to_all x1 -> x0, waiting for transfers between devices: 7.58 us -> none  [local(): lax.all_to_all(send_ends, everyone, split_axis=0, concat_axis=0, tiled=True)]
    all_to_all x1 -> x0, starting transfers between devices: 2.58 us -> none  [local(): lax.all_to_all(send_ends, everyone, split_axis=0, concat_axis=0, tiled=True)]
    unnamed x29 -> x27, local copies, waits for them, and re-layouts: 4.15 us -> 2.99 us
  transfers between devices with their start and end apart: 14 -> 13, of which waited for: 5 -> 3; matrix products, arithmetic and copies ran while one was open for 0% -> 0% of each run, Pallas kernels for 9% -> 11%
where the time goes in v5:
time: 64.8 us; the launch traced here: 64.4 us
  blocking collectives  23.3 us (36%)
  starting transfers between devices  16.2 us (25%)
  Pallas kernels  10.9 us (17%)
  waiting for transfers between devices  9.36 us (14%)
  local copies, waits for them, and re-layouts  3.1 us (5%)
  between operations  1.47 us (2%)
    ppermute x13, starting transfers between devices, swap(): return lax.ppermute(array, axis, [(i, i ^ k) for i in range(count)])  16.2 us
    all_to_all x1, blocking collectives, local(): lax.all_to_all(send_ends, everyone, split_axis=0, concat_axis=0, tiled=True)  13.3 us
    pallas_call x5, Pallas kernels, call(): pl.pallas_call(body, out_shape=outs, in_specs=[SPACES[space] for space, _...  10.9 us
    all_to_all x1, blocking collectives, local(): lax.all_to_all(send_back, everyone, split_axis=0, concat_axis=0, tiled=True)  10 us
    ppermute x13, waiting for transfers between devices, swap(): return lax.ppermute(array, axis, [(i, i ^ k) for i in range(count)])  9.36 us
    unnamed x27, local copies, waits for them, and re-layouts  2.99 us
  transfers between devices with their start and end apart: 13, of which 3 were waited for; matrix products, arithmetic and copies ran while one was open for 0% of the time, Pallas kernels for 11%

profile of v5, /device:TPU:0, one launch (start us, length us, event | category | flops | bytes accessed | tf_op | source)
XLA Modules:
  0.0 64.4 jit_solution(5421724277885552007)
XLA Ops:
  0.6 3.0 %collective-permute-start = (bf16[256,1024]{1,0:T(8,128)(2,1)}, bf16[256,1024]{1,0:T(8,128)(2,1)S(1)}, u32[]{:S(2)}, u32[]{:S(2)}) collective-permute-start(bf16[256,1024]{1,0:T(8,128)(2,1)} %refs_9_.1), channel_id=1, source_target_pairs={{0,2},{1,3},{2,0},{3,1},{4,6},{5,7},{6,4},{7,5},{8,10},{9,11},{10,... | collective-permute-start | bytes 1572872 | tf_op jit(solution)/shard_map/ppermute | solution.py:288
  3.7 2.8 %shard_map.158 = (bf16[32,1024]{1,0:T(8,128)(2,1)}, bf16[32,1024]{1,0:T(8,128)(2,1)}, bf16[32,1024]{1,0:T(8,128)(2,1)}, bf16[32,1024]{1,0:T(8,128)(2,1)}, bf16[3...) custom-call(s32[1,8]{1,0:T(1,128)} %bitcast.22, ...), custom_call_target="tpu_custom_call" | custom-call | tf_op jit(solution)/shard_map/pallas_call | solution.py:45
  6.5 2.7 %collective-permute-start.1 = (bf16[32,1024]{1,0:T(8,128)(2,1)}, bf16[32,1024]{1,0:T(8,128)(2,1)S(1)}, u32[]{:S(2)}, u32[]{:S(2)}) collective-permute-start(bf16[32,1024]{1,0:T(8,128)(2,1)} %get-tuple-element.37), channel_id=1, source_target_pairs={{0,16},{4,20},{8,24},{12,28},{16,0},{20,4},{24,8},{28,12},{1,17},{... | collective-permute-start | bytes 196616 | tf_op jit(solution)/shard_map/ppermute | solution.py:288
  9.1 1.3 %collective-permute-start.2 = (bf16[32,1024]{1,0:T(8,128)(2,1)}, bf16[32,1024]{1,0:T(8,128)(2,1)S(1)}, u32[]{:S(2)}, u32[]{:S(2)}) collective-permute-start(bf16[32,1024]{1,0:T(8,128)(2,1)} %get-tuple-element.38), channel_id=1, source_target_pairs={{0,20},{4,16},{8,28},{12,24},{16,4},{20,0},{24,12},{28,8},{1,21},{... | collective-permute-start | bytes 196616 | tf_op jit(solution)/shard_map/ppermute | solution.py:288
  10.4 3.6 %collective-permute-start.3 = (bf16[32,1024]{1,0:T(8,128)(2,1)}, bf16[32,1024]{1,0:T(8,128)(2,1)S(1)}, u32[]{:S(2)}, u32[]{:S(2)}) collective-permute-start(bf16[32,1024]{1,0:T(8,128)(2,1)} %get-tuple-element.39), channel_id=1, source_target_pairs={{0,24},{4,28},{8,16},{12,20},{16,8},{20,12},{24,0},{28,4},{1,25},{... | collective-permute-start | bytes 196616 | tf_op jit(solution)/shard_map/ppermute | solution.py:288
  14.0 0.2 collective-permute-start.4
  14.2 4.0 %collective-permute-done.2.refs_15_ = bf16[32,1024]{1,0:T(8,128)(2,1)S(1)} collective-permute-done((bf16[32,1024]{1,0:T(8,128)(2,1)}, bf16[32,1024]{1,0:T(8,128)(2,1)S(1)}, u32[]{:S(2)}, u32[]{:S(2)}) %collective-permute-start.2) | collective-permute-done | bytes 65568 | tf_op jit(solution)/shard_map/ppermute | solution.py:288
  18.2 3.0 %collective-permute-done.4.refs_17_ = bf16[32,1024]{1,0:T(8,128)(2,1)S(1)} collective-permute-done((bf16[32,1024]{1,0:T(8,128)(2,1)}, bf16[32,1024]{1,0:T(8,128)(2,1)S(1)}, u32[]{:S(2)}, u32[]{:S(2)}) %collective-permute-start.4) | collective-permute-done | bytes 65568 | tf_op jit(solution)/shard_map/ppermute | solution.py:288
  21.3 0.5 collective-permute-start.5
  21.8 0.5 collective-permute-start.10
  22.3 0.5 collective-permute-start.7
  22.8 1.7 %collective-permute-start.8 = (bf16[32,1024]{1,0:T(8,128)(2,1)}, bf16[32,1024]{1,0:T(8,128)(2,1)S(1)}, u32[]{:S(2)}, u32[]{:S(2)}) collective-permute-start(bf16[32,1024]{1,0:T(8,128)(2,1)} %get-tuple-element.45), channel_id=1, source_target_pairs={{0,8},{4,12},{8,0},{12,4},{16,24},{20,28},{24,16},{28,20},{1,9},{5... | collective-permute-start | bytes 196616 | tf_op jit(solution)/shard_map/ppermute | solution.py:288
  24.5 2.3 %collective-permute-done.7.refs_11_ = bf16[32,1024]{1,0:T(8,128)(2,1)S(1)} collective-permute-done((bf16[32,1024]{1,0:T(8,128)(2,1)}, bf16[32,1024]{1,0:T(8,128)(2,1)S(1)}, u32[]{:S(2)}, u32[]{:S(2)}) %collective-permute-start.7) | collective-permute-done | bytes 65568 | tf_op jit(solution)/shard_map/ppermute | solution.py:288
  26.8 1.6 %collective-permute-start.9 = (bf16[32,1024]{1,0:T(8,128)(2,1)}, bf16[32,1024]{1,0:T(8,128)(2,1)S(1)}, u32[]{:S(2)}, u32[]{:S(2)}) collective-permute-start(bf16[32,1024]{1,0:T(8,128)(2,1)} %get-tuple-element.46), channel_id=1, source_target_pairs={{0,12},{4,8},{8,4},{12,0},{16,28},{20,24},{24,20},{28,16},{1,13},{... | collective-permute-start | bytes 196616 | tf_op jit(solution)/shard_map/ppermute | solution.py:288
  28.4 0.1 copy.18
  28.5 0.1 reshape.23.refs_5_
  28.7 0.0 copy-start.5
  29.3 0.0 copy-start.8
  29.3 0.0 copy-start.10
  29.4 0.6 copy-done.8
  30.0 0.0 copy-done.10
  30.0 1.0 %copy-done.1 = bf16[256,1024]{1,0:T(8,128)(2,1)S(1)} copy-done((bf16[256,1024]{1,0:T(8,128)(2,1)S(1)}, bf16[256,1024]{1,0:T(8,128)(2,1)}, u32[]{:S(2)}) %copy-start.1) | copy-done | bytes 524312
  31.1 1.0 %copy-done.2 = bf16[512,512]{1,0:T(8,128)(2,1)S(1)} copy-done((bf16[512,512]{1,0:T(8,128)(2,1)S(1)}, bf16[512,512]{1,0:T(8,128)(2,1)}, u32[]{:S(2)}) %copy-start.2) | copy-done | bytes 524312
  32.1 0.8 %shard_map.157 = (f32[128,384]{1,0:T(8,128)S(1)}, bf16[2,128,384]{2,1,0:T(8,128)(2,1)S(1)}, bf16[32,1024]{1,0:T(8,128)(2,1)S(1)}, bf16[32,1024]{1,0:T(8,128)(2,1...) custom-call(s32[1,1]{1,0:T(1,128)S(6)} %copy.19.refs_0_, ...), custom_call_target="tpu_custom_call" | custom-call | tf_op jit(solution)/shard_map/pallas_call | solution.py:45
  32.9 0.1 copy-done
  33.1 3.6 %shard_map.159 = (bf16[128,1024]{1,0:T(8,128)(2,1)}, bf16[512,128]{1,0:T(8,128)(2,1)S(1)}) custom-call(bf16[128,1024]{1,0:T(8,128)(2,1)S(1)} %copy-done, f32[128,384]{1,0:T(8,128)S(1)} %get-tuple-element.31.refs_1_, bf16[2,128,384]{2,1,0:T(8,128)(2,1)S(1)} %get-tuple-element.32.refs_2_, bf16[32,1024]{1,0:T(8,128)(2,1)S(1)} %get-tuple-element.33.refs_3_, ...), custom_call_target="tpu_custom_call" | custom-call | tf_op jit(solution)/shard_map/pallas_call | solution.py:45
  36.7 0.1 collective-permute-start.11
  36.8 0.5 collective-permute-start.12
  37.3 13.3 %all_to_all.22 = bf16[32,16,128]{2,1,0:T(8,128)(2,1)S(1)} all-to-all(bf16[32,16,128]{2,1,0:T(8,128)(2,1)S(1)} %bitcast.14), channel_id=1, replica_groups=mesh['dom'=8,'edge'=4] {'dom','edge'}, dimensions={0} | all-to-all | bytes 262144 | tf_op jit(solution)/shard_map/all_to_all | solution.py:401
  50.6 2.7 %shard_map.160 = (f32[1,256]{1,0:T(1,128)}, bf16[512,128]{1,0:T(8,128)(2,1)S(1)}) custom-call(bf16[512,128]{1,0:T(8,128)(2,1)S(1)} %bitcast.12, bf16[2,256,64]{2,1,0:T(8,128)(2,1)S(1)} %get-tuple-element.49.refs_1_, bf16[2,64,256]{2,1,0:T(8,128)(2,1)S(1)} %get-tuple-element.50.refs_2_, f32[256,128]{1,0:T(8,128)S(1)} %get-tuple-element.51.refs_3_, ...), custom_call_target="tpu_custom_call" | custom-call | tf_op jit(solution)/shard_map/pallas_call | solution.py:45
  53.4 10.0 %all_to_all.23 = bf16[32,16,128]{2,1,0:T(8,128)(2,1)S(1)} all-to-all(bf16[32,16,128]{2,1,0:T(8,128)(2,1)S(1)} %bitcast.15), channel_id=1, replica_groups=mesh['dom'=8,'edge'=4] {'dom','edge'}, dimensions={0} | all-to-all | bytes 262144 | tf_op jit(solution)/shard_map/all_to_all | solution.py:420
  63.4 1.0 %shard_map.161 = f32[128,1024]{1,0:T(8,128)} custom-call(bf16[128,64]{1,0:T(8,128)(2,1)S(1)} %get-tuple-element.35.refs_5_.refs_0_, bf16[512,128]{1,0:T(8,128)(2,1)S(1)} %bitcast.13), custom_call_target="tpu_custom_call" | custom-call | tf_op jit(solution)/shard_map/pallas_call | solution.py:45
  (29 shorter events, 0.1 us)
Async XLA Ops:
  0.6 20.6 %collective-permute-start = (bf16[256,1024]{1,0:T(8,128)(2,1)}, bf16[256,1024]{1,0:T(8,128)(2,1)S(1)}, u32[]{:S(2)}, u32[]{:S(2)}) collective-permute-start(bf16[256,1024]{1,0:T(8,128)(2,1)} %refs_9_.1), channel_id=1, source_target_pairs={{0,2},{1,3},{2,0},{3,1},{4,6},{5,7},{6,4},{7,5},{8,10},{9,11},{10,... | collective-permute-start | bytes 1572872 | tf_op jit(solution)/shard_map/ppermute | solution.py:288
  6.5 7.7 %collective-permute-start.1 = (bf16[32,1024]{1,0:T(8,128)(2,1)}, bf16[32,1024]{1,0:T(8,128)(2,1)S(1)}, u32[]{:S(2)}, u32[]{:S(2)}) collective-permute-start(bf16[32,1024]{1,0:T(8,128)(2,1)} %get-tuple-element.37), channel_id=1, source_target_pairs={{0,16},{4,20},{8,24},{12,28},{16,0},{20,4},{24,8},{28,12},{1,17},{... | collective-permute-start | bytes 196616 | tf_op jit(solution)/shard_map/ppermute | solution.py:288
  9.1 9.1 %collective-permute-start.2 = (bf16[32,1024]{1,0:T(8,128)(2,1)}, bf16[32,1024]{1,0:T(8,128)(2,1)S(1)}, u32[]{:S(2)}, u32[]{:S(2)}) collective-permute-start(bf16[32,1024]{1,0:T(8,128)(2,1)} %get-tuple-element.38), channel_id=1, source_target_pairs={{0,20},{4,16},{8,28},{12,24},{16,4},{20,0},{24,12},{28,8},{1,21},{... | collective-permute-start | bytes 196616 | tf_op jit(solution)/shard_map/ppermute | solution.py:288
  10.4 18.0 %copy-start.12 = (s32[1,1,8,4,2]{2,4,3,1,0:T(2,128)S(1)}, s32[1,1,8,4,2]{2,4,3,1,0:T(2,128)}, u32[]{:S(2)}) copy-start(s32[1,1,8,4,2]{2,4,3,1,0:T(2,128)} %param.22) | copy-start | bytes 772
  10.4 7.8 %collective-permute-start.3 = (bf16[32,1024]{1,0:T(8,128)(2,1)}, bf16[32,1024]{1,0:T(8,128)(2,1)S(1)}, u32[]{:S(2)}, u32[]{:S(2)}) collective-permute-start(bf16[32,1024]{1,0:T(8,128)(2,1)} %get-tuple-element.39), channel_id=1, source_target_pairs={{0,24},{4,28},{8,16},{12,20},{16,8},{20,12},{24,0},{28,4},{1,25},{... | collective-permute-start | bytes 196616 | tf_op jit(solution)/shard_map/ppermute | solution.py:288
  14.0 7.3 %collective-permute-start.4 = (bf16[32,1024]{1,0:T(8,128)(2,1)}, bf16[32,1024]{1,0:T(8,128)(2,1)S(1)}, u32[]{:S(2)}, u32[]{:S(2)}) collective-permute-start(bf16[32,1024]{1,0:T(8,128)(2,1)} %get-tuple-element.40), channel_id=1, source_target_pairs={{0,28},{4,24},{8,20},{12,16},{16,12},{20,8},{24,4},{28,0},{1,29},{... | collective-permute-start | bytes 196616 | tf_op jit(solution)/shard_map/ppermute | solution.py:288
  21.3 11.6 %collective-permute-start.6 = (bf16[256,1024]{1,0:T(8,128)(2,1)S(1)}, bf16[256,1024]{1,0:T(8,128)(2,1)S(1)}, u32[]{:S(2)}, u32[]{:S(2)}) collective-permute-start(bf16[256,1024]{1,0:T(8,128)(2,1)S(1)} %collective-permute-done.refs_8_), channel_id=1, source_target_pairs={{0,1},{1,0},{2,3},{3,2},{4,5},{5,4},{6,7},{7,6},{8,9},{9,8},{10,11... | collective-permute-start | bytes 1572872 | tf_op jit(solution)/shard_map/ppermute | solution.py:288
  21.3 11.6 %collective-permute-start.5 = (bf16[256,1024]{1,0:T(8,128)(2,1)}, bf16[256,1024]{1,0:T(8,128)(2,1)S(1)}, u32[]{:S(2)}, u32[]{:S(2)}) collective-permute-start(bf16[256,1024]{1,0:T(8,128)(2,1)} %refs_9_.1), channel_id=1, source_target_pairs={{0,1},{1,0},{2,3},{3,2},{4,5},{5,4},{6,7},{7,6},{8,9},{9,8},{10,11... | collective-permute-start | bytes 1572872 | tf_op jit(solution)/shard_map/ppermute | solution.py:288
  21.8 14.9 %collective-permute-start.10 = (bf16[512,512]{1,0:T(8,128)(2,1)}, bf16[512,512]{1,0:T(8,128)(2,1)S(1)}, u32[]{:S(2)}, u32[]{:S(2)}) collective-permute-start(bf16[512,512]{1,0:T(8,128)(2,1)} %refs_10_.1), channel_id=1, source_target_pairs={{0,2},{1,3},{2,0},{3,1},{4,6},{5,7},{6,4},{7,5},{8,10},{9,11},{10,... | collective-permute-start | bytes 1572872 | tf_op jit(solution)/shard_map/ppermute | solution.py:288
  22.3 4.5 %collective-permute-start.7 = (bf16[32,1024]{1,0:T(8,128)(2,1)}, bf16[32,1024]{1,0:T(8,128)(2,1)S(1)}, u32[]{:S(2)}, u32[]{:S(2)}) collective-permute-start(bf16[32,1024]{1,0:T(8,128)(2,1)} %get-tuple-element.44), channel_id=1, source_target_pairs={{0,4},{4,0},{8,12},{12,8},{16,20},{20,16},{24,28},{28,24},{1,5},{5... | collective-permute-start | bytes 196616 | tf_op jit(solution)/shard_map/ppermute | solution.py:288
  22.8 10.0 %collective-permute-start.8 = (bf16[32,1024]{1,0:T(8,128)(2,1)}, bf16[32,1024]{1,0:T(8,128)(2,1)S(1)}, u32[]{:S(2)}, u32[]{:S(2)}) collective-permute-start(bf16[32,1024]{1,0:T(8,128)(2,1)} %get-tuple-element.45), channel_id=1, source_target_pairs={{0,8},{4,12},{8,0},{12,4},{16,24},{20,28},{24,16},{28,20},{1,9},{5... | collective-permute-start | bytes 196616 | tf_op jit(solution)/shard_map/ppermute | solution.py:288
  26.8 6.1 %collective-permute-start.9 = (bf16[32,1024]{1,0:T(8,128)(2,1)}, bf16[32,1024]{1,0:T(8,128)(2,1)S(1)}, u32[]{:S(2)}, u32[]{:S(2)}) collective-permute-start(bf16[32,1024]{1,0:T(8,128)(2,1)} %get-tuple-element.46), channel_id=1, source_target_pairs={{0,12},{4,8},{8,4},{12,0},{16,28},{20,24},{24,20},{28,16},{1,13},{... | collective-permute-start | bytes 196616 | tf_op jit(solution)/shard_map/ppermute | solution.py:288
  28.5 0.8 %copy-start.6 = (f32[8,128]{1,0:T(8,128)S(1)}, f32[8,128]{1,0:T(8,128)}, u32[]{:S(2)}) copy-start(f32[8,128]{1,0:T(8,128)} %refs_3_.1) | copy-start | bytes 12292
  28.5 0.8 %copy-start.7 = (f32[8,128]{1,0:T(8,128)S(1)}, f32[8,128]{1,0:T(8,128)}, u32[]{:S(2)}) copy-start(f32[8,128]{1,0:T(8,128)} %refs_4_.1) | copy-start | bytes 12292
  28.5 0.8 %copy-start.9 = (f32[512]{0:T(512)S(1)}, f32[512]{0:T(512)}, u32[]{:S(2)}) copy-start(f32[512]{0:T(512)} %param.27) | copy-start | bytes 6148
  28.5 0.8 %copy-start.11 = (s32[128]{0:T(128)S(1)}, s32[128]{0:T(128)}, u32[]{:S(2)}) copy-start(s32[128]{0:T(128)} %param.19) | copy-start | bytes 1540
  28.7 0.7 %copy-start.5 = (s32[128,16]{0,1:T(8,128)S(1)}, s32[128,16]{0,1:T(8,128)}, u32[]{:S(2)}) copy-start(s32[128,16]{0,1:T(8,128)} %param.18) | copy-start | bytes 24580
  29.3 0.7 %copy-start.8 = (s32[1,1,2,256]{3,2,1,0:T(2,128)S(1)}, s32[1,1,2,256]{3,2,1,0:T(2,128)}, u32[]{:S(2)}) copy-start(s32[1,1,2,256]{3,2,1,0:T(2,128)} %param.23) | copy-start | bytes 6148
  29.3 0.7 %copy-start.10 = (s32[1,1,256]{2,1,0:T(1,128)S(1)}, s32[1,1,256]{2,1,0:T(1,128)}, u32[]{:S(2)}) copy-start(s32[1,1,256]{2,1,0:T(1,128)} %param.25) | copy-start | bytes 3076
  30.0 1.0 %copy-start.1 = (bf16[256,1024]{1,0:T(8,128)(2,1)S(1)}, bf16[256,1024]{1,0:T(8,128)(2,1)}, u32[]{:S(2)}) copy-start(bf16[256,1024]{1,0:T(8,128)(2,1)} %refs_9_.1) | copy-start | bytes 1572868
  31.1 1.0 %copy-start.2 = (bf16[512,512]{1,0:T(8,128)(2,1)S(1)}, bf16[512,512]{1,0:T(8,128)(2,1)}, u32[]{:S(2)}) copy-start(bf16[512,512]{1,0:T(8,128)(2,1)} %refs_10_.1) | copy-start | bytes 1572868
  32.1 0.9 %copy-start = (bf16[128,1024]{1,0:T(8,128)(2,1)S(1)}, bf16[128,1024]{1,0:T(8,128)(2,1)}, u32[]{:S(2)}) copy-start(bf16[128,1024]{1,0:T(8,128)(2,1)} %refs_0_.2) | copy-start | bytes 786436
  32.1 1.0 %copy-start.4 = (bf16[32,1024]{1,0:T(8,128)(2,1)S(1)}, bf16[32,1024]{1,0:T(8,128)(2,1)}, u32[]{:S(2)}) copy-start(bf16[32,1024]{1,0:T(8,128)(2,1)} %get-tuple-element.43.refs_10_) | copy-start | bytes 196612
  33.1 3.7 %copy-start.3 = (bf16[512,512]{1,0:T(8,128)(2,1)S(1)}, bf16[512,512]{1,0:T(8,128)(2,1)}, u32[]{:S(2)}) copy-start(bf16[512,512]{1,0:T(8,128)(2,1)} %refs_10_.1) | copy-start | bytes 1572868
  36.7 13.9 %collective-permute-start.11 = (bf16[512,512]{1,0:T(8,128)(2,1)S(1)}, bf16[512,512]{1,0:T(8,128)(2,1)S(1)}, u32[]{:S(2)}, u32[]{:S(2)}) collective-permute-start(bf16[512,512]{1,0:T(8,128)(2,1)S(1)} %copy-done.3), channel_id=1, source_target_pairs={{0,1},{1,0},{2,3},{3,2},{4,5},{5,4},{6,7},{7,6},{8,9},{9,8},{10,11... | collective-permute-start | bytes 1572872 | tf_op jit(solution)/shard_map/ppermute | solution.py:288
  36.8 13.8 %collective-permute-start.12 = (bf16[512,512]{1,0:T(8,128)(2,1)S(1)}, bf16[512,512]{1,0:T(8,128)(2,1)S(1)}, u32[]{:S(2)}, u32[]{:S(2)}) collective-permute-start(bf16[512,512]{1,0:T(8,128)(2,1)S(1)} %collective-permute-done.10.refs_7_), channel_id=1, source_target_pairs={{0,1},{1,0},{2,3},{3,2},{4,5},{5,4},{6,7},{7,6},{8,9},{9,8},{10,11... | collective-permute-start | bytes 1572872 | tf_op jit(solution)/shard_map/ppermute | solution.py:288

commit v6 on v5

--- a/solution.py
+++ b/solution.py
@@ -54,15 +54,13 @@
     )(*[array for _, array in ins])
 
 
-def halo_kernel(ready, count_ref, rows_ref, feats_ref, *out_refs):
+def halo_kernel(ready, count_ref, rows_ref, feats_ref, out_ref):
     doms, block = rows_ref.shape
     at = lax.broadcasted_iota(jnp.int32, (1, block), 1)
-    me = lax.axis_index("dom")
     ready()
-    pieces = []
-    for k in range(doms):
-        s = me ^ k
-        pieces.append(jnp.where(at < count_ref[0, s], rows_ref[pl.ds(s, 1), :], -1))
+    pieces = [
+        jnp.where(at < count_ref[:, s : s + 1], rows_ref[s : s + 1, :], -1) for s in range(doms)
+    ]
     flat = jnp.concatenate(pieces, axis=1)
     total = doms * block
     nodes = feats_ref.shape[0]
@@ -74,11 +72,8 @@
         lax.broadcasted_iota(jnp.int32, (16, 128), 1) == 0
     )
     mark = jnp.where(mark_at, DEAD, 0.0).astype(BF16)
-    head = (rows[:, :128] + dot(dead, mark, ((0,), (0,)))).astype(BF16)
-    tail = rows[:, 128:].astype(BF16)
-    for k, out_ref in enumerate(out_refs):
-        out_ref[:, :128] = head[k * block : (k + 1) * block, :]
-        out_ref[:, 128:] = tail[k * block : (k + 1) * block, :]
+    out_ref[:, :128] = (rows[:, :128] + dot(dead, mark, ((0,), (0,)))).astype(BF16)
+    out_ref[:, 128:] = rows[:, 128:].astype(BF16)
 
 
 def block_diagonal(vectors):
@@ -93,7 +88,6 @@
 
 
 def prepare_kernel(
-    block,
     ready,
     live_ref,
     neigh_ref,
@@ -116,15 +110,12 @@
     known_ref,
     weight_ref,
     gat_own_ref,
-    mlp_own_ref,
+    *mlp_own_refs,
 ):
     ready()
     nodes, table = count_ref.shape
     slots = neigh_ref.shape[0]
     ids = neigh_ref[...]
-    past = ids - nodes
-    moved = nodes + ((past // block) ^ lax.axis_index("dom")) * block + past % block
-    ids = jnp.where(ids < nodes, ids, moved)
     ids = jnp.where(lax.broadcasted_iota(jnp.int32, ids.shape, 0) < degree_ref[...], ids, -1)
     for base in range(0, table, nodes):
         at = base + lax.broadcasted_iota(jnp.int32, (nodes, nodes), 0)
@@ -157,19 +148,27 @@
     known_ref[...] = known.T
     weight_ref[...] = out_w_ref[...]
     gat_own_ref[...] = gat_ref[...]
-    mlp_own_ref[...] = mlp_ref[...]
+    depth = mlp_own_refs[0].shape[0]
+    for i, ref in enumerate(mlp_own_refs):
+        ref[...] = mlp_ref[i * depth : (i + 1) * depth, :]
+
+
+def shard_row(i, shards):
+    depth = shards[0].shape[0]
+    parts = len(shards) // lax.axis_size("edge")
+    at = (lax.axis_index("edge") ^ (i // parts)) * parts + i % parts
+    return pl.multiple_of(at * depth, depth)
 
 
 def shard_dots(rows_ref, shards, whole_ref=None):
-    me = lax.axis_index("edge")
     depth = shards[0].shape[0]
     if depth % 128:
         for i, shard in enumerate(shards):
-            whole_ref[pl.ds(pl.multiple_of((me ^ i) * depth, depth), depth), :] = shard[...]
+            whole_ref[pl.ds(shard_row(i, shards), depth), :] = shard[...]
         return dot(rows_ref[...], whole_ref[...])
     total = None
     for i, shard in enumerate(shards):
-        cols = pl.ds(pl.multiple_of((me ^ i) * depth, depth), depth)
+        cols = pl.ds(shard_row(i, shards), depth)
         part = dot(rows_ref[:, cols], shard[...])
         total = part if total is None else total + part
     return total
@@ -179,6 +178,7 @@
     shard_count,
     ready,
     own_ref,
+    got_ref,
     count_ref,
     factor_ref,
     diag_src_ref,
@@ -186,17 +186,15 @@
     pick_ref,
     *rest,
 ):
-    shards, blocks = rest[:shard_count], rest[shard_count:-8]
+    shards = rest[:shard_count]
     out_ref, send_ref, proj_ref, stage_ref, rows_ref, bias_ref, mix_ref, whole_ref = rest[-8:]
     ready()
     nodes, width = own_ref.shape
     table = proj_ref.shape[0]
-    block = blocks[0].shape[0]
     heads = diag_src_ref.shape[0] // 4
     size = width // heads
     rows_ref[:nodes, :] = own_ref[...]
-    for k, ref in enumerate(blocks):
-        rows_ref[nodes + k * block : nodes + (k + 1) * block, :] = ref[...]
+    rows_ref[nodes:, :] = got_ref[...]
     proj_ref[...] = shard_dots(rows_ref, shards, whole_ref).astype(BF16)
     parts = dot(diag_src_ref[...], proj_ref[...], ((1,), (1,)))
     src = parts[:heads] + parts[heads : 2 * heads] + parts[2 * heads : 3 * heads]
@@ -267,11 +265,10 @@
         high = total.astype(BF16)
         sum_ref[i, :slots, :] = high
         sum_ref[i, slots:, :] = (total - high.astype(F32)).astype(BF16)
-    per_half = width // depth
     for i, shard in enumerate(shards):
-        at = lax.axis_index("edge") ^ i
-        half = at // per_half
-        col = pl.multiple_of((at % per_half) * depth, depth)
+        row = shard_row(i, shards)
+        half = row // width
+        col = pl.multiple_of(row % width, depth)
         both = dot(sum_ref[half], shard[...], ((1,), (1,)))
         grad_ref[half, :, pl.ds(col, depth)] = both[:slots] + both[slots:]
     pack_rows(grad_ref[0] + grad_ref[1], stage_ref, back_ref)
@@ -326,22 +323,24 @@
     shape = jax.ShapeDtypeStruct
 
     heads = attn_src.shape[0]
+    parts = 2 if mlp_weight.shape[0] % 256 == 0 else 1
     gat_across = across(gat_weight, edge_count)
-    blocks = call(
+    send_rows = call(
         halo_kernel,
-        [shape((block, width), BF16)] * dom_count,
-        [("s", halo_count[0]), ("f", halo_rows[0, 0]), ("f", node_feats)],
+        shape((halo, width), BF16),
+        [("f", halo_count[0]), ("f", halo_rows[0, 0]), ("f", node_feats)],
         vmem_mib=60,
     )
-    far = range(dom_count // 2, dom_count)
-    moved = {0: blocks[0]}
-    for k in [*far, *range(1, dom_count // 2)]:
-        moved[k] = swap(blocks[k], "dom", k)
-    gat_across = lax.optimization_barrier((*gat_across, *[moved[k] for k in far]))[: len(gat_across)]
-    held_mlp = lax.optimization_barrier((mlp_weight, *gat_across))[0]
+    gat_across = lax.optimization_barrier((*gat_across, send_rows))[: len(gat_across)]
+    got_rows = lax.all_to_all(send_rows, "dom", split_axis=0, concat_axis=0, tiled=True)
+    mlp_parts = jnp.split(lax.optimization_barrier((mlp_weight, send_rows))[0], parts)
+    mlp_across = [across(mlp_parts[0], edge_count)]
     gat_shards = from_core(gat_across)
+    for part in mlp_parts[1:]:
+        part = lax.optimization_barrier((part, *gat_across))[0]
+        mlp_across.append(across(part, edge_count))
     prepared = call(
-        functools.partial(prepare_kernel, block),
+        prepare_kernel,
         (
             shape((nodes, table), F32),
             shape((2, nodes, table), BF16),
@@ -353,8 +352,8 @@
             shape((cands, 128), F32),
             shape((1, hidden), F32),
             shape(gat_weight.shape, BF16),
-            shape(mlp_weight.shape, BF16),
-        ),
+        )
+        + (shape(mlp_parts[0].shape, BF16),) * parts,
         [
             ("s", cand_count),
             ("f", neighbours.T),
@@ -371,21 +370,20 @@
     )
     counts, factors, diag_src, diag_dst, pick, gather, scatter, known, out_row, *own = prepared
     gat_shards[0] = own[0]
-    mlp_across = across(held_mlp, edge_count)
     packed = pltpu.VMEM((slots * pieces, 128), F32)
     node_out, send_ends = call(
         functools.partial(attend_kernel, edge_count),
         (shape((nodes, width), BF16), shape((slots * pieces, 128), BF16)),
         [
             ("v", node_feats),
+            ("v", got_rows),
             ("v", counts),
             ("v", factors),
             ("v", diag_src),
             ("v", diag_dst),
             ("v", pick),
         ]
-        + [("v", w) for w in gat_shards]
-        + [("v", moved[k]) for k in range(dom_count)],
+        + [("v", w) for w in gat_shards],
         [
             pltpu.VMEM((table, width), BF16),
             packed,
@@ -395,12 +393,16 @@
             pltpu.VMEM((width if width // edge_count % 128 else 16, width), BF16),
         ],
     )
-    mlp_across = lax.optimization_barrier((send_ends, *mlp_across))[1:]
-    mlp_shards = from_core(mlp_across)
-    mlp_shards[0] = own[1]
+    mlp_across[-1] = lax.optimization_barrier((send_ends, *mlp_across[-1]))[1:]
+    for part in mlp_across[:-1]:
+        part[0] = lax.optimization_barrier((part[0], *gat_across))[0]
+    mlp_found = [from_core(part) for part in mlp_across]
+    for found, held in zip(mlp_found, own[1:]):
+        found[0] = held
+    mlp_shards = [found[e] for e in range(edge_count) for found in mlp_found]
     got_ends = lax.all_to_all(send_ends, everyone, split_axis=0, concat_axis=0, tiled=True)
     scores, send_back = call(
-        functools.partial(score_kernel, edge_count),
+        functools.partial(score_kernel, len(mlp_shards)),
         (shape((1, cands), F32), shape((slots * pieces, 128), BF16)),
         [
             ("v", got_ends),

time: 64.8 us -> 69.7 us (1.076)
  blocking collectives: 23.3 us -> 10 us
  local copies, waits for them, and re-layouts: 3.1 us -> 15.1 us
  waiting for transfers between devices: 9.36 us -> 12.1 us
  starting transfers between devices: 16.2 us -> 18.7 us
  Pallas kernels: 10.9 us -> 11.7 us
    all_to_all x1 -> x0, blocking collectives: 13.3 us -> none  [local(): lax.all_to_all(send_ends, everyone, split_axis=0, concat_axis=0, tiled=True)]
    all_to_all x0 -> x2, starting transfers between devices: none -> 12 us  [the longest x1 6.06 us: local(): lax.all_to_all(send_ends, everyone, split_axis=0, concat_axis=0, tiled=True)]
    unnamed x27 -> x59, local copies, waits for them, and re-layouts: 2.99 us -> 14.1 us
    ppermute x13 -> x9, starting transfers between devices: 16.2 us -> 6.65 us  [swap(): return lax.ppermute(array, axis, [(i, i ^ k) for i in range(count)])]
    all_to_all x0 -> x2, waiting for transfers between devices: none -> 8.21 us  [the longest x1 8.21 us: local(): lax.all_to_all(send_ends, everyone, split_axis=0, concat_axis=0, tiled=True)]
    ppermute x13 -> x9, waiting for transfers between devices: 9.36 us -> 3.88 us  [swap(): return lax.ppermute(array, axis, [(i, i ^ k) for i in range(count)])]
    split x0 -> x1, local copies, waits for them, and re-layouts: none -> 0.84 us  [local(): jnp.split(lax.optimization_barrier((mlp_weight, send_rows))[0], parts)]
    pallas_call x5, Pallas kernels: 10.9 us -> 11.7 us  [call(): pl.pallas_call(body, out_shape=outs, in_specs=[SPACES[space] for space, _...]
  transfers between devices with their start and end apart: 13 -> 11, of which waited for: 3 -> 2; matrix products, arithmetic and copies ran while one was open for 0% -> 2% of each run, Pallas kernels for 11% -> 10%
where the time goes in v6:
time: 69.7 us; the launch traced here: 69.1 us
  starting transfers between devices  18.7 us (27%)
  local copies, waits for them, and re-layouts  15.1 us (22%)
  waiting for transfers between devices  12.1 us (17%)
  Pallas kernels  11.7 us (17%)
  blocking collectives  10 us (14%)
  between operations  1.52 us (2%)
    unnamed x59, local copies, waits for them, and re-layouts  14.1 us
    pallas_call x5, Pallas kernels, call(): pl.pallas_call(body, out_shape=outs, in_specs=[SPACES[space] for space, _...  11.7 us
    all_to_all x1, blocking collectives, local(): lax.all_to_all(send_back, everyone, split_axis=0, concat_axis=0, tiled=True)  10 us
    all_to_all x1, waiting for transfers between devices, local(): lax.all_to_all(send_ends, everyone, split_axis=0, concat_axis=0, tiled=True)  8.21 us
    ppermute x9, starting transfers between devices, swap(): return lax.ppermute(array, axis, [(i, i ^ k) for i in range(count)])  6.65 us
    all_to_all x1, starting transfers between devices, local(): lax.all_to_all(send_ends, everyone, split_axis=0, concat_axis=0, tiled=True)  6.06 us
    all_to_all x1, starting transfers between devices, local(): lax.all_to_all(send_rows, 'dom', split_axis=0, concat_axis=0, tiled=True)  5.95 us
    ppermute x9, waiting for transfers between devices, swap(): return lax.ppermute(array, axis, [(i, i ^ k) for i in range(count)])  3.88 us
  transfers between devices with their start and end apart: 11, of which 2 were waited for; matrix products, arithmetic and copies ran while one was open for 2% of the time, Pallas kernels for 10%

profile of v6, /device:TPU:0, one launch (start us, length us, event | category | flops | bytes accessed | tf_op | source)
XLA Modules:
  0.0 69.1 jit_solution(13989614877269910219)
XLA Ops:
  0.6 3.0 %collective-permute-start = (bf16[256,1024]{1,0:T(8,128)(2,1)}, bf16[256,1024]{1,0:T(8,128)(2,1)S(1)}, u32[]{:S(2)}, u32[]{:S(2)}) collective-permute-start(bf16[256,1024]{1,0:T(8,128)(2,1)} %refs_9_.1), channel_id=1, source_target_pairs={{0,2},{1,3},{2,0},{3,1},{4,6},{5,7},{6,4},{7,5},{8,10},{9,11},{10,... | collective-permute-start | bytes 1572872 | tf_op jit(solution)/shard_map/ppermute | solution.py:285
  3.7 2.3 %shard_map.157 = bf16[256,1024]{1,0:T(8,128)(2,1)} custom-call(s32[1,8]{1,0:T(1,128)} %bitcast.25, s32[8,32]{1,0:T(8,128)} %bitcast.24, bf16[128,1024]{1,0:T(8,128)(2,1)} %refs_0_.2), custom_call_target="tpu_custom_call" | custom-call | tf_op jit(solution)/shard_map/pallas_call | solution.py:45
  6.0 6.0 %all-to-all-start = ((bf16[8,32,1024]{2,1,0:T(8,128)(2,1)}), bf16[8,32,1024]{2,1,0:T(8,128)(2,1)S(1)}, u32[]{:S(2)}, u32[]{:S(2)}) async-start(bf16[8,32,1024]{2,1,0:T(8,128)(2,1)} %bitcast.23), calls=%async_computation | async-start | bytes 1048576 | tf_op jit(solution)/shard_map/all_to_all | solution.py:335
  11.9 3.9 %collective-permute-done.refs_9_ = bf16[256,1024]{1,0:T(8,128)(2,1)S(1)} collective-permute-done((bf16[256,1024]{1,0:T(8,128)(2,1)}, bf16[256,1024]{1,0:T(8,128)(2,1)S(1)}, u32[]{:S(2)}, u32[]{:S(2)}) %collective-permute-start) | collective-permute-done | bytes 524320 | tf_op jit(solution)/shard_map/ppermute | solution.py:285
  16.3 0.8 %fusion = (bf16[256,512]{1,0:T(8,128)(2,1)}, bf16[256,512]{1,0:T(8,128)(2,1)}) fusion(bf16[512,512]{1,0:T(8,128)(2,1)S(1)} %copy-done), kind=kLoop, calls=%fused_computation | loop fusion | bytes 1048576 | tf_op jit(solution)/shard_map/split | solution.py:336
  17.2 1.7 %collective-permute-start.6 = (bf16[256,512]{1,0:T(8,128)(2,1)}, bf16[256,512]{1,0:T(8,128)(2,1)}, u32[]{:S(2)}, u32[]{:S(2)}) collective-permute-start(bf16[256,512]{1,0:T(8,128)(2,1)} %get-tuple-element.43), channel_id=1, source_target_pairs={{0,2},{1,3},{2,0},{3,1},{4,6},{5,7},{6,4},{7,5},{8,10},{9,11},{10,... | collective-permute-start | bytes 786440 | tf_op jit(solution)/shard_map/ppermute | solution.py:285
  20.2 0.6 copy-done.24
  20.8 0.8 %shard_map.158 = (f32[128,384]{1,0:T(8,128)S(1)}, bf16[2,128,384]{2,1,0:T(8,128)(2,1)S(1)}, bf16[32,1024]{1,0:T(8,128)(2,1)S(1)}, bf16[32,1024]{1,0:T(8,128)(2,1...) custom-call(s32[1,1]{1,0:T(1,128)S(6)} %copy.19.refs_0_, ...), custom_call_target="tpu_custom_call" | custom-call | tf_op jit(solution)/shard_map/pallas_call | solution.py:45
  21.6 0.8 %copy-done.3 = bf16[256,1024]{1,0:T(8,128)(2,1)} copy-done((bf16[256,1024]{1,0:T(8,128)(2,1)}, bf16[256,1024]{1,0:T(8,128)(2,1)S(1)}, u32[]{:S(2)}) %copy-start.3) | copy-done | bytes 524312
  22.3 0.7 %copy-done.5 = bf16[256,512]{1,0:T(8,128)(2,1)} copy-done((bf16[256,512]{1,0:T(8,128)(2,1)}, bf16[256,512]{1,0:T(8,128)(2,1)S(1)}, u32[]{:S(2)}) %copy-start.5) | copy-done | bytes 262168
  23.0 0.7 %copy-done.7 = bf16[256,512]{1,0:T(8,128)(2,1)} copy-done((bf16[256,512]{1,0:T(8,128)(2,1)}, bf16[256,512]{1,0:T(8,128)(2,1)S(1)}, u32[]{:S(2)}) %copy-start.7) | copy-done | bytes 262168
  23.7 0.7 copy-done.9
  24.4 0.7 copy-done.11
  25.1 0.6 copy-done.13
  25.7 0.6 copy-done.15
  26.4 0.6 copy-done.17
  27.0 0.6 copy-done.19
  27.6 0.5 collective-permute-start.3
  28.2 1.0 %copy-done.4 = bf16[256,1024]{1,0:T(8,128)(2,1)S(1)} copy-done((bf16[256,1024]{1,0:T(8,128)(2,1)S(1)}, bf16[256,1024]{1,0:T(8,128)(2,1)}, u32[]{:S(2)}) %copy-start.4) | copy-done | bytes 524312
  29.2 0.9 %copy-done.10 = f32[128,384]{1,0:T(8,128)S(1)} copy-done((f32[128,384]{1,0:T(8,128)S(1)}, f32[128,384]{1,0:T(8,128)}, u32[]{:S(2)}) %copy-start.10) | copy-done | bytes 196632
  30.1 0.9 %copy-done.12 = bf16[2,128,384]{2,1,0:T(8,128)(2,1)S(1)} copy-done((bf16[2,128,384]{2,1,0:T(8,128)(2,1)S(1)}, bf16[2,128,384]{2,1,0:T(8,128)(2,1)}, u32[]{:S(2)}) %copy-start.12) | copy-done | bytes 196632
  31.0 0.8 %copy-done.18 = bf16[32,1024]{1,0:T(8,128)(2,1)S(1)} copy-done((bf16[32,1024]{1,0:T(8,128)(2,1)S(1)}, bf16[32,1024]{1,0:T(8,128)(2,1)}, u32[]{:S(2)}) %copy-start.18) | copy-done | bytes 65560
  31.9 0.8 %copy-done.20 = bf16[32,1024]{1,0:T(8,128)(2,1)S(1)} copy-done((bf16[32,1024]{1,0:T(8,128)(2,1)S(1)}, bf16[32,1024]{1,0:T(8,128)(2,1)}, u32[]{:S(2)}) %copy-start.20) | copy-done | bytes 65560
  32.7 3.7 %shard_map.159 = (bf16[128,1024]{1,0:T(8,128)(2,1)}, bf16[512,128]{1,0:T(8,128)(2,1)}) custom-call(bf16[128,1024]{1,0:T(8,128)(2,1)S(1)} %copy-done.1, bf16[256,1024]{1,0:T(8,128)(2,1)S(1)} %bitcast.14, f32[128,384]{1,0:T(8,128)S(1)} %copy-done.10, bf16[2,128,384]{2,1,0:T(8,128)(2,1)S(1)} %copy-done.12, bf16[32,1024]{1,0:T(8,128)(2,1)S(1)} %copy-done.18, ...), custom_call_target="tpu_custom_call" | custom-call | tf_op jit(solution)/shard_map/pallas_call | solution.py:45
  37.1 6.1 %all-to-all-start.1 = ((bf16[32,16,128]{2,1,0:T(8,128)(2,1)}), bf16[32,16,128]{2,1,0:T(8,128)(2,1)S(1)}, u32[]{:S(2)}, u32[]{:S(2)}) async-start(bf16[32,16,128]{2,1,0:T(8,128)(2,1)} %bitcast.9), calls=%async_computation.1 | async-start | bytes 262144 | tf_op jit(solution)/shard_map/all_to_all | solution.py:403
  43.1 8.2 %all-to-all-done.1 = bf16[32,16,128]{2,1,0:T(8,128)(2,1)S(1)} async-done(((bf16[32,16,128]{2,1,0:T(8,128)(2,1)}), bf16[32,16,128]{2,1,0:T(8,128)(2,1)S(1)}, u32[]{:S(2)}, u32[]{:S(2)}) %all-to-all-start.1) | async-done | bytes 131104 | tf_op jit(solution)/shard_map/all_to_all | solution.py:403
  51.4 0.9 %copy-done.8 = bf16[256,512]{1,0:T(8,128)(2,1)S(1)} copy-done((bf16[256,512]{1,0:T(8,128)(2,1)S(1)}, bf16[256,512]{1,0:T(8,128)(2,1)}, u32[]{:S(2)}) %copy-start.8) | copy-done | bytes 262168
  52.3 0.9 %copy-done.14 = bf16[2,256,64]{2,1,0:T(8,128)(2,1)S(1)} copy-done((bf16[2,256,64]{2,1,0:T(8,128)(2,1)S(1)}, bf16[2,256,64]{2,1,0:T(8,128)(2,1)}, u32[]{:S(2)}) %copy-start.14) | copy-done | bytes 65560
  53.2 0.9 %copy-done.16 = f32[256,128]{1,0:T(8,128)S(1)} copy-done((f32[256,128]{1,0:T(8,128)S(1)}, f32[256,128]{1,0:T(8,128)}, u32[]{:S(2)}) %copy-start.16) | copy-done | bytes 131096
  54.1 3.9 %shard_map.160 = (f32[1,256]{1,0:T(1,128)}, bf16[512,128]{1,0:T(8,128)(2,1)S(1)}) custom-call(bf16[512,128]{1,0:T(8,128)(2,1)S(1)} %bitcast.15, bf16[2,256,64]{2,1,0:T(8,128)(2,1)S(1)} %copy-done.14, bf16[2,64,256]{2,1,0:T(8,128)(2,1)S(1)} %get-tuple-element.37.refs_2_, f32[256,128]{1,0:T(8,128)S(1)} %copy-done.16, f32[1,512]{1,0:T(1,128)S(1)} %get-tuple-element.39.refs_4_, ...), custom_call_target="tpu_custom_call" | custom-call | tf_op jit(solution)/shard_map/pallas_call | solution.py:45
  58.0 10.0 %all_to_all.33 = bf16[32,16,128]{2,1,0:T(8,128)(2,1)S(1)} all-to-all(bf16[32,16,128]{2,1,0:T(8,128)(2,1)S(1)} %bitcast.17), channel_id=1, replica_groups=mesh['dom'=8,'edge'=4] {'dom','edge'}, dimensions={0} | all-to-all | bytes 262144 | tf_op jit(solution)/shard_map/all_to_all | solution.py:422
  68.0 1.0 %shard_map.161 = f32[128,1024]{1,0:T(8,128)} custom-call(bf16[128,64]{1,0:T(8,128)(2,1)S(1)} %get-tuple-element.30.refs_6_.refs_0_, bf16[512,128]{1,0:T(8,128)(2,1)S(1)} %bitcast.16), custom_call_target="tpu_custom_call" | custom-call | tf_op jit(solution)/shard_map/pallas_call | solution.py:45
  (57 shorter events, 1.7 us)
Async XLA Ops:
  0.6 15.2 %collective-permute-start = (bf16[256,1024]{1,0:T(8,128)(2,1)}, bf16[256,1024]{1,0:T(8,128)(2,1)S(1)}, u32[]{:S(2)}, u32[]{:S(2)}) collective-permute-start(bf16[256,1024]{1,0:T(8,128)(2,1)} %refs_9_.1), channel_id=1, source_target_pairs={{0,2},{1,3},{2,0},{3,1},{4,6},{5,7},{6,4},{7,5},{8,10},{9,11},{10,... | collective-permute-start | bytes 1572872 | tf_op jit(solution)/shard_map/ppermute | solution.py:285
  6.0 9.8 %copy-start.2 = (bf16[256,1024]{1,0:T(8,128)(2,1)S(1)}, bf16[256,1024]{1,0:T(8,128)(2,1)}, u32[]{:S(2)}) copy-start(bf16[256,1024]{1,0:T(8,128)(2,1)} %refs_9_.1) | copy-start | bytes 1572868
  6.0 10.3 %copy-start = (bf16[512,512]{1,0:T(8,128)(2,1)S(1)}, bf16[512,512]{1,0:T(8,128)(2,1)}, u32[]{:S(2)}) copy-start(bf16[512,512]{1,0:T(8,128)(2,1)} %refs_10_.1) | copy-start | bytes 1572868
  6.0 22.1 %all-to-all-start = ((bf16[8,32,1024]{2,1,0:T(8,128)(2,1)}), bf16[8,32,1024]{2,1,0:T(8,128)(2,1)S(1)}, u32[]{:S(2)}, u32[]{:S(2)}) async-start(bf16[8,32,1024]{2,1,0:T(8,128)(2,1)} %bitcast.23), calls=%async_computation | async-start | bytes 1048576 | tf_op jit(solution)/shard_map/all_to_all | solution.py:335
  15.8 12.3 %collective-permute-start.2 = (bf16[256,1024]{1,0:T(8,128)(2,1)S(1)}, bf16[256,1024]{1,0:T(8,128)(2,1)S(1)}, u32[]{:S(2)}, u32[]{:S(2)}) collective-permute-start(bf16[256,1024]{1,0:T(8,128)(2,1)S(1)} %collective-permute-done.refs_9_), channel_id=1, source_target_pairs={{0,1},{1,0},{2,3},{3,2},{4,5},{5,4},{6,7},{7,6},{8,9},{9,8},{10,11... | collective-permute-start | bytes 1572872 | tf_op jit(solution)/shard_map/ppermute | solution.py:285
  15.8 12.3 %collective-permute-start.1 = (bf16[256,1024]{1,0:T(8,128)(2,1)S(1)}, bf16[256,1024]{1,0:T(8,128)(2,1)S(1)}, u32[]{:S(2)}, u32[]{:S(2)}) collective-permute-start(bf16[256,1024]{1,0:T(8,128)(2,1)S(1)} %copy-done.2), channel_id=1, source_target_pairs={{0,1},{1,0},{2,3},{3,2},{4,5},{5,4},{6,7},{7,6},{8,9},{9,8},{10,11... | collective-permute-start | bytes 1572872 | tf_op jit(solution)/shard_map/ppermute | solution.py:285
  16.3 2.9 %copy-start.28 = (s32[1,1,8,4,2]{2,4,3,1,0:T(2,128)S(1)}, s32[1,1,8,4,2]{2,4,3,1,0:T(2,128)}, u32[]{:S(2)}) copy-start(s32[1,1,8,4,2]{2,4,3,1,0:T(2,128)} %param.22) | copy-start | bytes 772
  17.2 10.5 %collective-permute-start.6 = (bf16[256,512]{1,0:T(8,128)(2,1)}, bf16[256,512]{1,0:T(8,128)(2,1)}, u32[]{:S(2)}, u32[]{:S(2)}) collective-permute-start(bf16[256,512]{1,0:T(8,128)(2,1)} %get-tuple-element.43), channel_id=1, source_target_pairs={{0,2},{1,3},{2,0},{3,1},{4,6},{5,7},{6,4},{7,5},{8,10},{9,11},{10,... | collective-permute-start | bytes 786440 | tf_op jit(solution)/shard_map/ppermute | solution.py:285
  18.9 17.6 %collective-permute-start.4 = (bf16[256,512]{1,0:T(8,128)(2,1)}, bf16[256,512]{1,0:T(8,128)(2,1)}, u32[]{:S(2)}, u32[]{:S(2)}) collective-permute-start(bf16[256,512]{1,0:T(8,128)(2,1)} %get-tuple-element.45), channel_id=1, source_target_pairs={{0,2},{1,3},{2,0},{3,1},{4,6},{5,7},{6,4},{7,5},{8,10},{9,11},{10,... | collective-permute-start | bytes 786440 | tf_op jit(solution)/shard_map/ppermute | solution.py:285
  19.2 0.9 %copy-start.25 = (f32[512]{0:T(512)S(1)}, f32[512]{0:T(512)}, u32[]{:S(2)}) copy-start(f32[512]{0:T(512)} %param.27) | copy-start | bytes 6148
  19.2 0.9 %copy-start.27 = (s32[128]{0:T(128)S(1)}, s32[128]{0:T(128)}, u32[]{:S(2)}) copy-start(s32[128]{0:T(128)} %param.19) | copy-start | bytes 1540
  19.3 0.8 %copy-start.22 = (f32[8,128]{1,0:T(8,128)S(1)}, f32[8,128]{1,0:T(8,128)}, u32[]{:S(2)}) copy-start(f32[8,128]{1,0:T(8,128)} %refs_3_.1) | copy-start | bytes 12292
  19.3 0.8 %copy-start.23 = (f32[8,128]{1,0:T(8,128)S(1)}, f32[8,128]{1,0:T(8,128)}, u32[]{:S(2)}) copy-start(f32[8,128]{1,0:T(8,128)} %refs_4_.1) | copy-start | bytes 12292
  19.4 0.7 %copy-start.21 = (s32[128,16]{0,1:T(8,128)S(1)}, s32[128,16]{0,1:T(8,128)}, u32[]{:S(2)}) copy-start(s32[128,16]{0,1:T(8,128)} %param.18) | copy-start | bytes 24580
  20.8 7.4 %copy-start.1 = (bf16[128,1024]{1,0:T(8,128)(2,1)S(1)}, bf16[128,1024]{1,0:T(8,128)(2,1)}, u32[]{:S(2)}) copy-start(bf16[128,1024]{1,0:T(8,128)(2,1)} %refs_0_.2) | copy-start | bytes 786436
  21.5 0.8 %copy-start.3 = (bf16[256,1024]{1,0:T(8,128)(2,1)}, bf16[256,1024]{1,0:T(8,128)(2,1)S(1)}, u32[]{:S(2)}) copy-start(bf16[256,1024]{1,0:T(8,128)(2,1)S(1)} %get-tuple-element.31.refs_7_) | copy-start | bytes 1572868
  22.3 0.7 %copy-start.5 = (bf16[256,512]{1,0:T(8,128)(2,1)}, bf16[256,512]{1,0:T(8,128)(2,1)S(1)}, u32[]{:S(2)}) copy-start(bf16[256,512]{1,0:T(8,128)(2,1)S(1)} %get-tuple-element.40.refs_5_) | copy-start | bytes 786436
  23.0 0.7 %copy-start.7 = (bf16[256,512]{1,0:T(8,128)(2,1)}, bf16[256,512]{1,0:T(8,128)(2,1)S(1)}, u32[]{:S(2)}) copy-start(bf16[256,512]{1,0:T(8,128)(2,1)S(1)} %get-tuple-element.41.refs_6_) | copy-start | bytes 786436
  27.6 15.5 %collective-permute-start.7 = (bf16[256,512]{1,0:T(8,128)(2,1)}, bf16[256,512]{1,0:T(8,128)(2,1)}, u32[]{:S(2)}, u32[]{:S(2)}) collective-permute-start(bf16[256,512]{1,0:T(8,128)(2,1)} %collective-permute-done.6.refs_9_), channel_id=1, source_target_pairs={{0,1},{1,0},{2,3},{3,2},{4,5},{5,4},{6,7},{7,6},{8,9},{9,8},{10,11... | collective-permute-start | bytes 786440 | tf_op jit(solution)/shard_map/ppermute | solution.py:285
  27.6 15.5 %collective-permute-start.3 = (bf16[256,512]{1,0:T(8,128)(2,1)}, bf16[256,512]{1,0:T(8,128)(2,1)}, u32[]{:S(2)}, u32[]{:S(2)}) collective-permute-start(bf16[256,512]{1,0:T(8,128)(2,1)} %get-tuple-element.43), channel_id=1, source_target_pairs={{0,1},{1,0},{2,3},{3,2},{4,5},{5,4},{6,7},{7,6},{8,9},{9,8},{10,11... | collective-permute-start | bytes 786440 | tf_op jit(solution)/shard_map/ppermute | solution.py:285
  28.1 1.0 %copy-start.4 = (bf16[256,1024]{1,0:T(8,128)(2,1)S(1)}, bf16[256,1024]{1,0:T(8,128)(2,1)}, u32[]{:S(2)}) copy-start(bf16[256,1024]{1,0:T(8,128)(2,1)} %copy-done.3) | copy-start | bytes 1572868
  29.2 0.9 %copy-start.10 = (f32[128,384]{1,0:T(8,128)S(1)}, f32[128,384]{1,0:T(8,128)}, u32[]{:S(2)}) copy-start(f32[128,384]{1,0:T(8,128)} %copy-done.9) | copy-start | bytes 589828
  30.1 0.9 %copy-start.12 = (bf16[2,128,384]{2,1,0:T(8,128)(2,1)S(1)}, bf16[2,128,384]{2,1,0:T(8,128)(2,1)}, u32[]{:S(2)}) copy-start(bf16[2,128,384]{2,1,0:T(8,128)(2,1)} %copy-done.11) | copy-start | bytes 589828
  31.0 0.8 %copy-start.18 = (bf16[32,1024]{1,0:T(8,128)(2,1)S(1)}, bf16[32,1024]{1,0:T(8,128)(2,1)}, u32[]{:S(2)}) copy-start(bf16[32,1024]{1,0:T(8,128)(2,1)} %copy-done.17) | copy-start | bytes 196612
  31.9 0.8 %copy-start.20 = (bf16[32,1024]{1,0:T(8,128)(2,1)S(1)}, bf16[32,1024]{1,0:T(8,128)(2,1)}, u32[]{:S(2)}) copy-start(bf16[32,1024]{1,0:T(8,128)(2,1)} %copy-done.19) | copy-start | bytes 196612
  36.5 14.9 %copy-start.6 = (bf16[256,512]{1,0:T(8,128)(2,1)S(1)}, bf16[256,512]{1,0:T(8,128)(2,1)}, u32[]{:S(2)}) copy-start(bf16[256,512]{1,0:T(8,128)(2,1)} %copy-done.5) | copy-start | bytes 786436
  36.5 14.9 %collective-permute-start.5 = (bf16[256,512]{1,0:T(8,128)(2,1)}, bf16[256,512]{1,0:T(8,128)(2,1)S(1)}, u32[]{:S(2)}, u32[]{:S(2)}) collective-permute-start(bf16[256,512]{1,0:T(8,128)(2,1)} %get-tuple-element.45), channel_id=1, source_target_pairs={{0,1},{1,0},{2,3},{3,2},{4,5},{5,4},{6,7},{7,6},{8,9},{9,8},{10,11... | collective-permute-start | bytes 786440 | tf_op jit(solution)/shard_map/ppermute | solution.py:285
  36.6 14.8 %collective-permute-start.8 = (bf16[256,512]{1,0:T(8,128)(2,1)}, bf16[256,512]{1,0:T(8,128)(2,1)S(1)}, u32[]{:S(2)}, u32[]{:S(2)}) collective-permute-start(bf16[256,512]{1,0:T(8,128)(2,1)} %collective-permute-done.4.refs_10_), channel_id=1, source_target_pairs={{0,1},{1,0},{2,3},{3,2},{4,5},{5,4},{6,7},{7,6},{8,9},{9,8},{10,11... | collective-permute-start | bytes 786440 | tf_op jit(solution)/shard_map/ppermute | solution.py:285
  37.1 14.3 %all-to-all-start.1 = ((bf16[32,16,128]{2,1,0:T(8,128)(2,1)}), bf16[32,16,128]{2,1,0:T(8,128)(2,1)S(1)}, u32[]{:S(2)}, u32[]{:S(2)}) async-start(bf16[32,16,128]{2,1,0:T(8,128)(2,1)} %bitcast.9), calls=%async_computation.1 | async-start | bytes 262144 | tf_op jit(solution)/shard_map/all_to_all | solution.py:403
  51.4 1.0 %copy-start.8 = (bf16[256,512]{1,0:T(8,128)(2,1)S(1)}, bf16[256,512]{1,0:T(8,128)(2,1)}, u32[]{:S(2)}) copy-start(bf16[256,512]{1,0:T(8,128)(2,1)} %copy-done.7) | copy-start | bytes 786436
  52.3 0.9 %copy-start.14 = (bf16[2,256,64]{2,1,0:T(8,128)(2,1)S(1)}, bf16[2,256,64]{2,1,0:T(8,128)(2,1)}, u32[]{:S(2)}) copy-start(bf16[2,256,64]{2,1,0:T(8,128)(2,1)} %copy-done.13) | copy-start | bytes 196612
  53.2 0.9 %copy-start.16 = (f32[256,128]{1,0:T(8,128)S(1)}, f32[256,128]{1,0:T(8,128)}, u32[]{:S(2)}) copy-start(f32[256,128]{1,0:T(8,128)} %copy-done.15) | copy-start | bytes 393220
  (8 other events, 5.3 us)

commit v7 on v6

--- a/solution.py
+++ b/solution.py
@@ -23,7 +23,7 @@
     return lax.dot_general(a, b, (dims, ((), ())), preferred_element_type=F32)
 
 
-def call(kernel, outs, ins, scratch=(), vmem_mib=48):
+def call(kernel, outs, ins, scratch=(), vmem_mib=20):
     fetched = [i for i, (space, _) in enumerate(ins) if space == "f"]
 
     def body(*refs):
@@ -110,7 +110,7 @@
     known_ref,
     weight_ref,
     gat_own_ref,
-    *mlp_own_refs,
+    mlp_own_ref,
 ):
     ready()
     nodes, table = count_ref.shape
@@ -148,16 +148,12 @@
     known_ref[...] = known.T
     weight_ref[...] = out_w_ref[...]
     gat_own_ref[...] = gat_ref[...]
-    depth = mlp_own_refs[0].shape[0]
-    for i, ref in enumerate(mlp_own_refs):
-        ref[...] = mlp_ref[i * depth : (i + 1) * depth, :]
+    mlp_own_ref[...] = mlp_ref[...]
 
 
 def shard_row(i, shards):
     depth = shards[0].shape[0]
-    parts = len(shards) // lax.axis_size("edge")
-    at = (lax.axis_index("edge") ^ (i // parts)) * parts + i % parts
-    return pl.multiple_of(at * depth, depth)
+    return pl.multiple_of((lax.axis_index("edge") ^ i) * depth, depth)
 
 
 def shard_dots(rows_ref, shards, whole_ref=None):
@@ -323,7 +319,6 @@
     shape = jax.ShapeDtypeStruct
 
     heads = attn_src.shape[0]
-    parts = 2 if mlp_weight.shape[0] % 256 == 0 else 1
     gat_across = across(gat_weight, edge_count)
     send_rows = call(
         halo_kernel,
@@ -333,12 +328,8 @@
     )
     gat_across = lax.optimization_barrier((*gat_across, send_rows))[: len(gat_across)]
     got_rows = lax.all_to_all(send_rows, "dom", split_axis=0, concat_axis=0, tiled=True)
-    mlp_parts = jnp.split(lax.optimization_barrier((mlp_weight, send_rows))[0], parts)
-    mlp_across = [across(mlp_parts[0], edge_count)]
+    mlp_across = across(lax.optimization_barrier((mlp_weight, send_rows))[0], edge_count)
     gat_shards = from_core(gat_across)
-    for part in mlp_parts[1:]:
-        part = lax.optimization_barrier((part, *gat_across))[0]
-        mlp_across.append(across(part, edge_count))
     prepared = call(
         prepare_kernel,
         (
@@ -352,8 +343,8 @@
             shape((cands, 128), F32),
             shape((1, hidden), F32),
             shape(gat_weight.shape, BF16),
-        )
-        + (shape(mlp_parts[0].shape, BF16),) * parts,
+            shape(mlp_weight.shape, BF16),
+        ),
         [
             ("s", cand_count),
             ("f", neighbours.T),
@@ -393,16 +384,12 @@
             pltpu.VMEM((width if width // edge_count % 128 else 16, width), BF16),
         ],
     )
-    mlp_across[-1] = lax.optimization_barrier((send_ends, *mlp_across[-1]))[1:]
-    for part in mlp_across[:-1]:
-        part[0] = lax.optimization_barrier((part[0], *gat_across))[0]
-    mlp_found = [from_core(part) for part in mlp_across]
-    for found, held in zip(mlp_found, own[1:]):
-        found[0] = held
-    mlp_shards = [found[e] for e in range(edge_count) for found in mlp_found]
+    mlp_across = lax.optimization_barrier((send_ends, *mlp_across))[1:]
+    mlp_shards = from_core(mlp_across)
+    mlp_shards[0] = own[1]
     got_ends = lax.all_to_all(send_ends, everyone, split_axis=0, concat_axis=0, tiled=True)
     scores, send_back = call(
-        functools.partial(score_kernel, len(mlp_shards)),
+        functools.partial(score_kernel, edge_count),
         (shape((1, cands), F32), shape((slots * pieces, 128), BF16)),
         [
             ("v", got_ends),

time: 69.7 us -> 62.4 us (0.90)
  blocking collectives: 10 us -> 21.8 us
  waiting for transfers between devices: 12.1 us -> 4.97 us
  starting transfers between devices: 18.7 us -> 11.8 us
  local copies, waits for them, and re-layouts: 15.1 us -> 10.2 us
    all_to_all x0 -> x1, blocking collectives: none -> 11.8 us  [local(): lax.all_to_all(send_ends, everyone, split_axis=0, concat_axis=0, tiled=True)]
    all_to_all x1 -> x0, waiting for transfers between devices: 8.21 us -> none  [local(): lax.all_to_all(send_ends, everyone, split_axis=0, concat_axis=0, tiled=True)]
    all_to_all x1 -> x0, starting transfers between devices: 6.06 us -> none  [local(): lax.all_to_all(send_ends, everyone, split_axis=0, concat_axis=0, tiled=True)]
    unnamed x59 -> x51, local copies, waits for them, and re-layouts: 14.1 us -> 10 us
    all_to_all x1, waiting for transfers between devices: 0.01 us -> 1.11 us  [local(): lax.all_to_all(send_rows, 'dom', split_axis=0, concat_axis=0, tiled=True)]
    split x1 -> x0, local copies, waits for them, and re-layouts: 0.84 us -> none  [local(): jnp.split(lax.optimization_barrier((mlp_weight, send_rows))[0], parts)]
    ppermute x9 -> x6, starting transfers between devices: 6.65 us -> 5.85 us  [swap(): return lax.ppermute(array, axis, [(i, i ^ k) for i in range(count)])]
    ppermute x9 -> x6, waiting for transfers between devices: 3.88 us -> 3.86 us  [swap(): return lax.ppermute(array, axis, [(i, i ^ k) for i in range(count)])]
  transfers between devices with their start and end apart: 11 -> 7, of which waited for: 2 -> 2; matrix products, arithmetic and copies ran while one was open for 2% -> 0% of each run, Pallas kernels for 10% -> 13%
where the time goes in v7:
time: 62.4 us; the launch traced here: 61.9 us
  blocking collectives  21.8 us (35%)
  starting transfers between devices  11.8 us (19%)
  Pallas kernels  11.7 us (19%)
  local copies, waits for them, and re-layouts  10.2 us (16%)
  waiting for transfers between devices  4.97 us (8%)
  between operations  1.44 us (2%)
    all_to_all x1, blocking collectives, local(): lax.all_to_all(send_ends, everyone, split_axis=0, concat_axis=0, tiled=True)  11.8 us
    pallas_call x5, Pallas kernels, call(): pl.pallas_call(body, out_shape=outs, in_specs=[SPACES[space] for space, _...  11.7 us
    unnamed x51, local copies, waits for them, and re-layouts  10 us
    all_to_all x1, blocking collectives, local(): lax.all_to_all(send_back, everyone, split_axis=0, concat_axis=0, tiled=True)  9.99 us
    all_to_all x1, starting transfers between devices, local(): lax.all_to_all(send_rows, 'dom', split_axis=0, concat_axis=0, tiled=True)  5.95 us
    ppermute x6, starting transfers between devices, swap(): return lax.ppermute(array, axis, [(i, i ^ k) for i in range(count)])  5.85 us
    ppermute x6, waiting for transfers between devices, swap(): return lax.ppermute(array, axis, [(i, i ^ k) for i in range(count)])  3.86 us
  transfers between devices with their start and end apart: 7, of which 2 were waited for; matrix products, arithmetic and copies ran while one was open for 0% of the time, Pallas kernels for 13%

profile of v7, /device:TPU:0, one launch (start us, length us, event | category | flops | bytes accessed | tf_op | source)
XLA Modules:
  0.0 61.9 jit_solution(12129901096738863424)
XLA Ops:
  0.6 3.0 %collective-permute-start = (bf16[256,1024]{1,0:T(8,128)(2,1)}, bf16[256,1024]{1,0:T(8,128)(2,1)S(1)}, u32[]{:S(2)}, u32[]{:S(2)}) collective-permute-start(bf16[256,1024]{1,0:T(8,128)(2,1)} %refs_9_.1), channel_id=1, source_target_pairs={{0,2},{1,3},{2,0},{3,1},{4,6},{5,7},{6,4},{7,5},{8,10},{9,11},{10,... | collective-permute-start | bytes 1572872 | tf_op jit(solution)/shard_map/ppermute | solution.py:281
  3.7 2.3 %shard_map.157 = bf16[256,1024]{1,0:T(8,128)(2,1)} custom-call(s32[1,8]{1,0:T(1,128)} %bitcast.26, s32[8,32]{1,0:T(8,128)} %bitcast.25, bf16[128,1024]{1,0:T(8,128)(2,1)} %refs_0_.2), custom_call_target="tpu_custom_call" | custom-call | tf_op jit(solution)/shard_map/pallas_call | solution.py:45
  6.0 5.9 %all-to-all-start = ((bf16[8,32,1024]{2,1,0:T(8,128)(2,1)}), bf16[8,32,1024]{2,1,0:T(8,128)(2,1)S(1)}, u32[]{:S(2)}, u32[]{:S(2)}) async-start(bf16[8,32,1024]{2,1,0:T(8,128)(2,1)} %bitcast.24), calls=%async_computation | async-start | bytes 1048576 | tf_op jit(solution)/shard_map/all_to_all | solution.py:330
  12.0 3.8 %collective-permute-done.refs_9_ = bf16[256,1024]{1,0:T(8,128)(2,1)S(1)} collective-permute-done((bf16[256,1024]{1,0:T(8,128)(2,1)}, bf16[256,1024]{1,0:T(8,128)(2,1)S(1)}, u32[]{:S(2)}, u32[]{:S(2)}) %collective-permute-start) | collective-permute-done | bytes 524320 | tf_op jit(solution)/shard_map/ppermute | solution.py:281
  15.8 0.5 collective-permute-start.2
  16.3 1.7 %collective-permute-start.3 = (bf16[512,512]{1,0:T(8,128)(2,1)S(1)}, bf16[512,512]{1,0:T(8,128)(2,1)S(1)}, u32[]{:S(2)}, u32[]{:S(2)}) collective-permute-start(bf16[512,512]{1,0:T(8,128)(2,1)S(1)} %copy-done.2), channel_id=1, source_target_pairs={{0,2},{1,3},{2,0},{3,1},{4,6},{5,7},{6,4},{7,5},{8,10},{9,11},{10,... | collective-permute-start | bytes 1572872 | tf_op jit(solution)/shard_map/ppermute | solution.py:281
  18.7 0.1 copy.18
  18.8 0.1 reshape.25.refs_5_
  19.0 0.5 copy-done.18
  19.5 0.0 copy-done.21
  19.6 0.1 copy-done.17
  19.7 0.8 %shard_map.158 = (f32[128,384]{1,0:T(8,128)S(1)}, bf16[2,128,384]{2,1,0:T(8,128)(2,1)S(1)}, bf16[32,1024]{1,0:T(8,128)(2,1)S(1)}, bf16[32,1024]{1,0:T(8,128)(2,1...) custom-call(s32[1,1]{1,0:T(1,128)S(6)} %copy.19.refs_0_, ...), custom_call_target="tpu_custom_call" | custom-call | tf_op jit(solution)/shard_map/pallas_call | solution.py:45
  20.4 0.8 %copy-done.3 = bf16[256,1024]{1,0:T(8,128)(2,1)} copy-done((bf16[256,1024]{1,0:T(8,128)(2,1)}, bf16[256,1024]{1,0:T(8,128)(2,1)S(1)}, u32[]{:S(2)}) %copy-start.3) | copy-done | bytes 524312
  21.2 0.7 %copy-done.5 = f32[128,384]{1,0:T(8,128)} copy-done((f32[128,384]{1,0:T(8,128)}, f32[128,384]{1,0:T(8,128)S(1)}, u32[]{:S(2)}) %copy-start.5) | copy-done | bytes 196632
  21.9 0.7 %copy-done.7 = bf16[2,128,384]{2,1,0:T(8,128)(2,1)} copy-done((bf16[2,128,384]{2,1,0:T(8,128)(2,1)}, bf16[2,128,384]{2,1,0:T(8,128)(2,1)S(1)}, u32[]{:S(2)}) %copy-start.7) | copy-done | bytes 196632
  22.6 0.6 %copy-done.9 = bf16[2,256,64]{2,1,0:T(8,128)(2,1)} copy-done((bf16[2,256,64]{2,1,0:T(8,128)(2,1)}, bf16[2,256,64]{2,1,0:T(8,128)(2,1)S(1)}, u32[]{:S(2)}) %copy-start.9) | copy-done | bytes 65560
  23.2 0.6 %copy-done.11 = f32[256,128]{1,0:T(8,128)} copy-done((f32[256,128]{1,0:T(8,128)}, f32[256,128]{1,0:T(8,128)S(1)}, u32[]{:S(2)}) %copy-start.11) | copy-done | bytes 131096
  23.9 0.6 copy-done.13
  24.5 0.6 copy-done.15
  25.1 1.1 %all-to-all-done = bf16[8,32,1024]{2,1,0:T(8,128)(2,1)S(1)} async-done(((bf16[8,32,1024]{2,1,0:T(8,128)(2,1)}), bf16[8,32,1024]{2,1,0:T(8,128)(2,1)S(1)}, u32[]{:S(2)}, u32[]{:S(2)}) %all-to-all-start) | async-done | bytes 524320 | tf_op jit(solution)/shard_map/all_to_all | solution.py:330
  26.2 1.0 %copy-done.4 = bf16[256,1024]{1,0:T(8,128)(2,1)S(1)} copy-done((bf16[256,1024]{1,0:T(8,128)(2,1)S(1)}, bf16[256,1024]{1,0:T(8,128)(2,1)}, u32[]{:S(2)}) %copy-start.4) | copy-done | bytes 524312
  27.3 0.9 %copy-done.6 = f32[128,384]{1,0:T(8,128)S(1)} copy-done((f32[128,384]{1,0:T(8,128)S(1)}, f32[128,384]{1,0:T(8,128)}, u32[]{:S(2)}) %copy-start.6) | copy-done | bytes 196632
  28.2 0.9 %copy-done.8 = bf16[2,128,384]{2,1,0:T(8,128)(2,1)S(1)} copy-done((bf16[2,128,384]{2,1,0:T(8,128)(2,1)S(1)}, bf16[2,128,384]{2,1,0:T(8,128)(2,1)}, u32[]{:S(2)}) %copy-start.8) | copy-done | bytes 196632
  29.1 0.8 %copy-done.14 = bf16[32,1024]{1,0:T(8,128)(2,1)S(1)} copy-done((bf16[32,1024]{1,0:T(8,128)(2,1)S(1)}, bf16[32,1024]{1,0:T(8,128)(2,1)}, u32[]{:S(2)}) %copy-start.14) | copy-done | bytes 65560
  30.0 0.8 %copy-done.16 = bf16[32,1024]{1,0:T(8,128)(2,1)S(1)} copy-done((bf16[32,1024]{1,0:T(8,128)(2,1)S(1)}, bf16[32,1024]{1,0:T(8,128)(2,1)}, u32[]{:S(2)}) %copy-start.16) | copy-done | bytes 65560
  30.8 4.9 %shard_map.159 = (bf16[128,1024]{1,0:T(8,128)(2,1)}, bf16[512,128]{1,0:T(8,128)(2,1)S(1)}) custom-call(bf16[128,1024]{1,0:T(8,128)(2,1)S(1)} %copy-done, bf16[256,1024]{1,0:T(8,128)(2,1)S(1)} %bitcast.14, f32[128,384]{1,0:T(8,128)S(1)} %copy-done.6, bf16[2,128,384]{2,1,0:T(8,128)(2,1)S(1)} %copy-done.8, bf16[32,1024]{1,0:T(8,128)(2,1)S(1)} %copy-done.14, ...), custom_call_target="tpu_custom_call" | custom-call | tf_op jit(solution)/shard_map/pallas_call | solution.py:45
  35.7 0.1 collective-permute-start.4
  35.8 0.5 collective-permute-start.5
  36.3 11.8 %all_to_all.33 = bf16[32,16,128]{2,1,0:T(8,128)(2,1)S(1)} all-to-all(bf16[32,16,128]{2,1,0:T(8,128)(2,1)S(1)} %bitcast.17), channel_id=1, replica_groups=mesh['dom'=8,'edge'=4] {'dom','edge'}, dimensions={0} | all-to-all | bytes 262144 | tf_op jit(solution)/shard_map/all_to_all | solution.py:390
  48.1 2.7 %shard_map.160 = (f32[1,256]{1,0:T(1,128)}, bf16[512,128]{1,0:T(8,128)(2,1)S(1)}) custom-call(bf16[512,128]{1,0:T(8,128)(2,1)S(1)} %bitcast.15, bf16[2,256,64]{2,1,0:T(8,128)(2,1)S(1)} %copy-done.10, bf16[2,64,256]{2,1,0:T(8,128)(2,1)S(1)} %get-tuple-element.34.refs_2_, f32[256,128]{1,0:T(8,128)S(1)} %copy-done.12, f32[1,512]{1,0:T(1,128)S(1)} %get-tuple-element.36.refs_4_, ...), custom_call_target="tpu_custom_call" | custom-call | tf_op jit(solution)/shard_map/pallas_call | solution.py:45
  50.8 10.0 %all_to_all.34 = bf16[32,16,128]{2,1,0:T(8,128)(2,1)S(1)} all-to-all(bf16[32,16,128]{2,1,0:T(8,128)(2,1)S(1)} %bitcast.18), channel_id=1, replica_groups=mesh['dom'=8,'edge'=4] {'dom','edge'}, dimensions={0} | all-to-all | bytes 262144 | tf_op jit(solution)/shard_map/all_to_all | solution.py:409
  60.8 1.0 %shard_map.161 = f32[128,1024]{1,0:T(8,128)} custom-call(bf16[128,64]{1,0:T(8,128)(2,1)S(1)} %get-tuple-element.27.refs_6_.refs_0_, bf16[512,128]{1,0:T(8,128)(2,1)S(1)} %bitcast.16), custom_call_target="tpu_custom_call" | custom-call | tf_op jit(solution)/shard_map/pallas_call | solution.py:45
  (41 shorter events, 0.1 us)
Async XLA Ops:
  0.6 15.2 %collective-permute-start = (bf16[256,1024]{1,0:T(8,128)(2,1)}, bf16[256,1024]{1,0:T(8,128)(2,1)S(1)}, u32[]{:S(2)}, u32[]{:S(2)}) collective-permute-start(bf16[256,1024]{1,0:T(8,128)(2,1)} %refs_9_.1), channel_id=1, source_target_pairs={{0,2},{1,3},{2,0},{3,1},{4,6},{5,7},{6,4},{7,5},{8,10},{9,11},{10,... | collective-permute-start | bytes 1572872 | tf_op jit(solution)/shard_map/ppermute | solution.py:281
  3.7 15.0 %copy-start.24 = (s32[1,1,8,4,2]{2,4,3,1,0:T(2,128)S(1)}, s32[1,1,8,4,2]{2,4,3,1,0:T(2,128)}, u32[]{:S(2)}) copy-start(s32[1,1,8,4,2]{2,4,3,1,0:T(2,128)} %param.22) | copy-start | bytes 772
  6.0 9.8 %copy-start.1 = (bf16[256,1024]{1,0:T(8,128)(2,1)S(1)}, bf16[256,1024]{1,0:T(8,128)(2,1)}, u32[]{:S(2)}) copy-start(bf16[256,1024]{1,0:T(8,128)(2,1)} %refs_9_.1) | copy-start | bytes 1572868
  6.0 10.3 %copy-start.2 = (bf16[512,512]{1,0:T(8,128)(2,1)S(1)}, bf16[512,512]{1,0:T(8,128)(2,1)}, u32[]{:S(2)}) copy-start(bf16[512,512]{1,0:T(8,128)(2,1)} %refs_10_.1) | copy-start | bytes 1572868
  6.0 20.2 %all-to-all-start = ((bf16[8,32,1024]{2,1,0:T(8,128)(2,1)}), bf16[8,32,1024]{2,1,0:T(8,128)(2,1)S(1)}, u32[]{:S(2)}, u32[]{:S(2)}) async-start(bf16[8,32,1024]{2,1,0:T(8,128)(2,1)} %bitcast.24), calls=%async_computation | async-start | bytes 1048576 | tf_op jit(solution)/shard_map/all_to_all | solution.py:330
  15.8 10.4 %collective-permute-start.1 = (bf16[256,1024]{1,0:T(8,128)(2,1)S(1)}, bf16[256,1024]{1,0:T(8,128)(2,1)}, u32[]{:S(2)}, u32[]{:S(2)}) collective-permute-start(bf16[256,1024]{1,0:T(8,128)(2,1)S(1)} %copy-done.1), channel_id=1, source_target_pairs={{0,1},{1,0},{2,3},{3,2},{4,5},{5,4},{6,7},{7,6},{8,9},{9,8},{10,11... | collective-permute-start | bytes 1572872 | tf_op jit(solution)/shard_map/ppermute | solution.py:281
  15.8 10.4 %collective-permute-start.2 = (bf16[256,1024]{1,0:T(8,128)(2,1)S(1)}, bf16[256,1024]{1,0:T(8,128)(2,1)}, u32[]{:S(2)}, u32[]{:S(2)}) collective-permute-start(bf16[256,1024]{1,0:T(8,128)(2,1)S(1)} %collective-permute-done.refs_9_), channel_id=1, source_target_pairs={{0,1},{1,0},{2,3},{3,2},{4,5},{5,4},{6,7},{7,6},{8,9},{9,8},{10,11... | collective-permute-start | bytes 1572872 | tf_op jit(solution)/shard_map/ppermute | solution.py:281
  16.3 19.4 %collective-permute-start.3 = (bf16[512,512]{1,0:T(8,128)(2,1)S(1)}, bf16[512,512]{1,0:T(8,128)(2,1)S(1)}, u32[]{:S(2)}, u32[]{:S(2)}) collective-permute-start(bf16[512,512]{1,0:T(8,128)(2,1)S(1)} %copy-done.2), channel_id=1, source_target_pairs={{0,2},{1,3},{2,0},{3,1},{4,6},{5,7},{6,4},{7,5},{8,10},{9,11},{10,... | collective-permute-start | bytes 1572872 | tf_op jit(solution)/shard_map/ppermute | solution.py:281
  18.8 0.7 %copy-start.18 = (f32[8,128]{1,0:T(8,128)S(1)}, f32[8,128]{1,0:T(8,128)}, u32[]{:S(2)}) copy-start(f32[8,128]{1,0:T(8,128)} %refs_3_.1) | copy-start | bytes 12292
  18.8 0.7 %copy-start.19 = (f32[8,128]{1,0:T(8,128)S(1)}, f32[8,128]{1,0:T(8,128)}, u32[]{:S(2)}) copy-start(f32[8,128]{1,0:T(8,128)} %refs_4_.1) | copy-start | bytes 12292
  18.8 0.7 %copy-start.20 = (s32[1,1,2,256]{3,2,1,0:T(2,128)S(1)}, s32[1,1,2,256]{3,2,1,0:T(2,128)}, u32[]{:S(2)}) copy-start(s32[1,1,2,256]{3,2,1,0:T(2,128)} %param.23) | copy-start | bytes 6148
  18.8 0.7 %copy-start.21 = (f32[512]{0:T(512)S(1)}, f32[512]{0:T(512)}, u32[]{:S(2)}) copy-start(f32[512]{0:T(512)} %param.27) | copy-start | bytes 6148
  18.8 0.7 %copy-start.23 = (s32[128]{0:T(128)S(1)}, s32[128]{0:T(128)}, u32[]{:S(2)}) copy-start(s32[128]{0:T(128)} %param.19) | copy-start | bytes 1540
  19.0 0.7 %copy-start.17 = (s32[128,16]{0,1:T(8,128)S(1)}, s32[128,16]{0,1:T(8,128)}, u32[]{:S(2)}) copy-start(s32[128,16]{0,1:T(8,128)} %param.18) | copy-start | bytes 24580
  19.0 0.7 %copy-start.22 = (s32[1,1,256]{2,1,0:T(1,128)S(1)}, s32[1,1,256]{2,1,0:T(1,128)}, u32[]{:S(2)}) copy-start(s32[1,1,256]{2,1,0:T(1,128)} %param.25) | copy-start | bytes 3076
  19.7 6.6 %copy-start = (bf16[128,1024]{1,0:T(8,128)(2,1)S(1)}, bf16[128,1024]{1,0:T(8,128)(2,1)}, u32[]{:S(2)}) copy-start(bf16[128,1024]{1,0:T(8,128)(2,1)} %refs_0_.2) | copy-start | bytes 786436
  20.4 0.8 %copy-start.3 = (bf16[256,1024]{1,0:T(8,128)(2,1)}, bf16[256,1024]{1,0:T(8,128)(2,1)S(1)}, u32[]{:S(2)}) copy-start(bf16[256,1024]{1,0:T(8,128)(2,1)S(1)} %get-tuple-element.28.refs_7_) | copy-start | bytes 1572868
  21.2 0.7 %copy-start.5 = (f32[128,384]{1,0:T(8,128)}, f32[128,384]{1,0:T(8,128)S(1)}, u32[]{:S(2)}) copy-start(f32[128,384]{1,0:T(8,128)S(1)} %get-tuple-element.23.refs_2_) | copy-start | bytes 589828
  21.9 0.7 %copy-start.7 = (bf16[2,128,384]{2,1,0:T(8,128)(2,1)}, bf16[2,128,384]{2,1,0:T(8,128)(2,1)S(1)}, u32[]{:S(2)}) copy-start(bf16[2,128,384]{2,1,0:T(8,128)(2,1)S(1)} %get-tuple-element.24.refs_3_) | copy-start | bytes 589828
  22.6 0.6 %copy-start.9 = (bf16[2,256,64]{2,1,0:T(8,128)(2,1)}, bf16[2,256,64]{2,1,0:T(8,128)(2,1)S(1)}, u32[]{:S(2)}) copy-start(bf16[2,256,64]{2,1,0:T(8,128)(2,1)S(1)} %get-tuple-element.33.refs_1_) | copy-start | bytes 196612
  23.2 0.7 %copy-start.11 = (f32[256,128]{1,0:T(8,128)}, f32[256,128]{1,0:T(8,128)S(1)}, u32[]{:S(2)}) copy-start(f32[256,128]{1,0:T(8,128)S(1)} %get-tuple-element.35.refs_3_) | copy-start | bytes 393220
  23.9 0.6 copy-start.13
  24.5 0.6 copy-start.15
  26.2 1.0 %copy-start.4 = (bf16[256,1024]{1,0:T(8,128)(2,1)S(1)}, bf16[256,1024]{1,0:T(8,128)(2,1)}, u32[]{:S(2)}) copy-start(bf16[256,1024]{1,0:T(8,128)(2,1)} %copy-done.3) | copy-start | bytes 1572868
  27.3 0.9 %copy-start.6 = (f32[128,384]{1,0:T(8,128)S(1)}, f32[128,384]{1,0:T(8,128)}, u32[]{:S(2)}) copy-start(f32[128,384]{1,0:T(8,128)} %copy-done.5) | copy-start | bytes 589828
  28.2 0.9 %copy-start.8 = (bf16[2,128,384]{2,1,0:T(8,128)(2,1)S(1)}, bf16[2,128,384]{2,1,0:T(8,128)(2,1)}, u32[]{:S(2)}) copy-start(bf16[2,128,384]{2,1,0:T(8,128)(2,1)} %copy-done.7) | copy-start | bytes 589828
  29.1 0.8 %copy-start.14 = (bf16[32,1024]{1,0:T(8,128)(2,1)S(1)}, bf16[32,1024]{1,0:T(8,128)(2,1)}, u32[]{:S(2)}) copy-start(bf16[32,1024]{1,0:T(8,128)(2,1)} %copy-done.13) | copy-start | bytes 196612
  30.0 0.8 %copy-start.16 = (bf16[32,1024]{1,0:T(8,128)(2,1)S(1)}, bf16[32,1024]{1,0:T(8,128)(2,1)}, u32[]{:S(2)}) copy-start(bf16[32,1024]{1,0:T(8,128)(2,1)} %copy-done.15) | copy-start | bytes 196612
  35.7 12.4 %collective-permute-start.4 = (bf16[512,512]{1,0:T(8,128)(2,1)S(1)}, bf16[512,512]{1,0:T(8,128)(2,1)S(1)}, u32[]{:S(2)}, u32[]{:S(2)}) collective-permute-start(bf16[512,512]{1,0:T(8,128)(2,1)S(1)} %copy-done.2), channel_id=1, source_target_pairs={{0,1},{1,0},{2,3},{3,2},{4,5},{5,4},{6,7},{7,6},{8,9},{9,8},{10,11... | collective-permute-start | bytes 1572872 | tf_op jit(solution)/shard_map/ppermute | solution.py:281
  35.8 12.3 %collective-permute-start.5 = (bf16[512,512]{1,0:T(8,128)(2,1)S(1)}, bf16[512,512]{1,0:T(8,128)(2,1)S(1)}, u32[]{:S(2)}, u32[]{:S(2)}) collective-permute-start(bf16[512,512]{1,0:T(8,128)(2,1)S(1)} %collective-permute-done.3.refs_7_), channel_id=1, source_target_pairs={{0,1},{1,0},{2,3},{3,2},{4,5},{5,4},{6,7},{7,6},{8,9},{9,8},{10,11... | collective-permute-start | bytes 1572872 | tf_op jit(solution)/shard_map/ppermute | solution.py:281
  36.3 11.8 %copy-start.10 = (bf16[2,256,64]{2,1,0:T(8,128)(2,1)S(1)}, bf16[2,256,64]{2,1,0:T(8,128)(2,1)}, u32[]{:S(2)}) copy-start(bf16[2,256,64]{2,1,0:T(8,128)(2,1)} %copy-done.9) | copy-start | bytes 196612
  36.3 11.8 %copy-start.12 = (f32[256,128]{1,0:T(8,128)S(1)}, f32[256,128]{1,0:T(8,128)}, u32[]{:S(2)}) copy-start(f32[256,128]{1,0:T(8,128)} %copy-done.11) | copy-start | bytes 393220

commit v8 on v7

--- a/solution.py
+++ b/solution.py
@@ -98,19 +98,14 @@
     cand_ref,
     labels_ref,
     out_w_ref,
-    gat_ref,
-    mlp_ref,
     count_ref,
-    factor_ref,
+    power_ref,
     diag_src_ref,
     diag_dst_ref,
     pick_ref,
-    gather_ref,
     scatter_ref,
     known_ref,
     weight_ref,
-    gat_own_ref,
-    mlp_own_ref,
 ):
     ready()
     nodes, table = count_ref.shape
@@ -129,9 +124,8 @@
         power = jnp.where(total > 2, 4.0, power)
         power = jnp.where(total > 5, 8.0, power)
         power = jnp.where(total > 13, 16.0, power)
-        count_ref[:, base : base + nodes] = total
-        factor_ref[0, :, base : base + nodes] = power.astype(BF16)
-        factor_ref[1, :, base : base + nodes] = (total - power).astype(BF16)
+        count_ref[:, base : base + nodes] = total.astype(BF16)
+        power_ref[:, base : base + nodes] = power.astype(BF16)
     diag_src_ref[...] = block_diagonal(src_ref[...])
     diag_dst_ref[...] = block_diagonal(dst_ref[...])
     ends = ends_ref.shape[1]
@@ -140,15 +134,11 @@
     cands = cand_ref.shape[1]
     slot_at = lax.broadcasted_iota(jnp.int32, (ends, cands), 0)
     for i in range(2):
-        one_hot = (slot_at == cand_ref[i : i + 1, :]).astype(F32)
-        scatter_ref[i] = one_hot.astype(BF16)
-        gather_ref[i] = one_hot.T.astype(BF16)
+        scatter_ref[i] = (slot_at == cand_ref[i : i + 1, :]).astype(F32).astype(BF16)
     live = (lax.broadcasted_iota(jnp.int32, (1, cands), 1) < live_ref[0, 0]).astype(F32)
     known = jnp.concatenate([live, labels_ref[...].astype(F32), jnp.zeros((126, cands), F32)], axis=0)
-    known_ref[...] = known.T
+    known_ref[...] = known.T.astype(BF16)
     weight_ref[...] = out_w_ref[...]
-    gat_own_ref[...] = gat_ref[...]
-    mlp_own_ref[...] = mlp_ref[...]
 
 
 def shard_row(i, shards):
@@ -176,7 +166,7 @@
     own_ref,
     got_ref,
     count_ref,
-    factor_ref,
+    power_ref,
     diag_src_ref,
     diag_dst_ref,
     pick_ref,
@@ -210,10 +200,12 @@
             logit = dst[here, h : h + 1] + src[h : h + 1, :]
             logit = jnp.maximum(logit, 0.2 * logit) + bias_ref[here, :]
             terms = jnp.exp2(logit - jnp.max(logit, axis=1, keepdims=True))
-            running = jnp.sum(count_ref[here, :] * terms, axis=1, keepdims=True)
+            count = count_ref[here, :]
+            power = power_ref[here, :]
+            running = jnp.sum(count.astype(F32) * terms, axis=1, keepdims=True)
             weight = (terms * (1.0 / running)).astype(BF16)
-            mix_ref[h % 2, here, :] = weight * factor_ref[0, here, :]
-            mix_ref[h % 2, nodes + r : nodes + r + chunk, :] = weight * factor_ref[1, here, :]
+            mix_ref[h % 2, here, :] = weight * power
+            mix_ref[h % 2, nodes + r : nodes + r + chunk, :] = weight * (count - power)
         both = dot(mix_ref[h % 2], proj_ref[:, h * size : (h + 1) * size])
         total = both[:nodes] + both[nodes:]
         total = jnp.where(total > 0, total, jnp.exp(jnp.minimum(total, 0.0)) - 1.0)
@@ -237,7 +229,7 @@
 
 
 def score_kernel(
-    shard_count, ready, got_ref, gather_ref, scatter_ref, known_ref, out_w_ref, *rest
+    shard_count, ready, got_ref, scatter_ref, known_ref, out_w_ref, *rest
 ):
     shards = rest[:shard_count]
     scores_ref, back_ref, pair_ref, stage_ref, sum_ref, grad_ref = rest[shard_count:]
@@ -247,14 +239,16 @@
     slots, width = grad_ref.shape[1:]
     rows = unpack_rows(got_ref, stage_ref, width // 128)
     for i in range(2):
-        pair_ref[:, i * width : (i + 1) * width] = dot(gather_ref[i], rows).astype(BF16)
+        pair_ref[:, i * width : (i + 1) * width] = dot(
+            scatter_ref[i], rows, ((0,), (0,))
+        ).astype(BF16)
     pre_act = shard_dots(pair_ref, shards)
     out_w = out_w_ref[...]
-    live = known_ref[:, :1]
+    live = known_ref[:, :1].astype(F32)
     gate = jax.nn.sigmoid(pre_act)
     score = jnp.sum(pre_act * gate * out_w, axis=1, keepdims=True) * live
     scores_ref[...] = jnp.broadcast_to(score, (cands, 128)).T[:1]
-    grad_score = (jax.nn.sigmoid(score) - known_ref[:, 1:2]) * live
+    grad_score = (jax.nn.sigmoid(score) - known_ref[:, 1:2].astype(F32)) * live
     grad_pre = (grad_score * out_w * (gate * (1.0 + pre_act * (1.0 - gate)))).astype(BF16)
     for i in range(2):
         total = dot(scatter_ref[i], grad_pre)
@@ -333,17 +327,14 @@
     prepared = call(
         prepare_kernel,
         (
-            shape((nodes, table), F32),
-            shape((2, nodes, table), BF16),
+            shape((nodes, table), BF16),
+            shape((nodes, table), BF16),
             shape((4 * heads, width), BF16),
             shape((4 * heads, width), BF16),
             shape((nodes, slots), BF16),
-            shape((2, cands, slots), BF16),
             shape((2, slots, cands), BF16),
-            shape((cands, 128), F32),
+            shape((cands, 128), BF16),
             shape((1, hidden), F32),
-            shape(gat_weight.shape, BF16),
-            shape(mlp_weight.shape, BF16),
         ),
         [
             ("s", cand_count),
@@ -355,12 +346,9 @@
             ("f", cand_ends[0, 0]),
             ("f", labels[0]),
             ("f", out_weight.reshape(1, hidden)),
-            ("f", gat_weight),
-            ("f", mlp_weight),
         ],
     )
-    counts, factors, diag_src, diag_dst, pick, gather, scatter, known, out_row, *own = prepared
-    gat_shards[0] = own[0]
+    counts, powers, diag_src, diag_dst, pick, scatter, known, out_row = prepared
     packed = pltpu.VMEM((slots * pieces, 128), F32)
     node_out, send_ends = call(
         functools.partial(attend_kernel, edge_count),
@@ -369,7 +357,7 @@
             ("v", node_feats),
             ("v", got_rows),
             ("v", counts),
-            ("v", factors),
+            ("v", powers),
             ("v", diag_src),
             ("v", diag_dst),
             ("v", pick),
@@ -386,14 +374,12 @@
     )
     mlp_across = lax.optimization_barrier((send_ends, *mlp_across))[1:]
     mlp_shards = from_core(mlp_across)
-    mlp_shards[0] = own[1]
     got_ends = lax.all_to_all(send_ends, everyone, split_axis=0, concat_axis=0, tiled=True)
     scores, send_back = call(
         functools.partial(score_kernel, edge_count),
         (shape((1, cands), F32), shape((slots * pieces, 128), BF16)),
         [
             ("v", got_ends),
-            ("v", gather),
             ("v", scatter),
             ("v", known),
             ("v", out_row),

time: 62.4 us -> 61 us (0.978)
  local copies, waits for them, and re-layouts: 10.2 us -> 9.08 us
    unnamed x51 -> x49, local copies, waits for them, and re-layouts: 10 us -> 8.46 us
  transfers between devices with their start and end apart: 7 -> 7, of which waited for: 2 -> 2; matrix products, arithmetic and copies ran while one was open for 0% -> 1% of each run, Pallas kernels for 13% -> 11%
where the time goes in v8:
time: 61 us; the launch traced here: 60.4 us
  blocking collectives  21.8 us (36%)
  starting transfers between devices  11.8 us (19%)
  Pallas kernels  11.3 us (19%)
  local copies, waits for them, and re-layouts  9.08 us (15%)
  waiting for transfers between devices  4.95 us (8%)
  between operations  1.43 us (2%)
    all_to_all x1, blocking collectives, local(): lax.all_to_all(send_ends, everyone, split_axis=0, concat_axis=0, tiled=True)  11.8 us
    pallas_call x5, Pallas kernels, call(): pl.pallas_call(body, out_shape=outs, in_specs=[SPACES[space] for space, _...  11.3 us
    all_to_all x1, blocking collectives, local(): lax.all_to_all(send_back, everyone, split_axis=0, concat_axis=0, tiled=True)  10 us
    unnamed x49, local copies, waits for them, and re-layouts  8.46 us
    all_to_all x1, starting transfers between devices, local(): lax.all_to_all(send_rows, 'dom', split_axis=0, concat_axis=0, tiled=True)  5.95 us
    ppermute x6, starting transfers between devices, swap(): return lax.ppermute(array, axis, [(i, i ^ k) for i in range(count)])  5.85 us
    ppermute x6, waiting for transfers between devices, swap(): return lax.ppermute(array, axis, [(i, i ^ k) for i in range(count)])  3.8 us
  transfers between devices with their start and end apart: 7, of which 2 were waited for; matrix products, arithmetic and copies ran while one was open for 1% of the time, Pallas kernels for 11%

profile of v8, /device:TPU:0, one launch (start us, length us, event | category | flops | bytes accessed | tf_op | source)
XLA Modules:
  0.0 60.4 jit_solution(6199139612928962696)
XLA Ops:
  0.6 3.0 %collective-permute-start = (bf16[256,1024]{1,0:T(8,128)(2,1)}, bf16[256,1024]{1,0:T(8,128)(2,1)S(1)}, u32[]{:S(2)}, u32[]{:S(2)}) collective-permute-start(bf16[256,1024]{1,0:T(8,128)(2,1)} %refs_7_), channel_id=1, source_target_pairs={{0,2},{1,3},{2,0},{3,1},{4,6},{5,7},{6,4},{7,5},{8,10},{9,11},{10,... | collective-permute-start | bytes 1572872 | tf_op jit(solution)/shard_map/ppermute | solution.py:275
  3.7 2.4 %shard_map.157 = bf16[256,1024]{1,0:T(8,128)(2,1)} custom-call(s32[1,8]{1,0:T(1,128)} %bitcast.26, s32[8,32]{1,0:T(8,128)} %bitcast.25, bf16[128,1024]{1,0:T(8,128)(2,1)} %refs_0_.2), custom_call_target="tpu_custom_call" | custom-call | tf_op jit(solution)/shard_map/pallas_call | solution.py:45
  6.1 5.9 %all-to-all-start = ((bf16[8,32,1024]{2,1,0:T(8,128)(2,1)}), bf16[8,32,1024]{2,1,0:T(8,128)(2,1)S(1)}, u32[]{:S(2)}, u32[]{:S(2)}) async-start(bf16[8,32,1024]{2,1,0:T(8,128)(2,1)} %bitcast.24), calls=%async_computation | async-start | bytes 1048576 | tf_op jit(solution)/shard_map/all_to_all | solution.py:324
  12.0 3.8 %collective-permute-done.refs_9_ = bf16[256,1024]{1,0:T(8,128)(2,1)S(1)} collective-permute-done((bf16[256,1024]{1,0:T(8,128)(2,1)}, bf16[256,1024]{1,0:T(8,128)(2,1)S(1)}, u32[]{:S(2)}, u32[]{:S(2)}) %collective-permute-start) | collective-permute-done | bytes 524320 | tf_op jit(solution)/shard_map/ppermute | solution.py:275
  15.8 0.5 collective-permute-start.2
  16.3 1.7 %collective-permute-start.3 = (bf16[512,512]{1,0:T(8,128)(2,1)S(1)}, bf16[512,512]{1,0:T(8,128)(2,1)}, u32[]{:S(2)}, u32[]{:S(2)}) collective-permute-start(bf16[512,512]{1,0:T(8,128)(2,1)S(1)} %copy-done.2), channel_id=1, source_target_pairs={{0,2},{1,3},{2,0},{3,1},{4,6},{5,7},{6,4},{7,5},{8,10},{9,11},{10,... | collective-permute-start | bytes 1572872 | tf_op jit(solution)/shard_map/ppermute | solution.py:275
  18.7 0.1 copy.18
  18.8 0.6 %reshape.25.refs_5_ = s32[1,64]{1,0:T(1,128)} reshape(s32[1,1,8,4,2]{4,3,2,1,0:T(4,128)S(1)} %copy.18) | data formatting | bytes 512 | tf_op jit(solution)/shard_map/reshape | solution.py:345
  19.5 0.0 copy-done.14
  19.5 0.0 copy-done.15
  19.5 0.0 copy-done.17
  19.6 0.6 copy-done.13
  20.2 0.7 %copy-done.21 = s32[1,1,256]{2,1,0:T(1,128)S(1)} copy-done((s32[1,1,256]{2,1,0:T(1,128)S(1)}, s32[1,1,256]{2,1,0:T(1,128)}, u32[]{:S(2)}) %copy-start.21) | copy-done | bytes 1048
  20.8 0.5 shard_map.158
  21.4 0.6 %copy-done.3 = bf16[128,384]{1,0:T(8,128)(2,1)} copy-done((bf16[128,384]{1,0:T(8,128)(2,1)}, bf16[128,384]{1,0:T(8,128)(2,1)S(1)}, u32[]{:S(2)}) %copy-start.3) | copy-done | bytes 98328
  22.0 0.6 %copy-done.5 = bf16[2,64,256]{2,1,0:T(8,128)(2,1)} copy-done((bf16[2,64,256]{2,1,0:T(8,128)(2,1)}, bf16[2,64,256]{2,1,0:T(8,128)(2,1)S(1)}, u32[]{:S(2)}) %copy-start.5) | copy-done | bytes 65560
  22.6 0.6 %copy-done.7 = bf16[256,128]{1,0:T(8,128)(2,1)} copy-done((bf16[256,128]{1,0:T(8,128)(2,1)}, bf16[256,128]{1,0:T(8,128)(2,1)S(1)}, u32[]{:S(2)}) %copy-start.7) | copy-done | bytes 65560
  23.3 0.6 %copy-done.9 = bf16[32,1024]{1,0:T(8,128)(2,1)} copy-done((bf16[32,1024]{1,0:T(8,128)(2,1)}, bf16[32,1024]{1,0:T(8,128)(2,1)S(1)}, u32[]{:S(2)}) %copy-start.9) | copy-done | bytes 65560
  23.9 0.6 %copy-done.11 = bf16[32,1024]{1,0:T(8,128)(2,1)} copy-done((bf16[32,1024]{1,0:T(8,128)(2,1)}, bf16[32,1024]{1,0:T(8,128)(2,1)S(1)}, u32[]{:S(2)}) %copy-start.11) | copy-done | bytes 65560
  24.5 0.6 copy-done.19
  25.1 1.1 %all-to-all-done = bf16[8,32,1024]{2,1,0:T(8,128)(2,1)S(1)} async-done(((bf16[8,32,1024]{2,1,0:T(8,128)(2,1)}), bf16[8,32,1024]{2,1,0:T(8,128)(2,1)S(1)}, u32[]{:S(2)}, u32[]{:S(2)}) %all-to-all-start) | async-done | bytes 524320 | tf_op jit(solution)/shard_map/all_to_all | solution.py:324
  26.3 0.9 %copy-done.4 = bf16[128,384]{1,0:T(8,128)(2,1)S(1)} copy-done((bf16[128,384]{1,0:T(8,128)(2,1)S(1)}, bf16[128,384]{1,0:T(8,128)(2,1)}, u32[]{:S(2)}) %copy-start.4) | copy-done | bytes 98328
  27.2 0.8 %copy-done.10 = bf16[32,1024]{1,0:T(8,128)(2,1)S(1)} copy-done((bf16[32,1024]{1,0:T(8,128)(2,1)S(1)}, bf16[32,1024]{1,0:T(8,128)(2,1)}, u32[]{:S(2)}) %copy-start.10) | copy-done | bytes 65560
  28.0 0.8 %copy-done.12 = bf16[32,1024]{1,0:T(8,128)(2,1)S(1)} copy-done((bf16[32,1024]{1,0:T(8,128)(2,1)S(1)}, bf16[32,1024]{1,0:T(8,128)(2,1)}, u32[]{:S(2)}) %copy-start.12) | copy-done | bytes 65560
  28.8 3.6 %shard_map.159 = (bf16[128,1024]{1,0:T(8,128)(2,1)}, bf16[512,128]{1,0:T(8,128)(2,1)S(1)}) custom-call(bf16[128,1024]{1,0:T(8,128)(2,1)S(1)} %copy-done, bf16[256,1024]{1,0:T(8,128)(2,1)S(1)} %bitcast.14, bf16[128,384]{1,0:T(8,128)(2,1)S(1)} %get-tuple-element.20.refs_2_, bf16[128,384]{1,0:T(8,128)(2,1)S(1)} %copy-done.4, bf16[32,1024]{1,0:T(8,128)(2,1)S(1)} %copy-done.10, ...), custom_call_target="tpu_custom_call" | custom-call | tf_op jit(solution)/shard_map/pallas_call | solution.py:45
  32.5 0.1 collective-permute-start.4
  32.5 0.5 collective-permute-start.5
  33.0 11.8 %all_to_all.33 = bf16[32,16,128]{2,1,0:T(8,128)(2,1)S(1)} all-to-all(bf16[32,16,128]{2,1,0:T(8,128)(2,1)S(1)} %bitcast.17), channel_id=1, replica_groups=mesh['dom'=8,'edge'=4] {'dom','edge'}, dimensions={0} | all-to-all | bytes 262144 | tf_op jit(solution)/shard_map/all_to_all | solution.py:377
  44.9 0.7 %copy-done.20 = f32[1,512]{1,0:T(1,128)S(1)} copy-done((f32[1,512]{1,0:T(1,128)S(1)}, f32[1,512]{1,0:T(1,128)}, u32[]{:S(2)}) %copy-start.20) | copy-done | bytes 2072
  45.6 3.8 %shard_map.160 = (f32[1,256]{1,0:T(1,128)}, bf16[512,128]{1,0:T(8,128)(2,1)S(1)}) custom-call(bf16[512,128]{1,0:T(8,128)(2,1)S(1)} %bitcast.16, bf16[2,64,256]{2,1,0:T(8,128)(2,1)S(1)} %copy-done.6, bf16[256,128]{1,0:T(8,128)(2,1)S(1)} %copy-done.8, f32[1,512]{1,0:T(1,128)S(1)} %copy-done.20, bf16[512,512]{1,0:T(8,128)(2,1)S(1)} %copy-done.2, ...), custom_call_target="tpu_custom_call" | custom-call | tf_op jit(solution)/shard_map/pallas_call | solution.py:45
  49.3 10.0 %all_to_all.34 = bf16[32,16,128]{2,1,0:T(8,128)(2,1)S(1)} all-to-all(bf16[32,16,128]{2,1,0:T(8,128)(2,1)S(1)} %bitcast.18), channel_id=1, replica_groups=mesh['dom'=8,'edge'=4] {'dom','edge'}, dimensions={0} | all-to-all | bytes 262144 | tf_op jit(solution)/shard_map/all_to_all | solution.py:395
  59.3 1.0 %shard_map.161 = f32[128,1024]{1,0:T(8,128)} custom-call(bf16[128,64]{1,0:T(8,128)(2,1)S(1)} %get-tuple-element.24.refs_6_.refs_0_, bf16[512,128]{1,0:T(8,128)(2,1)S(1)} %bitcast.15), custom_call_target="tpu_custom_call" | custom-call | tf_op jit(solution)/shard_map/pallas_call | solution.py:45
  (39 shorter events, 0.1 us)
Async XLA Ops:
  0.6 15.2 %collective-permute-start = (bf16[256,1024]{1,0:T(8,128)(2,1)}, bf16[256,1024]{1,0:T(8,128)(2,1)S(1)}, u32[]{:S(2)}, u32[]{:S(2)}) collective-permute-start(bf16[256,1024]{1,0:T(8,128)(2,1)} %refs_7_), channel_id=1, source_target_pairs={{0,2},{1,3},{2,0},{3,1},{4,6},{5,7},{6,4},{7,5},{8,10},{9,11},{10,... | collective-permute-start | bytes 1572872 | tf_op jit(solution)/shard_map/ppermute | solution.py:275
  3.7 12.7 %copy-start.2 = (bf16[512,512]{1,0:T(8,128)(2,1)S(1)}, bf16[512,512]{1,0:T(8,128)(2,1)}, u32[]{:S(2)}) copy-start(bf16[512,512]{1,0:T(8,128)(2,1)} %refs_4_.2) | copy-start | bytes 1572868
  6.0 9.8 %copy-start.1 = (bf16[256,1024]{1,0:T(8,128)(2,1)S(1)}, bf16[256,1024]{1,0:T(8,128)(2,1)}, u32[]{:S(2)}) copy-start(bf16[256,1024]{1,0:T(8,128)(2,1)} %refs_7_) | copy-start | bytes 1572868
  6.0 12.7 %copy-start.23 = (s32[1,1,8,4,2]{2,4,3,1,0:T(2,128)S(1)}, s32[1,1,8,4,2]{2,4,3,1,0:T(2,128)}, u32[]{:S(2)}) copy-start(s32[1,1,8,4,2]{2,4,3,1,0:T(2,128)} %param.22) | copy-start | bytes 772
  6.0 20.2 %copy-start = (bf16[128,1024]{1,0:T(8,128)(2,1)S(1)}, bf16[128,1024]{1,0:T(8,128)(2,1)}, u32[]{:S(2)}) copy-start(bf16[128,1024]{1,0:T(8,128)(2,1)} %refs_0_.2) | copy-start | bytes 786436
  6.1 20.2 %all-to-all-start = ((bf16[8,32,1024]{2,1,0:T(8,128)(2,1)}), bf16[8,32,1024]{2,1,0:T(8,128)(2,1)S(1)}, u32[]{:S(2)}, u32[]{:S(2)}) async-start(bf16[8,32,1024]{2,1,0:T(8,128)(2,1)} %bitcast.24), calls=%async_computation | async-start | bytes 1048576 | tf_op jit(solution)/shard_map/all_to_all | solution.py:324
  15.8 10.5 %collective-permute-start.1 = (bf16[256,1024]{1,0:T(8,128)(2,1)S(1)}, bf16[256,1024]{1,0:T(8,128)(2,1)S(1)}, u32[]{:S(2)}, u32[]{:S(2)}) collective-permute-start(bf16[256,1024]{1,0:T(8,128)(2,1)S(1)} %copy-done.1), channel_id=1, source_target_pairs={{0,1},{1,0},{2,3},{3,2},{4,5},{5,4},{6,7},{7,6},{8,9},{9,8},{10,11... | collective-permute-start | bytes 1572872 | tf_op jit(solution)/shard_map/ppermute | solution.py:275
  15.8 10.5 %collective-permute-start.2 = (bf16[256,1024]{1,0:T(8,128)(2,1)S(1)}, bf16[256,1024]{1,0:T(8,128)(2,1)S(1)}, u32[]{:S(2)}, u32[]{:S(2)}) collective-permute-start(bf16[256,1024]{1,0:T(8,128)(2,1)S(1)} %collective-permute-done.refs_9_), channel_id=1, source_target_pairs={{0,1},{1,0},{2,3},{3,2},{4,5},{5,4},{6,7},{7,6},{8,9},{9,8},{10,11... | collective-permute-start | bytes 1572872 | tf_op jit(solution)/shard_map/ppermute | solution.py:275
  16.3 16.1 %collective-permute-start.3 = (bf16[512,512]{1,0:T(8,128)(2,1)S(1)}, bf16[512,512]{1,0:T(8,128)(2,1)}, u32[]{:S(2)}, u32[]{:S(2)}) collective-permute-start(bf16[512,512]{1,0:T(8,128)(2,1)S(1)} %copy-done.2), channel_id=1, source_target_pairs={{0,2},{1,3},{2,0},{3,1},{4,6},{5,7},{6,4},{7,5},{8,10},{9,11},{10,... | collective-permute-start | bytes 1572872 | tf_op jit(solution)/shard_map/ppermute | solution.py:275
  18.8 0.7 %copy-start.14 = (f32[8,128]{1,0:T(8,128)S(1)}, f32[8,128]{1,0:T(8,128)}, u32[]{:S(2)}) copy-start(f32[8,128]{1,0:T(8,128)} %refs_3_.1) | copy-start | bytes 12292
  18.8 0.7 %copy-start.15 = (f32[8,128]{1,0:T(8,128)S(1)}, f32[8,128]{1,0:T(8,128)}, u32[]{:S(2)}) copy-start(f32[8,128]{1,0:T(8,128)} %refs_4_.1) | copy-start | bytes 12292
  18.8 0.7 %copy-start.16 = (s32[1,1,2,256]{3,2,1,0:T(2,128)S(1)}, s32[1,1,2,256]{3,2,1,0:T(2,128)}, u32[]{:S(2)}) copy-start(s32[1,1,2,256]{3,2,1,0:T(2,128)} %param.23) | copy-start | bytes 6148
  18.8 0.7 %copy-start.17 = (f32[512]{0:T(512)S(1)}, f32[512]{0:T(512)}, u32[]{:S(2)}) copy-start(f32[512]{0:T(512)} %param.27) | copy-start | bytes 6148
  19.5 0.7 %copy-start.13 = (s32[128,16]{0,1:T(8,128)S(1)}, s32[128,16]{0,1:T(8,128)}, u32[]{:S(2)}) copy-start(s32[128,16]{0,1:T(8,128)} %param.18) | copy-start | bytes 24580
  19.5 0.7 %copy-start.18 = (s32[1,64]{1,0:T(1,128)S(1)}, s32[1,64]{1,0:T(1,128)}, u32[]{:S(2)}) copy-start(s32[1,64]{1,0:T(1,128)} %reshape.25.refs_5_) | copy-start | bytes 772
  19.5 0.7 %copy-start.22 = (s32[128]{0:T(128)S(1)}, s32[128]{0:T(128)}, u32[]{:S(2)}) copy-start(s32[128]{0:T(128)} %param.19) | copy-start | bytes 1540
  20.2 0.7 %copy-start.21 = (s32[1,1,256]{2,1,0:T(1,128)S(1)}, s32[1,1,256]{2,1,0:T(1,128)}, u32[]{:S(2)}) copy-start(s32[1,1,256]{2,1,0:T(1,128)} %param.25) | copy-start | bytes 3076
  21.4 0.6 %copy-start.3 = (bf16[128,384]{1,0:T(8,128)(2,1)}, bf16[128,384]{1,0:T(8,128)(2,1)S(1)}, u32[]{:S(2)}) copy-start(bf16[128,384]{1,0:T(8,128)(2,1)S(1)} %get-tuple-element.21.refs_3_) | copy-start | bytes 294916
  22.0 0.6 %copy-start.5 = (bf16[2,64,256]{2,1,0:T(8,128)(2,1)}, bf16[2,64,256]{2,1,0:T(8,128)(2,1)S(1)}, u32[]{:S(2)}) copy-start(bf16[2,64,256]{2,1,0:T(8,128)(2,1)S(1)} %get-tuple-element.29.refs_1_) | copy-start | bytes 196612
  22.6 0.6 %copy-start.7 = (bf16[256,128]{1,0:T(8,128)(2,1)}, bf16[256,128]{1,0:T(8,128)(2,1)S(1)}, u32[]{:S(2)}) copy-start(bf16[256,128]{1,0:T(8,128)(2,1)S(1)} %get-tuple-element.30.refs_2_) | copy-start | bytes 196612
  23.3 0.6 %copy-start.9 = (bf16[32,1024]{1,0:T(8,128)(2,1)}, bf16[32,1024]{1,0:T(8,128)(2,1)S(1)}, u32[]{:S(2)}) copy-start(bf16[32,1024]{1,0:T(8,128)(2,1)S(1)} %get-tuple-element.22.refs_4_) | copy-start | bytes 196612
  23.9 0.6 %copy-start.11 = (bf16[32,1024]{1,0:T(8,128)(2,1)}, bf16[32,1024]{1,0:T(8,128)(2,1)S(1)}, u32[]{:S(2)}) copy-start(bf16[32,1024]{1,0:T(8,128)(2,1)S(1)} %get-tuple-element.23.refs_5_) | copy-start | bytes 196612
  24.5 0.6 copy-start.19
  26.3 0.9 %copy-start.4 = (bf16[128,384]{1,0:T(8,128)(2,1)S(1)}, bf16[128,384]{1,0:T(8,128)(2,1)}, u32[]{:S(2)}) copy-start(bf16[128,384]{1,0:T(8,128)(2,1)} %copy-done.3) | copy-start | bytes 294916
  27.2 0.8 %copy-start.10 = (bf16[32,1024]{1,0:T(8,128)(2,1)S(1)}, bf16[32,1024]{1,0:T(8,128)(2,1)}, u32[]{:S(2)}) copy-start(bf16[32,1024]{1,0:T(8,128)(2,1)} %copy-done.9) | copy-start | bytes 196612
  28.0 0.8 %copy-start.12 = (bf16[32,1024]{1,0:T(8,128)(2,1)S(1)}, bf16[32,1024]{1,0:T(8,128)(2,1)}, u32[]{:S(2)}) copy-start(bf16[32,1024]{1,0:T(8,128)(2,1)} %copy-done.11) | copy-start | bytes 196612
  32.5 12.4 %collective-permute-start.4 = (bf16[512,512]{1,0:T(8,128)(2,1)S(1)}, bf16[512,512]{1,0:T(8,128)(2,1)S(1)}, u32[]{:S(2)}, u32[]{:S(2)}) collective-permute-start(bf16[512,512]{1,0:T(8,128)(2,1)S(1)} %copy-done.2), channel_id=1, source_target_pairs={{0,1},{1,0},{2,3},{3,2},{4,5},{5,4},{6,7},{7,6},{8,9},{9,8},{10,11... | collective-permute-start | bytes 1572872 | tf_op jit(solution)/shard_map/ppermute | solution.py:275
  32.5 12.3 %collective-permute-start.5 = (bf16[512,512]{1,0:T(8,128)(2,1)}, bf16[512,512]{1,0:T(8,128)(2,1)S(1)}, u32[]{:S(2)}, u32[]{:S(2)}) collective-permute-start(bf16[512,512]{1,0:T(8,128)(2,1)} %collective-permute-done.3.refs_6_), channel_id=1, source_target_pairs={{0,1},{1,0},{2,3},{3,2},{4,5},{5,4},{6,7},{7,6},{8,9},{9,8},{10,11... | collective-permute-start | bytes 1572872 | tf_op jit(solution)/shard_map/ppermute | solution.py:275
  33.0 11.8 %copy-start.6 = (bf16[2,64,256]{2,1,0:T(8,128)(2,1)S(1)}, bf16[2,64,256]{2,1,0:T(8,128)(2,1)}, u32[]{:S(2)}) copy-start(bf16[2,64,256]{2,1,0:T(8,128)(2,1)} %copy-done.5) | copy-start | bytes 196612
  33.0 11.9 %copy-start.8 = (bf16[256,128]{1,0:T(8,128)(2,1)S(1)}, bf16[256,128]{1,0:T(8,128)(2,1)}, u32[]{:S(2)}) copy-start(bf16[256,128]{1,0:T(8,128)(2,1)} %copy-done.7) | copy-start | bytes 196612
  44.9 0.7 %copy-start.20 = (f32[1,512]{1,0:T(1,128)S(1)}, f32[1,512]{1,0:T(1,128)}, u32[]{:S(2)}) copy-start(f32[1,512]{1,0:T(1,128)} %copy-done.19) | copy-start | bytes 6148

commit v9 on v8

--- a/solution.py
+++ b/solution.py
@@ -88,6 +88,7 @@
 
 
 def prepare_kernel(
+    table,
     ready,
     live_ref,
     neigh_ref,
@@ -98,17 +99,13 @@
     cand_ref,
     labels_ref,
     out_w_ref,
-    count_ref,
-    power_ref,
-    diag_src_ref,
-    diag_dst_ref,
+    for_attend_ref,
+    for_score_ref,
     pick_ref,
-    scatter_ref,
-    known_ref,
-    weight_ref,
 ):
     ready()
-    nodes, table = count_ref.shape
+    nodes, ends = pick_ref.shape
+    heads, size = src_ref.shape
     slots = neigh_ref.shape[0]
     ids = neigh_ref[...]
     ids = jnp.where(lax.broadcasted_iota(jnp.int32, ids.shape, 0) < degree_ref[...], ids, -1)
@@ -124,21 +121,28 @@
         power = jnp.where(total > 2, 4.0, power)
         power = jnp.where(total > 5, 8.0, power)
         power = jnp.where(total > 13, 16.0, power)
-        count_ref[:, base : base + nodes] = total.astype(BF16)
-        power_ref[:, base : base + nodes] = power.astype(BF16)
-    diag_src_ref[...] = block_diagonal(src_ref[...])
-    diag_dst_ref[...] = block_diagonal(dst_ref[...])
-    ends = ends_ref.shape[1]
+        for_attend_ref[:nodes, base : base + nodes] = total.astype(BF16)
+        for_attend_ref[:nodes, table + base : table + base + nodes] = power.astype(BF16)
     node_at = lax.broadcasted_iota(jnp.int32, (nodes, ends), 0)
-    pick_ref[...] = (node_at == ends_ref[...]).astype(F32).astype(BF16)
+    pick = (node_at == ends_ref[...]).astype(F32).astype(BF16)
+    pick_ref[...] = pick
+    for_attend_ref[:nodes, 2 * table : 2 * table + ends] = pick
+    for_attend_ref[nodes : nodes + 4 * heads, : heads * size] = block_diagonal(src_ref[...])
+    for_attend_ref[nodes + 4 * heads :, : heads * size] = block_diagonal(dst_ref[...])
     cands = cand_ref.shape[1]
+    hidden = out_w_ref.shape[1]
     slot_at = lax.broadcasted_iota(jnp.int32, (ends, cands), 0)
     for i in range(2):
-        scatter_ref[i] = (slot_at == cand_ref[i : i + 1, :]).astype(F32).astype(BF16)
+        one_hot = (slot_at == cand_ref[i : i + 1, :]).astype(F32).astype(BF16)
+        for_score_ref[:ends, i * cands : (i + 1) * cands] = one_hot
     live = (lax.broadcasted_iota(jnp.int32, (1, cands), 1) < live_ref[0, 0]).astype(F32)
-    known = jnp.concatenate([live, labels_ref[...].astype(F32), jnp.zeros((126, cands), F32)], axis=0)
-    known_ref[...] = known.T.astype(BF16)
-    weight_ref[...] = out_w_ref[...]
+    known = jnp.concatenate([live, labels_ref[...].astype(F32), jnp.zeros((14, cands), F32)], axis=0)
+    for_score_ref[ends : ends + 16, :cands] = known.astype(BF16)
+    high = out_w_ref[...].astype(BF16).astype(F32)
+    middle = (out_w_ref[...] - high).astype(BF16).astype(F32)
+    low = out_w_ref[...] - high - middle
+    whole = jnp.concatenate([high, middle, low, jnp.zeros((13, hidden), F32)], axis=0)
+    for_score_ref[ends + 16 :, :hidden] = whole.astype(BF16)
 
 
 def shard_row(i, shards):
@@ -160,25 +164,18 @@
     return total
 
 
-def attend_kernel(
-    shard_count,
-    ready,
-    own_ref,
-    got_ref,
-    count_ref,
-    power_ref,
-    diag_src_ref,
-    diag_dst_ref,
-    pick_ref,
-    *rest,
-):
+def attend_kernel(shard_count, heads, slots, ready, own_ref, got_ref, known_ref, *rest):
     shards = rest[:shard_count]
     out_ref, send_ref, proj_ref, stage_ref, rows_ref, bias_ref, mix_ref, whole_ref = rest[-8:]
     ready()
     nodes, width = own_ref.shape
     table = proj_ref.shape[0]
-    heads = diag_src_ref.shape[0] // 4
     size = width // heads
+    diag_src_ref = known_ref.at[nodes : nodes + 4 * heads, :width]
+    diag_dst_ref = known_ref.at[nodes + 4 * heads :, :width]
+    count_ref = known_ref.at[:nodes, :table]
+    power_ref = known_ref.at[:nodes, table : 2 * table]
+    pick_ref = known_ref.at[:nodes, 2 * table : 2 * table + slots]
     rows_ref[:nodes, :] = own_ref[...]
     rows_ref[nodes:, :] = got_ref[...]
     proj_ref[...] = shard_dots(rows_ref, shards, whole_ref).astype(BF16)
@@ -228,30 +225,30 @@
     return jnp.concatenate(parts, axis=1).astype(BF16)
 
 
-def score_kernel(
-    shard_count, ready, got_ref, scatter_ref, known_ref, out_w_ref, *rest
-):
+def score_kernel(shard_count, cands, ready, got_ref, known_ref, *rest):
     shards = rest[:shard_count]
     scores_ref, back_ref, pair_ref, stage_ref, sum_ref, grad_ref = rest[shard_count:]
     ready()
-    cands = known_ref.shape[0]
-    depth = shards[0].shape[0]
+    depth, hidden = shards[0].shape
     slots, width = grad_ref.shape[1:]
+    picks = [known_ref[:slots, i * cands : (i + 1) * cands] for i in range(2)]
+    known = known_ref[slots : slots + 16, :cands].astype(F32).T
+    live, label = known[:, :1], known[:, 1:2]
+    out_w = known_ref[slots + 16 :, :hidden].astype(F32)
+    out_w = out_w[:1] + out_w[1:2] + out_w[2:3]
     rows = unpack_rows(got_ref, stage_ref, width // 128)
     for i in range(2):
         pair_ref[:, i * width : (i + 1) * width] = dot(
-            scatter_ref[i], rows, ((0,), (0,))
+            picks[i], rows, ((0,), (0,))
         ).astype(BF16)
     pre_act = shard_dots(pair_ref, shards)
-    out_w = out_w_ref[...]
-    live = known_ref[:, :1].astype(F32)
     gate = jax.nn.sigmoid(pre_act)
     score = jnp.sum(pre_act * gate * out_w, axis=1, keepdims=True) * live
     scores_ref[...] = jnp.broadcast_to(score, (cands, 128)).T[:1]
-    grad_score = (jax.nn.sigmoid(score) - known_ref[:, 1:2].astype(F32)) * live
+    grad_score = (jax.nn.sigmoid(score) - label) * live
     grad_pre = (grad_score * out_w * (gate * (1.0 + pre_act * (1.0 - gate)))).astype(BF16)
     for i in range(2):
-        total = dot(scatter_ref[i], grad_pre)
+        total = dot(picks[i], grad_pre)
         high = total.astype(BF16)
         sum_ref[i, :slots, :] = high
         sum_ref[i, slots:, :] = (total - high.astype(F32)).astype(BF16)
@@ -313,28 +310,22 @@
     shape = jax.ShapeDtypeStruct
 
     heads = attn_src.shape[0]
-    gat_across = across(gat_weight, edge_count)
     send_rows = call(
         halo_kernel,
         shape((halo, width), BF16),
         [("f", halo_count[0]), ("f", halo_rows[0, 0]), ("f", node_feats)],
         vmem_mib=60,
     )
-    gat_across = lax.optimization_barrier((*gat_across, send_rows))[: len(gat_across)]
     got_rows = lax.all_to_all(send_rows, "dom", split_axis=0, concat_axis=0, tiled=True)
-    mlp_across = across(lax.optimization_barrier((mlp_weight, send_rows))[0], edge_count)
-    gat_shards = from_core(gat_across)
-    prepared = call(
-        prepare_kernel,
+    gat_shards = from_core(across(gat_weight, edge_count))
+    mlp_shards = from_core(across(mlp_weight, edge_count))
+    lanes = -(-max(2 * table + slots, width) // 128) * 128
+    for_attend, for_score, pick = call(
+        functools.partial(prepare_kernel, table),
         (
-            shape((nodes, table), BF16),
-            shape((nodes, table), BF16),
-            shape((4 * heads, width), BF16),
-            shape((4 * heads, width), BF16),
+            shape((nodes + 8 * heads, lanes), BF16),
+            shape((slots + 32, max(2 * cands, hidden)), BF16),
             shape((nodes, slots), BF16),
-            shape((2, slots, cands), BF16),
-            shape((cands, 128), BF16),
-            shape((1, hidden), F32),
         ),
         [
             ("s", cand_count),
@@ -347,22 +338,13 @@
             ("f", labels[0]),
             ("f", out_weight.reshape(1, hidden)),
         ],
-    )
-    counts, powers, diag_src, diag_dst, pick, scatter, known, out_row = prepared
+        vmem_mib=60,
+    )
     packed = pltpu.VMEM((slots * pieces, 128), F32)
     node_out, send_ends = call(
-        functools.partial(attend_kernel, edge_count),
+        functools.partial(attend_kernel, edge_count, heads, slots),
         (shape((nodes, width), BF16), shape((slots * pieces, 128), BF16)),
-        [
-            ("v", node_feats),
-            ("v", got_rows),
-            ("v", counts),
-            ("v", powers),
-            ("v", diag_src),
-            ("v", diag_dst),
-            ("v", pick),
-        ]
-        + [("v", w) for w in gat_shards],
+        [("v", node_feats), ("v", got_rows), ("v", for_attend)] + [("v", w) for w in gat_shards],
         [
             pltpu.VMEM((table, width), BF16),
             packed,
@@ -372,18 +354,11 @@
             pltpu.VMEM((width if width // edge_count % 128 else 16, width), BF16),
         ],
     )
-    mlp_across = lax.optimization_barrier((send_ends, *mlp_across))[1:]
-    mlp_shards = from_core(mlp_across)
     got_ends = lax.all_to_all(send_ends, everyone, split_axis=0, concat_axis=0, tiled=True)
     scores, send_back = call(
-        functools.partial(score_kernel, edge_count),
+        functools.partial(score_kernel, edge_count, cands),
         (shape((1, cands), F32), shape((slots * pieces, 128), BF16)),
-        [
-            ("v", got_ends),
-            ("v", scatter),
-            ("v", known),
-            ("v", out_row),
-        ]
+        [("v", got_ends), ("v", for_score)]
         + [("v", w) for w in mlp_shards],
         [
             pltpu.VMEM((cands, 2 * width), BF16),

time: 61 us -> 65.5 us (1.074)
  waiting for transfers between devices: 4.95 us -> 22.3 us
  blocking collectives: 21.8 us -> 10 us
  local copies, waits for them, and re-layouts: 9.08 us -> 1.75 us
  starting transfers between devices: 11.8 us -> 16.3 us
  Pallas kernels: 11.3 us -> 13.3 us
    all_to_all x1 -> x0, blocking collectives: 11.8 us -> none  [local(): lax.all_to_all(send_ends, everyone, split_axis=0, concat_axis=0, tiled=True)]
    ppermute x6, waiting for transfers between devices: 3.8 us -> 14 us  [swap(): return lax.ppermute(array, axis, [(i, i ^ k) for i in range(count)])]
    all_to_all x0 -> x1, waiting for transfers between devices: none -> 8.21 us  [local(): lax.all_to_all(send_ends, everyone, split_axis=0, concat_axis=0, tiled=True)]
    unnamed x49 -> x15, local copies, waits for them, and re-layouts: 8.46 us -> 1.13 us
    all_to_all x0 -> x1, starting transfers between devices: none -> 6.19 us  [local(): lax.all_to_all(send_ends, everyone, split_axis=0, concat_axis=0, tiled=True)]
    pallas_call x5, Pallas kernels: 11.3 us -> 13.3 us  [call(): pl.pallas_call(body, out_shape=outs, in_specs=[SPACES[space] for space, _...]
    ppermute x6, starting transfers between devices: 5.85 us -> 4.12 us  [swap(): return lax.ppermute(array, axis, [(i, i ^ k) for i in range(count)])]
    all_to_all x1, waiting for transfers between devices: 1.15 us -> 0.01 us  [local(): lax.all_to_all(send_rows, 'dom', split_axis=0, concat_axis=0, tiled=True)]
  transfers between devices with their start and end apart: 7 -> 8, of which waited for: 2 -> 3; matrix products, arithmetic and copies ran while one was open for 1% -> 1% of each run, Pallas kernels for 11% -> 13%
where the time goes in v9:
time: 65.5 us; the launch traced here: 65 us
  waiting for transfers between devices  22.3 us (34%)
  starting transfers between devices  16.3 us (25%)
  Pallas kernels  13.3 us (20%)
  blocking collectives  10 us (15%)
  local copies, waits for them, and re-layouts  1.75 us (3%)
  between operations  1.44 us (2%)
    ppermute x6, waiting for transfers between devices, swap(): return lax.ppermute(array, axis, [(i, i ^ k) for i in range(count)])  14 us
    pallas_call x5, Pallas kernels, call(): pl.pallas_call(body, out_shape=outs, in_specs=[SPACES[space] for space, _...  13.3 us
    all_to_all x1, blocking collectives, local(): lax.all_to_all(send_back, everyone, split_axis=0, concat_axis=0, tiled=True)  10 us
    all_to_all x1, waiting for transfers between devices, local(): lax.all_to_all(send_ends, everyone, split_axis=0, concat_axis=0, tiled=True)  8.21 us
    all_to_all x1, starting transfers between devices, local(): lax.all_to_all(send_ends, everyone, split_axis=0, concat_axis=0, tiled=True)  6.19 us
    all_to_all x1, starting transfers between devices, local(): lax.all_to_all(send_rows, 'dom', split_axis=0, concat_axis=0, tiled=True)  5.95 us
    ppermute x6, starting transfers between devices, swap(): return lax.ppermute(array, axis, [(i, i ^ k) for i in range(count)])  4.12 us
  transfers between devices with their start and end apart: 8, of which 3 were waited for; matrix products, arithmetic and copies ran while one was open for 1% of the time, Pallas kernels for 13%

profile of v9, /device:TPU:0, one launch (start us, length us, event | category | flops | bytes accessed | tf_op | source)
XLA Modules:
  0.0 65.0 jit_solution(14041192657736026775)
XLA Ops:
  0.6 3.0 %collective-permute-start.1 = (bf16[256,1024]{1,0:T(8,128)(2,1)}, bf16[256,1024]{1,0:T(8,128)(2,1)S(1)}, u32[]{:S(2)}, u32[]{:S(2)}) collective-permute-start(bf16[256,1024]{1,0:T(8,128)(2,1)} %refs_3_.3), channel_id=1, source_target_pairs={{0,2},{1,3},{2,0},{3,1},{4,6},{5,7},{6,4},{7,5},{8,10},{9,11},{10,... | collective-permute-start | bytes 1572872 | tf_op jit(solution)/shard_map/ppermute | solution.py:272
  3.7 2.4 %shard_map.157 = bf16[256,1024]{1,0:T(8,128)(2,1)} custom-call(s32[1,8]{1,0:T(1,128)} %bitcast.25, s32[8,32]{1,0:T(8,128)} %bitcast.20, bf16[128,1024]{1,0:T(8,128)(2,1)} %refs_0_.2), custom_call_target="tpu_custom_call" | custom-call | tf_op jit(solution)/shard_map/pallas_call | solution.py:45
  6.0 0.0 copy-start.1
  6.0 0.0 copy-start.6
  6.0 0.0 copy-start
  6.1 5.9 %all-to-all-start = ((bf16[8,32,1024]{2,1,0:T(8,128)(2,1)}), bf16[8,32,1024]{2,1,0:T(8,128)(2,1)S(1)}, u32[]{:S(2)}, u32[]{:S(2)}) async-start(bf16[8,32,1024]{2,1,0:T(8,128)(2,1)} %bitcast.18), calls=%async_computation | async-start | bytes 1048576 | tf_op jit(solution)/shard_map/all_to_all | solution.py:319
  12.0 0.0 copy-done.2
  12.0 0.6 collective-permute-start.4
  12.6 0.0 collective-permute-start
  12.6 4.0 %collective-permute-done.1.refs_5_ = bf16[256,1024]{1,0:T(8,128)(2,1)S(1)} collective-permute-done((bf16[256,1024]{1,0:T(8,128)(2,1)}, bf16[256,1024]{1,0:T(8,128)(2,1)S(1)}, u32[]{:S(2)}, u32[]{:S(2)}) %collective-permute-start.1) | collective-permute-done | bytes 524320 | tf_op jit(solution)/shard_map/ppermute | solution.py:272
  16.6 0.0 collective-permute-start.2
  16.6 0.5 collective-permute-start.3
  17.1 10.0 %collective-permute-done.4.refs_4_ = bf16[512,512]{1,0:T(8,128)(2,1)} collective-permute-done((bf16[512,512]{1,0:T(8,128)(2,1)S(1)}, bf16[512,512]{1,0:T(8,128)(2,1)}, u32[]{:S(2)}, u32[]{:S(2)}) %collective-permute-start.4) | collective-permute-done | bytes 524320 | tf_op jit(solution)/shard_map/ppermute | solution.py:272
  27.1 0.0 collective-permute-start.5
  27.8 0.0 copy-done.6
  27.8 0.1 copy.18
  27.9 0.6 reshape.25.refs_5_
  28.5 2.1 %shard_map.158 = (bf16[192,1024]{1,0:T(8,128)(2,1)}, bf16[96,512]{1,0:T(8,128)(2,1)}, bf16[128,64]{1,0:T(8,128)(2,1)}) custom-call(s32[1,1]{1,0:T(1,128)S(6)} %copy.19.refs_0_, s32[16,128]{1,0:T(8,128)} %bitcast.19, s32[1,128]{1,0:T(1,128)} %bitcast.24, f32[8,128]{1,0:T(8,128)} %refs_3_.2, f32[8,128]{1,0:T(8,128)} %refs_4_.1, s32[1,64]{1,0:T(1,128)} %reshape.25.refs_5_, ...), custom_call_target="tpu_custom_call" | custom-call | tf_op jit(solution)/shard_map/pallas_call | solution.py:45
  30.6 0.0 collective-permute-done.refs_4_
  30.7 0.0 all-to-all-done
  30.7 0.0 collective-permute-done.2.refs_6_
  30.7 1.0 %copy-done.3 = bf16[192,1024]{1,0:T(8,128)(2,1)S(1)} copy-done((bf16[192,1024]{1,0:T(8,128)(2,1)S(1)}, bf16[192,1024]{1,0:T(8,128)(2,1)}, u32[]{:S(2)}) %copy-start.3) | copy-done | bytes 393240
  31.7 3.7 %shard_map.159 = (bf16[128,1024]{1,0:T(8,128)(2,1)}, bf16[512,128]{1,0:T(8,128)(2,1)}) custom-call(bf16[128,1024]{1,0:T(8,128)(2,1)S(1)} %copy-done, bf16[256,1024]{1,0:T(8,128)(2,1)S(1)} %bitcast.14, bf16[192,1024]{1,0:T(8,128)(2,1)S(1)} %copy-done.3, bf16[256,1024]{1,0:T(8,128)(2,1)S(1)} %copy-done.1, bf16[256,1024]{1,0:T(8,128)(2,1)S(1)} %collective-permute-done.refs_4_, ...), custom_call_target="tpu_custom_call" | custom-call | tf_op jit(solution)/shard_map/pallas_call | solution.py:45
  35.4 6.2 %all-to-all-start.1 = ((bf16[32,16,128]{2,1,0:T(8,128)(2,1)}), bf16[32,16,128]{2,1,0:T(8,128)(2,1)S(1)}, u32[]{:S(2)}, u32[]{:S(2)}) async-start(bf16[32,16,128]{2,1,0:T(8,128)(2,1)} %bitcast.9), calls=%async_computation.1 | async-start | bytes 262144 | tf_op jit(solution)/shard_map/all_to_all | solution.py:357
  41.6 0.0 collective-permute-done.3.refs_3_
  41.6 0.0 collective-permute-done.5.refs_5_
  41.6 8.2 %all-to-all-done.1 = bf16[32,16,128]{2,1,0:T(8,128)(2,1)S(1)} async-done(((bf16[32,16,128]{2,1,0:T(8,128)(2,1)}), bf16[32,16,128]{2,1,0:T(8,128)(2,1)S(1)}, u32[]{:S(2)}, u32[]{:S(2)}) %all-to-all-start.1) | async-done | bytes 131104 | tf_op jit(solution)/shard_map/all_to_all | solution.py:357
  49.8 0.0 copy-done.4
  49.8 4.1 %shard_map.160 = (f32[1,256]{1,0:T(1,128)}, bf16[512,128]{1,0:T(8,128)(2,1)S(1)}) custom-call(bf16[512,128]{1,0:T(8,128)(2,1)S(1)} %bitcast.15, bf16[96,512]{1,0:T(8,128)(2,1)S(1)} %copy-done.4, bf16[512,512]{1,0:T(8,128)(2,1)S(1)} %copy-done.2, bf16[512,512]{1,0:T(8,128)(2,1)} %collective-permute-done.3.refs_3_, ...), custom_call_target="tpu_custom_call" | custom-call | tf_op jit(solution)/shard_map/pallas_call | solution.py:45
  54.0 0.0 copy-start.5
  54.0 10.0 %all_to_all.33 = bf16[32,16,128]{2,1,0:T(8,128)(2,1)S(1)} all-to-all(bf16[32,16,128]{2,1,0:T(8,128)(2,1)S(1)} %bitcast.17), channel_id=1, replica_groups=mesh['dom'=8,'edge'=4] {'dom','edge'}, dimensions={0} | all-to-all | bytes 262144 | tf_op jit(solution)/shard_map/all_to_all | solution.py:370
  64.0 1.0 %shard_map.161 = f32[128,1024]{1,0:T(8,128)} custom-call(bf16[128,64]{1,0:T(8,128)(2,1)S(1)} %copy-done.5, bf16[512,128]{1,0:T(8,128)(2,1)S(1)} %bitcast.16), custom_call_target="tpu_custom_call" | custom-call | tf_op jit(solution)/shard_map/pallas_call | solution.py:45
  (6 shorter events, 0.0 us)
Async XLA Ops:
  0.6 16.0 %collective-permute-start.1 = (bf16[256,1024]{1,0:T(8,128)(2,1)}, bf16[256,1024]{1,0:T(8,128)(2,1)S(1)}, u32[]{:S(2)}, u32[]{:S(2)}) collective-permute-start(bf16[256,1024]{1,0:T(8,128)(2,1)} %refs_3_.3), channel_id=1, source_target_pairs={{0,2},{1,3},{2,0},{3,1},{4,6},{5,7},{6,4},{7,5},{8,10},{9,11},{10,... | collective-permute-start | bytes 1572872 | tf_op jit(solution)/shard_map/ppermute | solution.py:272
  3.7 8.3 %copy-start.2 = (bf16[512,512]{1,0:T(8,128)(2,1)S(1)}, bf16[512,512]{1,0:T(8,128)(2,1)}, u32[]{:S(2)}) copy-start(bf16[512,512]{1,0:T(8,128)(2,1)} %refs_2_.3) | copy-start | bytes 1572868
  6.0 6.6 %copy-start.1 = (bf16[256,1024]{1,0:T(8,128)(2,1)S(1)}, bf16[256,1024]{1,0:T(8,128)(2,1)}, u32[]{:S(2)}) copy-start(bf16[256,1024]{1,0:T(8,128)(2,1)} %refs_3_.3) | copy-start | bytes 1572868
  6.0 21.8 %copy-start.6 = (s32[1,1,8,4,2]{2,4,3,1,0:T(2,128)S(1)}, s32[1,1,8,4,2]{2,4,3,1,0:T(2,128)}, u32[]{:S(2)}) copy-start(s32[1,1,8,4,2]{2,4,3,1,0:T(2,128)} %param.22) | copy-start | bytes 772
  6.0 24.6 %copy-start = (bf16[128,1024]{1,0:T(8,128)(2,1)S(1)}, bf16[128,1024]{1,0:T(8,128)(2,1)}, u32[]{:S(2)}) copy-start(bf16[128,1024]{1,0:T(8,128)(2,1)} %refs_0_.2) | copy-start | bytes 786436
  6.1 24.6 %all-to-all-start = ((bf16[8,32,1024]{2,1,0:T(8,128)(2,1)}), bf16[8,32,1024]{2,1,0:T(8,128)(2,1)S(1)}, u32[]{:S(2)}, u32[]{:S(2)}) async-start(bf16[8,32,1024]{2,1,0:T(8,128)(2,1)} %bitcast.18), calls=%async_computation | async-start | bytes 1048576 | tf_op jit(solution)/shard_map/all_to_all | solution.py:319
  12.0 15.1 %collective-permute-start.4 = (bf16[512,512]{1,0:T(8,128)(2,1)S(1)}, bf16[512,512]{1,0:T(8,128)(2,1)}, u32[]{:S(2)}, u32[]{:S(2)}) collective-permute-start(bf16[512,512]{1,0:T(8,128)(2,1)S(1)} %copy-done.2), channel_id=1, source_target_pairs={{0,2},{1,3},{2,0},{3,1},{4,6},{5,7},{6,4},{7,5},{8,10},{9,11},{10,... | collective-permute-start | bytes 1572872 | tf_op jit(solution)/shard_map/ppermute | solution.py:272
  12.6 18.1 %collective-permute-start = (bf16[256,1024]{1,0:T(8,128)(2,1)S(1)}, bf16[256,1024]{1,0:T(8,128)(2,1)S(1)}, u32[]{:S(2)}, u32[]{:S(2)}) collective-permute-start(bf16[256,1024]{1,0:T(8,128)(2,1)S(1)} %copy-done.1), channel_id=1, source_target_pairs={{0,1},{1,0},{2,3},{3,2},{4,5},{5,4},{6,7},{7,6},{8,9},{9,8},{10,11... | collective-permute-start | bytes 1572872 | tf_op jit(solution)/shard_map/ppermute | solution.py:272
  16.6 14.0 %collective-permute-start.2 = (bf16[256,1024]{1,0:T(8,128)(2,1)S(1)}, bf16[256,1024]{1,0:T(8,128)(2,1)S(1)}, u32[]{:S(2)}, u32[]{:S(2)}) collective-permute-start(bf16[256,1024]{1,0:T(8,128)(2,1)S(1)} %collective-permute-done.1.refs_5_), channel_id=1, source_target_pairs={{0,1},{1,0},{2,3},{3,2},{4,5},{5,4},{6,7},{7,6},{8,9},{9,8},{10,11... | collective-permute-start | bytes 1572872 | tf_op jit(solution)/shard_map/ppermute | solution.py:272
  16.6 25.0 %collective-permute-start.3 = (bf16[512,512]{1,0:T(8,128)(2,1)S(1)}, bf16[512,512]{1,0:T(8,128)(2,1)}, u32[]{:S(2)}, u32[]{:S(2)}) collective-permute-start(bf16[512,512]{1,0:T(8,128)(2,1)S(1)} %copy-done.2), channel_id=1, source_target_pairs={{0,1},{1,0},{2,3},{3,2},{4,5},{5,4},{6,7},{7,6},{8,9},{9,8},{10,11... | collective-permute-start | bytes 1572872 | tf_op jit(solution)/shard_map/ppermute | solution.py:272
  27.1 14.5 %collective-permute-start.5 = (bf16[512,512]{1,0:T(8,128)(2,1)}, bf16[512,512]{1,0:T(8,128)(2,1)}, u32[]{:S(2)}, u32[]{:S(2)}) collective-permute-start(bf16[512,512]{1,0:T(8,128)(2,1)} %collective-permute-done.4.refs_4_), channel_id=1, source_target_pairs={{0,1},{1,0},{2,3},{3,2},{4,5},{5,4},{6,7},{7,6},{8,9},{9,8},{10,11... | collective-permute-start | bytes 1572872 | tf_op jit(solution)/shard_map/ppermute | solution.py:272
  30.7 1.0 %copy-start.3 = (bf16[192,1024]{1,0:T(8,128)(2,1)S(1)}, bf16[192,1024]{1,0:T(8,128)(2,1)}, u32[]{:S(2)}) copy-start(bf16[192,1024]{1,0:T(8,128)(2,1)} %get-tuple-element.10.refs_2_) | copy-start | bytes 1179652
  35.4 14.4 %copy-start.4 = (bf16[96,512]{1,0:T(8,128)(2,1)S(1)}, bf16[96,512]{1,0:T(8,128)(2,1)}, u32[]{:S(2)}) copy-start(bf16[96,512]{1,0:T(8,128)(2,1)} %get-tuple-element.13.refs_1_) | copy-start | bytes 294916
  35.4 14.4 %all-to-all-start.1 = ((bf16[32,16,128]{2,1,0:T(8,128)(2,1)}), bf16[32,16,128]{2,1,0:T(8,128)(2,1)S(1)}, u32[]{:S(2)}, u32[]{:S(2)}) async-start(bf16[32,16,128]{2,1,0:T(8,128)(2,1)} %bitcast.9), calls=%async_computation.1 | async-start | bytes 262144 | tf_op jit(solution)/shard_map/all_to_all | solution.py:357
  54.0 10.0 %copy-start.5 = (bf16[128,64]{1,0:T(8,128)(2,1)S(1)}, bf16[128,64]{1,0:T(8,128)(2,1)}, u32[]{:S(2)}) copy-start(bf16[128,64]{1,0:T(8,128)(2,1)} %get-tuple-element.15.refs_0_) | copy-start | bytes 49156

commit v10 on v9

--- a/solution.py
+++ b/solution.py
@@ -16,6 +16,7 @@
     "v": VMEM,
     "s": pl.BlockSpec(memory_space=pltpu.SMEM),
     "f": pl.BlockSpec(memory_space=pl.ANY),
+    "any": pl.BlockSpec(memory_space=pl.ANY),
 }
 
 
@@ -23,7 +24,7 @@
     return lax.dot_general(a, b, (dims, ((), ())), preferred_element_type=F32)
 
 
-def call(kernel, outs, ins, scratch=(), vmem_mib=20):
+def call(kernel, outs, ins, scratch=(), vmem_mib=20, out_space="v"):
     fetched = [i for i, (space, _) in enumerate(ins) if space == "f"]
 
     def body(*refs):
@@ -46,7 +47,7 @@
         body,
         out_shape=outs,
         in_specs=[SPACES[space] for space, _ in ins],
-        out_specs=jax.tree.map(lambda _: VMEM, outs),
+        out_specs=jax.tree.map(lambda _: SPACES[out_space], outs),
         scratch_shapes=list(scratch)
         + [pltpu.VMEM(ins[i][1].shape, ins[i][1].dtype) for i in fetched]
         + [pltpu.SemaphoreType.DMA((max(1, len(fetched)),))],
@@ -54,26 +55,47 @@
     )(*[array for _, array in ins])
 
 
-def halo_kernel(ready, count_ref, rows_ref, feats_ref, out_ref):
+def halo_kernel(
+    ready, count_ref, rows_ref, feats_ref, out_ref, held_ref, done_ref, in_sems, out_sems
+):
+    chunks = in_sems.shape[0]
+    wide = feats_ref.shape[1] // chunks
+    cols = [pl.ds(i * wide, wide) for i in range(chunks)]
+    loads = [
+        pltpu.make_async_copy(feats_ref.at[:, c], held_ref.at[:, c], in_sems.at[i])
+        for i, c in enumerate(cols)
+    ]
+    stores = [
+        pltpu.make_async_copy(done_ref.at[:, c], out_ref.at[:, c], out_sems.at[i])
+        for i, c in enumerate(cols)
+    ]
+    for load in loads:
+        load.start()
     doms, block = rows_ref.shape
+    total = doms * block
+    nodes = feats_ref.shape[0]
     at = lax.broadcasted_iota(jnp.int32, (1, block), 1)
     ready()
     pieces = [
         jnp.where(at < count_ref[:, s : s + 1], rows_ref[s : s + 1, :], -1) for s in range(doms)
     ]
     flat = jnp.concatenate(pieces, axis=1)
-    total = doms * block
-    nodes = feats_ref.shape[0]
     pick = (lax.broadcasted_iota(jnp.int32, (nodes, total), 0) == flat).astype(F32).astype(BF16)
-    rows = dot(pick, feats_ref[...], ((0,), (0,)))
     first = lax.broadcasted_iota(jnp.int32, (16, total), 0) == 0
     dead = jnp.where(first & (flat < 0), 1.0, 0.0).astype(BF16)
-    mark_at = (lax.broadcasted_iota(jnp.int32, (16, 128), 0) == 0) & (
-        lax.broadcasted_iota(jnp.int32, (16, 128), 1) == 0
+    mark_at = (lax.broadcasted_iota(jnp.int32, (16, wide), 0) == 0) & (
+        lax.broadcasted_iota(jnp.int32, (16, wide), 1) == 0
     )
     mark = jnp.where(mark_at, DEAD, 0.0).astype(BF16)
-    out_ref[:, :128] = (rows[:, :128] + dot(dead, mark, ((0,), (0,)))).astype(BF16)
-    out_ref[:, 128:] = rows[:, 128:].astype(BF16)
+    for i, c in enumerate(cols):
+        loads[i].wait()
+        rows = dot(pick, held_ref[:, c], ((0,), (0,)))
+        if i == 0:
+            rows = rows + dot(dead, mark, ((0,), (0,)))
+        done_ref[:, c] = rows.astype(BF16)
+        stores[i].start()
+    for store in stores:
+        store.wait()
 
 
 def block_diagonal(vectors):
@@ -227,7 +249,7 @@
 
 def score_kernel(shard_count, cands, ready, got_ref, known_ref, *rest):
     shards = rest[:shard_count]
-    scores_ref, back_ref, pair_ref, stage_ref, sum_ref, grad_ref = rest[shard_count:]
+    scores_ref, back_ref, rows_ref, stage_ref, sum_ref, grad_ref, part_ref = rest[shard_count:]
     ready()
     depth, hidden = shards[0].shape
     slots, width = grad_ref.shape[1:]
@@ -237,11 +259,26 @@
     out_w = known_ref[slots + 16 :, :hidden].astype(F32)
     out_w = out_w[:1] + out_w[1:2] + out_w[2:3]
     rows = unpack_rows(got_ref, stage_ref, width // 128)
-    for i in range(2):
-        pair_ref[:, i * width : (i + 1) * width] = dot(
-            picks[i], rows, ((0,), (0,))
-        ).astype(BF16)
-    pre_act = shard_dots(pair_ref, shards)
+    if slots > cands:
+        for i in range(2):
+            pair = dot(picks[i], rows, ((0,), (0,)))
+            rows_ref[:, i * width : (i + 1) * width] = pair.astype(BF16)
+        pre_act = shard_dots(rows_ref, shards)
+    else:
+        rows_ref[...] = rows
+        part_ref[...] = jnp.zeros_like(part_ref)
+        for i, shard in enumerate(shards):
+            row = shard_row(i, shards)
+            cols = pl.ds(pl.multiple_of(row % width, depth), depth)
+            part_ref[row // width] += dot(rows_ref[:, cols], shard[...])
+        pre_act = None
+        for i in range(2):
+            rest = part_ref[i]
+            for _ in range(3):
+                high = rest.astype(BF16)
+                rest = rest - high.astype(F32)
+                term = dot(picks[i], high, ((0,), (0,)))
+                pre_act = term if pre_act is None else pre_act + term
     gate = jax.nn.sigmoid(pre_act)
     score = jnp.sum(pre_act * gate * out_w, axis=1, keepdims=True) * live
     scores_ref[...] = jnp.broadcast_to(score, (cands, 128)).T[:1]
@@ -313,12 +350,19 @@
     send_rows = call(
         halo_kernel,
         shape((halo, width), BF16),
-        [("f", halo_count[0]), ("f", halo_rows[0, 0]), ("f", node_feats)],
+        [("f", halo_count[0]), ("f", halo_rows[0, 0]), ("any", node_feats)],
+        [
+            pltpu.VMEM((nodes, width), BF16),
+            pltpu.VMEM((halo, width), BF16),
+            pltpu.SemaphoreType.DMA((4,)),
+            pltpu.SemaphoreType.DMA((4,)),
+        ],
         vmem_mib=60,
+        out_space="any",
     )
     got_rows = lax.all_to_all(send_rows, "dom", split_axis=0, concat_axis=0, tiled=True)
-    gat_shards = from_core(across(gat_weight, edge_count))
-    mlp_shards = from_core(across(mlp_weight, edge_count))
+    gat_across = across(gat_weight, edge_count)
+    mlp_across = across(mlp_weight, edge_count)
     lanes = -(-max(2 * table + slots, width) // 128) * 128
     for_attend, for_score, pick = call(
         functools.partial(prepare_kernel, table),
@@ -340,6 +384,8 @@
         ],
         vmem_mib=60,
     )
+    gat_across = lax.optimization_barrier((*gat_across, for_attend))[:-1]
+    gat_shards = from_core(gat_across)
     packed = pltpu.VMEM((slots * pieces, 128), F32)
     node_out, send_ends = call(
         functools.partial(attend_kernel, edge_count, heads, slots),
@@ -354,6 +400,7 @@
             pltpu.VMEM((width if width // edge_count % 128 else 16, width), BF16),
         ],
     )
+    mlp_shards = from_core(lax.optimization_barrier((*mlp_across, send_ends))[:-1])
     got_ends = lax.all_to_all(send_ends, everyone, split_axis=0, concat_axis=0, tiled=True)
     scores, send_back = call(
         functools.partial(score_kernel, edge_count, cands),
@@ -361,10 +408,11 @@
         [("v", got_ends), ("v", for_score)]
         + [("v", w) for w in mlp_shards],
         [
-            pltpu.VMEM((cands, 2 * width), BF16),
+            pltpu.VMEM((cands, 2 * width) if slots > cands else (slots, width), BF16),
             packed,
             pltpu.VMEM((2, 2 * slots, hidden), BF16),
             pltpu.VMEM((2, slots, width), F32),
+            pltpu.VMEM((2, slots, hidden), F32),
         ],
     )
     got_back = lax.all_to_all(send_back, everyone, split_axis=0, concat_axis=0, tiled=True)

time: 65.5 us -> 60.2 us (0.919)
  waiting for transfers between devices: 22.3 us -> 8.53 us
  blocking collectives: 10 us -> 23.1 us
  starting transfers between devices: 16.3 us -> 11.8 us
    ppermute x6, waiting for transfers between devices: 14 us -> 0.05 us  [swap(): return lax.ppermute(array, axis, [(i, i ^ k) for i in range(count)])]
    all_to_all x0 -> x1, blocking collectives: none -> 13.1 us  [local(): lax.all_to_all(send_ends, everyone, split_axis=0, concat_axis=0, tiled=True)]
    all_to_all x1, waiting for transfers between devices: 0.01 us -> 8.49 us  [local(): lax.all_to_all(send_rows, 'dom', split_axis=0, concat_axis=0, tiled=True)]
    all_to_all x1 -> x0, waiting for transfers between devices: 8.21 us -> none  [local(): lax.all_to_all(send_ends, everyone, split_axis=0, concat_axis=0, tiled=True)]
    all_to_all x1 -> x0, starting transfers between devices: 6.19 us -> none  [local(): lax.all_to_all(send_ends, everyone, split_axis=0, concat_axis=0, tiled=True)]
    ppermute x6, starting transfers between devices: 4.12 us -> 5.84 us  [swap(): return lax.ppermute(array, axis, [(i, i ^ k) for i in range(count)])]
  transfers between devices with their start and end apart: 8 -> 7, of which waited for: 3 -> 1; matrix products, arithmetic and copies ran while one was open for 1% -> 1% of each run, Pallas kernels for 13% -> 14%
where the time goes in v10:
time: 60.2 us; the launch traced here: 59.7 us
  blocking collectives  23.1 us (38%)
  Pallas kernels  13.1 us (22%)
  starting transfers between devices  11.8 us (20%)
  waiting for transfers between devices  8.53 us (14%)
  local copies, waits for them, and re-layouts  1.75 us (3%)
  between operations  1.4 us (2%)
    all_to_all x1, blocking collectives, local(): lax.all_to_all(send_ends, everyone, split_axis=0, concat_axis=0, tiled=True)  13.1 us
    pallas_call x5, Pallas kernels, call(): pl.pallas_call(body, out_shape=outs, in_specs=[SPACES[space] for space, _...  13.1 us
    all_to_all x1, blocking collectives, local(): lax.all_to_all(send_back, everyone, split_axis=0, concat_axis=0, tiled=True)  10 us
    all_to_all x1, waiting for transfers between devices, local(): lax.all_to_all(send_rows, 'dom', split_axis=0, concat_axis=0, tiled=True)  8.49 us
    all_to_all x1, starting transfers between devices, local(): lax.all_to_all(send_rows, 'dom', split_axis=0, concat_axis=0, tiled=True)  5.95 us
    ppermute x6, starting transfers between devices, swap(): return lax.ppermute(array, axis, [(i, i ^ k) for i in range(count)])  5.84 us
  transfers between devices with their start and end apart: 7, of which 1 were waited for; matrix products, arithmetic and copies ran while one was open for 1% of the time, Pallas kernels for 14%

profile of v10, /device:TPU:0, one launch (start us, length us, event | category | flops | bytes accessed | tf_op | source)
XLA Modules:
  0.0 59.7 jit_solution(13612211161682529694)
XLA Ops:
  0.6 3.0 %collective-permute-start = (bf16[256,1024]{1,0:T(8,128)(2,1)}, bf16[256,1024]{1,0:T(8,128)(2,1)S(1)}, u32[]{:S(2)}, u32[]{:S(2)}) collective-permute-start(bf16[256,1024]{1,0:T(8,128)(2,1)} %refs_3_.2), channel_id=1, source_target_pairs={{0,2},{1,3},{2,0},{3,1},{4,6},{5,7},{6,4},{7,5},{8,10},{9,11},{10,... | collective-permute-start | bytes 1572872 | tf_op jit(solution)/shard_map/ppermute | solution.py:309
  3.7 2.6 %shard_map.157 = bf16[256,1024]{1,0:T(8,128)(2,1)} custom-call(s32[1,8]{1,0:T(1,128)} %bitcast.26, s32[8,32]{1,0:T(8,128)} %bitcast.21, bf16[128,1024]{1,0:T(8,128)(2,1)} %refs_0_.2), custom_call_target="tpu_custom_call" | custom-call | tf_op jit(solution)/shard_map/pallas_call | solution.py:46
  6.3 0.0 copy-start.6
  6.3 0.0 copy-start.1
  6.3 0.0 copy-start
  6.3 6.0 %all-to-all-start = ((bf16[8,32,1024]{2,1,0:T(8,128)(2,1)}), bf16[8,32,1024]{2,1,0:T(8,128)(2,1)S(1)}, u32[]{:S(2)}, u32[]{:S(2)}) async-start(bf16[8,32,1024]{2,1,0:T(8,128)(2,1)} %bitcast.19), calls=%async_computation | async-start | bytes 1048576 | tf_op jit(solution)/shard_map/all_to_all | solution.py:363
  12.9 0.0 copy-done.6
  12.9 0.1 copy.18
  13.1 0.6 %reshape.25.refs_5_ = s32[1,64]{1,0:T(1,128)} reshape(s32[1,1,8,4,2]{4,3,2,1,0:T(4,128)S(1)} %copy.18) | data formatting | bytes 512 | tf_op jit(solution)/shard_map/reshape | solution.py:380
  13.7 2.1 %shard_map.158 = (bf16[192,1024]{1,0:T(8,128)(2,1)}, bf16[96,512]{1,0:T(8,128)(2,1)}, bf16[128,64]{1,0:T(8,128)(2,1)}) custom-call(s32[1,1]{1,0:T(1,128)S(6)} %copy.19.refs_0_, s32[16,128]{1,0:T(8,128)} %bitcast.20, s32[1,128]{1,0:T(1,128)} %bitcast.25, f32[8,128]{1,0:T(8,128)} %refs_3_.1, f32[8,128]{1,0:T(8,128)} %refs_4_.1, s32[1,64]{1,0:T(1,128)} %reshape.25.refs_5_, ...), custom_call_target="tpu_custom_call" | custom-call | tf_op jit(solution)/shard_map/pallas_call | solution.py:46
  15.8 0.0 collective-permute-done.refs_5_
  15.8 0.0 copy-done.1
  15.8 0.1 collective-permute-start.1
  15.9 0.5 collective-permute-start.2
  16.4 0.0 copy-done.2
  16.4 1.7 %collective-permute-start.3 = (bf16[512,512]{1,0:T(8,128)(2,1)S(1)}, bf16[512,512]{1,0:T(8,128)(2,1)}, u32[]{:S(2)}, u32[]{:S(2)}) collective-permute-start(bf16[512,512]{1,0:T(8,128)(2,1)S(1)} %copy-done.2), channel_id=1, source_target_pairs={{0,2},{1,3},{2,0},{3,1},{4,6},{5,7},{6,4},{7,5},{8,10},{9,11},{10,... | collective-permute-start | bytes 1572872 | tf_op jit(solution)/shard_map/ppermute | solution.py:309
  18.1 8.5 %all-to-all-done = bf16[8,32,1024]{2,1,0:T(8,128)(2,1)S(1)} async-done(((bf16[8,32,1024]{2,1,0:T(8,128)(2,1)}), bf16[8,32,1024]{2,1,0:T(8,128)(2,1)S(1)}, u32[]{:S(2)}, u32[]{:S(2)}) %all-to-all-start) | async-done | bytes 524320 | tf_op jit(solution)/shard_map/all_to_all | solution.py:363
  26.5 0.0 collective-permute-done.1.refs_4_
  26.5 0.0 collective-permute-done.2.refs_6_
  26.5 0.0 copy-done
  26.6 0.0 copy-start.3
  26.6 1.0 %copy-done.3 = bf16[192,1024]{1,0:T(8,128)(2,1)S(1)} copy-done((bf16[192,1024]{1,0:T(8,128)(2,1)S(1)}, bf16[192,1024]{1,0:T(8,128)(2,1)}, u32[]{:S(2)}) %copy-start.3) | copy-done | bytes 393240
  27.6 3.6 %shard_map.159 = (bf16[128,1024]{1,0:T(8,128)(2,1)}, bf16[512,128]{1,0:T(8,128)(2,1)S(1)}) custom-call(bf16[128,1024]{1,0:T(8,128)(2,1)S(1)} %copy-done, bf16[256,1024]{1,0:T(8,128)(2,1)S(1)} %bitcast.14, bf16[192,1024]{1,0:T(8,128)(2,1)S(1)} %copy-done.3, bf16[256,1024]{1,0:T(8,128)(2,1)S(1)} %copy-done.1, ...), custom_call_target="tpu_custom_call" | custom-call | tf_op jit(solution)/shard_map/pallas_call | solution.py:46
  31.2 0.0 collective-permute-done.3.refs_4_
  31.2 0.1 collective-permute-start.4
  31.2 0.5 collective-permute-start.5
  31.7 13.1 %all_to_all.33 = bf16[32,16,128]{2,1,0:T(8,128)(2,1)S(1)} all-to-all(bf16[32,16,128]{2,1,0:T(8,128)(2,1)S(1)} %bitcast.17), channel_id=1, replica_groups=mesh['dom'=8,'edge'=4] {'dom','edge'}, dimensions={0} | all-to-all | bytes 262144 | tf_op jit(solution)/shard_map/all_to_all | solution.py:404
  44.9 0.0 collective-permute-done.4.refs_3_
  44.9 0.0 collective-permute-done.5.refs_5_
  44.9 3.8 %shard_map.160 = (f32[1,256]{1,0:T(1,128)}, bf16[512,128]{1,0:T(8,128)(2,1)S(1)}) custom-call(bf16[512,128]{1,0:T(8,128)(2,1)S(1)} %bitcast.15, bf16[96,512]{1,0:T(8,128)(2,1)S(1)} %copy-done.4, bf16[512,512]{1,0:T(8,128)(2,1)S(1)} %copy-done.2, bf16[512,512]{1,0:T(8,128)(2,1)S(1)} %collective-permute-done.4.refs_3_, ...), custom_call_target="tpu_custom_call" | custom-call | tf_op jit(solution)/shard_map/pallas_call | solution.py:46
  48.7 10.0 %all_to_all.34 = bf16[32,16,128]{2,1,0:T(8,128)(2,1)S(1)} all-to-all(bf16[32,16,128]{2,1,0:T(8,128)(2,1)S(1)} %bitcast.18), channel_id=1, replica_groups=mesh['dom'=8,'edge'=4] {'dom','edge'}, dimensions={0} | all-to-all | bytes 262144 | tf_op jit(solution)/shard_map/all_to_all | solution.py:418
  58.7 1.0 %shard_map.161 = f32[128,1024]{1,0:T(8,128)} custom-call(bf16[128,64]{1,0:T(8,128)(2,1)S(1)} %copy-done.5, bf16[512,128]{1,0:T(8,128)(2,1)S(1)} %bitcast.16), custom_call_target="tpu_custom_call" | custom-call | tf_op jit(solution)/shard_map/pallas_call | solution.py:46
  (5 shorter events, 0.0 us)
Async XLA Ops:
  0.6 15.2 %collective-permute-start = (bf16[256,1024]{1,0:T(8,128)(2,1)}, bf16[256,1024]{1,0:T(8,128)(2,1)S(1)}, u32[]{:S(2)}, u32[]{:S(2)}) collective-permute-start(bf16[256,1024]{1,0:T(8,128)(2,1)} %refs_3_.2), channel_id=1, source_target_pairs={{0,2},{1,3},{2,0},{3,1},{4,6},{5,7},{6,4},{7,5},{8,10},{9,11},{10,... | collective-permute-start | bytes 1572872 | tf_op jit(solution)/shard_map/ppermute | solution.py:309
  3.7 12.7 %copy-start.2 = (bf16[512,512]{1,0:T(8,128)(2,1)S(1)}, bf16[512,512]{1,0:T(8,128)(2,1)}, u32[]{:S(2)}) copy-start(bf16[512,512]{1,0:T(8,128)(2,1)} %refs_2_.2) | copy-start | bytes 1572868
  6.3 6.6 %copy-start.6 = (s32[1,1,8,4,2]{2,4,3,1,0:T(2,128)S(1)}, s32[1,1,8,4,2]{2,4,3,1,0:T(2,128)}, u32[]{:S(2)}) copy-start(s32[1,1,8,4,2]{2,4,3,1,0:T(2,128)} %param.22) | copy-start | bytes 772
  6.3 9.5 %copy-start.1 = (bf16[256,1024]{1,0:T(8,128)(2,1)S(1)}, bf16[256,1024]{1,0:T(8,128)(2,1)}, u32[]{:S(2)}) copy-start(bf16[256,1024]{1,0:T(8,128)(2,1)} %refs_3_.2) | copy-start | bytes 1572868
  6.3 20.2 %copy-start = (bf16[128,1024]{1,0:T(8,128)(2,1)S(1)}, bf16[128,1024]{1,0:T(8,128)(2,1)}, u32[]{:S(2)}) copy-start(bf16[128,1024]{1,0:T(8,128)(2,1)} %refs_0_.2) | copy-start | bytes 786436
  6.3 20.2 %all-to-all-start = ((bf16[8,32,1024]{2,1,0:T(8,128)(2,1)}), bf16[8,32,1024]{2,1,0:T(8,128)(2,1)S(1)}, u32[]{:S(2)}, u32[]{:S(2)}) async-start(bf16[8,32,1024]{2,1,0:T(8,128)(2,1)} %bitcast.19), calls=%async_computation | async-start | bytes 1048576 | tf_op jit(solution)/shard_map/all_to_all | solution.py:363
  15.8 10.7 %collective-permute-start.1 = (bf16[256,1024]{1,0:T(8,128)(2,1)S(1)}, bf16[256,1024]{1,0:T(8,128)(2,1)S(1)}, u32[]{:S(2)}, u32[]{:S(2)}) collective-permute-start(bf16[256,1024]{1,0:T(8,128)(2,1)S(1)} %copy-done.1), channel_id=1, source_target_pairs={{0,1},{1,0},{2,3},{3,2},{4,5},{5,4},{6,7},{7,6},{8,9},{9,8},{10,11... | collective-permute-start | bytes 1572872 | tf_op jit(solution)/shard_map/ppermute | solution.py:309
  15.9 10.7 %collective-permute-start.2 = (bf16[256,1024]{1,0:T(8,128)(2,1)S(1)}, bf16[256,1024]{1,0:T(8,128)(2,1)S(1)}, u32[]{:S(2)}, u32[]{:S(2)}) collective-permute-start(bf16[256,1024]{1,0:T(8,128)(2,1)S(1)} %collective-permute-done.refs_5_), channel_id=1, source_target_pairs={{0,1},{1,0},{2,3},{3,2},{4,5},{5,4},{6,7},{7,6},{8,9},{9,8},{10,11... | collective-permute-start | bytes 1572872 | tf_op jit(solution)/shard_map/ppermute | solution.py:309
  16.4 14.8 %collective-permute-start.3 = (bf16[512,512]{1,0:T(8,128)(2,1)S(1)}, bf16[512,512]{1,0:T(8,128)(2,1)}, u32[]{:S(2)}, u32[]{:S(2)}) collective-permute-start(bf16[512,512]{1,0:T(8,128)(2,1)S(1)} %copy-done.2), channel_id=1, source_target_pairs={{0,2},{1,3},{2,0},{3,1},{4,6},{5,7},{6,4},{7,5},{8,10},{9,11},{10,... | collective-permute-start | bytes 1572872 | tf_op jit(solution)/shard_map/ppermute | solution.py:309
  26.6 1.0 %copy-start.3 = (bf16[192,1024]{1,0:T(8,128)(2,1)S(1)}, bf16[192,1024]{1,0:T(8,128)(2,1)}, u32[]{:S(2)}) copy-start(bf16[192,1024]{1,0:T(8,128)(2,1)} %get-tuple-element.14.refs_2_) | copy-start | bytes 1179652
  31.2 13.7 %collective-permute-start.4 = (bf16[512,512]{1,0:T(8,128)(2,1)S(1)}, bf16[512,512]{1,0:T(8,128)(2,1)S(1)}, u32[]{:S(2)}, u32[]{:S(2)}) collective-permute-start(bf16[512,512]{1,0:T(8,128)(2,1)S(1)} %copy-done.2), channel_id=1, source_target_pairs={{0,1},{1,0},{2,3},{3,2},{4,5},{5,4},{6,7},{7,6},{8,9},{9,8},{10,11... | collective-permute-start | bytes 1572872 | tf_op jit(solution)/shard_map/ppermute | solution.py:309
  31.2 13.6 %collective-permute-start.5 = (bf16[512,512]{1,0:T(8,128)(2,1)}, bf16[512,512]{1,0:T(8,128)(2,1)S(1)}, u32[]{:S(2)}, u32[]{:S(2)}) collective-permute-start(bf16[512,512]{1,0:T(8,128)(2,1)} %collective-permute-done.3.refs_4_), channel_id=1, source_target_pairs={{0,1},{1,0},{2,3},{3,2},{4,5},{5,4},{6,7},{7,6},{8,9},{9,8},{10,11... | collective-permute-start | bytes 1572872 | tf_op jit(solution)/shard_map/ppermute | solution.py:309
  31.7 13.1 %copy-start.4 = (bf16[96,512]{1,0:T(8,128)(2,1)S(1)}, bf16[96,512]{1,0:T(8,128)(2,1)}, u32[]{:S(2)}) copy-start(bf16[96,512]{1,0:T(8,128)(2,1)} %get-tuple-element.19.refs_1_) | copy-start | bytes 294916
  48.6 10.0 %copy-start.5 = (bf16[128,64]{1,0:T(8,128)(2,1)S(1)}, bf16[128,64]{1,0:T(8,128)(2,1)}, u32[]{:S(2)}) copy-start(bf16[128,64]{1,0:T(8,128)(2,1)} %get-tuple-element.23.refs_0_) | copy-start | bytes 49156

commit v11 on v9

--- a/solution.py
+++ b/solution.py
@@ -16,6 +16,7 @@
     "v": VMEM,
     "s": pl.BlockSpec(memory_space=pltpu.SMEM),
     "f": pl.BlockSpec(memory_space=pl.ANY),
+    "any": pl.BlockSpec(memory_space=pl.ANY),
 }
 
 
@@ -23,7 +24,7 @@
     return lax.dot_general(a, b, (dims, ((), ())), preferred_element_type=F32)
 
 
-def call(kernel, outs, ins, scratch=(), vmem_mib=20):
+def call(kernel, outs, ins, scratch=(), vmem_mib=20, out_space="v"):
     fetched = [i for i, (space, _) in enumerate(ins) if space == "f"]
 
     def body(*refs):
@@ -46,7 +47,7 @@
         body,
         out_shape=outs,
         in_specs=[SPACES[space] for space, _ in ins],
-        out_specs=jax.tree.map(lambda _: VMEM, outs),
+        out_specs=jax.tree.map(lambda _: SPACES[out_space], outs),
         scratch_shapes=list(scratch)
         + [pltpu.VMEM(ins[i][1].shape, ins[i][1].dtype) for i in fetched]
         + [pltpu.SemaphoreType.DMA((max(1, len(fetched)),))],
@@ -76,15 +77,19 @@
     out_ref[:, 128:] = rows[:, 128:].astype(BF16)
 
 
-def block_diagonal(vectors):
-    heads, size = vectors.shape
-    wide = jnp.concatenate([vectors] * heads, axis=1)
-    lane_head = lax.broadcasted_iota(jnp.int32, wide.shape, 1) // size
-    wide = jnp.where(lane_head == lax.broadcasted_iota(jnp.int32, wide.shape, 0), wide, 0.0)
-    high = wide.astype(BF16).astype(F32)
-    middle = (wide - high).astype(BF16).astype(F32)
-    low = (wide - high - middle).astype(BF16).astype(F32)
-    return jnp.concatenate([high, middle, low, jnp.zeros_like(wide)], axis=0).astype(BF16)
+def three_parts(values):
+    high = values.astype(BF16).astype(F32)
+    middle = (values - high).astype(BF16).astype(F32)
+    return jnp.concatenate([high, middle, values - high - middle], axis=0)
+
+
+def block_diagonal(parts, heads):
+    parts = parts.astype(F32)
+    wide = jnp.concatenate([parts] * heads, axis=1)
+    lane_head = lax.broadcasted_iota(jnp.int32, wide.shape, 1) // parts.shape[1]
+    row_head = lax.broadcasted_iota(jnp.int32, wide.shape, 0) % heads
+    wide = jnp.where(lane_head == row_head, wide, 0.0)
+    return jnp.concatenate([wide, jnp.zeros((heads, wide.shape[1]), F32)], axis=0).astype(BF16)
 
 
 def prepare_kernel(
@@ -121,14 +126,15 @@
         power = jnp.where(total > 2, 4.0, power)
         power = jnp.where(total > 5, 8.0, power)
         power = jnp.where(total > 13, 16.0, power)
-        for_attend_ref[:nodes, base : base + nodes] = total.astype(BF16)
-        for_attend_ref[:nodes, table + base : table + base + nodes] = power.astype(BF16)
+        for_attend_ref[:, base : base + nodes] = total.astype(BF16)
+        for_attend_ref[:, table + base : table + base + nodes] = power.astype(BF16)
     node_at = lax.broadcasted_iota(jnp.int32, (nodes, ends), 0)
     pick = (node_at == ends_ref[...]).astype(F32).astype(BF16)
     pick_ref[...] = pick
-    for_attend_ref[:nodes, 2 * table : 2 * table + ends] = pick
-    for_attend_ref[nodes : nodes + 4 * heads, : heads * size] = block_diagonal(src_ref[...])
-    for_attend_ref[nodes + 4 * heads :, : heads * size] = block_diagonal(dst_ref[...])
+    first = 2 * table + size
+    for_attend_ref[:, first : first + ends] = pick
+    vectors = [three_parts(src_ref[...]), three_parts(dst_ref[...])]
+    for_attend_ref[: 6 * heads, 2 * table : first] = jnp.concatenate(vectors, axis=0).astype(BF16)
     cands = cand_ref.shape[1]
     hidden = out_w_ref.shape[1]
     slot_at = lax.broadcasted_iota(jnp.int32, (ends, cands), 0)
@@ -138,15 +144,11 @@
     live = (lax.broadcasted_iota(jnp.int32, (1, cands), 1) < live_ref[0, 0]).astype(F32)
     known = jnp.concatenate([live, labels_ref[...].astype(F32), jnp.zeros((14, cands), F32)], axis=0)
     for_score_ref[ends : ends + 16, :cands] = known.astype(BF16)
-    high = out_w_ref[...].astype(BF16).astype(F32)
-    middle = (out_w_ref[...] - high).astype(BF16).astype(F32)
-    low = out_w_ref[...] - high - middle
-    whole = jnp.concatenate([high, middle, low, jnp.zeros((13, hidden), F32)], axis=0)
+    whole = jnp.concatenate([three_parts(out_w_ref[...]), jnp.zeros((13, hidden), F32)], axis=0)
     for_score_ref[ends + 16 :, :hidden] = whole.astype(BF16)
 
 
-def shard_row(i, shards):
-    depth = shards[0].shape[0]
+def shard_row(i, depth):
     return pl.multiple_of((lax.axis_index("edge") ^ i) * depth, depth)
 
 
@@ -154,11 +156,11 @@
     depth = shards[0].shape[0]
     if depth % 128:
         for i, shard in enumerate(shards):
-            whole_ref[pl.ds(shard_row(i, shards), depth), :] = shard[...]
+            whole_ref[pl.ds(shard_row(i, depth), depth), :] = shard[...]
         return dot(rows_ref[...], whole_ref[...])
     total = None
     for i, shard in enumerate(shards):
-        cols = pl.ds(shard_row(i, shards), depth)
+        cols = pl.ds(shard_row(i, depth), depth)
         part = dot(rows_ref[:, cols], shard[...])
         total = part if total is None else total + part
     return total
@@ -171,18 +173,19 @@
     nodes, width = own_ref.shape
     table = proj_ref.shape[0]
     size = width // heads
-    diag_src_ref = known_ref.at[nodes : nodes + 4 * heads, :width]
-    diag_dst_ref = known_ref.at[nodes + 4 * heads :, :width]
-    count_ref = known_ref.at[:nodes, :table]
-    power_ref = known_ref.at[:nodes, table : 2 * table]
-    pick_ref = known_ref.at[:nodes, 2 * table : 2 * table + slots]
+    count_ref = known_ref.at[:, :table]
+    power_ref = known_ref.at[:, table : 2 * table]
+    pick_ref = known_ref.at[:, 2 * table + size : 2 * table + size + slots]
+    vectors = known_ref[: 6 * heads, 2 * table : 2 * table + size]
+    diag_src = block_diagonal(vectors[: 3 * heads], heads)
+    diag_dst = block_diagonal(vectors[3 * heads :], heads)
     rows_ref[:nodes, :] = own_ref[...]
     rows_ref[nodes:, :] = got_ref[...]
     proj_ref[...] = shard_dots(rows_ref, shards, whole_ref).astype(BF16)
-    parts = dot(diag_src_ref[...], proj_ref[...], ((1,), (1,)))
+    parts = dot(diag_src, proj_ref[...], ((1,), (1,)))
     src = parts[:heads] + parts[heads : 2 * heads] + parts[2 * heads : 3 * heads]
     src = src.astype(BF16).astype(F32) * LOG2_E
-    parts = dot(proj_ref[:nodes, :], diag_dst_ref[...], ((1,), (1,)))
+    parts = dot(proj_ref[:nodes, :], diag_dst, ((1,), (1,)))
     dst = parts[:, :heads] + parts[:, heads : 2 * heads] + parts[:, 2 * heads : 3 * heads]
     dst = dst * LOG2_E
     first_lane = (lax.broadcasted_iota(jnp.int32, (16, 128), 1) == 0).astype(F32).astype(BF16)
@@ -225,9 +228,36 @@
     return jnp.concatenate(parts, axis=1).astype(BF16)
 
 
-def score_kernel(shard_count, cands, ready, got_ref, known_ref, *rest):
-    shards = rest[:shard_count]
-    scores_ref, back_ref, pair_ref, stage_ref, sum_ref, grad_ref = rest[shard_count:]
+def add_shards(rows_ref, indices, shards, part_ref):
+    depth = shards[0].shape[0]
+    span = rows_ref.shape[1]
+    for i, shard in zip(indices, shards):
+        row = shard_row(i, depth)
+        cols = pl.ds(pl.multiple_of(row % span, depth), depth)
+        part_ref[row // span] += dot(rows_ref[:, cols], shard[...])
+
+
+def first_kernel(indices, cands, ready, got_ref, known_ref, *rest):
+    shards = rest[:-3]
+    rows_ref, part_ref, stage_ref = rest[-3:]
+    ready()
+    slots = known_ref.shape[0] - 32
+    width = got_ref.shape[0] * 128 // slots
+    rows = unpack_rows(got_ref, stage_ref, width // 128)
+    if slots > cands:
+        for i in range(2):
+            pick = known_ref[:slots, i * cands : (i + 1) * cands]
+            pair = dot(pick, rows, ((0,), (0,)))
+            rows_ref[:, i * width : (i + 1) * width] = pair.astype(BF16)
+    else:
+        rows_ref[...] = rows
+    part_ref[...] = jnp.zeros_like(part_ref)
+    add_shards(rows_ref, indices, shards, part_ref)
+
+
+def score_kernel(late, cands, ready, rows_ref, first_ref, known_ref, *rest):
+    shards = rest[:-6]
+    scores_ref, back_ref, stage_ref, sum_ref, grad_ref, part_ref = rest[-6:]
     ready()
     depth, hidden = shards[0].shape
     slots, width = grad_ref.shape[1:]
@@ -236,12 +266,19 @@
     live, label = known[:, :1], known[:, 1:2]
     out_w = known_ref[slots + 16 :, :hidden].astype(F32)
     out_w = out_w[:1] + out_w[1:2] + out_w[2:3]
-    rows = unpack_rows(got_ref, stage_ref, width // 128)
-    for i in range(2):
-        pair_ref[:, i * width : (i + 1) * width] = dot(
-            picks[i], rows, ((0,), (0,))
-        ).astype(BF16)
-    pre_act = shard_dots(pair_ref, shards)
+    part_ref[...] = first_ref[...]
+    add_shards(rows_ref, late, [shards[i] for i in late], part_ref)
+    if slots > cands:
+        pre_act = part_ref[0]
+    else:
+        pre_act = None
+        for i in range(2):
+            rest = part_ref[i]
+            for _ in range(3):
+                high = rest.astype(BF16)
+                rest = rest - high.astype(F32)
+                term = dot(picks[i], high, ((0,), (0,)))
+                pre_act = term if pre_act is None else pre_act + term
     gate = jax.nn.sigmoid(pre_act)
     score = jnp.sum(pre_act * gate * out_w, axis=1, keepdims=True) * live
     scores_ref[...] = jnp.broadcast_to(score, (cands, 128)).T[:1]
@@ -253,7 +290,7 @@
         sum_ref[i, :slots, :] = high
         sum_ref[i, slots:, :] = (total - high.astype(F32)).astype(BF16)
     for i, shard in enumerate(shards):
-        row = shard_row(i, shards)
+        row = shard_row(i, depth)
         half = row // width
         col = pl.multiple_of(row % width, depth)
         both = dot(sum_ref[half], shard[...], ((1,), (1,)))
@@ -317,13 +354,13 @@
         vmem_mib=60,
     )
     got_rows = lax.all_to_all(send_rows, "dom", split_axis=0, concat_axis=0, tiled=True)
-    gat_shards = from_core(across(gat_weight, edge_count))
-    mlp_shards = from_core(across(mlp_weight, edge_count))
-    lanes = -(-max(2 * table + slots, width) // 128) * 128
+    gat_across = across(gat_weight, edge_count)
+    mlp_across = across(mlp_weight, edge_count)
+    lanes = -(-(2 * table + attn_src.shape[1] + slots) // 128) * 128
     for_attend, for_score, pick = call(
         functools.partial(prepare_kernel, table),
         (
-            shape((nodes + 8 * heads, lanes), BF16),
+            shape((nodes, lanes), BF16),
             shape((slots + 32, max(2 * cands, hidden)), BF16),
             shape((nodes, slots), BF16),
         ),
@@ -338,8 +375,9 @@
             ("f", labels[0]),
             ("f", out_weight.reshape(1, hidden)),
         ],
-        vmem_mib=60,
-    )
+    )
+    gat_across = lax.optimization_barrier((*gat_across, for_attend))[:-1]
+    gat_shards = from_core(gat_across)
     packed = pltpu.VMEM((slots * pieces, 128), F32)
     node_out, send_ends = call(
         functools.partial(attend_kernel, edge_count, heads, slots),
@@ -355,16 +393,31 @@
         ],
     )
     got_ends = lax.all_to_all(send_ends, everyone, split_axis=0, concat_axis=0, tiled=True)
+    mlp_shards = [mlp_across[0], swap(mlp_across[0], "edge", 1)]
+    tied = lax.optimization_barrier((*mlp_across[1:], got_ends))[:-1]
+    for shard, held in zip(mlp_across[1:], tied):
+        mlp_shards += [shard, swap(held, "edge", 1)]
+    early = [i for i in range(edge_count) if i < 2 or i % 2 == 0]
+    late = [i for i in range(edge_count) if i not in early]
+    many = slots > cands
+    rows, part = call(
+        functools.partial(first_kernel, early, cands),
+        (
+            shape((cands, 2 * width) if many else (slots, width), BF16),
+            shape((1, cands, hidden) if many else (2, slots, hidden), F32),
+        ),
+        [("v", got_ends), ("v", for_score)] + [("v", mlp_shards[i]) for i in early],
+        [packed],
+    )
     scores, send_back = call(
-        functools.partial(score_kernel, edge_count, cands),
+        functools.partial(score_kernel, late, cands),
         (shape((1, cands), F32), shape((slots * pieces, 128), BF16)),
-        [("v", got_ends), ("v", for_score)]
-        + [("v", w) for w in mlp_shards],
+        [("v", rows), ("v", part), ("v", for_score)] + [("v", w) for w in mlp_shards],
         [
-            pltpu.VMEM((cands, 2 * width), BF16),
             packed,
             pltpu.VMEM((2, 2 * slots, hidden), BF16),
             pltpu.VMEM((2, slots, width), F32),
+            pltpu.VMEM(part.shape, F32),
         ],
     )
     got_back = lax.all_to_all(send_back, everyone, split_axis=0, concat_axis=0, tiled=True)

time: 65.5 us -> 59.3 us (0.905)
  waiting for transfers between devices: 22.3 us -> 18.3 us
  Pallas kernels: 13.3 us -> 11.4 us
  starting transfers between devices: 16.3 us -> 14.5 us
  local copies, waits for them, and re-layouts: 1.75 us -> 3.22 us
    ppermute x6, waiting for transfers between devices: 14 us -> 2.19 us  [swap(): return lax.ppermute(array, axis, [(i, i ^ k) for i in range(count)])]
    all_to_all x1, waiting for transfers between devices: 0.01 us -> 8.2 us  [local(): lax.all_to_all(send_rows, 'dom', split_axis=0, concat_axis=0, tiled=True)]
    all_to_all x1, starting transfers between devices: 6.19 us -> 2.72 us  [local(): lax.all_to_all(send_ends, everyone, split_axis=0, concat_axis=0, tiled=True)]
    unnamed x15 -> x29, local copies, waits for them, and re-layouts: 1.13 us -> 3.11 us
    pallas_call x5 -> x6, Pallas kernels: 13.3 us -> 11.4 us  [call(): pl.pallas_call(body, out_shape=outs, in_specs=[SPACES[space] for space, _...]
    ppermute x6, starting transfers between devices: 4.12 us -> 5.82 us  [swap(): return lax.ppermute(array, axis, [(i, i ^ k) for i in range(count)])]
  transfers between devices with their start and end apart: 8 -> 8, of which waited for: 3 -> 4; matrix products, arithmetic and copies ran while one was open for 1% -> 0% of each run, Pallas kernels for 13% -> 14%
where the time goes in v11:
time: 59.3 us; the launch traced here: 58.9 us
  waiting for transfers between devices  18.3 us (31%)
  starting transfers between devices  14.5 us (24%)
  Pallas kernels  11.4 us (19%)
  blocking collectives  10 us (17%)
  local copies, waits for them, and re-layouts  3.22 us (5%)
  between operations  1.44 us (2%)
    pallas_call x6, Pallas kernels, call(): pl.pallas_call(body, out_shape=outs, in_specs=[SPACES[space] for space, _...  11.4 us
    all_to_all x1, blocking collectives, local(): lax.all_to_all(send_back, everyone, split_axis=0, concat_axis=0, tiled=True)  10 us
    all_to_all x1, waiting for transfers between devices, local(): lax.all_to_all(send_rows, 'dom', split_axis=0, concat_axis=0, tiled=True)  8.2 us
    all_to_all x1, waiting for transfers between devices, local(): lax.all_to_all(send_ends, everyone, split_axis=0, concat_axis=0, tiled=True)  7.91 us
    all_to_all x1, starting transfers between devices, local(): lax.all_to_all(send_rows, 'dom', split_axis=0, concat_axis=0, tiled=True)  5.95 us
    ppermute x6, starting transfers between devices, swap(): return lax.ppermute(array, axis, [(i, i ^ k) for i in range(count)])  5.82 us
    unnamed x29, local copies, waits for them, and re-layouts  3.11 us
    all_to_all x1, starting transfers between devices, local(): lax.all_to_all(send_ends, everyone, split_axis=0, concat_axis=0, tiled=True)  2.72 us
  transfers between devices with their start and end apart: 8, of which 4 were waited for; matrix products, arithmetic and copies ran while one was open for 0% of the time, Pallas kernels for 14%

profile of v11, /device:TPU:0, one launch (start us, length us, event | category | flops | bytes accessed | tf_op | source)
XLA Modules:
  0.0 58.9 jit_solution(11263781879006721423)
XLA Ops:
  0.6 3.0 %collective-permute-start = (bf16[256,1024]{1,0:T(8,128)(2,1)}, bf16[256,1024]{1,0:T(8,128)(2,1)S(1)}, u32[]{:S(2)}, u32[]{:S(2)}) collective-permute-start(bf16[256,1024]{1,0:T(8,128)(2,1)} %refs_3_.3), channel_id=1, source_target_pairs={{0,2},{1,3},{2,0},{3,1},{4,6},{5,7},{6,4},{7,5},{8,10},{9,11},{10,... | collective-permute-start | bytes 1572872 | tf_op jit(solution)/shard_map/ppermute | solution.py:309
  3.7 2.4 %shard_map.157 = bf16[256,1024]{1,0:T(8,128)(2,1)} custom-call(s32[1,8]{1,0:T(1,128)} %bitcast.26, s32[8,32]{1,0:T(8,128)} %bitcast.25, bf16[128,1024]{1,0:T(8,128)(2,1)} %refs_0_.2), custom_call_target="tpu_custom_call" | custom-call | tf_op jit(solution)/shard_map/pallas_call | solution.py:46
  6.0 0.0 copy-start.1
  6.1 5.9 %all-to-all-start = ((bf16[8,32,1024]{2,1,0:T(8,128)(2,1)}), bf16[8,32,1024]{2,1,0:T(8,128)(2,1)S(1)}, u32[]{:S(2)}, u32[]{:S(2)}) async-start(bf16[8,32,1024]{2,1,0:T(8,128)(2,1)} %bitcast.24), calls=%async_computation | async-start | bytes 1048576 | tf_op jit(solution)/shard_map/all_to_all | solution.py:356
  12.7 0.1 copy.18
  12.8 0.0 copy-start.12
  12.8 0.1 reshape.25.refs_5_
  12.9 0.0 copy-start.6
  12.9 0.5 copy-done.7
  13.5 0.0 copy-done.8
  13.5 0.0 copy-done.9
  13.5 0.0 copy-done.10
  13.5 0.1 copy-done.6
  13.6 0.5 shard_map.158
  14.2 0.7 %copy-done.3 = bf16[128,1024]{1,0:T(8,128)(2,1)} copy-done((bf16[128,1024]{1,0:T(8,128)(2,1)}, bf16[128,1024]{1,0:T(8,128)(2,1)S(1)}, u32[]{:S(2)}) %copy-start.3) | copy-done | bytes 262168
  14.9 0.9 %collective-permute-done.refs_5_ = bf16[256,1024]{1,0:T(8,128)(2,1)S(1)} collective-permute-done((bf16[256,1024]{1,0:T(8,128)(2,1)}, bf16[256,1024]{1,0:T(8,128)(2,1)S(1)}, u32[]{:S(2)}, u32[]{:S(2)}) %collective-permute-start) | collective-permute-done | bytes 524320 | tf_op jit(solution)/shard_map/ppermute | solution.py:309
  15.8 0.5 collective-permute-start.2
  16.3 1.7 %collective-permute-start.4 = (bf16[512,512]{1,0:T(8,128)(2,1)S(1)}, bf16[512,512]{1,0:T(8,128)(2,1)S(1)}, u32[]{:S(2)}, u32[]{:S(2)}) collective-permute-start(bf16[512,512]{1,0:T(8,128)(2,1)S(1)} %copy-done), channel_id=1, source_target_pairs={{0,2},{1,3},{2,0},{3,1},{4,6},{5,7},{6,4},{7,5},{8,10},{9,11},{10,... | collective-permute-start | bytes 1572872 | tf_op jit(solution)/shard_map/ppermute | solution.py:309
  18.1 8.2 %all-to-all-done = bf16[8,32,1024]{2,1,0:T(8,128)(2,1)S(1)} async-done(((bf16[8,32,1024]{2,1,0:T(8,128)(2,1)}), bf16[8,32,1024]{2,1,0:T(8,128)(2,1)S(1)}, u32[]{:S(2)}, u32[]{:S(2)}) %all-to-all-start) | async-done | bytes 524320 | tf_op jit(solution)/shard_map/all_to_all | solution.py:356
  26.3 0.9 %copy-done.4 = bf16[128,1024]{1,0:T(8,128)(2,1)S(1)} copy-done((bf16[128,1024]{1,0:T(8,128)(2,1)S(1)}, bf16[128,1024]{1,0:T(8,128)(2,1)}, u32[]{:S(2)}) %copy-start.4) | copy-done | bytes 262168
  27.2 4.6 %shard_map.159 = (bf16[128,1024]{1,0:T(8,128)(2,1)}, bf16[512,128]{1,0:T(8,128)(2,1)S(1)}) custom-call(bf16[128,1024]{1,0:T(8,128)(2,1)S(1)} %copy-done.1, bf16[256,1024]{1,0:T(8,128)(2,1)S(1)} %bitcast.14, bf16[128,1024]{1,0:T(8,128)(2,1)S(1)} %copy-done.4, bf16[256,1024]{1,0:T(8,128)(2,1)S(1)} %copy-done.2, ...), custom_call_target="tpu_custom_call" | custom-call | tf_op jit(solution)/shard_map/pallas_call | solution.py:46
  31.9 0.0 copy-start.5
  31.9 0.6 %copy-done.5 = bf16[512,128]{1,0:T(8,128)(2,1)} copy-done((bf16[512,128]{1,0:T(8,128)(2,1)}, bf16[512,128]{1,0:T(8,128)(2,1)S(1)}, u32[]{:S(2)}) %copy-start.5) | copy-done | bytes 131096
  32.5 2.7 %all-to-all-start.1 = ((bf16[32,16,128]{2,1,0:T(8,128)(2,1)}), bf16[32,16,128]{2,1,0:T(8,128)(2,1)S(1)}, u32[]{:S(2)}, u32[]{:S(2)}) async-start(bf16[32,16,128]{2,1,0:T(8,128)(2,1)} %bitcast.17), calls=%async_computation.1 | async-start | bytes 262144 | tf_op jit(solution)/shard_map/all_to_all | solution.py:395
  35.3 0.3 collective-permute-start.3
  35.6 7.9 %all-to-all-done.1 = bf16[32,16,128]{2,1,0:T(8,128)(2,1)S(1)} async-done(((bf16[32,16,128]{2,1,0:T(8,128)(2,1)}), bf16[32,16,128]{2,1,0:T(8,128)(2,1)S(1)}, u32[]{:S(2)}, u32[]{:S(2)}) %all-to-all-start.1) | async-done | bytes 131104 | tf_op jit(solution)/shard_map/all_to_all | solution.py:395
  43.5 0.2 collective-permute-start.5
  43.7 0.4 shard_map.160
  44.2 1.2 %collective-permute-done.5.refs_6_ = bf16[512,512]{1,0:T(8,128)(2,1)S(1)} collective-permute-done((bf16[512,512]{1,0:T(8,128)(2,1)S(1)}, bf16[512,512]{1,0:T(8,128)(2,1)S(1)}, u32[]{:S(2)}, u32[]{:S(2)}) %collective-permute-start.5) | collective-permute-done | bytes 524320 | tf_op jit(solution)/shard_map/ppermute | solution.py:309
  45.4 2.4 %shard_map.161 = (f32[1,256]{1,0:T(1,128)}, bf16[512,128]{1,0:T(8,128)(2,1)S(1)}) custom-call(bf16[64,1024]{1,0:T(8,128)(2,1)S(1)} %get-tuple-element.21.refs_0_, f32[2,64,512]{2,1,0:T(8,128)S(1)} %get-tuple-element.22.refs_1_, bf16[96,512]{1,0:T(8,128)(2,1)S(1)} %get-tuple-element.20.refs_1_.refs_2_, bf16[512,512]{1,0:T(8,128)(2,1)S(1)} %copy-done, ...), custom_call_target="tpu_custom_call" | custom-call | tf_op jit(solution)/shard_map/pallas_call | solution.py:46
  47.8 10.0 %all_to_all.33 = bf16[32,16,128]{2,1,0:T(8,128)(2,1)S(1)} all-to-all(bf16[32,16,128]{2,1,0:T(8,128)(2,1)S(1)} %bitcast.18), channel_id=1, replica_groups=mesh['dom'=8,'edge'=4] {'dom','edge'}, dimensions={0} | all-to-all | bytes 262144 | tf_op jit(solution)/shard_map/all_to_all | solution.py:423
  57.8 1.0 %shard_map.162 = f32[128,1024]{1,0:T(8,128)} custom-call(bf16[128,64]{1,0:T(8,128)(2,1)S(1)} %get-tuple-element.25.refs_0_, bf16[512,128]{1,0:T(8,128)(2,1)S(1)} %bitcast.16), custom_call_target="tpu_custom_call" | custom-call | tf_op jit(solution)/shard_map/pallas_call | solution.py:46
  (21 shorter events, 0.1 us)
Async XLA Ops:
  0.6 15.2 %collective-permute-start = (bf16[256,1024]{1,0:T(8,128)(2,1)}, bf16[256,1024]{1,0:T(8,128)(2,1)S(1)}, u32[]{:S(2)}, u32[]{:S(2)}) collective-permute-start(bf16[256,1024]{1,0:T(8,128)(2,1)} %refs_3_.3), channel_id=1, source_target_pairs={{0,2},{1,3},{2,0},{3,1},{4,6},{5,7},{6,4},{7,5},{8,10},{9,11},{10,... | collective-permute-start | bytes 1572872 | tf_op jit(solution)/shard_map/ppermute | solution.py:309
  3.7 12.1 %copy-start.2 = (bf16[256,1024]{1,0:T(8,128)(2,1)S(1)}, bf16[256,1024]{1,0:T(8,128)(2,1)}, u32[]{:S(2)}) copy-start(bf16[256,1024]{1,0:T(8,128)(2,1)} %refs_3_.3) | copy-start | bytes 1572868
  6.0 6.6 %copy-start.13 = (s32[1,1,8,4,2]{2,4,3,1,0:T(2,128)S(1)}, s32[1,1,8,4,2]{2,4,3,1,0:T(2,128)}, u32[]{:S(2)}) copy-start(s32[1,1,8,4,2]{2,4,3,1,0:T(2,128)} %param.22) | copy-start | bytes 772
  6.0 10.3 %copy-start = (bf16[512,512]{1,0:T(8,128)(2,1)S(1)}, bf16[512,512]{1,0:T(8,128)(2,1)}, u32[]{:S(2)}) copy-start(bf16[512,512]{1,0:T(8,128)(2,1)} %refs_3_.4) | copy-start | bytes 1572868
  6.0 20.2 %copy-start.1 = (bf16[128,1024]{1,0:T(8,128)(2,1)S(1)}, bf16[128,1024]{1,0:T(8,128)(2,1)}, u32[]{:S(2)}) copy-start(bf16[128,1024]{1,0:T(8,128)(2,1)} %refs_0_.2) | copy-start | bytes 786436
  6.1 20.2 %all-to-all-start = ((bf16[8,32,1024]{2,1,0:T(8,128)(2,1)}), bf16[8,32,1024]{2,1,0:T(8,128)(2,1)S(1)}, u32[]{:S(2)}, u32[]{:S(2)}) async-start(bf16[8,32,1024]{2,1,0:T(8,128)(2,1)} %bitcast.24), calls=%async_computation | async-start | bytes 1048576 | tf_op jit(solution)/shard_map/all_to_all | solution.py:356
  12.8 0.7 %copy-start.7 = (f32[8,128]{1,0:T(8,128)S(1)}, f32[8,128]{1,0:T(8,128)}, u32[]{:S(2)}) copy-start(f32[8,128]{1,0:T(8,128)} %refs_3_.2) | copy-start | bytes 12292
  12.8 0.7 %copy-start.8 = (f32[8,128]{1,0:T(8,128)S(1)}, f32[8,128]{1,0:T(8,128)}, u32[]{:S(2)}) copy-start(f32[8,128]{1,0:T(8,128)} %refs_4_.1) | copy-start | bytes 12292
  12.8 0.7 %copy-start.9 = (s32[1,1,2,256]{3,2,1,0:T(2,128)S(1)}, s32[1,1,2,256]{3,2,1,0:T(2,128)}, u32[]{:S(2)}) copy-start(s32[1,1,2,256]{3,2,1,0:T(2,128)} %param.23) | copy-start | bytes 6148
  12.8 0.7 %copy-start.10 = (f32[512]{0:T(512)S(1)}, f32[512]{0:T(512)}, u32[]{:S(2)}) copy-start(f32[512]{0:T(512)} %param.27) | copy-start | bytes 6148
  12.8 0.7 %copy-start.12 = (s32[128]{0:T(128)S(1)}, s32[128]{0:T(128)}, u32[]{:S(2)}) copy-start(s32[128]{0:T(128)} %param.19) | copy-start | bytes 1540
  12.9 0.7 %copy-start.6 = (s32[128,16]{0,1:T(8,128)S(1)}, s32[128,16]{0,1:T(8,128)}, u32[]{:S(2)}) copy-start(s32[128,16]{0,1:T(8,128)} %param.18) | copy-start | bytes 24580
  12.9 0.7 %copy-start.11 = (s32[1,1,256]{2,1,0:T(1,128)S(1)}, s32[1,1,256]{2,1,0:T(1,128)}, u32[]{:S(2)}) copy-start(s32[1,1,256]{2,1,0:T(1,128)} %param.25) | copy-start | bytes 3076
  14.2 0.7 %copy-start.3 = (bf16[128,1024]{1,0:T(8,128)(2,1)}, bf16[128,1024]{1,0:T(8,128)(2,1)S(1)}, u32[]{:S(2)}) copy-start(bf16[128,1024]{1,0:T(8,128)(2,1)S(1)} %get-tuple-element.15.refs_2_) | copy-start | bytes 786436
  15.8 10.5 %collective-permute-start.1 = (bf16[256,1024]{1,0:T(8,128)(2,1)S(1)}, bf16[256,1024]{1,0:T(8,128)(2,1)S(1)}, u32[]{:S(2)}, u32[]{:S(2)}) collective-permute-start(bf16[256,1024]{1,0:T(8,128)(2,1)S(1)} %copy-done.2), channel_id=1, source_target_pairs={{0,1},{1,0},{2,3},{3,2},{4,5},{5,4},{6,7},{7,6},{8,9},{9,8},{10,11... | collective-permute-start | bytes 1572872 | tf_op jit(solution)/shard_map/ppermute | solution.py:309
  15.8 10.5 %collective-permute-start.2 = (bf16[256,1024]{1,0:T(8,128)(2,1)S(1)}, bf16[256,1024]{1,0:T(8,128)(2,1)}, u32[]{:S(2)}, u32[]{:S(2)}) collective-permute-start(bf16[256,1024]{1,0:T(8,128)(2,1)S(1)} %collective-permute-done.refs_5_), channel_id=1, source_target_pairs={{0,1},{1,0},{2,3},{3,2},{4,5},{5,4},{6,7},{7,6},{8,9},{9,8},{10,11... | collective-permute-start | bytes 1572872 | tf_op jit(solution)/shard_map/ppermute | solution.py:309
  16.3 19.3 %collective-permute-start.4 = (bf16[512,512]{1,0:T(8,128)(2,1)S(1)}, bf16[512,512]{1,0:T(8,128)(2,1)S(1)}, u32[]{:S(2)}, u32[]{:S(2)}) collective-permute-start(bf16[512,512]{1,0:T(8,128)(2,1)S(1)} %copy-done), channel_id=1, source_target_pairs={{0,2},{1,3},{2,0},{3,1},{4,6},{5,7},{6,4},{7,5},{8,10},{9,11},{10,... | collective-permute-start | bytes 1572872 | tf_op jit(solution)/shard_map/ppermute | solution.py:309
  26.3 1.0 %copy-start.4 = (bf16[128,1024]{1,0:T(8,128)(2,1)S(1)}, bf16[128,1024]{1,0:T(8,128)(2,1)}, u32[]{:S(2)}) copy-start(bf16[128,1024]{1,0:T(8,128)(2,1)} %copy-done.3) | copy-start | bytes 786436
  31.9 0.7 %copy-start.5 = (bf16[512,128]{1,0:T(8,128)(2,1)}, bf16[512,128]{1,0:T(8,128)(2,1)S(1)}, u32[]{:S(2)}) copy-start(bf16[512,128]{1,0:T(8,128)(2,1)S(1)} %get-tuple-element.19) | copy-start | bytes 393220
  32.5 11.0 %all-to-all-start.1 = ((bf16[32,16,128]{2,1,0:T(8,128)(2,1)}), bf16[32,16,128]{2,1,0:T(8,128)(2,1)S(1)}, u32[]{:S(2)}, u32[]{:S(2)}) async-start(bf16[32,16,128]{2,1,0:T(8,128)(2,1)} %bitcast.17), calls=%async_computation.1 | async-start | bytes 262144 | tf_op jit(solution)/shard_map/all_to_all | solution.py:395
  35.3 8.4 %collective-permute-start.3 = (bf16[512,512]{1,0:T(8,128)(2,1)S(1)}, bf16[512,512]{1,0:T(8,128)(2,1)S(1)}, u32[]{:S(2)}, u32[]{:S(2)}) collective-permute-start(bf16[512,512]{1,0:T(8,128)(2,1)S(1)} %copy-done), channel_id=1, source_target_pairs={{0,1},{1,0},{2,3},{3,2},{4,5},{5,4},{6,7},{7,6},{8,9},{9,8},{10,11... | collective-permute-start | bytes 1572872 | tf_op jit(solution)/shard_map/ppermute | solution.py:309
  43.5 1.9 %collective-permute-start.5 = (bf16[512,512]{1,0:T(8,128)(2,1)S(1)}, bf16[512,512]{1,0:T(8,128)(2,1)S(1)}, u32[]{:S(2)}, u32[]{:S(2)}) collective-permute-start(bf16[512,512]{1,0:T(8,128)(2,1)S(1)} %collective-permute-done.4.refs_4_.refs_5_), channel_id=1, source_target_pairs={{0,1},{1,0},{2,3},{3,2},{4,5},{5,4},{6,7},{7,6},{8,9},{9,8},{10,11... | collective-permute-start | bytes 1572872 | tf_op jit(solution)/shard_map/ppermute | solution.py:309

commit v12 on v11

--- a/solution.py
+++ b/solution.py
@@ -104,9 +104,11 @@
     cand_ref,
     labels_ref,
     out_w_ref,
+    mlp_ref,
     for_attend_ref,
     for_score_ref,
     pick_ref,
+    *mlp_part_refs,
 ):
     ready()
     nodes, ends = pick_ref.shape
@@ -146,21 +148,27 @@
     for_score_ref[ends : ends + 16, :cands] = known.astype(BF16)
     whole = jnp.concatenate([three_parts(out_w_ref[...]), jnp.zeros((13, hidden), F32)], axis=0)
     for_score_ref[ends + 16 :, :hidden] = whole.astype(BF16)
-
-
-def shard_row(i, depth):
-    return pl.multiple_of((lax.axis_index("edge") ^ i) * depth, depth)
+    depth = mlp_part_refs[0].shape[0]
+    for i, ref in enumerate(mlp_part_refs):
+        ref[...] = mlp_ref[i * depth : (i + 1) * depth, :]
+
+
+def shard_row(i, shards):
+    depth = shards[0].shape[0]
+    parts = len(shards) // lax.axis_size("edge")
+    at = (lax.axis_index("edge") ^ (i // parts)) * parts + i % parts
+    return pl.multiple_of(at * depth, depth)
 
 
 def shard_dots(rows_ref, shards, whole_ref=None):
     depth = shards[0].shape[0]
     if depth % 128:
         for i, shard in enumerate(shards):
-            whole_ref[pl.ds(shard_row(i, depth), depth), :] = shard[...]
+            whole_ref[pl.ds(shard_row(i, shards), depth), :] = shard[...]
         return dot(rows_ref[...], whole_ref[...])
     total = None
     for i, shard in enumerate(shards):
-        cols = pl.ds(shard_row(i, depth), depth)
+        cols = pl.ds(shard_row(i, shards), depth)
         part = dot(rows_ref[:, cols], shard[...])
         total = part if total is None else total + part
     return total
@@ -228,36 +236,18 @@
     return jnp.concatenate(parts, axis=1).astype(BF16)
 
 
-def add_shards(rows_ref, indices, shards, part_ref):
+def add_shards(rows_ref, shards, part_ref):
     depth = shards[0].shape[0]
     span = rows_ref.shape[1]
-    for i, shard in zip(indices, shards):
-        row = shard_row(i, depth)
+    for i, shard in enumerate(shards):
+        row = shard_row(i, shards)
         cols = pl.ds(pl.multiple_of(row % span, depth), depth)
         part_ref[row // span] += dot(rows_ref[:, cols], shard[...])
 
 
-def first_kernel(indices, cands, ready, got_ref, known_ref, *rest):
-    shards = rest[:-3]
-    rows_ref, part_ref, stage_ref = rest[-3:]
-    ready()
-    slots = known_ref.shape[0] - 32
-    width = got_ref.shape[0] * 128 // slots
-    rows = unpack_rows(got_ref, stage_ref, width // 128)
-    if slots > cands:
-        for i in range(2):
-            pick = known_ref[:slots, i * cands : (i + 1) * cands]
-            pair = dot(pick, rows, ((0,), (0,)))
-            rows_ref[:, i * width : (i + 1) * width] = pair.astype(BF16)
-    else:
-        rows_ref[...] = rows
-    part_ref[...] = jnp.zeros_like(part_ref)
-    add_shards(rows_ref, indices, shards, part_ref)
-
-
-def score_kernel(late, cands, ready, rows_ref, first_ref, known_ref, *rest):
-    shards = rest[:-6]
-    scores_ref, back_ref, stage_ref, sum_ref, grad_ref, part_ref = rest[-6:]
+def score_kernel(cands, ready, got_ref, known_ref, *rest):
+    shards = rest[:-7]
+    scores_ref, back_ref, stage_ref, sum_ref, grad_ref, part_ref, rows_ref = rest[-7:]
     ready()
     depth, hidden = shards[0].shape
     slots, width = grad_ref.shape[1:]
@@ -266,8 +256,15 @@
     live, label = known[:, :1], known[:, 1:2]
     out_w = known_ref[slots + 16 :, :hidden].astype(F32)
     out_w = out_w[:1] + out_w[1:2] + out_w[2:3]
-    part_ref[...] = first_ref[...]
-    add_shards(rows_ref, late, [shards[i] for i in late], part_ref)
+    rows = unpack_rows(got_ref, stage_ref, width // 128)
+    if slots > cands:
+        for i in range(2):
+            pair = dot(picks[i], rows, ((0,), (0,)))
+            rows_ref[:, i * width : (i + 1) * width] = pair.astype(BF16)
+    else:
+        rows_ref[...] = rows
+    part_ref[...] = jnp.zeros_like(part_ref)
+    add_shards(rows_ref, shards, part_ref)
     if slots > cands:
         pre_act = part_ref[0]
     else:
@@ -290,7 +287,7 @@
         sum_ref[i, :slots, :] = high
         sum_ref[i, slots:, :] = (total - high.astype(F32)).astype(BF16)
     for i, shard in enumerate(shards):
-        row = shard_row(i, depth)
+        row = shard_row(i, shards)
         half = row // width
         col = pl.multiple_of(row % width, depth)
         both = dot(sum_ref[half], shard[...], ((1,), (1,)))
@@ -355,15 +352,17 @@
     )
     got_rows = lax.all_to_all(send_rows, "dom", split_axis=0, concat_axis=0, tiled=True)
     gat_across = across(gat_weight, edge_count)
-    mlp_across = across(mlp_weight, edge_count)
+    held_mlp = lax.optimization_barrier((mlp_weight, send_rows))[0]
+    parts = 2 if mlp_weight.shape[0] % 256 == 0 else 1
     lanes = -(-(2 * table + attn_src.shape[1] + slots) // 128) * 128
-    for_attend, for_score, pick = call(
+    for_attend, for_score, pick, *mlp_parts = call(
         functools.partial(prepare_kernel, table),
         (
             shape((nodes, lanes), BF16),
             shape((slots + 32, max(2 * cands, hidden)), BF16),
             shape((nodes, slots), BF16),
-        ),
+        )
+        + (shape((mlp_weight.shape[0] // parts, hidden), BF16),) * parts,
         [
             ("s", cand_count),
             ("f", neighbours.T),
@@ -374,10 +373,15 @@
             ("f", cand_ends[0, 0]),
             ("f", labels[0]),
             ("f", out_weight.reshape(1, hidden)),
+            ("f", held_mlp),
         ],
+        vmem_mib=60,
     )
     gat_across = lax.optimization_barrier((*gat_across, for_attend))[:-1]
     gat_shards = from_core(gat_across)
+    mlp_across = [across(part, edge_count) for part in mlp_parts]
+    if parts > 1:
+        got_rows, *mlp_across[0] = lax.optimization_barrier((got_rows, *mlp_across[0]))
     packed = pltpu.VMEM((slots * pieces, 128), F32)
     node_out, send_ends = call(
         functools.partial(attend_kernel, edge_count, heads, slots),
@@ -392,32 +396,21 @@
             pltpu.VMEM((width if width // edge_count % 128 else 16, width), BF16),
         ],
     )
+    mlp_across[-1] = lax.optimization_barrier((*mlp_across[-1], send_ends))[:-1]
+    mlp_found = [from_core(part) for part in mlp_across]
+    mlp_shards = [found[e] for e in range(edge_count) for found in mlp_found]
     got_ends = lax.all_to_all(send_ends, everyone, split_axis=0, concat_axis=0, tiled=True)
-    mlp_shards = [mlp_across[0], swap(mlp_across[0], "edge", 1)]
-    tied = lax.optimization_barrier((*mlp_across[1:], got_ends))[:-1]
-    for shard, held in zip(mlp_across[1:], tied):
-        mlp_shards += [shard, swap(held, "edge", 1)]
-    early = [i for i in range(edge_count) if i < 2 or i % 2 == 0]
-    late = [i for i in range(edge_count) if i not in early]
     many = slots > cands
-    rows, part = call(
-        functools.partial(first_kernel, early, cands),
-        (
-            shape((cands, 2 * width) if many else (slots, width), BF16),
-            shape((1, cands, hidden) if many else (2, slots, hidden), F32),
-        ),
-        [("v", got_ends), ("v", for_score)] + [("v", mlp_shards[i]) for i in early],
-        [packed],
-    )
     scores, send_back = call(
-        functools.partial(score_kernel, late, cands),
+        functools.partial(score_kernel, cands),
         (shape((1, cands), F32), shape((slots * pieces, 128), BF16)),
-        [("v", rows), ("v", part), ("v", for_score)] + [("v", w) for w in mlp_shards],
+        [("v", got_ends), ("v", for_score)] + [("v", w) for w in mlp_shards],
         [
             packed,
             pltpu.VMEM((2, 2 * slots, hidden), BF16),
             pltpu.VMEM((2, slots, width), F32),
-            pltpu.VMEM(part.shape, F32),
+            pltpu.VMEM((1, cands, hidden) if many else (2, slots, hidden), F32),
+            pltpu.VMEM((cands, 2 * width) if many else (slots, width), BF16),
         ],
     )
     got_back = lax.all_to_all(send_back, everyone, split_axis=0, concat_axis=0, tiled=True)

time: 59.3 us -> 61.2 us (1.032)
  starting transfers between devices: 14.5 us -> 18.2 us
  waiting for transfers between devices: 18.3 us -> 15.9 us
  Pallas kernels: 11.4 us -> 13.5 us
  local copies, waits for them, and re-layouts: 3.22 us -> 1.71 us
    all_to_all x1, waiting for transfers between devices: 8.2 us -> 0.33 us  [local(): lax.all_to_all(send_rows, 'dom', split_axis=0, concat_axis=0, tiled=True)]
    ppermute x6 -> x9, waiting for transfers between devices: 2.19 us -> 7.37 us  [swap(): return lax.ppermute(array, axis, [(i, i ^ k) for i in range(count)])]
    all_to_all x1, starting transfers between devices: 2.72 us -> 5.58 us  [local(): lax.all_to_all(send_ends, everyone, split_axis=0, concat_axis=0, tiled=True)]
    pallas_call x6 -> x5, Pallas kernels: 11.4 us -> 13.5 us  [call(): pl.pallas_call(body, out_shape=outs, in_specs=[SPACES[space] for space, _...]
    unnamed x29 -> x17, local copies, waits for them, and re-layouts: 3.11 us -> 1.09 us
    ppermute x6 -> x9, starting transfers between devices: 5.82 us -> 6.7 us  [swap(): return lax.ppermute(array, axis, [(i, i ^ k) for i in range(count)])]
  transfers between devices with their start and end apart: 8 -> 11, of which waited for: 4 -> 3; matrix products, arithmetic and copies ran while one was open for 0% -> 1% of each run, Pallas kernels for 14% -> 14%
where the time goes in v12:
time: 61.2 us; the launch traced here: 60.8 us
  starting transfers between devices  18.2 us (30%)
  waiting for transfers between devices  15.9 us (26%)
  Pallas kernels  13.5 us (22%)
  blocking collectives  10 us (16%)
  local copies, waits for them, and re-layouts  1.71 us (3%)
  between operations  1.46 us (2%)
    pallas_call x5, Pallas kernels, call(): pl.pallas_call(body, out_shape=outs, in_specs=[SPACES[space] for space, _...  13.5 us
    all_to_all x1, blocking collectives, local(): lax.all_to_all(send_back, everyone, split_axis=0, concat_axis=0, tiled=True)  10 us
    all_to_all x1, waiting for transfers between devices, local(): lax.all_to_all(send_ends, everyone, split_axis=0, concat_axis=0, tiled=True)  8.21 us
    ppermute x9, waiting for transfers between devices, swap(): return lax.ppermute(array, axis, [(i, i ^ k) for i in range(count)])  7.37 us
    ppermute x9, starting transfers between devices, swap(): return lax.ppermute(array, axis, [(i, i ^ k) for i in range(count)])  6.7 us
    all_to_all x1, starting transfers between devices, local(): lax.all_to_all(send_rows, 'dom', split_axis=0, concat_axis=0, tiled=True)  5.95 us
    all_to_all x1, starting transfers between devices, local(): lax.all_to_all(send_ends, everyone, split_axis=0, concat_axis=0, tiled=True)  5.58 us
  transfers between devices with their start and end apart: 11, of which 3 were waited for; matrix products, arithmetic and copies ran while one was open for 1% of the time, Pallas kernels for 14%

profile of v12, /device:TPU:0, one launch (start us, length us, event | category | flops | bytes accessed | tf_op | source)
XLA Modules:
  0.0 60.8 jit_solution(13615883250315436943)
XLA Ops:
  0.6 3.0 %collective-permute-start.1 = (bf16[256,1024]{1,0:T(8,128)(2,1)}, bf16[256,1024]{1,0:T(8,128)(2,1)S(1)}, u32[]{:S(2)}, u32[]{:S(2)}) collective-permute-start(bf16[256,1024]{1,0:T(8,128)(2,1)} %refs_3_.2), channel_id=1, source_target_pairs={{0,2},{1,3},{2,0},{3,1},{4,6},{5,7},{6,4},{7,5},{8,10},{9,11},{10,... | collective-permute-start | bytes 1572872 | tf_op jit(solution)/shard_map/ppermute | solution.py:306
  3.7 2.3 %shard_map.157 = bf16[256,1024]{1,0:T(8,128)(2,1)} custom-call(s32[1,8]{1,0:T(1,128)} %bitcast.25, s32[8,32]{1,0:T(8,128)} %bitcast.20, bf16[128,1024]{1,0:T(8,128)(2,1)} %refs_0_.2), custom_call_target="tpu_custom_call" | custom-call | tf_op jit(solution)/shard_map/pallas_call | solution.py:46
  6.0 0.0 copy-start.7
  6.0 0.0 copy-start.1
  6.0 6.0 %all-to-all-start = ((bf16[8,32,1024]{2,1,0:T(8,128)(2,1)}), bf16[8,32,1024]{2,1,0:T(8,128)(2,1)S(1)}, u32[]{:S(2)}, u32[]{:S(2)}) async-start(bf16[8,32,1024]{2,1,0:T(8,128)(2,1)} %bitcast.18), calls=%async_computation | async-start | bytes 1048576 | tf_op jit(solution)/shard_map/all_to_all | solution.py:353
  11.9 0.1 copy.18
  12.0 0.6 %reshape.25.refs_5_ = s32[1,64]{1,0:T(1,128)} reshape(s32[1,1,8,4,2]{4,3,2,1,0:T(4,128)S(1)} %copy.18) | data formatting | bytes 512 | tf_op jit(solution)/shard_map/reshape | solution.py:372
  13.3 0.0 copy-start
  13.3 2.5 %shard_map.158 = (bf16[128,1024]{1,0:T(8,128)(2,1)}, bf16[96,512]{1,0:T(8,128)(2,1)}, bf16[128,64]{1,0:T(8,128)(2,1)}, bf16[256,512]{1,0:T(8,128)(2,1)}, bf16[256,512]{1,0:T(8,128)(2,1)}) custom-call(s32[1,1]{1,0:T(1,128)S(6)} %copy.19.refs_0_, s32[16,128]{1,0:T(8,128)} %bitcast.19, s32[1,128]{1,0:T(1,128)} %bitcast.24, f32[8,128]{1,0:T(8,128)} %refs_3_.1, ...), custom_call_target="tpu_custom_call" | custom-call | tf_op jit(solution)/shard_map/pallas_call | solution.py:46
  15.9 0.0 collective-permute-done.1.refs_5_
  15.9 0.1 collective-permute-start.2
  16.0 0.5 collective-permute-start.3
  16.5 1.6 %collective-permute-start = (bf16[256,512]{1,0:T(8,128)(2,1)}, bf16[256,512]{1,0:T(8,128)(2,1)S(1)}, u32[]{:S(2)}, u32[]{:S(2)}) collective-permute-start(bf16[256,512]{1,0:T(8,128)(2,1)} %get-tuple-element.29.refs_2_), channel_id=1, source_target_pairs={{0,2},{1,3},{2,0},{3,1},{4,6},{5,7},{6,4},{7,5},{8,10},{9,11},{10,... | collective-permute-start | bytes 786440 | tf_op jit(solution)/shard_map/ppermute | solution.py:306
  18.1 0.5 collective-permute-start.4
  18.5 7.3 %collective-permute-done.refs_6_ = bf16[256,512]{1,0:T(8,128)(2,1)S(1)} collective-permute-done((bf16[256,512]{1,0:T(8,128)(2,1)}, bf16[256,512]{1,0:T(8,128)(2,1)S(1)}, u32[]{:S(2)}, u32[]{:S(2)}) %collective-permute-start) | collective-permute-done | bytes 262176 | tf_op jit(solution)/shard_map/ppermute | solution.py:306
  25.9 0.3 all-to-all-done
  26.2 0.0 collective-permute-start.5
  26.2 0.5 collective-permute-start.7
  26.7 0.0 collective-permute-done.2.refs_4_
  26.7 0.0 collective-permute-done.3.refs_6_
  26.7 0.0 copy-start.4
  26.7 0.9 %copy-done.4 = bf16[128,1024]{1,0:T(8,128)(2,1)S(1)} copy-done((bf16[128,1024]{1,0:T(8,128)(2,1)S(1)}, bf16[128,1024]{1,0:T(8,128)(2,1)}, u32[]{:S(2)}) %copy-start.4) | copy-done | bytes 262168
  27.7 3.7 %shard_map.159 = (bf16[128,1024]{1,0:T(8,128)(2,1)}, bf16[512,128]{1,0:T(8,128)(2,1)}) custom-call(bf16[128,1024]{1,0:T(8,128)(2,1)S(1)} %copy-done, bf16[256,1024]{1,0:T(8,128)(2,1)S(1)} %bitcast.14, bf16[128,1024]{1,0:T(8,128)(2,1)S(1)} %copy-done.4, bf16[256,1024]{1,0:T(8,128)(2,1)S(1)} %copy-done.1, ...), custom_call_target="tpu_custom_call" | custom-call | tf_op jit(solution)/shard_map/pallas_call | solution.py:46
  31.4 0.0 collective-permute-done.4.refs_7_
  31.4 0.1 collective-permute-start.6
  31.5 0.5 collective-permute-start.8
  32.0 5.6 %all-to-all-start.1 = ((bf16[32,16,128]{2,1,0:T(8,128)(2,1)}), bf16[32,16,128]{2,1,0:T(8,128)(2,1)S(1)}, u32[]{:S(2)}, u32[]{:S(2)}) async-start(bf16[32,16,128]{2,1,0:T(8,128)(2,1)} %bitcast.9), calls=%async_computation.1 | async-start | bytes 262144 | tf_op jit(solution)/shard_map/all_to_all | solution.py:402
  37.6 0.0 collective-permute-done.5.refs_4_
  37.6 8.2 %all-to-all-done.1 = bf16[32,16,128]{2,1,0:T(8,128)(2,1)S(1)} async-done(((bf16[32,16,128]{2,1,0:T(8,128)(2,1)}), bf16[32,16,128]{2,1,0:T(8,128)(2,1)S(1)}, u32[]{:S(2)}, u32[]{:S(2)}) %all-to-all-start.1) | async-done | bytes 131104 | tf_op jit(solution)/shard_map/all_to_all | solution.py:402
  45.8 3.9 %shard_map.160 = (f32[1,256]{1,0:T(1,128)}, bf16[512,128]{1,0:T(8,128)(2,1)S(1)}) custom-call(bf16[512,128]{1,0:T(8,128)(2,1)S(1)} %bitcast.15, bf16[96,512]{1,0:T(8,128)(2,1)S(1)} %copy-done.5, bf16[256,512]{1,0:T(8,128)(2,1)S(1)} %copy-done.2, bf16[256,512]{1,0:T(8,128)(2,1)S(1)} %copy-done.3, bf16[256,512]{1,0:T(8,128)(2,1)} %collective-permute-done.5.refs_4_, ...), custom_call_target="tpu_custom_call" | custom-call | tf_op jit(solution)/shard_map/pallas_call | solution.py:46
  49.7 10.0 %all_to_all.34 = bf16[32,16,128]{2,1,0:T(8,128)(2,1)S(1)} all-to-all(bf16[32,16,128]{2,1,0:T(8,128)(2,1)S(1)} %bitcast.17), channel_id=1, replica_groups=mesh['dom'=8,'edge'=4] {'dom','edge'}, dimensions={0} | all-to-all | bytes 262144 | tf_op jit(solution)/shard_map/all_to_all | solution.py:416
  59.7 1.0 %shard_map.161 = f32[128,1024]{1,0:T(8,128)} custom-call(bf16[128,64]{1,0:T(8,128)(2,1)S(1)} %copy-done.6, bf16[512,128]{1,0:T(8,128)(2,1)S(1)} %bitcast.16), custom_call_target="tpu_custom_call" | custom-call | tf_op jit(solution)/shard_map/pallas_call | solution.py:46
  (14 shorter events, 0.0 us)
Async XLA Ops:
  0.6 15.3 %collective-permute-start.1 = (bf16[256,1024]{1,0:T(8,128)(2,1)}, bf16[256,1024]{1,0:T(8,128)(2,1)S(1)}, u32[]{:S(2)}, u32[]{:S(2)}) collective-permute-start(bf16[256,1024]{1,0:T(8,128)(2,1)} %refs_3_.2), channel_id=1, source_target_pairs={{0,2},{1,3},{2,0},{3,1},{4,6},{5,7},{6,4},{7,5},{8,10},{9,11},{10,... | collective-permute-start | bytes 1572872 | tf_op jit(solution)/shard_map/ppermute | solution.py:306
  6.0 6.0 %copy-start.7 = (s32[1,1,8,4,2]{2,4,3,1,0:T(2,128)S(1)}, s32[1,1,8,4,2]{2,4,3,1,0:T(2,128)}, u32[]{:S(2)}) copy-start(s32[1,1,8,4,2]{2,4,3,1,0:T(2,128)} %param.22) | copy-start | bytes 772
  6.0 9.9 %copy-start.1 = (bf16[256,1024]{1,0:T(8,128)(2,1)S(1)}, bf16[256,1024]{1,0:T(8,128)(2,1)}, u32[]{:S(2)}) copy-start(bf16[256,1024]{1,0:T(8,128)(2,1)} %refs_3_.2) | copy-start | bytes 1572868
  6.0 20.2 %all-to-all-start = ((bf16[8,32,1024]{2,1,0:T(8,128)(2,1)}), bf16[8,32,1024]{2,1,0:T(8,128)(2,1)S(1)}, u32[]{:S(2)}, u32[]{:S(2)}) async-start(bf16[8,32,1024]{2,1,0:T(8,128)(2,1)} %bitcast.18), calls=%async_computation | async-start | bytes 1048576 | tf_op jit(solution)/shard_map/all_to_all | solution.py:353
  13.3 13.4 %copy-start = (bf16[128,1024]{1,0:T(8,128)(2,1)S(1)}, bf16[128,1024]{1,0:T(8,128)(2,1)}, u32[]{:S(2)}) copy-start(bf16[128,1024]{1,0:T(8,128)(2,1)} %refs_0_.2) | copy-start | bytes 786436
  15.9 10.8 %collective-permute-start.2 = (bf16[256,1024]{1,0:T(8,128)(2,1)S(1)}, bf16[256,1024]{1,0:T(8,128)(2,1)S(1)}, u32[]{:S(2)}, u32[]{:S(2)}) collective-permute-start(bf16[256,1024]{1,0:T(8,128)(2,1)S(1)} %copy-done.1), channel_id=1, source_target_pairs={{0,1},{1,0},{2,3},{3,2},{4,5},{5,4},{6,7},{7,6},{8,9},{9,8},{10,11... | collective-permute-start | bytes 1572872 | tf_op jit(solution)/shard_map/ppermute | solution.py:306
  16.0 10.7 %collective-permute-start.3 = (bf16[256,1024]{1,0:T(8,128)(2,1)S(1)}, bf16[256,1024]{1,0:T(8,128)(2,1)S(1)}, u32[]{:S(2)}, u32[]{:S(2)}) collective-permute-start(bf16[256,1024]{1,0:T(8,128)(2,1)S(1)} %collective-permute-done.1.refs_5_), channel_id=1, source_target_pairs={{0,1},{1,0},{2,3},{3,2},{4,5},{5,4},{6,7},{7,6},{8,9},{9,8},{10,11... | collective-permute-start | bytes 1572872 | tf_op jit(solution)/shard_map/ppermute | solution.py:306
  16.5 9.4 %collective-permute-start = (bf16[256,512]{1,0:T(8,128)(2,1)}, bf16[256,512]{1,0:T(8,128)(2,1)S(1)}, u32[]{:S(2)}, u32[]{:S(2)}) collective-permute-start(bf16[256,512]{1,0:T(8,128)(2,1)} %get-tuple-element.29.refs_2_), channel_id=1, source_target_pairs={{0,2},{1,3},{2,0},{3,1},{4,6},{5,7},{6,4},{7,5},{8,10},{9,11},{10,... | collective-permute-start | bytes 786440 | tf_op jit(solution)/shard_map/ppermute | solution.py:306
  18.1 13.3 %collective-permute-start.4 = (bf16[256,512]{1,0:T(8,128)(2,1)}, bf16[256,512]{1,0:T(8,128)(2,1)}, u32[]{:S(2)}, u32[]{:S(2)}) collective-permute-start(bf16[256,512]{1,0:T(8,128)(2,1)} %get-tuple-element.31.refs_3_), channel_id=1, source_target_pairs={{0,2},{1,3},{2,0},{3,1},{4,6},{5,7},{6,4},{7,5},{8,10},{9,11},{10,... | collective-permute-start | bytes 786440 | tf_op jit(solution)/shard_map/ppermute | solution.py:306
  26.2 5.2 %copy-start.3 = (bf16[256,512]{1,0:T(8,128)(2,1)S(1)}, bf16[256,512]{1,0:T(8,128)(2,1)}, u32[]{:S(2)}) copy-start(bf16[256,512]{1,0:T(8,128)(2,1)} %get-tuple-element.31.refs_3_) | copy-start | bytes 786436
  26.2 11.4 %collective-permute-start.5 = (bf16[256,512]{1,0:T(8,128)(2,1)}, bf16[256,512]{1,0:T(8,128)(2,1)}, u32[]{:S(2)}, u32[]{:S(2)}) collective-permute-start(bf16[256,512]{1,0:T(8,128)(2,1)} %get-tuple-element.29.refs_2_), channel_id=1, source_target_pairs={{0,1},{1,0},{2,3},{3,2},{4,5},{5,4},{6,7},{7,6},{8,9},{9,8},{10,11... | collective-permute-start | bytes 786440 | tf_op jit(solution)/shard_map/ppermute | solution.py:306
  26.2 11.4 %collective-permute-start.7 = (bf16[256,512]{1,0:T(8,128)(2,1)S(1)}, bf16[256,512]{1,0:T(8,128)(2,1)}, u32[]{:S(2)}, u32[]{:S(2)}) collective-permute-start(bf16[256,512]{1,0:T(8,128)(2,1)S(1)} %collective-permute-done.refs_6_), channel_id=1, source_target_pairs={{0,1},{1,0},{2,3},{3,2},{4,5},{5,4},{6,7},{7,6},{8,9},{9,8},{10,11... | collective-permute-start | bytes 786440 | tf_op jit(solution)/shard_map/ppermute | solution.py:306
  26.7 1.0 %copy-start.4 = (bf16[128,1024]{1,0:T(8,128)(2,1)S(1)}, bf16[128,1024]{1,0:T(8,128)(2,1)}, u32[]{:S(2)}) copy-start(bf16[128,1024]{1,0:T(8,128)(2,1)} %get-tuple-element.23.refs_2_) | copy-start | bytes 786436
  27.7 18.1 %copy-start.5 = (bf16[96,512]{1,0:T(8,128)(2,1)S(1)}, bf16[96,512]{1,0:T(8,128)(2,1)}, u32[]{:S(2)}) copy-start(bf16[96,512]{1,0:T(8,128)(2,1)} %get-tuple-element.28.refs_1_) | copy-start | bytes 294916
  31.4 14.4 %copy-start.2 = (bf16[256,512]{1,0:T(8,128)(2,1)S(1)}, bf16[256,512]{1,0:T(8,128)(2,1)}, u32[]{:S(2)}) copy-start(bf16[256,512]{1,0:T(8,128)(2,1)} %get-tuple-element.29.refs_2_) | copy-start | bytes 786436
  31.4 14.4 %collective-permute-start.6 = (bf16[256,512]{1,0:T(8,128)(2,1)S(1)}, bf16[256,512]{1,0:T(8,128)(2,1)S(1)}, u32[]{:S(2)}, u32[]{:S(2)}) collective-permute-start(bf16[256,512]{1,0:T(8,128)(2,1)S(1)} %copy-done.3), channel_id=1, source_target_pairs={{0,1},{1,0},{2,3},{3,2},{4,5},{5,4},{6,7},{7,6},{8,9},{9,8},{10,11... | collective-permute-start | bytes 786440 | tf_op jit(solution)/shard_map/ppermute | solution.py:306
  31.5 14.3 %collective-permute-start.8 = (bf16[256,512]{1,0:T(8,128)(2,1)}, bf16[256,512]{1,0:T(8,128)(2,1)S(1)}, u32[]{:S(2)}, u32[]{:S(2)}) collective-permute-start(bf16[256,512]{1,0:T(8,128)(2,1)} %collective-permute-done.4.refs_7_), channel_id=1, source_target_pairs={{0,1},{1,0},{2,3},{3,2},{4,5},{5,4},{6,7},{7,6},{8,9},{9,8},{10,11... | collective-permute-start | bytes 786440 | tf_op jit(solution)/shard_map/ppermute | solution.py:306
  32.0 13.8 %all-to-all-start.1 = ((bf16[32,16,128]{2,1,0:T(8,128)(2,1)}), bf16[32,16,128]{2,1,0:T(8,128)(2,1)S(1)}, u32[]{:S(2)}, u32[]{:S(2)}) async-start(bf16[32,16,128]{2,1,0:T(8,128)(2,1)} %bitcast.9), calls=%async_computation.1 | async-start | bytes 262144 | tf_op jit(solution)/shard_map/all_to_all | solution.py:402
  49.7 10.0 %copy-start.6 = (bf16[128,64]{1,0:T(8,128)(2,1)S(1)}, bf16[128,64]{1,0:T(8,128)(2,1)}, u32[]{:S(2)}) copy-start(bf16[128,64]{1,0:T(8,128)(2,1)} %get-tuple-element.35.refs_0_) | copy-start | bytes 49156

commit v13 on v11

--- a/solution.py
+++ b/solution.py
@@ -24,7 +24,8 @@
     return lax.dot_general(a, b, (dims, ((), ())), preferred_element_type=F32)
 
 
-def call(kernel, outs, ins, scratch=(), vmem_mib=20, out_space="v"):
+def call(kernel, outs, ins, scratch=(), vmem_mib=20, out_space=None):
+    out_space = out_space or jax.tree.map(lambda _: "v", outs)
     fetched = [i for i, (space, _) in enumerate(ins) if space == "f"]
 
     def body(*refs):
@@ -47,7 +48,7 @@
         body,
         out_shape=outs,
         in_specs=[SPACES[space] for space, _ in ins],
-        out_specs=jax.tree.map(lambda _: SPACES[out_space], outs),
+        out_specs=jax.tree.map(lambda space: SPACES[space], out_space),
         scratch_shapes=list(scratch)
         + [pltpu.VMEM(ins[i][1].shape, ins[i][1].dtype) for i in fetched]
         + [pltpu.SemaphoreType.DMA((max(1, len(fetched)),))],
@@ -55,7 +56,9 @@
     )(*[array for _, array in ins])
 
 
-def halo_kernel(ready, count_ref, rows_ref, feats_ref, out_ref):
+def halo_kernel(ready, count_ref, rows_ref, feats_ref, mlp_ref, out_ref, held_ref, sem):
+    hold = pltpu.make_async_copy(mlp_ref, held_ref, sem)
+    hold.start()
     doms, block = rows_ref.shape
     at = lax.broadcasted_iota(jnp.int32, (1, block), 1)
     ready()
@@ -75,6 +78,7 @@
     mark = jnp.where(mark_at, DEAD, 0.0).astype(BF16)
     out_ref[:, :128] = (rows[:, :128] + dot(dead, mark, ((0,), (0,)))).astype(BF16)
     out_ref[:, 128:] = rows[:, 128:].astype(BF16)
+    hold.wait()
 
 
 def three_parts(values):
@@ -347,15 +351,22 @@
     shape = jax.ShapeDtypeStruct
 
     heads = attn_src.shape[0]
-    send_rows = call(
+    send_rows, held_mlp = call(
         halo_kernel,
-        shape((halo, width), BF16),
-        [("f", halo_count[0]), ("f", halo_rows[0, 0]), ("f", node_feats)],
+        (shape((halo, width), BF16), shape(mlp_weight.shape, BF16)),
+        [
+            ("f", halo_count[0]),
+            ("f", halo_rows[0, 0]),
+            ("f", node_feats),
+            ("any", mlp_weight),
+        ],
+        [pltpu.SemaphoreType.DMA],
         vmem_mib=60,
+        out_space=("v", "any"),
     )
     got_rows = lax.all_to_all(send_rows, "dom", split_axis=0, concat_axis=0, tiled=True)
     gat_across = across(gat_weight, edge_count)
-    mlp_across = across(mlp_weight, edge_count)
+    mlp_across = across(held_mlp, edge_count)
     lanes = -(-(2 * table + attn_src.shape[1] + slots) // 128) * 128
     for_attend, for_score, pick = call(
         functools.partial(prepare_kernel, table),
@@ -393,8 +404,8 @@
         ],
     )
     got_ends = lax.all_to_all(send_ends, everyone, split_axis=0, concat_axis=0, tiled=True)
-    mlp_shards = [mlp_across[0], swap(mlp_across[0], "edge", 1)]
-    tied = lax.optimization_barrier((*mlp_across[1:], got_ends))[:-1]
+    mlp_shards = [mlp_weight, swap(held_mlp, "edge", 1)]
+    tied = lax.optimization_barrier((*mlp_across[1:], send_ends))[:-1]
     for shard, held in zip(mlp_across[1:], tied):
         mlp_shards += [shard, swap(held, "edge", 1)]
     early = [i for i in range(edge_count) if i < 2 or i % 2 == 0]

time: 59.3 us -> 75.3 us (1.27)
  Pallas kernels: 11.4 us -> 26.9 us
  local copies, waits for them, and re-layouts: 3.22 us -> 5.06 us
  starting transfers between devices: 14.5 us -> 12.8 us
    pallas_call x6, Pallas kernels: 11.4 us -> 26.9 us  [call(): pl.pallas_call(body, out_shape=outs, in_specs=[SPACES[space] for space, _...]
    all_to_all x1, waiting for transfers between devices: 8.2 us -> 10.4 us  [local(): lax.all_to_all(send_rows, 'dom', split_axis=0, concat_axis=0, tiled=True)]
    ppermute x6, waiting for transfers between devices: 2.19 us -> 0.02 us  [swap(): return lax.ppermute(array, axis, [(i, i ^ k) for i in range(count)])]
    unnamed x29 -> x33, local copies, waits for them, and re-layouts: 3.11 us -> 4.96 us
    ppermute x6, starting transfers between devices: 5.82 us -> 4.05 us  [swap(): return lax.ppermute(array, axis, [(i, i ^ k) for i in range(count)])]
  transfers between devices with their start and end apart: 8 -> 8, of which waited for: 4 -> 2; matrix products, arithmetic and copies ran while one was open for 0% -> 0% of each run, Pallas kernels for 14% -> 31%
where the time goes in v13:
time: 75.3 us; the launch traced here: 74.9 us
  Pallas kernels  26.9 us (36%)
  waiting for transfers between devices  18.6 us (25%)
  starting transfers between devices  12.8 us (17%)
  blocking collectives  10 us (13%)
  local copies, waits for them, and re-layouts  5.06 us (7%)
  between operations  1.45 us (2%)
    pallas_call x6, Pallas kernels, call(): pl.pallas_call(body, out_shape=outs, in_specs=[SPACES[space] for space, _...  26.9 us
    all_to_all x1, waiting for transfers between devices, local(): lax.all_to_all(send_rows, 'dom', split_axis=0, concat_axis=0, tiled=True)  10.4 us
    all_to_all x1, blocking collectives, local(): lax.all_to_all(send_back, everyone, split_axis=0, concat_axis=0, tiled=True)  10 us
    all_to_all x1, waiting for transfers between devices, local(): lax.all_to_all(send_ends, everyone, split_axis=0, concat_axis=0, tiled=True)  8.22 us
    all_to_all x1, starting transfers between devices, local(): lax.all_to_all(send_rows, 'dom', split_axis=0, concat_axis=0, tiled=True)  5.95 us
    unnamed x33, local copies, waits for them, and re-layouts  4.96 us
    ppermute x6, starting transfers between devices, swap(): return lax.ppermute(array, axis, [(i, i ^ k) for i in range(count)])  4.05 us
    all_to_all x1, starting transfers between devices, local(): lax.all_to_all(send_ends, everyone, split_axis=0, concat_axis=0, tiled=True)  2.83 us
  transfers between devices with their start and end apart: 8, of which 2 were waited for; matrix products, arithmetic and copies ran while one was open for 0% of the time, Pallas kernels for 31%

profile of v13, /device:TPU:0, one launch (start us, length us, event | category | flops | bytes accessed | tf_op | source)
XLA Modules:
  0.0 74.9 jit_solution(2057689434112259616)
XLA Ops:
  0.6 3.0 %collective-permute-start = (bf16[256,1024]{1,0:T(8,128)(2,1)}, bf16[256,1024]{1,0:T(8,128)(2,1)S(1)}, u32[]{:S(2)}, u32[]{:S(2)}) collective-permute-start(bf16[256,1024]{1,0:T(8,128)(2,1)} %refs_3_.5), channel_id=1, source_target_pairs={{0,2},{1,3},{2,0},{3,1},{4,6},{5,7},{6,4},{7,5},{8,10},{9,11},{10,... | collective-permute-start | bytes 1572872 | tf_op jit(solution)/shard_map/ppermute | solution.py:313
  3.7 17.8 %shard_map.157 = (bf16[256,1024]{1,0:T(8,128)(2,1)}, bf16[512,512]{1,0:T(8,128)(2,1)}) custom-call(s32[1,8]{1,0:T(1,128)} %bitcast.26, s32[8,32]{1,0:T(8,128)} %bitcast.25, bf16[128,1024]{1,0:T(8,128)(2,1)} %refs_0_.2, bf16[512,512]{1,0:T(8,128)(2,1)} %refs_3_.6), custom_call_target="tpu_custom_call" | custom-call | tf_op jit(solution)/shard_map/pallas_call | solution.py:47
  21.5 0.0 copy-start.15
  21.5 0.0 copy-start.2
  21.5 0.0 copy-start.1
  21.5 5.9 %all-to-all-start = ((bf16[8,32,1024]{2,1,0:T(8,128)(2,1)}), bf16[8,32,1024]{2,1,0:T(8,128)(2,1)S(1)}, u32[]{:S(2)}, u32[]{:S(2)}) async-start(bf16[8,32,1024]{2,1,0:T(8,128)(2,1)} %bitcast.24), calls=%async_computation | async-start | bytes 1048576 | tf_op jit(solution)/shard_map/all_to_all | solution.py:367
  28.1 0.1 copy.18
  28.2 0.0 copy-start.14
  28.3 0.1 reshape.25.refs_5_
  28.4 0.0 copy-start.8
  28.4 0.0 copy-start.13
  28.4 0.5 copy-done.9
  28.9 0.0 copy-done.10
  28.9 0.0 copy-done.11
  28.9 0.0 copy-done.12
  29.0 0.1 copy-done.8
  29.1 0.5 shard_map.158
  29.6 0.7 copy-done.5
  30.3 0.5 collective-permute-start.2
  30.8 0.5 collective-permute-start.4
  31.3 10.4 %all-to-all-done = bf16[8,32,1024]{2,1,0:T(8,128)(2,1)S(1)} async-done(((bf16[8,32,1024]{2,1,0:T(8,128)(2,1)}), bf16[8,32,1024]{2,1,0:T(8,128)(2,1)S(1)}, u32[]{:S(2)}, u32[]{:S(2)}) %all-to-all-start) | async-done | bytes 524320 | tf_op jit(solution)/shard_map/all_to_all | solution.py:367
  41.7 0.8 %copy-done.3 = bf16[256,1024]{1,0:T(8,128)(2,1)} copy-done((bf16[256,1024]{1,0:T(8,128)(2,1)}, bf16[256,1024]{1,0:T(8,128)(2,1)S(1)}, u32[]{:S(2)}) %copy-start.3) | copy-done | bytes 524312
  42.5 1.0 %copy-done.4 = bf16[256,1024]{1,0:T(8,128)(2,1)S(1)} copy-done((bf16[256,1024]{1,0:T(8,128)(2,1)S(1)}, bf16[256,1024]{1,0:T(8,128)(2,1)}, u32[]{:S(2)}) %copy-start.4) | copy-done | bytes 524312
  43.6 0.9 %copy-done.6 = bf16[128,1024]{1,0:T(8,128)(2,1)S(1)} copy-done((bf16[128,1024]{1,0:T(8,128)(2,1)S(1)}, bf16[128,1024]{1,0:T(8,128)(2,1)}, u32[]{:S(2)}) %copy-start.6) | copy-done | bytes 262168
  44.5 4.7 %shard_map.159 = (bf16[128,1024]{1,0:T(8,128)(2,1)}, bf16[512,128]{1,0:T(8,128)(2,1)S(1)}) custom-call(bf16[128,1024]{1,0:T(8,128)(2,1)S(1)} %copy-done.1, bf16[256,1024]{1,0:T(8,128)(2,1)S(1)} %bitcast.14, bf16[128,1024]{1,0:T(8,128)(2,1)S(1)} %copy-done.6, bf16[256,1024]{1,0:T(8,128)(2,1)S(1)} %copy-done.2, bf16[256,1024]{1,0:T(8,128)(2,1)S(1)} %copy-done.4, ...), custom_call_target="tpu_custom_call" | custom-call | tf_op jit(solution)/shard_map/pallas_call | solution.py:47
  49.2 0.6 copy-done.7
  49.9 2.8 %all-to-all-start.1 = ((bf16[32,16,128]{2,1,0:T(8,128)(2,1)}), bf16[32,16,128]{2,1,0:T(8,128)(2,1)S(1)}, u32[]{:S(2)}, u32[]{:S(2)}) async-start(bf16[32,16,128]{2,1,0:T(8,128)(2,1)} %bitcast.17), calls=%async_computation.1 | async-start | bytes 262144 | tf_op jit(solution)/shard_map/all_to_all | solution.py:406
  52.7 8.2 %all-to-all-done.1 = bf16[32,16,128]{2,1,0:T(8,128)(2,1)S(1)} async-done(((bf16[32,16,128]{2,1,0:T(8,128)(2,1)}), bf16[32,16,128]{2,1,0:T(8,128)(2,1)S(1)}, u32[]{:S(2)}, u32[]{:S(2)}) %all-to-all-start.1) | async-done | bytes 131104 | tf_op jit(solution)/shard_map/all_to_all | solution.py:406
  61.0 0.4 shard_map.160
  61.4 2.4 %shard_map.161 = (f32[1,256]{1,0:T(1,128)}, bf16[512,128]{1,0:T(8,128)(2,1)S(1)}) custom-call(bf16[64,1024]{1,0:T(8,128)(2,1)S(1)} %get-tuple-element.25.refs_0_, f32[2,64,512]{2,1,0:T(8,128)S(1)} %get-tuple-element.26.refs_1_, bf16[96,512]{1,0:T(8,128)(2,1)S(1)} %get-tuple-element.23.refs_1_.refs_2_, bf16[512,512]{1,0:T(8,128)(2,1)S(1)} %copy-done, ...), custom_call_target="tpu_custom_call" | custom-call | tf_op jit(solution)/shard_map/pallas_call | solution.py:47
  63.8 10.0 %all_to_all.33 = bf16[32,16,128]{2,1,0:T(8,128)(2,1)S(1)} all-to-all(bf16[32,16,128]{2,1,0:T(8,128)(2,1)S(1)} %bitcast.18), channel_id=1, replica_groups=mesh['dom'=8,'edge'=4] {'dom','edge'}, dimensions={0} | all-to-all | bytes 262144 | tf_op jit(solution)/shard_map/all_to_all | solution.py:434
  73.9 1.0 %shard_map.162 = f32[128,1024]{1,0:T(8,128)} custom-call(bf16[128,64]{1,0:T(8,128)(2,1)S(1)} %get-tuple-element.29.refs_0_, bf16[512,128]{1,0:T(8,128)(2,1)S(1)} %bitcast.16), custom_call_target="tpu_custom_call" | custom-call | tf_op jit(solution)/shard_map/pallas_call | solution.py:47
  (25 shorter events, 0.1 us)
Async XLA Ops:
  0.6 29.7 %collective-permute-start = (bf16[256,1024]{1,0:T(8,128)(2,1)}, bf16[256,1024]{1,0:T(8,128)(2,1)S(1)}, u32[]{:S(2)}, u32[]{:S(2)}) collective-permute-start(bf16[256,1024]{1,0:T(8,128)(2,1)} %refs_3_.5), channel_id=1, source_target_pairs={{0,2},{1,3},{2,0},{3,1},{4,6},{5,7},{6,4},{7,5},{8,10},{9,11},{10,... | collective-permute-start | bytes 1572872 | tf_op jit(solution)/shard_map/ppermute | solution.py:313
  21.5 6.6 %copy-start.15 = (s32[1,1,8,4,2]{2,4,3,1,0:T(2,128)S(1)}, s32[1,1,8,4,2]{2,4,3,1,0:T(2,128)}, u32[]{:S(2)}) copy-start(s32[1,1,8,4,2]{2,4,3,1,0:T(2,128)} %param.22) | copy-start | bytes 772
  21.5 8.8 %copy-start.2 = (bf16[256,1024]{1,0:T(8,128)(2,1)S(1)}, bf16[256,1024]{1,0:T(8,128)(2,1)}, u32[]{:S(2)}) copy-start(bf16[256,1024]{1,0:T(8,128)(2,1)} %refs_3_.5) | copy-start | bytes 1572868
  21.5 21.0 %copy-start.1 = (bf16[128,1024]{1,0:T(8,128)(2,1)S(1)}, bf16[128,1024]{1,0:T(8,128)(2,1)}, u32[]{:S(2)}) copy-start(bf16[128,1024]{1,0:T(8,128)(2,1)} %refs_0_.2) | copy-start | bytes 786436
  21.5 20.2 %all-to-all-start = ((bf16[8,32,1024]{2,1,0:T(8,128)(2,1)}), bf16[8,32,1024]{2,1,0:T(8,128)(2,1)S(1)}, u32[]{:S(2)}, u32[]{:S(2)}) async-start(bf16[8,32,1024]{2,1,0:T(8,128)(2,1)} %bitcast.24), calls=%async_computation | async-start | bytes 1048576 | tf_op jit(solution)/shard_map/all_to_all | solution.py:367
  28.2 0.7 copy-start.9
  28.2 0.7 copy-start.10
  28.2 0.7 copy-start.11
  28.2 0.7 copy-start.12
  28.2 0.7 copy-start.14
  28.4 0.7 copy-start.8
  28.4 0.7 copy-start.13
  29.6 0.7 copy-start.5
  30.3 11.4 %collective-permute-start.1 = (bf16[256,1024]{1,0:T(8,128)(2,1)S(1)}, bf16[256,1024]{1,0:T(8,128)(2,1)S(1)}, u32[]{:S(2)}, u32[]{:S(2)}) collective-permute-start(bf16[256,1024]{1,0:T(8,128)(2,1)S(1)} %copy-done.2), channel_id=1, source_target_pairs={{0,1},{1,0},{2,3},{3,2},{4,5},{5,4},{6,7},{7,6},{8,9},{9,8},{10,11... | collective-permute-start | bytes 1572872 | tf_op jit(solution)/shard_map/ppermute | solution.py:313
  30.3 12.2 %collective-permute-start.2 = (bf16[256,1024]{1,0:T(8,128)(2,1)S(1)}, bf16[256,1024]{1,0:T(8,128)(2,1)}, u32[]{:S(2)}, u32[]{:S(2)}) collective-permute-start(bf16[256,1024]{1,0:T(8,128)(2,1)S(1)} %collective-permute-done.refs_5_), channel_id=1, source_target_pairs={{0,1},{1,0},{2,3},{3,2},{4,5},{5,4},{6,7},{7,6},{8,9},{9,8},{10,11... | collective-permute-start | bytes 1572872 | tf_op jit(solution)/shard_map/ppermute | solution.py:313
  30.8 19.1 %collective-permute-start.4 = (bf16[512,512]{1,0:T(8,128)(2,1)}, bf16[512,512]{1,0:T(8,128)(2,1)S(1)}, u32[]{:S(2)}, u32[]{:S(2)}) collective-permute-start(bf16[512,512]{1,0:T(8,128)(2,1)} %get-tuple-element.24), channel_id=1, source_target_pairs={{0,2},{1,3},{2,0},{3,1},{4,6},{5,7},{6,4},{7,5},{8,10},{9,11},{10,... | collective-permute-start | bytes 1572872 | tf_op jit(solution)/shard_map/ppermute | solution.py:313
  31.3 21.4 %collective-permute-start.3 = (bf16[512,512]{1,0:T(8,128)(2,1)}, bf16[512,512]{1,0:T(8,128)(2,1)S(1)}, u32[]{:S(2)}, u32[]{:S(2)}) collective-permute-start(bf16[512,512]{1,0:T(8,128)(2,1)} %get-tuple-element.24), channel_id=1, source_target_pairs={{0,1},{1,0},{2,3},{3,2},{4,5},{5,4},{6,7},{7,6},{8,9},{9,8},{10,11... | collective-permute-start | bytes 1572872 | tf_op jit(solution)/shard_map/ppermute | solution.py:313
  41.7 0.8 %copy-start.3 = (bf16[256,1024]{1,0:T(8,128)(2,1)}, bf16[256,1024]{1,0:T(8,128)(2,1)S(1)}, u32[]{:S(2)}) copy-start(bf16[256,1024]{1,0:T(8,128)(2,1)S(1)} %collective-permute-done.1.refs_4_) | copy-start | bytes 1572868
  42.5 1.0 %copy-start.4 = (bf16[256,1024]{1,0:T(8,128)(2,1)S(1)}, bf16[256,1024]{1,0:T(8,128)(2,1)}, u32[]{:S(2)}) copy-start(bf16[256,1024]{1,0:T(8,128)(2,1)} %copy-done.3) | copy-start | bytes 1572868
  43.6 0.9 %copy-start.6 = (bf16[128,1024]{1,0:T(8,128)(2,1)S(1)}, bf16[128,1024]{1,0:T(8,128)(2,1)}, u32[]{:S(2)}) copy-start(bf16[128,1024]{1,0:T(8,128)(2,1)} %copy-done.5) | copy-start | bytes 786436
  44.5 16.4 %copy-start = (bf16[512,512]{1,0:T(8,128)(2,1)S(1)}, bf16[512,512]{1,0:T(8,128)(2,1)}, u32[]{:S(2)}) copy-start(bf16[512,512]{1,0:T(8,128)(2,1)} %refs_3_.6) | copy-start | bytes 1572868
  49.2 0.7 copy-start.7
  49.9 11.5 %collective-permute-start.5 = (bf16[512,512]{1,0:T(8,128)(2,1)S(1)}, bf16[512,512]{1,0:T(8,128)(2,1)S(1)}, u32[]{:S(2)}, u32[]{:S(2)}) collective-permute-start(bf16[512,512]{1,0:T(8,128)(2,1)S(1)} %collective-permute-done.4.refs_4_.refs_5_), channel_id=1, source_target_pairs={{0,1},{1,0},{2,3},{3,2},{4,5},{5,4},{6,7},{7,6},{8,9},{9,8},{10,11... | collective-permute-start | bytes 1572872 | tf_op jit(solution)/shard_map/ppermute | solution.py:313
  49.9 11.1 %all-to-all-start.1 = ((bf16[32,16,128]{2,1,0:T(8,128)(2,1)}), bf16[32,16,128]{2,1,0:T(8,128)(2,1)S(1)}, u32[]{:S(2)}, u32[]{:S(2)}) async-start(bf16[32,16,128]{2,1,0:T(8,128)(2,1)} %bitcast.17), calls=%async_computation.1 | async-start | bytes 262144 | tf_op jit(solution)/shard_map/all_to_all | solution.py:406

commit v14 on v11

--- a/solution.py
+++ b/solution.py
@@ -24,7 +24,7 @@
     return lax.dot_general(a, b, (dims, ((), ())), preferred_element_type=F32)
 
 
-def call(kernel, outs, ins, scratch=(), vmem_mib=20, out_space="v"):
+def call(kernel, outs, ins, scratch=(), vmem_mib=20, out_space="v", cost=None):
     fetched = [i for i, (space, _) in enumerate(ins) if space == "f"]
 
     def body(*refs):
@@ -51,6 +51,7 @@
         scratch_shapes=list(scratch)
         + [pltpu.VMEM(ins[i][1].shape, ins[i][1].dtype) for i in fetched]
         + [pltpu.SemaphoreType.DMA((max(1, len(fetched)),))],
+        cost_estimate=cost,
         compiler_params=pltpu.CompilerParams(vmem_limit_bytes=vmem_mib * 1024 * 1024),
     )(*[array for _, array in ins])
 
@@ -375,6 +376,7 @@
             ("f", labels[0]),
             ("f", out_weight.reshape(1, hidden)),
         ],
+        vmem_mib=60,
     )
     gat_across = lax.optimization_barrier((*gat_across, for_attend))[:-1]
     gat_shards = from_core(gat_across)
@@ -394,7 +396,7 @@
     )
     got_ends = lax.all_to_all(send_ends, everyone, split_axis=0, concat_axis=0, tiled=True)
     mlp_shards = [mlp_across[0], swap(mlp_across[0], "edge", 1)]
-    tied = lax.optimization_barrier((*mlp_across[1:], got_ends))[:-1]
+    tied = lax.optimization_barrier((*mlp_across[1:], send_ends))[:-1]
     for shard, held in zip(mlp_across[1:], tied):
         mlp_shards += [shard, swap(held, "edge", 1)]
     early = [i for i in range(edge_count) if i < 2 or i % 2 == 0]
@@ -408,6 +410,7 @@
         ),
         [("v", got_ends), ("v", for_score)] + [("v", mlp_shards[i]) for i in early],
         [packed],
+        cost=pl.CostEstimate(flops=20 * 10**9, bytes_accessed=60 * 10**6, transcendentals=0),
     )
     scores, send_back = call(
         functools.partial(score_kernel, late, cands),

time: 59.3 us -> 57.5 us (0.970)
  waiting for transfers between devices: 18.3 us -> 16.5 us
  Pallas kernels: 11.4 us -> 13.2 us
  local copies, waits for them, and re-layouts: 3.22 us -> 1.71 us
    unnamed x29 -> x15, local copies, waits for them, and re-layouts: 3.11 us -> 1.08 us
    ppermute x6, waiting for transfers between devices: 2.19 us -> 0.39 us  [swap(): return lax.ppermute(array, axis, [(i, i ^ k) for i in range(count)])]
    pallas_call x6, Pallas kernels: 11.4 us -> 13.2 us  [call(): pl.pallas_call(body, out_shape=outs, in_specs=[SPACES[space] for space, _...]
  transfers between devices with their start and end apart: 8 -> 8, of which waited for: 4 -> 3; matrix products, arithmetic and copies ran while one was open for 0% -> 1% of each run, Pallas kernels for 14% -> 17%
where the time goes in v14:
time: 57.5 us; the launch traced here: 57.1 us
  waiting for transfers between devices  16.5 us (29%)
  starting transfers between devices  14.3 us (25%)
  Pallas kernels  13.2 us (23%)
  blocking collectives  10 us (17%)
  local copies, waits for them, and re-layouts  1.71 us (3%)
  between operations  1.42 us (2%)
    pallas_call x6, Pallas kernels, call(): pl.pallas_call(body, out_shape=outs, in_specs=[SPACES[space] for space, _...  13.2 us
    all_to_all x1, blocking collectives, local(): lax.all_to_all(send_back, everyone, split_axis=0, concat_axis=0, tiled=True)  10 us
    all_to_all x1, waiting for transfers between devices, local(): lax.all_to_all(send_rows, 'dom', split_axis=0, concat_axis=0, tiled=True)  8.2 us
    all_to_all x1, waiting for transfers between devices, local(): lax.all_to_all(send_ends, everyone, split_axis=0, concat_axis=0, tiled=True)  7.9 us
    all_to_all x1, starting transfers between devices, local(): lax.all_to_all(send_rows, 'dom', split_axis=0, concat_axis=0, tiled=True)  5.95 us
    ppermute x6, starting transfers between devices, swap(): return lax.ppermute(array, axis, [(i, i ^ k) for i in range(count)])  5.6 us
    all_to_all x1, starting transfers between devices, local(): lax.all_to_all(send_ends, everyone, split_axis=0, concat_axis=0, tiled=True)  2.74 us
  transfers between devices with their start and end apart: 8, of which 3 were waited for; matrix products, arithmetic and copies ran while one was open for 1% of the time, Pallas kernels for 17%

profile of v14, /device:TPU:0, one launch (start us, length us, event | category | flops | bytes accessed | tf_op | source)
XLA Modules:
  0.0 57.1 jit_solution(17227872324469534619)
XLA Ops:
  0.6 3.0 %collective-permute-start = (bf16[256,1024]{1,0:T(8,128)(2,1)}, bf16[256,1024]{1,0:T(8,128)(2,1)S(1)}, u32[]{:S(2)}, u32[]{:S(2)}) collective-permute-start(bf16[256,1024]{1,0:T(8,128)(2,1)} %refs_3_.3), channel_id=1, source_target_pairs={{0,2},{1,3},{2,0},{3,1},{4,6},{5,7},{6,4},{7,5},{8,10},{9,11},{10,... | collective-permute-start | bytes 1572872 | tf_op jit(solution)/shard_map/ppermute | solution.py:310
  3.7 2.4 %shard_map.157 = bf16[256,1024]{1,0:T(8,128)(2,1)} custom-call(s32[1,8]{1,0:T(1,128)} %bitcast.25, s32[8,32]{1,0:T(8,128)} %bitcast.20, bf16[128,1024]{1,0:T(8,128)(2,1)} %refs_0_.2), custom_call_target="tpu_custom_call" | custom-call | tf_op jit(solution)/shard_map/pallas_call | solution.py:46
  6.0 0.0 copy-start.6
  6.0 0.0 copy-start.1
  6.0 0.0 copy-start
  6.1 5.9 %all-to-all-start = ((bf16[8,32,1024]{2,1,0:T(8,128)(2,1)}), bf16[8,32,1024]{2,1,0:T(8,128)(2,1)S(1)}, u32[]{:S(2)}, u32[]{:S(2)}) async-start(bf16[8,32,1024]{2,1,0:T(8,128)(2,1)} %bitcast.18), calls=%async_computation | async-start | bytes 1048576 | tf_op jit(solution)/shard_map/all_to_all | solution.py:357
  12.7 0.1 copy.18
  12.8 0.6 %reshape.25.refs_5_ = s32[1,64]{1,0:T(1,128)} reshape(s32[1,1,8,4,2]{4,3,2,1,0:T(4,128)S(1)} %copy.18) | data formatting | bytes 512 | tf_op jit(solution)/shard_map/reshape | solution.py:374
  13.4 2.0 %shard_map.158 = (bf16[128,1024]{1,0:T(8,128)(2,1)}, bf16[96,512]{1,0:T(8,128)(2,1)}, bf16[128,64]{1,0:T(8,128)(2,1)}) custom-call(s32[1,1]{1,0:T(1,128)S(6)} %copy.19.refs_0_, s32[16,128]{1,0:T(8,128)} %bitcast.19, s32[1,128]{1,0:T(1,128)} %bitcast.24, f32[8,128]{1,0:T(8,128)} %refs_3_.2, f32[8,128]{1,0:T(8,128)} %refs_4_.1, s32[1,64]{1,0:T(1,128)} %reshape.25.refs_5_, ...), custom_call_target="tpu_custom_call" | custom-call | tf_op jit(solution)/shard_map/pallas_call | solution.py:46
  15.4 0.4 collective-permute-done.refs_5_
  15.8 0.0 collective-permute-start.1
  15.8 0.5 collective-permute-start.2
  16.3 0.0 copy-done.1
  16.3 1.7 %collective-permute-start.4 = (bf16[512,512]{1,0:T(8,128)(2,1)S(1)}, bf16[512,512]{1,0:T(8,128)(2,1)S(1)}, u32[]{:S(2)}, u32[]{:S(2)}) collective-permute-start(bf16[512,512]{1,0:T(8,128)(2,1)S(1)} %copy-done.1), channel_id=1, source_target_pairs={{0,2},{1,3},{2,0},{3,1},{4,6},{5,7},{6,4},{7,5},{8,10},{9,11},{10,... | collective-permute-start | bytes 1572872 | tf_op jit(solution)/shard_map/ppermute | solution.py:310
  18.1 0.0 collective-permute-start.3
  18.1 8.2 %all-to-all-done = bf16[8,32,1024]{2,1,0:T(8,128)(2,1)S(1)} async-done(((bf16[8,32,1024]{2,1,0:T(8,128)(2,1)}), bf16[8,32,1024]{2,1,0:T(8,128)(2,1)S(1)}, u32[]{:S(2)}, u32[]{:S(2)}) %all-to-all-start) | async-done | bytes 524320 | tf_op jit(solution)/shard_map/all_to_all | solution.py:357
  26.3 0.0 collective-permute-done.1.refs_4_
  26.3 0.0 collective-permute-done.2.refs_6_
  26.3 0.0 copy-start.3
  26.3 0.9 %copy-done.3 = bf16[128,1024]{1,0:T(8,128)(2,1)S(1)} copy-done((bf16[128,1024]{1,0:T(8,128)(2,1)S(1)}, bf16[128,1024]{1,0:T(8,128)(2,1)}, u32[]{:S(2)}) %copy-start.3) | copy-done | bytes 262168
  27.2 4.9 %shard_map.159 = (bf16[128,1024]{1,0:T(8,128)(2,1)}, bf16[512,128]{1,0:T(8,128)(2,1)}) custom-call(bf16[128,1024]{1,0:T(8,128)(2,1)S(1)} %copy-done, bf16[256,1024]{1,0:T(8,128)(2,1)S(1)} %bitcast.14, bf16[128,1024]{1,0:T(8,128)(2,1)S(1)} %copy-done.3, bf16[256,1024]{1,0:T(8,128)(2,1)S(1)} %copy-done.2, bf16[256,1024]{1,0:T(8,128)(2,1)} %collective-permute-done.1.refs_4_, ...), custom_call_target="tpu_custom_call" | custom-call | tf_op jit(solution)/shard_map/pallas_call | solution.py:46
  32.2 2.7 %all-to-all-start.1 = ((bf16[32,16,128]{2,1,0:T(8,128)(2,1)}), bf16[32,16,128]{2,1,0:T(8,128)(2,1)S(1)}, u32[]{:S(2)}, u32[]{:S(2)}) async-start(bf16[32,16,128]{2,1,0:T(8,128)(2,1)} %bitcast.9), calls=%async_computation.1 | async-start | bytes 262144 | tf_op jit(solution)/shard_map/all_to_all | solution.py:397
  34.9 0.0 collective-permute-done.4.refs_4_.refs_5_
  34.9 0.3 collective-permute-start.5
  35.2 0.0 collective-permute-done.3.refs_3_.refs_4_
  35.2 7.9 %all-to-all-done.1 = bf16[32,16,128]{2,1,0:T(8,128)(2,1)S(1)} async-done(((bf16[32,16,128]{2,1,0:T(8,128)(2,1)}), bf16[32,16,128]{2,1,0:T(8,128)(2,1)S(1)}, u32[]{:S(2)}, u32[]{:S(2)}) %all-to-all-start.1) | async-done | bytes 131104 | tf_op jit(solution)/shard_map/all_to_all | solution.py:397
  43.1 0.4 shard_map.160
  43.6 0.0 collective-permute-done.5.refs_6_
  43.6 2.4 %shard_map.161 = (f32[1,256]{1,0:T(1,128)}, bf16[512,128]{1,0:T(8,128)(2,1)S(1)}) custom-call(bf16[64,1024]{1,0:T(8,128)(2,1)S(1)} %get-tuple-element.21.refs_0_, f32[2,64,512]{2,1,0:T(8,128)S(1)} %get-tuple-element.22.refs_1_, bf16[96,512]{1,0:T(8,128)(2,1)S(1)} %copy-done.4, bf16[512,512]{1,0:T(8,128)(2,1)S(1)} %copy-done.1, ...), custom_call_target="tpu_custom_call" | custom-call | tf_op jit(solution)/shard_map/pallas_call | solution.py:46
  46.0 10.0 %all_to_all.33 = bf16[32,16,128]{2,1,0:T(8,128)(2,1)S(1)} all-to-all(bf16[32,16,128]{2,1,0:T(8,128)(2,1)S(1)} %bitcast.17), channel_id=1, replica_groups=mesh['dom'=8,'edge'=4] {'dom','edge'}, dimensions={0} | all-to-all | bytes 262144 | tf_op jit(solution)/shard_map/all_to_all | solution.py:426
  56.0 0.0 copy-done.5
  56.0 1.0 %shard_map.162 = f32[128,1024]{1,0:T(8,128)} custom-call(bf16[128,64]{1,0:T(8,128)(2,1)S(1)} %copy-done.5, bf16[512,128]{1,0:T(8,128)(2,1)S(1)} %bitcast.15), custom_call_target="tpu_custom_call" | custom-call | tf_op jit(solution)/shard_map/pallas_call | solution.py:46
  (7 shorter events, 0.0 us)
Async XLA Ops:
  0.6 15.2 %collective-permute-start = (bf16[256,1024]{1,0:T(8,128)(2,1)}, bf16[256,1024]{1,0:T(8,128)(2,1)S(1)}, u32[]{:S(2)}, u32[]{:S(2)}) collective-permute-start(bf16[256,1024]{1,0:T(8,128)(2,1)} %refs_3_.3), channel_id=1, source_target_pairs={{0,2},{1,3},{2,0},{3,1},{4,6},{5,7},{6,4},{7,5},{8,10},{9,11},{10,... | collective-permute-start | bytes 1572872 | tf_op jit(solution)/shard_map/ppermute | solution.py:310
  3.7 12.1 %copy-start.2 = (bf16[256,1024]{1,0:T(8,128)(2,1)S(1)}, bf16[256,1024]{1,0:T(8,128)(2,1)}, u32[]{:S(2)}) copy-start(bf16[256,1024]{1,0:T(8,128)(2,1)} %refs_3_.3) | copy-start | bytes 1572868
  6.0 6.6 %copy-start.6 = (s32[1,1,8,4,2]{2,4,3,1,0:T(2,128)S(1)}, s32[1,1,8,4,2]{2,4,3,1,0:T(2,128)}, u32[]{:S(2)}) copy-start(s32[1,1,8,4,2]{2,4,3,1,0:T(2,128)} %param.22) | copy-start | bytes 772
  6.0 10.3 %copy-start.1 = (bf16[512,512]{1,0:T(8,128)(2,1)S(1)}, bf16[512,512]{1,0:T(8,128)(2,1)}, u32[]{:S(2)}) copy-start(bf16[512,512]{1,0:T(8,128)(2,1)} %refs_3_.4) | copy-start | bytes 1572868
  6.0 20.2 %copy-start = (bf16[128,1024]{1,0:T(8,128)(2,1)S(1)}, bf16[128,1024]{1,0:T(8,128)(2,1)}, u32[]{:S(2)}) copy-start(bf16[128,1024]{1,0:T(8,128)(2,1)} %refs_0_.2) | copy-start | bytes 786436
  6.1 20.2 %all-to-all-start = ((bf16[8,32,1024]{2,1,0:T(8,128)(2,1)}), bf16[8,32,1024]{2,1,0:T(8,128)(2,1)S(1)}, u32[]{:S(2)}, u32[]{:S(2)}) async-start(bf16[8,32,1024]{2,1,0:T(8,128)(2,1)} %bitcast.18), calls=%async_computation | async-start | bytes 1048576 | tf_op jit(solution)/shard_map/all_to_all | solution.py:357
  15.8 10.5 %collective-permute-start.1 = (bf16[256,1024]{1,0:T(8,128)(2,1)S(1)}, bf16[256,1024]{1,0:T(8,128)(2,1)}, u32[]{:S(2)}, u32[]{:S(2)}) collective-permute-start(bf16[256,1024]{1,0:T(8,128)(2,1)S(1)} %copy-done.2), channel_id=1, source_target_pairs={{0,1},{1,0},{2,3},{3,2},{4,5},{5,4},{6,7},{7,6},{8,9},{9,8},{10,11... | collective-permute-start | bytes 1572872 | tf_op jit(solution)/shard_map/ppermute | solution.py:310
  15.8 10.5 %collective-permute-start.2 = (bf16[256,1024]{1,0:T(8,128)(2,1)S(1)}, bf16[256,1024]{1,0:T(8,128)(2,1)}, u32[]{:S(2)}, u32[]{:S(2)}) collective-permute-start(bf16[256,1024]{1,0:T(8,128)(2,1)S(1)} %collective-permute-done.refs_5_), channel_id=1, source_target_pairs={{0,1},{1,0},{2,3},{3,2},{4,5},{5,4},{6,7},{7,6},{8,9},{9,8},{10,11... | collective-permute-start | bytes 1572872 | tf_op jit(solution)/shard_map/ppermute | solution.py:310
  16.3 18.6 %collective-permute-start.4 = (bf16[512,512]{1,0:T(8,128)(2,1)S(1)}, bf16[512,512]{1,0:T(8,128)(2,1)S(1)}, u32[]{:S(2)}, u32[]{:S(2)}) collective-permute-start(bf16[512,512]{1,0:T(8,128)(2,1)S(1)} %copy-done.1), channel_id=1, source_target_pairs={{0,2},{1,3},{2,0},{3,1},{4,6},{5,7},{6,4},{7,5},{8,10},{9,11},{10,... | collective-permute-start | bytes 1572872 | tf_op jit(solution)/shard_map/ppermute | solution.py:310
  18.1 17.2 %collective-permute-start.3 = (bf16[512,512]{1,0:T(8,128)(2,1)S(1)}, bf16[512,512]{1,0:T(8,128)(2,1)S(1)}, u32[]{:S(2)}, u32[]{:S(2)}) collective-permute-start(bf16[512,512]{1,0:T(8,128)(2,1)S(1)} %copy-done.1), channel_id=1, source_target_pairs={{0,1},{1,0},{2,3},{3,2},{4,5},{5,4},{6,7},{7,6},{8,9},{9,8},{10,11... | collective-permute-start | bytes 1572872 | tf_op jit(solution)/shard_map/ppermute | solution.py:310
  26.3 1.0 %copy-start.3 = (bf16[128,1024]{1,0:T(8,128)(2,1)S(1)}, bf16[128,1024]{1,0:T(8,128)(2,1)}, u32[]{:S(2)}) copy-start(bf16[128,1024]{1,0:T(8,128)(2,1)} %get-tuple-element.15.refs_2_) | copy-start | bytes 786436
  32.2 11.0 %copy-start.4 = (bf16[96,512]{1,0:T(8,128)(2,1)S(1)}, bf16[96,512]{1,0:T(8,128)(2,1)}, u32[]{:S(2)}) copy-start(bf16[96,512]{1,0:T(8,128)(2,1)} %get-tuple-element.20.refs_1_.refs_2_) | copy-start | bytes 294916
  32.2 11.0 %all-to-all-start.1 = ((bf16[32,16,128]{2,1,0:T(8,128)(2,1)}), bf16[32,16,128]{2,1,0:T(8,128)(2,1)S(1)}, u32[]{:S(2)}, u32[]{:S(2)}) async-start(bf16[32,16,128]{2,1,0:T(8,128)(2,1)} %bitcast.9), calls=%async_computation.1 | async-start | bytes 262144 | tf_op jit(solution)/shard_map/all_to_all | solution.py:397
  34.9 8.7 %collective-permute-start.5 = (bf16[512,512]{1,0:T(8,128)(2,1)S(1)}, bf16[512,512]{1,0:T(8,128)(2,1)S(1)}, u32[]{:S(2)}, u32[]{:S(2)}) collective-permute-start(bf16[512,512]{1,0:T(8,128)(2,1)S(1)} %collective-permute-done.4.refs_4_.refs_5_), channel_id=1, source_target_pairs={{0,1},{1,0},{2,3},{3,2},{4,5},{5,4},{6,7},{7,6},{8,9},{9,8},{10,11... | collective-permute-start | bytes 1572872 | tf_op jit(solution)/shard_map/ppermute | solution.py:310
  46.0 10.0 %copy-start.5 = (bf16[128,64]{1,0:T(8,128)(2,1)S(1)}, bf16[128,64]{1,0:T(8,128)(2,1)}, u32[]{:S(2)}) copy-start(bf16[128,64]{1,0:T(8,128)(2,1)} %get-tuple-element.25.refs_0_) | copy-start | bytes 49156

commit v15 on v14

--- a/solution.py
+++ b/solution.py
@@ -146,7 +146,11 @@
     known = jnp.concatenate([live, labels_ref[...].astype(F32), jnp.zeros((14, cands), F32)], axis=0)
     for_score_ref[ends : ends + 16, :cands] = known.astype(BF16)
     whole = jnp.concatenate([three_parts(out_w_ref[...]), jnp.zeros((13, hidden), F32)], axis=0)
-    for_score_ref[ends + 16 :, :hidden] = whole.astype(BF16)
+    for_score_ref[ends + 16 : ends + 32, :hidden] = whole.astype(BF16)
+    if ends <= cands:
+        place = lax.broadcasted_iota(jnp.int32, (3 * ends, cands), 0) % ends
+        stacked = [(place == cand_ref[i : i + 1, :]).astype(F32) for i in range(2)]
+        for_score_ref[ends + 32 :, : 6 * ends] = jnp.concatenate(stacked, axis=0).T.astype(BF16)
 
 
 def shard_row(i, depth):
@@ -238,11 +242,11 @@
         part_ref[row // span] += dot(rows_ref[:, cols], shard[...])
 
 
-def first_kernel(indices, cands, ready, got_ref, known_ref, *rest):
+def first_kernel(indices, cands, slot_total, ready, got_ref, known_ref, *rest):
     shards = rest[:-3]
     rows_ref, part_ref, stage_ref = rest[-3:]
     ready()
-    slots = known_ref.shape[0] - 32
+    slots = slot_total
     width = got_ref.shape[0] * 128 // slots
     rows = unpack_rows(got_ref, stage_ref, width // 128)
     if slots > cands:
@@ -265,21 +269,20 @@
     picks = [known_ref[:slots, i * cands : (i + 1) * cands] for i in range(2)]
     known = known_ref[slots : slots + 16, :cands].astype(F32).T
     live, label = known[:, :1], known[:, 1:2]
-    out_w = known_ref[slots + 16 :, :hidden].astype(F32)
+    out_w = known_ref[slots + 16 : slots + 32, :hidden].astype(F32)
     out_w = out_w[:1] + out_w[1:2] + out_w[2:3]
     part_ref[...] = first_ref[...]
     add_shards(rows_ref, late, [shards[i] for i in late], part_ref)
     if slots > cands:
         pre_act = part_ref[0]
     else:
-        pre_act = None
+        parts = []
         for i in range(2):
             rest = part_ref[i]
             for _ in range(3):
-                high = rest.astype(BF16)
-                rest = rest - high.astype(F32)
-                term = dot(picks[i], high, ((0,), (0,)))
-                pre_act = term if pre_act is None else pre_act + term
+                parts.append(rest.astype(BF16))
+                rest = rest - parts[-1].astype(F32)
+        pre_act = dot(known_ref[slots + 32 :, : 6 * slots], jnp.concatenate(parts, axis=0))
     gate = jax.nn.sigmoid(pre_act)
     score = jnp.sum(pre_act * gate * out_w, axis=1, keepdims=True) * live
     scores_ref[...] = jnp.broadcast_to(score, (cands, 128)).T[:1]
@@ -356,13 +359,16 @@
     )
     got_rows = lax.all_to_all(send_rows, "dom", split_axis=0, concat_axis=0, tiled=True)
     gat_across = across(gat_weight, edge_count)
-    mlp_across = across(mlp_weight, edge_count)
+    held_mlp = lax.optimization_barrier((mlp_weight, got_rows))[0]
+    mlp_across = across(held_mlp, edge_count)
     lanes = -(-(2 * table + attn_src.shape[1] + slots) // 128) * 128
     for_attend, for_score, pick = call(
         functools.partial(prepare_kernel, table),
         (
             shape((nodes, lanes), BF16),
-            shape((slots + 32, max(2 * cands, hidden)), BF16),
+            shape((slots + 32, max(2 * cands, hidden)), BF16)
+            if slots > cands
+            else shape((slots + 32 + cands, max(2 * cands, hidden, 6 * slots)), BF16),
             shape((nodes, slots), BF16),
         ),
         [
@@ -395,15 +401,16 @@
         ],
     )
     got_ends = lax.all_to_all(send_ends, everyone, split_axis=0, concat_axis=0, tiled=True)
-    mlp_shards = [mlp_across[0], swap(mlp_across[0], "edge", 1)]
-    tied = lax.optimization_barrier((*mlp_across[1:], send_ends))[:-1]
-    for shard, held in zip(mlp_across[1:], tied):
+    tied = lax.optimization_barrier((*mlp_across, send_ends))[:-1]
+    mlp_across[0] = mlp_weight
+    mlp_shards = []
+    for shard, held in zip(mlp_across, tied):
         mlp_shards += [shard, swap(held, "edge", 1)]
-    early = [i for i in range(edge_count) if i < 2 or i % 2 == 0]
-    late = [i for i in range(edge_count) if i not in early]
+    early = list(range(0, edge_count, 2))
+    late = list(range(1, edge_count, 2))
     many = slots > cands
     rows, part = call(
-        functools.partial(first_kernel, early, cands),
+        functools.partial(first_kernel, early, cands, slots),
         (
             shape((cands, 2 * width) if many else (slots, width), BF16),
             shape((1, cands, hidden) if many else (2, slots, hidden), F32),

time: 57.5 us -> 61.5 us (1.070)
  starting transfers between devices: 14.3 us -> 17.2 us
  local copies, waits for them, and re-layouts: 1.71 us -> 2.69 us
    ppermute x6, waiting for transfers between devices: 0.39 us -> 8.76 us  [swap(): return lax.ppermute(array, axis, [(i, i ^ k) for i in range(count)])]
    all_to_all x1, waiting for transfers between devices: 8.2 us -> 0.52 us  [local(): lax.all_to_all(send_rows, 'dom', split_axis=0, concat_axis=0, tiled=True)]
    all_to_all x1, starting transfers between devices: 2.74 us -> 5.7 us  [local(): lax.all_to_all(send_ends, everyone, split_axis=0, concat_axis=0, tiled=True)]
    ppermute x6, starting transfers between devices: 5.6 us -> 4.13 us  [swap(): return lax.ppermute(array, axis, [(i, i ^ k) for i in range(count)])]
    all_to_all x1, starting transfers between devices: 5.95 us -> 7.4 us  [local(): lax.all_to_all(send_rows, 'dom', split_axis=0, concat_axis=0, tiled=True)]
    unnamed x15, local copies, waits for them, and re-layouts: 1.08 us -> 2.07 us
  transfers between devices with their start and end apart: 8 -> 8, of which waited for: 3 -> 6; matrix products, arithmetic and copies ran while one was open for 1% -> 1% of each run, Pallas kernels for 17% -> 12%
where the time goes in v15:
time: 61.5 us; the launch traced here: 61 us
  starting transfers between devices  17.2 us (28%)
  waiting for transfers between devices  16.8 us (27%)
  Pallas kernels  12.9 us (21%)
  blocking collectives  10 us (16%)
  local copies, waits for them, and re-layouts  2.69 us (4%)
  between operations  1.41 us (2%)
    pallas_call x6, Pallas kernels, call(): pl.pallas_call(body, out_shape=outs, in_specs=[SPACES[space] for space, _...  12.9 us
    all_to_all x1, blocking collectives, local(): lax.all_to_all(send_back, everyone, split_axis=0, concat_axis=0, tiled=True)  10 us
    ppermute x6, waiting for transfers between devices, swap(): return lax.ppermute(array, axis, [(i, i ^ k) for i in range(count)])  8.76 us
    all_to_all x1, waiting for transfers between devices, local(): lax.all_to_all(send_ends, everyone, split_axis=0, concat_axis=0, tiled=True)  7.53 us
    all_to_all x1, starting transfers between devices, local(): lax.all_to_all(send_rows, 'dom', split_axis=0, concat_axis=0, tiled=True)  7.4 us
    all_to_all x1, starting transfers between devices, local(): lax.all_to_all(send_ends, everyone, split_axis=0, concat_axis=0, tiled=True)  5.7 us
    ppermute x6, starting transfers between devices, swap(): return lax.ppermute(array, axis, [(i, i ^ k) for i in range(count)])  4.13 us
    unnamed x15, local copies, waits for them, and re-layouts  2.07 us
  transfers between devices with their start and end apart: 8, of which 6 were waited for; matrix products, arithmetic and copies ran while one was open for 1% of the time, Pallas kernels for 12%

profile of v15, /device:TPU:0, one launch (start us, length us, event | category | flops | bytes accessed | tf_op | source)
XLA Modules:
  0.0 61.0 jit_solution(16064176608214664623)
XLA Ops:
  0.6 2.4 %shard_map.157 = bf16[256,1024]{1,0:T(8,128)(2,1)} custom-call(s32[1,8]{1,0:T(1,128)} %bitcast.25, s32[8,32]{1,0:T(8,128)} %bitcast.20, bf16[128,1024]{1,0:T(8,128)(2,1)} %refs_0_.2), custom_call_target="tpu_custom_call" | custom-call | tf_op jit(solution)/shard_map/pallas_call | solution.py:46
  3.0 0.0 copy-start.1
  3.0 0.0 copy-start.6
  3.0 0.0 copy-start
  3.0 7.4 %all-to-all-start = ((bf16[8,32,1024]{2,1,0:T(8,128)(2,1)}), bf16[8,32,1024]{2,1,0:T(8,128)(2,1)S(1)}, u32[]{:S(2)}, u32[]{:S(2)}) async-start(bf16[8,32,1024]{2,1,0:T(8,128)(2,1)} %bitcast.18), calls=%async_computation | async-start | bytes 1048576 | tf_op jit(solution)/shard_map/all_to_all | solution.py:360
  10.4 0.0 copy-done.1
  10.4 1.6 %collective-permute-start = (bf16[256,1024]{1,0:T(8,128)(2,1)S(1)}, bf16[256,1024]{1,0:T(8,128)(2,1)S(1)}, u32[]{:S(2)}, u32[]{:S(2)}) collective-permute-start(bf16[256,1024]{1,0:T(8,128)(2,1)S(1)} %copy-done.1), channel_id=1, source_target_pairs={{0,2},{1,3},{2,0},{3,1},{4,6},{5,7},{6,4},{7,5},{8,10},{9,11},{10,... | collective-permute-start | bytes 1572872 | tf_op jit(solution)/shard_map/ppermute | solution.py:313
  12.7 0.1 copy.18
  12.8 0.6 %reshape.25.refs_5_ = s32[1,64]{1,0:T(1,128)} reshape(s32[1,1,8,4,2]{4,3,2,1,0:T(4,128)S(1)} %copy.18) | data formatting | bytes 512 | tf_op jit(solution)/shard_map/reshape | solution.py:380
  13.4 2.1 %shard_map.158 = (bf16[128,1024]{1,0:T(8,128)(2,1)}, bf16[352,512]{1,0:T(8,128)(2,1)}, bf16[128,64]{1,0:T(8,128)(2,1)}) custom-call(s32[1,1]{1,0:T(1,128)S(6)} %copy.19.refs_0_, s32[16,128]{1,0:T(8,128)} %bitcast.19, s32[1,128]{1,0:T(1,128)} %bitcast.24, f32[8,128]{1,0:T(8,128)} %refs_3_.2, f32[8,128]{1,0:T(8,128)} %refs_4_.1, s32[1,64]{1,0:T(1,128)} %reshape.25.refs_5_, ...), custom_call_target="tpu_custom_call" | custom-call | tf_op jit(solution)/shard_map/pallas_call | solution.py:46
  15.6 8.3 %collective-permute-done.refs_5_ = bf16[256,1024]{1,0:T(8,128)(2,1)S(1)} collective-permute-done((bf16[256,1024]{1,0:T(8,128)(2,1)S(1)}, bf16[256,1024]{1,0:T(8,128)(2,1)S(1)}, u32[]{:S(2)}, u32[]{:S(2)}) %collective-permute-start) | collective-permute-done | bytes 524320 | tf_op jit(solution)/shard_map/ppermute | solution.py:313
  23.9 0.0 collective-permute-start.1
  23.9 0.5 collective-permute-start.2
  24.4 0.5 all-to-all-done
  24.9 1.5 %collective-permute-start.3 = (bf16[512,512]{1,0:T(8,128)(2,1)S(1)}, bf16[512,512]{1,0:T(8,128)(2,1)S(1)}, u32[]{:S(2)}, u32[]{:S(2)}) collective-permute-start(bf16[512,512]{1,0:T(8,128)(2,1)S(1)} %copy-done.2), channel_id=1, source_target_pairs={{0,2},{1,3},{2,0},{3,1},{4,6},{5,7},{6,4},{7,5},{8,10},{9,11},{10,... | collective-permute-start | bytes 1572872 | tf_op jit(solution)/shard_map/ppermute | solution.py:313
  26.4 0.1 collective-permute-done.1.refs_4_
  26.5 0.2 collective-permute-done.2.refs_6_
  26.7 0.9 %copy-done.4 = bf16[128,1024]{1,0:T(8,128)(2,1)S(1)} copy-done((bf16[128,1024]{1,0:T(8,128)(2,1)S(1)}, bf16[128,1024]{1,0:T(8,128)(2,1)}, u32[]{:S(2)}) %copy-start.4) | copy-done | bytes 262168
  27.6 4.8 %shard_map.159 = (bf16[128,1024]{1,0:T(8,128)(2,1)}, bf16[512,128]{1,0:T(8,128)(2,1)}) custom-call(bf16[128,1024]{1,0:T(8,128)(2,1)S(1)} %copy-done, bf16[256,1024]{1,0:T(8,128)(2,1)S(1)} %bitcast.14, bf16[128,1024]{1,0:T(8,128)(2,1)S(1)} %copy-done.4, bf16[256,1024]{1,0:T(8,128)(2,1)S(1)} %copy-done.1, ...), custom_call_target="tpu_custom_call" | custom-call | tf_op jit(solution)/shard_map/pallas_call | solution.py:46
  32.4 5.7 %all-to-all-start.1 = ((bf16[32,16,128]{2,1,0:T(8,128)(2,1)}), bf16[32,16,128]{2,1,0:T(8,128)(2,1)S(1)}, u32[]{:S(2)}, u32[]{:S(2)}) async-start(bf16[32,16,128]{2,1,0:T(8,128)(2,1)} %bitcast.9), calls=%async_computation.1 | async-start | bytes 262144 | tf_op jit(solution)/shard_map/all_to_all | solution.py:403
  38.1 0.2 collective-permute-done.3.refs_3_.refs_5_
  38.3 0.1 collective-permute-start.4
  38.4 0.4 collective-permute-start.5
  38.8 7.5 %all-to-all-done.1 = bf16[32,16,128]{2,1,0:T(8,128)(2,1)S(1)} async-done(((bf16[32,16,128]{2,1,0:T(8,128)(2,1)}), bf16[32,16,128]{2,1,0:T(8,128)(2,1)S(1)}, u32[]{:S(2)}, u32[]{:S(2)}) %all-to-all-start.1) | async-done | bytes 131104 | tf_op jit(solution)/shard_map/all_to_all | solution.py:403
  46.3 1.0 %copy-done.3 = bf16[352,512]{1,0:T(8,128)(2,1)S(1)} copy-done((bf16[352,512]{1,0:T(8,128)(2,1)S(1)}, bf16[352,512]{1,0:T(8,128)(2,1)}, u32[]{:S(2)}) %copy-start.3) | copy-done | bytes 360472
  47.3 0.3 shard_map.160
  47.7 0.0 collective-permute-done.4.refs_4_
  47.7 0.0 collective-permute-done.5.refs_6_
  47.7 2.2 %shard_map.161 = (f32[1,256]{1,0:T(1,128)}, bf16[512,128]{1,0:T(8,128)(2,1)S(1)}) custom-call(bf16[64,1024]{1,0:T(8,128)(2,1)S(1)} %get-tuple-element.24.refs_0_, f32[2,64,512]{2,1,0:T(8,128)S(1)} %get-tuple-element.25.refs_1_, bf16[352,512]{1,0:T(8,128)(2,1)S(1)} %copy-done.3, bf16[512,512]{1,0:T(8,128)(2,1)S(1)} %copy-done.2, ...), custom_call_target="tpu_custom_call" | custom-call | tf_op jit(solution)/shard_map/pallas_call | solution.py:46
  49.9 0.0 copy-start.5
  49.9 10.0 %all_to_all.33 = bf16[32,16,128]{2,1,0:T(8,128)(2,1)S(1)} all-to-all(bf16[32,16,128]{2,1,0:T(8,128)(2,1)S(1)} %bitcast.17), channel_id=1, replica_groups=mesh['dom'=8,'edge'=4] {'dom','edge'}, dimensions={0} | all-to-all | bytes 262144 | tf_op jit(solution)/shard_map/all_to_all | solution.py:433
  60.0 1.0 %shard_map.162 = f32[128,1024]{1,0:T(8,128)} custom-call(bf16[128,64]{1,0:T(8,128)(2,1)S(1)} %copy-done.5, bf16[512,128]{1,0:T(8,128)(2,1)S(1)} %bitcast.15), custom_call_target="tpu_custom_call" | custom-call | tf_op jit(solution)/shard_map/pallas_call | solution.py:46
  (7 shorter events, 0.0 us)
Async XLA Ops:
  0.6 24.3 %copy-start.2 = (bf16[512,512]{1,0:T(8,128)(2,1)S(1)}, bf16[512,512]{1,0:T(8,128)(2,1)}, u32[]{:S(2)}) copy-start(bf16[512,512]{1,0:T(8,128)(2,1)} %refs_3_.4) | copy-start | bytes 1572868
  3.0 7.4 %copy-start.1 = (bf16[256,1024]{1,0:T(8,128)(2,1)S(1)}, bf16[256,1024]{1,0:T(8,128)(2,1)}, u32[]{:S(2)}) copy-start(bf16[256,1024]{1,0:T(8,128)(2,1)} %refs_3_.3) | copy-start | bytes 1572868
  3.0 9.7 %copy-start.6 = (s32[1,1,8,4,2]{2,4,3,1,0:T(2,128)S(1)}, s32[1,1,8,4,2]{2,4,3,1,0:T(2,128)}, u32[]{:S(2)}) copy-start(s32[1,1,8,4,2]{2,4,3,1,0:T(2,128)} %param.22) | copy-start | bytes 772
  3.0 23.7 %copy-start = (bf16[128,1024]{1,0:T(8,128)(2,1)S(1)}, bf16[128,1024]{1,0:T(8,128)(2,1)}, u32[]{:S(2)}) copy-start(bf16[128,1024]{1,0:T(8,128)(2,1)} %refs_0_.2) | copy-start | bytes 786436
  3.0 21.9 %all-to-all-start = ((bf16[8,32,1024]{2,1,0:T(8,128)(2,1)}), bf16[8,32,1024]{2,1,0:T(8,128)(2,1)S(1)}, u32[]{:S(2)}, u32[]{:S(2)}) async-start(bf16[8,32,1024]{2,1,0:T(8,128)(2,1)} %bitcast.18), calls=%async_computation | async-start | bytes 1048576 | tf_op jit(solution)/shard_map/all_to_all | solution.py:360
  10.4 13.4 %collective-permute-start = (bf16[256,1024]{1,0:T(8,128)(2,1)S(1)}, bf16[256,1024]{1,0:T(8,128)(2,1)S(1)}, u32[]{:S(2)}, u32[]{:S(2)}) collective-permute-start(bf16[256,1024]{1,0:T(8,128)(2,1)S(1)} %copy-done.1), channel_id=1, source_target_pairs={{0,2},{1,3},{2,0},{3,1},{4,6},{5,7},{6,4},{7,5},{8,10},{9,11},{10,... | collective-permute-start | bytes 1572872 | tf_op jit(solution)/shard_map/ppermute | solution.py:313
  23.9 2.6 %collective-permute-start.1 = (bf16[256,1024]{1,0:T(8,128)(2,1)S(1)}, bf16[256,1024]{1,0:T(8,128)(2,1)S(1)}, u32[]{:S(2)}, u32[]{:S(2)}) collective-permute-start(bf16[256,1024]{1,0:T(8,128)(2,1)S(1)} %copy-done.1), channel_id=1, source_target_pairs={{0,1},{1,0},{2,3},{3,2},{4,5},{5,4},{6,7},{7,6},{8,9},{9,8},{10,11... | collective-permute-start | bytes 1572872 | tf_op jit(solution)/shard_map/ppermute | solution.py:313
  23.9 2.8 %collective-permute-start.2 = (bf16[256,1024]{1,0:T(8,128)(2,1)S(1)}, bf16[256,1024]{1,0:T(8,128)(2,1)}, u32[]{:S(2)}, u32[]{:S(2)}) collective-permute-start(bf16[256,1024]{1,0:T(8,128)(2,1)S(1)} %collective-permute-done.refs_5_), channel_id=1, source_target_pairs={{0,1},{1,0},{2,3},{3,2},{4,5},{5,4},{6,7},{7,6},{8,9},{9,8},{10,11... | collective-permute-start | bytes 1572872 | tf_op jit(solution)/shard_map/ppermute | solution.py:313
  24.9 13.4 %collective-permute-start.3 = (bf16[512,512]{1,0:T(8,128)(2,1)S(1)}, bf16[512,512]{1,0:T(8,128)(2,1)S(1)}, u32[]{:S(2)}, u32[]{:S(2)}) collective-permute-start(bf16[512,512]{1,0:T(8,128)(2,1)S(1)} %copy-done.2), channel_id=1, source_target_pairs={{0,2},{1,3},{2,0},{3,1},{4,6},{5,7},{6,4},{7,5},{8,10},{9,11},{10,... | collective-permute-start | bytes 1572872 | tf_op jit(solution)/shard_map/ppermute | solution.py:313
  26.7 1.0 %copy-start.4 = (bf16[128,1024]{1,0:T(8,128)(2,1)S(1)}, bf16[128,1024]{1,0:T(8,128)(2,1)}, u32[]{:S(2)}) copy-start(bf16[128,1024]{1,0:T(8,128)(2,1)} %get-tuple-element.17.refs_2_) | copy-start | bytes 786436
  32.4 13.9 %all-to-all-start.1 = ((bf16[32,16,128]{2,1,0:T(8,128)(2,1)}), bf16[32,16,128]{2,1,0:T(8,128)(2,1)S(1)}, u32[]{:S(2)}, u32[]{:S(2)}) async-start(bf16[32,16,128]{2,1,0:T(8,128)(2,1)} %bitcast.9), calls=%async_computation.1 | async-start | bytes 262144 | tf_op jit(solution)/shard_map/all_to_all | solution.py:403
  38.3 9.4 %collective-permute-start.4 = (bf16[512,512]{1,0:T(8,128)(2,1)S(1)}, bf16[512,512]{1,0:T(8,128)(2,1)S(1)}, u32[]{:S(2)}, u32[]{:S(2)}) collective-permute-start(bf16[512,512]{1,0:T(8,128)(2,1)S(1)} %copy-done.2), channel_id=1, source_target_pairs={{0,1},{1,0},{2,3},{3,2},{4,5},{5,4},{6,7},{7,6},{8,9},{9,8},{10,11... | collective-permute-start | bytes 1572872 | tf_op jit(solution)/shard_map/ppermute | solution.py:313
  38.4 9.3 %collective-permute-start.5 = (bf16[512,512]{1,0:T(8,128)(2,1)S(1)}, bf16[512,512]{1,0:T(8,128)(2,1)S(1)}, u32[]{:S(2)}, u32[]{:S(2)}) collective-permute-start(bf16[512,512]{1,0:T(8,128)(2,1)S(1)} %collective-permute-done.3.refs_3_.refs_5_), channel_id=1, source_target_pairs={{0,1},{1,0},{2,3},{3,2},{4,5},{5,4},{6,7},{7,6},{8,9},{9,8},{10,11... | collective-permute-start | bytes 1572872 | tf_op jit(solution)/shard_map/ppermute | solution.py:313
  46.3 1.0 %copy-start.3 = (bf16[352,512]{1,0:T(8,128)(2,1)S(1)}, bf16[352,512]{1,0:T(8,128)(2,1)}, u32[]{:S(2)}) copy-start(bf16[352,512]{1,0:T(8,128)(2,1)} %get-tuple-element.22.refs_1_.refs_2_) | copy-start | bytes 1081348
  49.9 10.0 %copy-start.5 = (bf16[128,64]{1,0:T(8,128)(2,1)S(1)}, bf16[128,64]{1,0:T(8,128)(2,1)}, u32[]{:S(2)}) copy-start(bf16[128,64]{1,0:T(8,128)(2,1)} %get-tuple-element.29.refs_0_) | copy-start | bytes 49156

commit v16 on v14

--- a/solution.py
+++ b/solution.py
@@ -395,12 +395,12 @@
         ],
     )
     got_ends = lax.all_to_all(send_ends, everyone, split_axis=0, concat_axis=0, tiled=True)
-    mlp_shards = [mlp_across[0], swap(mlp_across[0], "edge", 1)]
-    tied = lax.optimization_barrier((*mlp_across[1:], send_ends))[:-1]
-    for shard, held in zip(mlp_across[1:], tied):
+    tied = lax.optimization_barrier((*mlp_across, send_ends))[:-1]
+    mlp_shards = []
+    for shard, held in zip(mlp_across, tied):
         mlp_shards += [shard, swap(held, "edge", 1)]
-    early = [i for i in range(edge_count) if i < 2 or i % 2 == 0]
-    late = [i for i in range(edge_count) if i not in early]
+    early = list(range(0, edge_count, 2))
+    late = list(range(1, edge_count, 2))
     many = slots > cands
     rows, part = call(
         functools.partial(first_kernel, early, cands),

time: 57.5 us -> 57.4 us (level)
  no operation moved by 1% of the time
where the time goes in v16:
time: 57.4 us; the launch traced here: 56.9 us
  waiting for transfers between devices  16.2 us (28%)
  starting transfers between devices  14.5 us (25%)
  Pallas kernels  13 us (23%)
  blocking collectives  10 us (17%)
  local copies, waits for them, and re-layouts  1.71 us (3%)
  between operations  1.42 us (2%)
    pallas_call x6, Pallas kernels, call(): pl.pallas_call(body, out_shape=outs, in_specs=[SPACES[space] for space, _...  13 us
    all_to_all x1, blocking collectives, local(): lax.all_to_all(send_back, everyone, split_axis=0, concat_axis=0, tiled=True)  10 us
    all_to_all x1, waiting for transfers between devices, local(): lax.all_to_all(send_rows, 'dom', split_axis=0, concat_axis=0, tiled=True)  8.2 us
    all_to_all x1, waiting for transfers between devices, local(): lax.all_to_all(send_ends, everyone, split_axis=0, concat_axis=0, tiled=True)  7.64 us
    all_to_all x1, starting transfers between devices, local(): lax.all_to_all(send_rows, 'dom', split_axis=0, concat_axis=0, tiled=True)  5.95 us
    ppermute x6, starting transfers between devices, swap(): return lax.ppermute(array, axis, [(i, i ^ k) for i in range(count)])  5.86 us
    all_to_all x1, starting transfers between devices, local(): lax.all_to_all(send_ends, everyone, split_axis=0, concat_axis=0, tiled=True)  2.73 us
  transfers between devices with their start and end apart: 8, of which 3 were waited for; matrix products, arithmetic and copies ran while one was open for 1% of the time, Pallas kernels for 17%

profile of v16, /device:TPU:0, one launch (start us, length us, event | category | flops | bytes accessed | tf_op | source)
XLA Modules:
  0.0 56.9 jit_solution(6843482185456143818)
XLA Ops:
  0.6 3.0 %collective-permute-start = (bf16[256,1024]{1,0:T(8,128)(2,1)}, bf16[256,1024]{1,0:T(8,128)(2,1)S(1)}, u32[]{:S(2)}, u32[]{:S(2)}) collective-permute-start(bf16[256,1024]{1,0:T(8,128)(2,1)} %refs_3_.3), channel_id=1, source_target_pairs={{0,2},{1,3},{2,0},{3,1},{4,6},{5,7},{6,4},{7,5},{8,10},{9,11},{10,... | collective-permute-start | bytes 1572872 | tf_op jit(solution)/shard_map/ppermute | solution.py:310
  3.7 2.4 %shard_map.157 = bf16[256,1024]{1,0:T(8,128)(2,1)} custom-call(s32[1,8]{1,0:T(1,128)} %bitcast.25, s32[8,32]{1,0:T(8,128)} %bitcast.20, bf16[128,1024]{1,0:T(8,128)(2,1)} %refs_0_.2), custom_call_target="tpu_custom_call" | custom-call | tf_op jit(solution)/shard_map/pallas_call | solution.py:46
  6.0 0.0 copy-start.6
  6.0 0.0 copy-start.1
  6.0 0.0 copy-start
  6.1 5.9 %all-to-all-start = ((bf16[8,32,1024]{2,1,0:T(8,128)(2,1)}), bf16[8,32,1024]{2,1,0:T(8,128)(2,1)S(1)}, u32[]{:S(2)}, u32[]{:S(2)}) async-start(bf16[8,32,1024]{2,1,0:T(8,128)(2,1)} %bitcast.18), calls=%async_computation | async-start | bytes 1048576 | tf_op jit(solution)/shard_map/all_to_all | solution.py:357
  12.7 0.1 copy.18
  12.8 0.6 %reshape.25.refs_5_ = s32[1,64]{1,0:T(1,128)} reshape(s32[1,1,8,4,2]{4,3,2,1,0:T(4,128)S(1)} %copy.18) | data formatting | bytes 512 | tf_op jit(solution)/shard_map/reshape | solution.py:374
  13.4 2.0 %shard_map.158 = (bf16[128,1024]{1,0:T(8,128)(2,1)}, bf16[96,512]{1,0:T(8,128)(2,1)}, bf16[128,64]{1,0:T(8,128)(2,1)}) custom-call(s32[1,1]{1,0:T(1,128)S(6)} %copy.19.refs_0_, s32[16,128]{1,0:T(8,128)} %bitcast.19, s32[1,128]{1,0:T(1,128)} %bitcast.24, f32[8,128]{1,0:T(8,128)} %refs_3_.2, f32[8,128]{1,0:T(8,128)} %refs_4_.1, s32[1,64]{1,0:T(1,128)} %reshape.25.refs_5_, ...), custom_call_target="tpu_custom_call" | custom-call | tf_op jit(solution)/shard_map/pallas_call | solution.py:46
  15.4 0.4 collective-permute-done.refs_5_
  15.8 0.0 collective-permute-start.1
  15.8 0.5 collective-permute-start.2
  16.3 0.0 copy-done.1
  16.3 1.7 %collective-permute-start.3 = (bf16[512,512]{1,0:T(8,128)(2,1)S(1)}, bf16[512,512]{1,0:T(8,128)(2,1)S(1)}, u32[]{:S(2)}, u32[]{:S(2)}) collective-permute-start(bf16[512,512]{1,0:T(8,128)(2,1)S(1)} %copy-done.1), channel_id=1, source_target_pairs={{0,2},{1,3},{2,0},{3,1},{4,6},{5,7},{6,4},{7,5},{8,10},{9,11},{10,... | collective-permute-start | bytes 1572872 | tf_op jit(solution)/shard_map/ppermute | solution.py:310
  18.1 8.2 %all-to-all-done = bf16[8,32,1024]{2,1,0:T(8,128)(2,1)S(1)} async-done(((bf16[8,32,1024]{2,1,0:T(8,128)(2,1)}), bf16[8,32,1024]{2,1,0:T(8,128)(2,1)S(1)}, u32[]{:S(2)}, u32[]{:S(2)}) %all-to-all-start) | async-done | bytes 524320 | tf_op jit(solution)/shard_map/all_to_all | solution.py:357
  26.3 0.0 collective-permute-done.1.refs_4_
  26.3 0.0 collective-permute-done.2.refs_6_
  26.3 0.0 copy-start.3
  26.3 0.9 %copy-done.3 = bf16[128,1024]{1,0:T(8,128)(2,1)S(1)} copy-done((bf16[128,1024]{1,0:T(8,128)(2,1)S(1)}, bf16[128,1024]{1,0:T(8,128)(2,1)}, u32[]{:S(2)}) %copy-start.3) | copy-done | bytes 262168
  27.2 4.8 %shard_map.159 = (bf16[128,1024]{1,0:T(8,128)(2,1)}, bf16[512,128]{1,0:T(8,128)(2,1)}) custom-call(bf16[128,1024]{1,0:T(8,128)(2,1)S(1)} %copy-done, bf16[256,1024]{1,0:T(8,128)(2,1)S(1)} %bitcast.14, bf16[128,1024]{1,0:T(8,128)(2,1)S(1)} %copy-done.3, bf16[256,1024]{1,0:T(8,128)(2,1)S(1)} %copy-done.2, ...), custom_call_target="tpu_custom_call" | custom-call | tf_op jit(solution)/shard_map/pallas_call | solution.py:46
  32.0 2.7 %all-to-all-start.1 = ((bf16[32,16,128]{2,1,0:T(8,128)(2,1)}), bf16[32,16,128]{2,1,0:T(8,128)(2,1)S(1)}, u32[]{:S(2)}, u32[]{:S(2)}) async-start(bf16[32,16,128]{2,1,0:T(8,128)(2,1)} %bitcast.9), calls=%async_computation.1 | async-start | bytes 262144 | tf_op jit(solution)/shard_map/all_to_all | solution.py:397
  34.8 0.0 collective-permute-done.3.refs_3_.refs_5_
  34.8 0.3 collective-permute-start.4
  35.1 0.3 collective-permute-start.5
  35.3 7.6 %all-to-all-done.1 = bf16[32,16,128]{2,1,0:T(8,128)(2,1)S(1)} async-done(((bf16[32,16,128]{2,1,0:T(8,128)(2,1)}), bf16[32,16,128]{2,1,0:T(8,128)(2,1)S(1)}, u32[]{:S(2)}, u32[]{:S(2)}) %all-to-all-start.1) | async-done | bytes 131104 | tf_op jit(solution)/shard_map/all_to_all | solution.py:397
  43.0 0.4 shard_map.160
  43.3 0.0 collective-permute-done.4.refs_4_
  43.4 0.0 collective-permute-done.5.refs_6_
  43.4 2.5 %shard_map.161 = (f32[1,256]{1,0:T(1,128)}, bf16[512,128]{1,0:T(8,128)(2,1)S(1)}) custom-call(bf16[64,1024]{1,0:T(8,128)(2,1)S(1)} %get-tuple-element.22.refs_0_, f32[2,64,512]{2,1,0:T(8,128)S(1)} %get-tuple-element.23.refs_1_, bf16[96,512]{1,0:T(8,128)(2,1)S(1)} %copy-done.4, bf16[512,512]{1,0:T(8,128)(2,1)S(1)} %copy-done.1, ...), custom_call_target="tpu_custom_call" | custom-call | tf_op jit(solution)/shard_map/pallas_call | solution.py:46
  45.9 10.0 %all_to_all.33 = bf16[32,16,128]{2,1,0:T(8,128)(2,1)S(1)} all-to-all(bf16[32,16,128]{2,1,0:T(8,128)(2,1)S(1)} %bitcast.17), channel_id=1, replica_groups=mesh['dom'=8,'edge'=4] {'dom','edge'}, dimensions={0} | all-to-all | bytes 262144 | tf_op jit(solution)/shard_map/all_to_all | solution.py:426
  55.9 0.0 copy-done.5
  55.9 1.0 %shard_map.162 = f32[128,1024]{1,0:T(8,128)} custom-call(bf16[128,64]{1,0:T(8,128)(2,1)S(1)} %copy-done.5, bf16[512,128]{1,0:T(8,128)(2,1)S(1)} %bitcast.15), custom_call_target="tpu_custom_call" | custom-call | tf_op jit(solution)/shard_map/pallas_call | solution.py:46
  (7 shorter events, 0.0 us)
Async XLA Ops:
  0.6 15.2 %collective-permute-start = (bf16[256,1024]{1,0:T(8,128)(2,1)}, bf16[256,1024]{1,0:T(8,128)(2,1)S(1)}, u32[]{:S(2)}, u32[]{:S(2)}) collective-permute-start(bf16[256,1024]{1,0:T(8,128)(2,1)} %refs_3_.3), channel_id=1, source_target_pairs={{0,2},{1,3},{2,0},{3,1},{4,6},{5,7},{6,4},{7,5},{8,10},{9,11},{10,... | collective-permute-start | bytes 1572872 | tf_op jit(solution)/shard_map/ppermute | solution.py:310
  3.7 12.1 %copy-start.2 = (bf16[256,1024]{1,0:T(8,128)(2,1)S(1)}, bf16[256,1024]{1,0:T(8,128)(2,1)}, u32[]{:S(2)}) copy-start(bf16[256,1024]{1,0:T(8,128)(2,1)} %refs_3_.3) | copy-start | bytes 1572868
  6.0 6.6 %copy-start.6 = (s32[1,1,8,4,2]{2,4,3,1,0:T(2,128)S(1)}, s32[1,1,8,4,2]{2,4,3,1,0:T(2,128)}, u32[]{:S(2)}) copy-start(s32[1,1,8,4,2]{2,4,3,1,0:T(2,128)} %param.22) | copy-start | bytes 772
  6.0 10.3 %copy-start.1 = (bf16[512,512]{1,0:T(8,128)(2,1)S(1)}, bf16[512,512]{1,0:T(8,128)(2,1)}, u32[]{:S(2)}) copy-start(bf16[512,512]{1,0:T(8,128)(2,1)} %refs_3_.4) | copy-start | bytes 1572868
  6.0 20.2 %copy-start = (bf16[128,1024]{1,0:T(8,128)(2,1)S(1)}, bf16[128,1024]{1,0:T(8,128)(2,1)}, u32[]{:S(2)}) copy-start(bf16[128,1024]{1,0:T(8,128)(2,1)} %refs_0_.2) | copy-start | bytes 786436
  6.1 20.2 %all-to-all-start = ((bf16[8,32,1024]{2,1,0:T(8,128)(2,1)}), bf16[8,32,1024]{2,1,0:T(8,128)(2,1)S(1)}, u32[]{:S(2)}, u32[]{:S(2)}) async-start(bf16[8,32,1024]{2,1,0:T(8,128)(2,1)} %bitcast.18), calls=%async_computation | async-start | bytes 1048576 | tf_op jit(solution)/shard_map/all_to_all | solution.py:357
  15.8 10.5 %collective-permute-start.1 = (bf16[256,1024]{1,0:T(8,128)(2,1)S(1)}, bf16[256,1024]{1,0:T(8,128)(2,1)S(1)}, u32[]{:S(2)}, u32[]{:S(2)}) collective-permute-start(bf16[256,1024]{1,0:T(8,128)(2,1)S(1)} %copy-done.2), channel_id=1, source_target_pairs={{0,1},{1,0},{2,3},{3,2},{4,5},{5,4},{6,7},{7,6},{8,9},{9,8},{10,11... | collective-permute-start | bytes 1572872 | tf_op jit(solution)/shard_map/ppermute | solution.py:310
  15.8 10.5 %collective-permute-start.2 = (bf16[256,1024]{1,0:T(8,128)(2,1)S(1)}, bf16[256,1024]{1,0:T(8,128)(2,1)}, u32[]{:S(2)}, u32[]{:S(2)}) collective-permute-start(bf16[256,1024]{1,0:T(8,128)(2,1)S(1)} %collective-permute-done.refs_5_), channel_id=1, source_target_pairs={{0,1},{1,0},{2,3},{3,2},{4,5},{5,4},{6,7},{7,6},{8,9},{9,8},{10,11... | collective-permute-start | bytes 1572872 | tf_op jit(solution)/shard_map/ppermute | solution.py:310
  16.3 18.4 %collective-permute-start.3 = (bf16[512,512]{1,0:T(8,128)(2,1)S(1)}, bf16[512,512]{1,0:T(8,128)(2,1)S(1)}, u32[]{:S(2)}, u32[]{:S(2)}) collective-permute-start(bf16[512,512]{1,0:T(8,128)(2,1)S(1)} %copy-done.1), channel_id=1, source_target_pairs={{0,2},{1,3},{2,0},{3,1},{4,6},{5,7},{6,4},{7,5},{8,10},{9,11},{10,... | collective-permute-start | bytes 1572872 | tf_op jit(solution)/shard_map/ppermute | solution.py:310
  26.3 1.0 %copy-start.3 = (bf16[128,1024]{1,0:T(8,128)(2,1)S(1)}, bf16[128,1024]{1,0:T(8,128)(2,1)}, u32[]{:S(2)}) copy-start(bf16[128,1024]{1,0:T(8,128)(2,1)} %get-tuple-element.16.refs_2_) | copy-start | bytes 786436
  32.0 11.0 %copy-start.4 = (bf16[96,512]{1,0:T(8,128)(2,1)S(1)}, bf16[96,512]{1,0:T(8,128)(2,1)}, u32[]{:S(2)}) copy-start(bf16[96,512]{1,0:T(8,128)(2,1)} %get-tuple-element.21.refs_1_.refs_2_) | copy-start | bytes 294916
  32.0 11.0 %all-to-all-start.1 = ((bf16[32,16,128]{2,1,0:T(8,128)(2,1)}), bf16[32,16,128]{2,1,0:T(8,128)(2,1)S(1)}, u32[]{:S(2)}, u32[]{:S(2)}) async-start(bf16[32,16,128]{2,1,0:T(8,128)(2,1)} %bitcast.9), calls=%async_computation.1 | async-start | bytes 262144 | tf_op jit(solution)/shard_map/all_to_all | solution.py:397
  34.8 8.6 %collective-permute-start.4 = (bf16[512,512]{1,0:T(8,128)(2,1)S(1)}, bf16[512,512]{1,0:T(8,128)(2,1)S(1)}, u32[]{:S(2)}, u32[]{:S(2)}) collective-permute-start(bf16[512,512]{1,0:T(8,128)(2,1)S(1)} %copy-done.1), channel_id=1, source_target_pairs={{0,1},{1,0},{2,3},{3,2},{4,5},{5,4},{6,7},{7,6},{8,9},{9,8},{10,11... | collective-permute-start | bytes 1572872 | tf_op jit(solution)/shard_map/ppermute | solution.py:310
  35.1 8.3 %collective-permute-start.5 = (bf16[512,512]{1,0:T(8,128)(2,1)S(1)}, bf16[512,512]{1,0:T(8,128)(2,1)S(1)}, u32[]{:S(2)}, u32[]{:S(2)}) collective-permute-start(bf16[512,512]{1,0:T(8,128)(2,1)S(1)} %collective-permute-done.3.refs_3_.refs_5_), channel_id=1, source_target_pairs={{0,1},{1,0},{2,3},{3,2},{4,5},{5,4},{6,7},{7,6},{8,9},{9,8},{10,11... | collective-permute-start | bytes 1572872 | tf_op jit(solution)/shard_map/ppermute | solution.py:310
  45.9 10.0 %copy-start.5 = (bf16[128,64]{1,0:T(8,128)(2,1)S(1)}, bf16[128,64]{1,0:T(8,128)(2,1)}, u32[]{:S(2)}) copy-start(bf16[128,64]{1,0:T(8,128)(2,1)} %get-tuple-element.27.refs_0_) | copy-start | bytes 49156

commit v17 on v16

--- a/solution.py
+++ b/solution.py
@@ -153,23 +153,38 @@
     return pl.multiple_of((lax.axis_index("edge") ^ i) * depth, depth)
 
 
-def shard_dots(rows_ref, shards, whole_ref=None):
+def shard_dots(rows_ref, shards, whole_ref=None, arriving=None):
     depth = shards[0].shape[0]
+    arriving = arriving or {}
     if depth % 128:
+        for copy in arriving.values():
+            copy.wait()
         for i, shard in enumerate(shards):
             whole_ref[pl.ds(shard_row(i, depth), depth), :] = shard[...]
         return dot(rows_ref[...], whole_ref[...])
     total = None
     for i, shard in enumerate(shards):
         cols = pl.ds(shard_row(i, depth), depth)
+        if i in arriving:
+            arriving[i].wait()
         part = dot(rows_ref[:, cols], shard[...])
         total = part if total is None else total + part
     return total
 
 
+def second_hop(edge_count):
+    return [i for i in range(edge_count) if i > 1 and i % 2]
+
+
 def attend_kernel(shard_count, heads, slots, ready, own_ref, got_ref, known_ref, *rest):
-    shards = rest[:shard_count]
-    out_ref, send_ref, proj_ref, stage_ref, rows_ref, bias_ref, mix_ref, whole_ref = rest[-8:]
+    shards = list(rest[:shard_count])
+    out_ref, send_ref, proj_ref, stage_ref, rows_ref, bias_ref, mix_ref, whole_ref = rest[shard_count:-2]
+    late_ref, late_sems = rest[-2:]
+    arriving = {}
+    for j, i in enumerate(second_hop(shard_count)):
+        arriving[i] = pltpu.make_async_copy(shards[i], late_ref.at[j], late_sems.at[j])
+        arriving[i].start()
+        shards[i] = late_ref.at[j]
     ready()
     nodes, width = own_ref.shape
     table = proj_ref.shape[0]
@@ -182,7 +197,7 @@
     diag_dst = block_diagonal(vectors[3 * heads :], heads)
     rows_ref[:nodes, :] = own_ref[...]
     rows_ref[nodes:, :] = got_ref[...]
-    proj_ref[...] = shard_dots(rows_ref, shards, whole_ref).astype(BF16)
+    proj_ref[...] = shard_dots(rows_ref, shards, whole_ref, arriving).astype(BF16)
     parts = dot(diag_src, proj_ref[...], ((1,), (1,)))
     src = parts[:heads] + parts[heads : 2 * heads] + parts[2 * heads : 3 * heads]
     src = src.astype(BF16).astype(F32) * LOG2_E
@@ -381,10 +396,12 @@
     gat_across = lax.optimization_barrier((*gat_across, for_attend))[:-1]
     gat_shards = from_core(gat_across)
     packed = pltpu.VMEM((slots * pieces, 128), F32)
+    late_count = max(1, len(second_hop(edge_count)))
     node_out, send_ends = call(
         functools.partial(attend_kernel, edge_count, heads, slots),
         (shape((nodes, width), BF16), shape((slots * pieces, 128), BF16)),
-        [("v", node_feats), ("v", got_rows), ("v", for_attend)] + [("v", w) for w in gat_shards],
+        [("v", node_feats), ("v", got_rows), ("v", for_attend)]
+        + [("any" if i in second_hop(edge_count) else "v", w) for i, w in enumerate(gat_shards)],
         [
             pltpu.VMEM((table, width), BF16),
             packed,
@@ -392,6 +409,8 @@
             pltpu.VMEM((nodes, table), F32),
             pltpu.VMEM((2, 2 * nodes, table), BF16),
             pltpu.VMEM((width if width // edge_count % 128 else 16, width), BF16),
+            pltpu.VMEM((late_count, *gat_weight.shape), BF16),
+            pltpu.SemaphoreType.DMA((late_count,)),
         ],
     )
     got_ends = lax.all_to_all(send_ends, everyone, split_axis=0, concat_axis=0, tiled=True)

time: 57.4 us -> 57.3 us (level)
  transfers between devices with their start and end apart: 8 -> 8, of which waited for: 3 -> 3; matrix products, arithmetic and copies ran while one was open for 1% -> 1% of each run, Pallas kernels for 17% -> 16%
where the time goes in v17:
time: 57.3 us; the launch traced here: 56.8 us
  waiting for transfers between devices  16.2 us (28%)
  starting transfers between devices  14.5 us (25%)
  Pallas kernels  12.9 us (23%)
  blocking collectives  10 us (17%)
  local copies, waits for them, and re-layouts  1.71 us (3%)
  between operations  1.42 us (2%)
    pallas_call x6, Pallas kernels, call(): pl.pallas_call(body, out_shape=outs, in_specs=[SPACES[space] for space, _...  12.9 us
    all_to_all x1, blocking collectives, local(): lax.all_to_all(send_back, everyone, split_axis=0, concat_axis=0, tiled=True)  10 us
    all_to_all x1, waiting for transfers between devices, local(): lax.all_to_all(send_rows, 'dom', split_axis=0, concat_axis=0, tiled=True)  8.2 us
    all_to_all x1, waiting for transfers between devices, local(): lax.all_to_all(send_ends, everyone, split_axis=0, concat_axis=0, tiled=True)  7.64 us
    all_to_all x1, starting transfers between devices, local(): lax.all_to_all(send_rows, 'dom', split_axis=0, concat_axis=0, tiled=True)  5.95 us
    ppermute x6, starting transfers between devices, swap(): return lax.ppermute(array, axis, [(i, i ^ k) for i in range(count)])  5.86 us
    all_to_all x1, starting transfers between devices, local(): lax.all_to_all(send_ends, everyone, split_axis=0, concat_axis=0, tiled=True)  2.73 us
  transfers between devices with their start and end apart: 8, of which 3 were waited for; matrix products, arithmetic and copies ran while one was open for 1% of the time, Pallas kernels for 16%

profile of v17, /device:TPU:0, one launch (start us, length us, event | category | flops | bytes accessed | tf_op | source)
XLA Modules:
  0.0 56.8 jit_solution(13012874096609385305)
XLA Ops:
  0.6 3.0 %collective-permute-start = (bf16[256,1024]{1,0:T(8,128)(2,1)}, bf16[256,1024]{1,0:T(8,128)(2,1)S(1)}, u32[]{:S(2)}, u32[]{:S(2)}) collective-permute-start(bf16[256,1024]{1,0:T(8,128)(2,1)} %refs_3_.3), channel_id=1, source_target_pairs={{0,2},{1,3},{2,0},{3,1},{4,6},{5,7},{6,4},{7,5},{8,10},{9,11},{10,... | collective-permute-start | bytes 1572872 | tf_op jit(solution)/shard_map/ppermute | solution.py:325
  3.7 2.4 %shard_map.157 = bf16[256,1024]{1,0:T(8,128)(2,1)} custom-call(s32[1,8]{1,0:T(1,128)} %bitcast.25, s32[8,32]{1,0:T(8,128)} %bitcast.20, bf16[128,1024]{1,0:T(8,128)(2,1)} %refs_0_.2), custom_call_target="tpu_custom_call" | custom-call | tf_op jit(solution)/shard_map/pallas_call | solution.py:46
  6.0 0.0 copy-start.6
  6.0 0.0 copy-start.1
  6.0 0.0 copy-start
  6.1 5.9 %all-to-all-start = ((bf16[8,32,1024]{2,1,0:T(8,128)(2,1)}), bf16[8,32,1024]{2,1,0:T(8,128)(2,1)S(1)}, u32[]{:S(2)}, u32[]{:S(2)}) async-start(bf16[8,32,1024]{2,1,0:T(8,128)(2,1)} %bitcast.18), calls=%async_computation | async-start | bytes 1048576 | tf_op jit(solution)/shard_map/all_to_all | solution.py:372
  12.7 0.1 copy.18
  12.8 0.6 %reshape.25.refs_5_ = s32[1,64]{1,0:T(1,128)} reshape(s32[1,1,8,4,2]{4,3,2,1,0:T(4,128)S(1)} %copy.18) | data formatting | bytes 512 | tf_op jit(solution)/shard_map/reshape | solution.py:389
  13.4 2.0 %shard_map.158 = (bf16[128,1024]{1,0:T(8,128)(2,1)}, bf16[96,512]{1,0:T(8,128)(2,1)}, bf16[128,64]{1,0:T(8,128)(2,1)}) custom-call(s32[1,1]{1,0:T(1,128)S(6)} %copy.19.refs_0_, s32[16,128]{1,0:T(8,128)} %bitcast.19, s32[1,128]{1,0:T(1,128)} %bitcast.24, f32[8,128]{1,0:T(8,128)} %refs_3_.2, f32[8,128]{1,0:T(8,128)} %refs_4_.1, s32[1,64]{1,0:T(1,128)} %reshape.25.refs_5_, ...), custom_call_target="tpu_custom_call" | custom-call | tf_op jit(solution)/shard_map/pallas_call | solution.py:46
  15.4 0.4 collective-permute-done.refs_5_
  15.8 0.0 collective-permute-start.1
  15.8 0.5 collective-permute-start.2
  16.3 0.0 copy-done.1
  16.3 1.7 %collective-permute-start.3 = (bf16[512,512]{1,0:T(8,128)(2,1)S(1)}, bf16[512,512]{1,0:T(8,128)(2,1)S(1)}, u32[]{:S(2)}, u32[]{:S(2)}) collective-permute-start(bf16[512,512]{1,0:T(8,128)(2,1)S(1)} %copy-done.1), channel_id=1, source_target_pairs={{0,2},{1,3},{2,0},{3,1},{4,6},{5,7},{6,4},{7,5},{8,10},{9,11},{10,... | collective-permute-start | bytes 1572872 | tf_op jit(solution)/shard_map/ppermute | solution.py:325
  18.1 8.2 %all-to-all-done = bf16[8,32,1024]{2,1,0:T(8,128)(2,1)S(1)} async-done(((bf16[8,32,1024]{2,1,0:T(8,128)(2,1)}), bf16[8,32,1024]{2,1,0:T(8,128)(2,1)S(1)}, u32[]{:S(2)}, u32[]{:S(2)}) %all-to-all-start) | async-done | bytes 524320 | tf_op jit(solution)/shard_map/all_to_all | solution.py:372
  26.3 0.0 collective-permute-done.1.refs_4_
  26.3 0.0 collective-permute-done.2.refs_6_
  26.3 0.0 copy-start.3
  26.3 0.9 %copy-done.3 = bf16[128,1024]{1,0:T(8,128)(2,1)S(1)} copy-done((bf16[128,1024]{1,0:T(8,128)(2,1)S(1)}, bf16[128,1024]{1,0:T(8,128)(2,1)}, u32[]{:S(2)}) %copy-start.3) | copy-done | bytes 262168
  27.2 4.6 %shard_map.159 = (bf16[128,1024]{1,0:T(8,128)(2,1)}, bf16[512,128]{1,0:T(8,128)(2,1)}) custom-call(bf16[128,1024]{1,0:T(8,128)(2,1)S(1)} %copy-done, bf16[256,1024]{1,0:T(8,128)(2,1)S(1)} %bitcast.14, bf16[128,1024]{1,0:T(8,128)(2,1)S(1)} %copy-done.3, bf16[256,1024]{1,0:T(8,128)(2,1)S(1)} %copy-done.2, ...), custom_call_target="tpu_custom_call" | custom-call | tf_op jit(solution)/shard_map/pallas_call | solution.py:46
  31.9 2.7 %all-to-all-start.1 = ((bf16[32,16,128]{2,1,0:T(8,128)(2,1)}), bf16[32,16,128]{2,1,0:T(8,128)(2,1)S(1)}, u32[]{:S(2)}, u32[]{:S(2)}) async-start(bf16[32,16,128]{2,1,0:T(8,128)(2,1)} %bitcast.9), calls=%async_computation.1 | async-start | bytes 262144 | tf_op jit(solution)/shard_map/all_to_all | solution.py:416
  34.6 0.0 collective-permute-done.3.refs_3_.refs_5_
  34.6 0.3 collective-permute-start.4
  34.9 0.3 collective-permute-start.5
  35.2 7.6 %all-to-all-done.1 = bf16[32,16,128]{2,1,0:T(8,128)(2,1)S(1)} async-done(((bf16[32,16,128]{2,1,0:T(8,128)(2,1)}), bf16[32,16,128]{2,1,0:T(8,128)(2,1)S(1)}, u32[]{:S(2)}, u32[]{:S(2)}) %all-to-all-start.1) | async-done | bytes 131104 | tf_op jit(solution)/shard_map/all_to_all | solution.py:416
  42.8 0.0 copy-done.4
  42.9 0.3 shard_map.160
  43.2 0.0 collective-permute-done.4.refs_4_
  43.2 0.0 collective-permute-done.5.refs_6_
  43.2 2.5 %shard_map.161 = (f32[1,256]{1,0:T(1,128)}, bf16[512,128]{1,0:T(8,128)(2,1)S(1)}) custom-call(bf16[64,1024]{1,0:T(8,128)(2,1)S(1)} %get-tuple-element.22.refs_0_, f32[2,64,512]{2,1,0:T(8,128)S(1)} %get-tuple-element.23.refs_1_, bf16[96,512]{1,0:T(8,128)(2,1)S(1)} %copy-done.4, bf16[512,512]{1,0:T(8,128)(2,1)S(1)} %copy-done.1, ...), custom_call_target="tpu_custom_call" | custom-call | tf_op jit(solution)/shard_map/pallas_call | solution.py:46
  45.8 10.0 %all_to_all.33 = bf16[32,16,128]{2,1,0:T(8,128)(2,1)S(1)} all-to-all(bf16[32,16,128]{2,1,0:T(8,128)(2,1)S(1)} %bitcast.17), channel_id=1, replica_groups=mesh['dom'=8,'edge'=4] {'dom','edge'}, dimensions={0} | all-to-all | bytes 262144 | tf_op jit(solution)/shard_map/all_to_all | solution.py:445
  55.8 1.0 %shard_map.162 = f32[128,1024]{1,0:T(8,128)} custom-call(bf16[128,64]{1,0:T(8,128)(2,1)S(1)} %copy-done.5, bf16[512,128]{1,0:T(8,128)(2,1)S(1)} %bitcast.15), custom_call_target="tpu_custom_call" | custom-call | tf_op jit(solution)/shard_map/pallas_call | solution.py:46
  (7 shorter events, 0.0 us)
Async XLA Ops:
  0.6 15.2 %collective-permute-start = (bf16[256,1024]{1,0:T(8,128)(2,1)}, bf16[256,1024]{1,0:T(8,128)(2,1)S(1)}, u32[]{:S(2)}, u32[]{:S(2)}) collective-permute-start(bf16[256,1024]{1,0:T(8,128)(2,1)} %refs_3_.3), channel_id=1, source_target_pairs={{0,2},{1,3},{2,0},{3,1},{4,6},{5,7},{6,4},{7,5},{8,10},{9,11},{10,... | collective-permute-start | bytes 1572872 | tf_op jit(solution)/shard_map/ppermute | solution.py:325
  3.7 12.1 %copy-start.2 = (bf16[256,1024]{1,0:T(8,128)(2,1)S(1)}, bf16[256,1024]{1,0:T(8,128)(2,1)}, u32[]{:S(2)}) copy-start(bf16[256,1024]{1,0:T(8,128)(2,1)} %refs_3_.3) | copy-start | bytes 1572868
  6.0 6.6 %copy-start.6 = (s32[1,1,8,4,2]{2,4,3,1,0:T(2,128)S(1)}, s32[1,1,8,4,2]{2,4,3,1,0:T(2,128)}, u32[]{:S(2)}) copy-start(s32[1,1,8,4,2]{2,4,3,1,0:T(2,128)} %param.22) | copy-start | bytes 772
  6.0 10.3 %copy-start.1 = (bf16[512,512]{1,0:T(8,128)(2,1)S(1)}, bf16[512,512]{1,0:T(8,128)(2,1)}, u32[]{:S(2)}) copy-start(bf16[512,512]{1,0:T(8,128)(2,1)} %refs_3_.4) | copy-start | bytes 1572868
  6.0 20.2 %copy-start = (bf16[128,1024]{1,0:T(8,128)(2,1)S(1)}, bf16[128,1024]{1,0:T(8,128)(2,1)}, u32[]{:S(2)}) copy-start(bf16[128,1024]{1,0:T(8,128)(2,1)} %refs_0_.2) | copy-start | bytes 786436
  6.1 20.2 %all-to-all-start = ((bf16[8,32,1024]{2,1,0:T(8,128)(2,1)}), bf16[8,32,1024]{2,1,0:T(8,128)(2,1)S(1)}, u32[]{:S(2)}, u32[]{:S(2)}) async-start(bf16[8,32,1024]{2,1,0:T(8,128)(2,1)} %bitcast.18), calls=%async_computation | async-start | bytes 1048576 | tf_op jit(solution)/shard_map/all_to_all | solution.py:372
  15.8 10.5 %collective-permute-start.1 = (bf16[256,1024]{1,0:T(8,128)(2,1)S(1)}, bf16[256,1024]{1,0:T(8,128)(2,1)S(1)}, u32[]{:S(2)}, u32[]{:S(2)}) collective-permute-start(bf16[256,1024]{1,0:T(8,128)(2,1)S(1)} %copy-done.2), channel_id=1, source_target_pairs={{0,1},{1,0},{2,3},{3,2},{4,5},{5,4},{6,7},{7,6},{8,9},{9,8},{10,11... | collective-permute-start | bytes 1572872 | tf_op jit(solution)/shard_map/ppermute | solution.py:325
  15.8 10.5 %collective-permute-start.2 = (bf16[256,1024]{1,0:T(8,128)(2,1)S(1)}, bf16[256,1024]{1,0:T(8,128)(2,1)}, u32[]{:S(2)}, u32[]{:S(2)}) collective-permute-start(bf16[256,1024]{1,0:T(8,128)(2,1)S(1)} %collective-permute-done.refs_5_), channel_id=1, source_target_pairs={{0,1},{1,0},{2,3},{3,2},{4,5},{5,4},{6,7},{7,6},{8,9},{9,8},{10,11... | collective-permute-start | bytes 1572872 | tf_op jit(solution)/shard_map/ppermute | solution.py:325
  16.3 18.3 %collective-permute-start.3 = (bf16[512,512]{1,0:T(8,128)(2,1)S(1)}, bf16[512,512]{1,0:T(8,128)(2,1)S(1)}, u32[]{:S(2)}, u32[]{:S(2)}) collective-permute-start(bf16[512,512]{1,0:T(8,128)(2,1)S(1)} %copy-done.1), channel_id=1, source_target_pairs={{0,2},{1,3},{2,0},{3,1},{4,6},{5,7},{6,4},{7,5},{8,10},{9,11},{10,... | collective-permute-start | bytes 1572872 | tf_op jit(solution)/shard_map/ppermute | solution.py:325
  26.3 1.0 %copy-start.3 = (bf16[128,1024]{1,0:T(8,128)(2,1)S(1)}, bf16[128,1024]{1,0:T(8,128)(2,1)}, u32[]{:S(2)}) copy-start(bf16[128,1024]{1,0:T(8,128)(2,1)} %get-tuple-element.16.refs_2_) | copy-start | bytes 786436
  31.9 11.0 %copy-start.4 = (bf16[96,512]{1,0:T(8,128)(2,1)S(1)}, bf16[96,512]{1,0:T(8,128)(2,1)}, u32[]{:S(2)}) copy-start(bf16[96,512]{1,0:T(8,128)(2,1)} %get-tuple-element.21.refs_1_.refs_2_) | copy-start | bytes 294916
  31.9 11.0 %all-to-all-start.1 = ((bf16[32,16,128]{2,1,0:T(8,128)(2,1)}), bf16[32,16,128]{2,1,0:T(8,128)(2,1)S(1)}, u32[]{:S(2)}, u32[]{:S(2)}) async-start(bf16[32,16,128]{2,1,0:T(8,128)(2,1)} %bitcast.9), calls=%async_computation.1 | async-start | bytes 262144 | tf_op jit(solution)/shard_map/all_to_all | solution.py:416
  34.6 8.6 %collective-permute-start.4 = (bf16[512,512]{1,0:T(8,128)(2,1)S(1)}, bf16[512,512]{1,0:T(8,128)(2,1)S(1)}, u32[]{:S(2)}, u32[]{:S(2)}) collective-permute-start(bf16[512,512]{1,0:T(8,128)(2,1)S(1)} %copy-done.1), channel_id=1, source_target_pairs={{0,1},{1,0},{2,3},{3,2},{4,5},{5,4},{6,7},{7,6},{8,9},{9,8},{10,11... | collective-permute-start | bytes 1572872 | tf_op jit(solution)/shard_map/ppermute | solution.py:325
  34.9 8.3 %collective-permute-start.5 = (bf16[512,512]{1,0:T(8,128)(2,1)S(1)}, bf16[512,512]{1,0:T(8,128)(2,1)S(1)}, u32[]{:S(2)}, u32[]{:S(2)}) collective-permute-start(bf16[512,512]{1,0:T(8,128)(2,1)S(1)} %collective-permute-done.3.refs_3_.refs_5_), channel_id=1, source_target_pairs={{0,1},{1,0},{2,3},{3,2},{4,5},{5,4},{6,7},{7,6},{8,9},{9,8},{10,11... | collective-permute-start | bytes 1572872 | tf_op jit(solution)/shard_map/ppermute | solution.py:325
  45.7 10.0 %copy-start.5 = (bf16[128,64]{1,0:T(8,128)(2,1)S(1)}, bf16[128,64]{1,0:T(8,128)(2,1)}, u32[]{:S(2)}) copy-start(bf16[128,64]{1,0:T(8,128)(2,1)} %get-tuple-element.27.refs_0_) | copy-start | bytes 49156

commit v18 on v16

--- a/solution.py
+++ b/solution.py
@@ -356,7 +356,8 @@
     )
     got_rows = lax.all_to_all(send_rows, "dom", split_axis=0, concat_axis=0, tiled=True)
     gat_across = across(gat_weight, edge_count)
-    mlp_across = across(mlp_weight, edge_count)
+    held_mlp = lax.optimization_barrier((mlp_weight, got_rows))[0]
+    mlp_across = across(held_mlp, edge_count)
     lanes = -(-(2 * table + attn_src.shape[1] + slots) // 128) * 128
     for_attend, for_score, pick = call(
         functools.partial(prepare_kernel, table),
@@ -376,7 +377,7 @@
             ("f", labels[0]),
             ("f", out_weight.reshape(1, hidden)),
         ],
-        vmem_mib=60,
+        cost=pl.CostEstimate(flops=10**6, bytes_accessed=10**5, transcendentals=0),
     )
     gat_across = lax.optimization_barrier((*gat_across, for_attend))[:-1]
     gat_shards = from_core(gat_across)

time: 57.4 us -> 60.7 us (1.057)
  starting transfers between devices: 14.5 us -> 17.2 us
  Pallas kernels: 13 us -> 11.5 us
  waiting for transfers between devices: 16.2 us -> 17.5 us
  local copies, waits for them, and re-layouts: 1.71 us -> 2.58 us
    ppermute x6, waiting for transfers between devices: 0.4 us -> 9.45 us  [swap(): return lax.ppermute(array, axis, [(i, i ^ k) for i in range(count)])]
    all_to_all x1, waiting for transfers between devices: 8.2 us -> 0.52 us  [local(): lax.all_to_all(send_rows, 'dom', split_axis=0, concat_axis=0, tiled=True)]
    all_to_all x1, starting transfers between devices: 2.73 us -> 5.7 us  [local(): lax.all_to_all(send_ends, everyone, split_axis=0, concat_axis=0, tiled=True)]
    ppermute x6, starting transfers between devices: 5.86 us -> 4.13 us  [swap(): return lax.ppermute(array, axis, [(i, i ^ k) for i in range(count)])]
    pallas_call x6, Pallas kernels: 13 us -> 11.5 us  [call(): pl.pallas_call(body, out_shape=outs, in_specs=[SPACES[space] for space, _...]
    all_to_all x1, starting transfers between devices: 5.95 us -> 7.4 us  [local(): lax.all_to_all(send_rows, 'dom', split_axis=0, concat_axis=0, tiled=True)]
    unnamed x15 -> x27, local copies, waits for them, and re-layouts: 1.08 us -> 2.47 us
  transfers between devices with their start and end apart: 8 -> 8, of which waited for: 3 -> 6; matrix products, arithmetic and copies ran while one was open for 1% -> 0% of each run, Pallas kernels for 17% -> 9%
where the time goes in v18:
time: 60.7 us; the launch traced here: 60.3 us
  waiting for transfers between devices  17.5 us (29%)
  starting transfers between devices  17.2 us (28%)
  Pallas kernels  11.5 us (19%)
  blocking collectives  10 us (16%)
  local copies, waits for them, and re-layouts  2.58 us (4%)
  between operations  1.44 us (2%)
    pallas_call x6, Pallas kernels, call(): pl.pallas_call(body, out_shape=outs, in_specs=[SPACES[space] for space, _...  11.5 us
    all_to_all x1, blocking collectives, local(): lax.all_to_all(send_back, everyone, split_axis=0, concat_axis=0, tiled=True)  10 us
    ppermute x6, waiting for transfers between devices, swap(): return lax.ppermute(array, axis, [(i, i ^ k) for i in range(count)])  9.45 us
    all_to_all x1, waiting for transfers between devices, local(): lax.all_to_all(send_ends, everyone, split_axis=0, concat_axis=0, tiled=True)  7.53 us
    all_to_all x1, starting transfers between devices, local(): lax.all_to_all(send_rows, 'dom', split_axis=0, concat_axis=0, tiled=True)  7.4 us
    all_to_all x1, starting transfers between devices, local(): lax.all_to_all(send_ends, everyone, split_axis=0, concat_axis=0, tiled=True)  5.7 us
    ppermute x6, starting transfers between devices, swap(): return lax.ppermute(array, axis, [(i, i ^ k) for i in range(count)])  4.13 us
    unnamed x27, local copies, waits for them, and re-layouts  2.47 us
  transfers between devices with their start and end apart: 8, of which 6 were waited for; matrix products, arithmetic and copies ran while one was open for 0% of the time, Pallas kernels for 9%

profile of v18, /device:TPU:0, one launch (start us, length us, event | category | flops | bytes accessed | tf_op | source)
XLA Modules:
  0.0 60.3 jit_solution(16978305984827073758)
XLA Ops:
  0.6 2.4 %shard_map.157 = bf16[256,1024]{1,0:T(8,128)(2,1)} custom-call(s32[1,8]{1,0:T(1,128)} %bitcast.25, s32[8,32]{1,0:T(8,128)} %bitcast.24, bf16[128,1024]{1,0:T(8,128)(2,1)} %refs_0_.2), custom_call_target="tpu_custom_call" | custom-call | tf_op jit(solution)/shard_map/pallas_call | solution.py:46
  3.0 0.0 copy-start.1
  3.0 0.0 copy-start
  3.0 7.4 %all-to-all-start = ((bf16[8,32,1024]{2,1,0:T(8,128)(2,1)}), bf16[8,32,1024]{2,1,0:T(8,128)(2,1)S(1)}, u32[]{:S(2)}, u32[]{:S(2)}) async-start(bf16[8,32,1024]{2,1,0:T(8,128)(2,1)} %bitcast.23), calls=%async_computation | async-start | bytes 1048576 | tf_op jit(solution)/shard_map/all_to_all | solution.py:357
  10.4 1.6 %collective-permute-start = (bf16[256,1024]{1,0:T(8,128)(2,1)S(1)}, bf16[256,1024]{1,0:T(8,128)(2,1)S(1)}, u32[]{:S(2)}, u32[]{:S(2)}) collective-permute-start(bf16[256,1024]{1,0:T(8,128)(2,1)S(1)} %copy-done.2), channel_id=1, source_target_pairs={{0,2},{1,3},{2,0},{3,1},{4,6},{5,7},{6,4},{7,5},{8,10},{9,11},{10,... | collective-permute-start | bytes 1572872 | tf_op jit(solution)/shard_map/ppermute | solution.py:310
  12.7 0.1 copy.18
  12.8 0.0 copy-start.11
  12.8 0.1 reshape.25.refs_5_
  12.9 0.5 copy-done.6
  13.5 0.0 copy-done.7
  13.5 0.0 copy-done.8
  13.5 0.0 copy-done.9
  13.5 0.1 copy-done.5
  13.6 0.5 shard_map.158
  14.2 0.7 %copy-done.3 = bf16[128,1024]{1,0:T(8,128)(2,1)} copy-done((bf16[128,1024]{1,0:T(8,128)(2,1)}, bf16[128,1024]{1,0:T(8,128)(2,1)S(1)}, u32[]{:S(2)}) %copy-start.3) | copy-done | bytes 262168
  14.9 9.0 %collective-permute-done.refs_5_ = bf16[256,1024]{1,0:T(8,128)(2,1)S(1)} collective-permute-done((bf16[256,1024]{1,0:T(8,128)(2,1)S(1)}, bf16[256,1024]{1,0:T(8,128)(2,1)S(1)}, u32[]{:S(2)}, u32[]{:S(2)}) %collective-permute-start) | collective-permute-done | bytes 524320 | tf_op jit(solution)/shard_map/ppermute | solution.py:310
  23.9 0.5 collective-permute-start.2
  24.4 0.5 all-to-all-done
  24.9 1.5 %collective-permute-start.3 = (bf16[512,512]{1,0:T(8,128)(2,1)S(1)}, bf16[512,512]{1,0:T(8,128)(2,1)S(1)}, u32[]{:S(2)}, u32[]{:S(2)}) collective-permute-start(bf16[512,512]{1,0:T(8,128)(2,1)S(1)} %copy-done.1), channel_id=1, source_target_pairs={{0,2},{1,3},{2,0},{3,1},{4,6},{5,7},{6,4},{7,5},{8,10},{9,11},{10,... | collective-permute-start | bytes 1572872 | tf_op jit(solution)/shard_map/ppermute | solution.py:310
  26.4 0.1 collective-permute-done.1.refs_4_
  26.5 0.2 collective-permute-done.2.refs_6_
  26.7 0.9 %copy-done.4 = bf16[128,1024]{1,0:T(8,128)(2,1)S(1)} copy-done((bf16[128,1024]{1,0:T(8,128)(2,1)S(1)}, bf16[128,1024]{1,0:T(8,128)(2,1)}, u32[]{:S(2)}) %copy-start.4) | copy-done | bytes 262168
  27.6 4.8 %shard_map.159 = (bf16[128,1024]{1,0:T(8,128)(2,1)}, bf16[512,128]{1,0:T(8,128)(2,1)}) custom-call(bf16[128,1024]{1,0:T(8,128)(2,1)S(1)} %copy-done, bf16[256,1024]{1,0:T(8,128)(2,1)S(1)} %bitcast.14, bf16[128,1024]{1,0:T(8,128)(2,1)S(1)} %copy-done.4, bf16[256,1024]{1,0:T(8,128)(2,1)S(1)} %copy-done.2, ...), custom_call_target="tpu_custom_call" | custom-call | tf_op jit(solution)/shard_map/pallas_call | solution.py:46
  32.4 5.7 %all-to-all-start.1 = ((bf16[32,16,128]{2,1,0:T(8,128)(2,1)}), bf16[32,16,128]{2,1,0:T(8,128)(2,1)S(1)}, u32[]{:S(2)}, u32[]{:S(2)}) async-start(bf16[32,16,128]{2,1,0:T(8,128)(2,1)} %bitcast.9), calls=%async_computation.1 | async-start | bytes 262144 | tf_op jit(solution)/shard_map/all_to_all | solution.py:398
  38.1 0.2 collective-permute-done.3.refs_3_.refs_5_
  38.3 0.1 collective-permute-start.4
  38.4 0.4 collective-permute-start.5
  38.8 7.5 %all-to-all-done.1 = bf16[32,16,128]{2,1,0:T(8,128)(2,1)S(1)} async-done(((bf16[32,16,128]{2,1,0:T(8,128)(2,1)}), bf16[32,16,128]{2,1,0:T(8,128)(2,1)S(1)}, u32[]{:S(2)}, u32[]{:S(2)}) %all-to-all-start.1) | async-done | bytes 131104 | tf_op jit(solution)/shard_map/all_to_all | solution.py:398
  46.3 0.4 shard_map.160
  46.7 2.5 %shard_map.161 = (f32[1,256]{1,0:T(1,128)}, bf16[512,128]{1,0:T(8,128)(2,1)S(1)}) custom-call(bf16[64,1024]{1,0:T(8,128)(2,1)S(1)} %get-tuple-element.24.refs_0_, f32[2,64,512]{2,1,0:T(8,128)S(1)} %get-tuple-element.25.refs_1_, bf16[96,512]{1,0:T(8,128)(2,1)S(1)} %get-tuple-element.22.refs_1_.refs_2_, bf16[512,512]{1,0:T(8,128)(2,1)S(1)} %copy-done.1, ...), custom_call_target="tpu_custom_call" | custom-call | tf_op jit(solution)/shard_map/pallas_call | solution.py:46
  49.2 10.0 %all_to_all.33 = bf16[32,16,128]{2,1,0:T(8,128)(2,1)S(1)} all-to-all(bf16[32,16,128]{2,1,0:T(8,128)(2,1)S(1)} %bitcast.17), channel_id=1, replica_groups=mesh['dom'=8,'edge'=4] {'dom','edge'}, dimensions={0} | all-to-all | bytes 262144 | tf_op jit(solution)/shard_map/all_to_all | solution.py:427
  59.2 1.0 %shard_map.162 = f32[128,1024]{1,0:T(8,128)} custom-call(bf16[128,64]{1,0:T(8,128)(2,1)S(1)} %get-tuple-element.29.refs_0_, bf16[512,128]{1,0:T(8,128)(2,1)S(1)} %bitcast.15), custom_call_target="tpu_custom_call" | custom-call | tf_op jit(solution)/shard_map/pallas_call | solution.py:46
  (19 shorter events, 0.0 us)
Async XLA Ops:
  0.6 9.8 %copy-start.2 = (bf16[256,1024]{1,0:T(8,128)(2,1)S(1)}, bf16[256,1024]{1,0:T(8,128)(2,1)}, u32[]{:S(2)}) copy-start(bf16[256,1024]{1,0:T(8,128)(2,1)} %refs_3_.2) | copy-start | bytes 1572868
  3.0 9.7 %copy-start.12 = (s32[1,1,8,4,2]{2,4,3,1,0:T(2,128)S(1)}, s32[1,1,8,4,2]{2,4,3,1,0:T(2,128)}, u32[]{:S(2)}) copy-start(s32[1,1,8,4,2]{2,4,3,1,0:T(2,128)} %param.22) | copy-start | bytes 772
  3.0 21.9 %copy-start.1 = (bf16[512,512]{1,0:T(8,128)(2,1)S(1)}, bf16[512,512]{1,0:T(8,128)(2,1)}, u32[]{:S(2)}) copy-start(bf16[512,512]{1,0:T(8,128)(2,1)} %refs_3_.3) | copy-start | bytes 1572868
  3.0 23.7 %copy-start = (bf16[128,1024]{1,0:T(8,128)(2,1)S(1)}, bf16[128,1024]{1,0:T(8,128)(2,1)}, u32[]{:S(2)}) copy-start(bf16[128,1024]{1,0:T(8,128)(2,1)} %refs_0_.2) | copy-start | bytes 786436
  3.0 21.9 %all-to-all-start = ((bf16[8,32,1024]{2,1,0:T(8,128)(2,1)}), bf16[8,32,1024]{2,1,0:T(8,128)(2,1)S(1)}, u32[]{:S(2)}, u32[]{:S(2)}) async-start(bf16[8,32,1024]{2,1,0:T(8,128)(2,1)} %bitcast.23), calls=%async_computation | async-start | bytes 1048576 | tf_op jit(solution)/shard_map/all_to_all | solution.py:357
  10.4 13.4 %collective-permute-start = (bf16[256,1024]{1,0:T(8,128)(2,1)S(1)}, bf16[256,1024]{1,0:T(8,128)(2,1)S(1)}, u32[]{:S(2)}, u32[]{:S(2)}) collective-permute-start(bf16[256,1024]{1,0:T(8,128)(2,1)S(1)} %copy-done.2), channel_id=1, source_target_pairs={{0,2},{1,3},{2,0},{3,1},{4,6},{5,7},{6,4},{7,5},{8,10},{9,11},{10,... | collective-permute-start | bytes 1572872 | tf_op jit(solution)/shard_map/ppermute | solution.py:310
  12.8 0.7 %copy-start.6 = (f32[8,128]{1,0:T(8,128)S(1)}, f32[8,128]{1,0:T(8,128)}, u32[]{:S(2)}) copy-start(f32[8,128]{1,0:T(8,128)} %refs_3_.1) | copy-start | bytes 12292
  12.8 0.7 %copy-start.7 = (f32[8,128]{1,0:T(8,128)S(1)}, f32[8,128]{1,0:T(8,128)}, u32[]{:S(2)}) copy-start(f32[8,128]{1,0:T(8,128)} %refs_4_.1) | copy-start | bytes 12292
  12.8 0.7 %copy-start.8 = (s32[1,1,2,256]{3,2,1,0:T(2,128)S(1)}, s32[1,1,2,256]{3,2,1,0:T(2,128)}, u32[]{:S(2)}) copy-start(s32[1,1,2,256]{3,2,1,0:T(2,128)} %param.23) | copy-start | bytes 6148
  12.8 0.7 %copy-start.9 = (f32[512]{0:T(512)S(1)}, f32[512]{0:T(512)}, u32[]{:S(2)}) copy-start(f32[512]{0:T(512)} %param.27) | copy-start | bytes 6148
  12.8 0.7 %copy-start.11 = (s32[128]{0:T(128)S(1)}, s32[128]{0:T(128)}, u32[]{:S(2)}) copy-start(s32[128]{0:T(128)} %param.19) | copy-start | bytes 1540
  12.9 0.7 %copy-start.5 = (s32[128,16]{0,1:T(8,128)S(1)}, s32[128,16]{0,1:T(8,128)}, u32[]{:S(2)}) copy-start(s32[128,16]{0,1:T(8,128)} %param.18) | copy-start | bytes 24580
  12.9 0.7 %copy-start.10 = (s32[1,1,256]{2,1,0:T(1,128)S(1)}, s32[1,1,256]{2,1,0:T(1,128)}, u32[]{:S(2)}) copy-start(s32[1,1,256]{2,1,0:T(1,128)} %param.25) | copy-start | bytes 3076
  14.2 0.7 %copy-start.3 = (bf16[128,1024]{1,0:T(8,128)(2,1)}, bf16[128,1024]{1,0:T(8,128)(2,1)S(1)}, u32[]{:S(2)}) copy-start(bf16[128,1024]{1,0:T(8,128)(2,1)S(1)} %get-tuple-element.17.refs_2_) | copy-start | bytes 786436
  23.9 2.6 %collective-permute-start.1 = (bf16[256,1024]{1,0:T(8,128)(2,1)S(1)}, bf16[256,1024]{1,0:T(8,128)(2,1)S(1)}, u32[]{:S(2)}, u32[]{:S(2)}) collective-permute-start(bf16[256,1024]{1,0:T(8,128)(2,1)S(1)} %copy-done.2), channel_id=1, source_target_pairs={{0,1},{1,0},{2,3},{3,2},{4,5},{5,4},{6,7},{7,6},{8,9},{9,8},{10,11... | collective-permute-start | bytes 1572872 | tf_op jit(solution)/shard_map/ppermute | solution.py:310
  23.9 2.8 %collective-permute-start.2 = (bf16[256,1024]{1,0:T(8,128)(2,1)S(1)}, bf16[256,1024]{1,0:T(8,128)(2,1)}, u32[]{:S(2)}, u32[]{:S(2)}) collective-permute-start(bf16[256,1024]{1,0:T(8,128)(2,1)S(1)} %collective-permute-done.refs_5_), channel_id=1, source_target_pairs={{0,1},{1,0},{2,3},{3,2},{4,5},{5,4},{6,7},{7,6},{8,9},{9,8},{10,11... | collective-permute-start | bytes 1572872 | tf_op jit(solution)/shard_map/ppermute | solution.py:310
  24.9 13.4 %collective-permute-start.3 = (bf16[512,512]{1,0:T(8,128)(2,1)S(1)}, bf16[512,512]{1,0:T(8,128)(2,1)S(1)}, u32[]{:S(2)}, u32[]{:S(2)}) collective-permute-start(bf16[512,512]{1,0:T(8,128)(2,1)S(1)} %copy-done.1), channel_id=1, source_target_pairs={{0,2},{1,3},{2,0},{3,1},{4,6},{5,7},{6,4},{7,5},{8,10},{9,11},{10,... | collective-permute-start | bytes 1572872 | tf_op jit(solution)/shard_map/ppermute | solution.py:310
  26.7 1.0 %copy-start.4 = (bf16[128,1024]{1,0:T(8,128)(2,1)S(1)}, bf16[128,1024]{1,0:T(8,128)(2,1)}, u32[]{:S(2)}) copy-start(bf16[128,1024]{1,0:T(8,128)(2,1)} %copy-done.3) | copy-start | bytes 786436
  32.4 13.9 %all-to-all-start.1 = ((bf16[32,16,128]{2,1,0:T(8,128)(2,1)}), bf16[32,16,128]{2,1,0:T(8,128)(2,1)S(1)}, u32[]{:S(2)}, u32[]{:S(2)}) async-start(bf16[32,16,128]{2,1,0:T(8,128)(2,1)} %bitcast.9), calls=%async_computation.1 | async-start | bytes 262144 | tf_op jit(solution)/shard_map/all_to_all | solution.py:398
  38.3 8.4 %collective-permute-start.4 = (bf16[512,512]{1,0:T(8,128)(2,1)S(1)}, bf16[512,512]{1,0:T(8,128)(2,1)S(1)}, u32[]{:S(2)}, u32[]{:S(2)}) collective-permute-start(bf16[512,512]{1,0:T(8,128)(2,1)S(1)} %copy-done.1), channel_id=1, source_target_pairs={{0,1},{1,0},{2,3},{3,2},{4,5},{5,4},{6,7},{7,6},{8,9},{9,8},{10,11... | collective-permute-start | bytes 1572872 | tf_op jit(solution)/shard_map/ppermute | solution.py:310
  38.4 8.3 %collective-permute-start.5 = (bf16[512,512]{1,0:T(8,128)(2,1)S(1)}, bf16[512,512]{1,0:T(8,128)(2,1)S(1)}, u32[]{:S(2)}, u32[]{:S(2)}) collective-permute-start(bf16[512,512]{1,0:T(8,128)(2,1)S(1)} %collective-permute-done.3.refs_3_.refs_5_), channel_id=1, source_target_pairs={{0,1},{1,0},{2,3},{3,2},{4,5},{5,4},{6,7},{7,6},{8,9},{9,8},{10,11... | collective-permute-start | bytes 1572872 | tf_op jit(solution)/shard_map/ppermute | solution.py:310

commit v19 on v16

--- a/solution.py
+++ b/solution.py
@@ -393,6 +393,11 @@
             pltpu.VMEM((2, 2 * nodes, table), BF16),
             pltpu.VMEM((width if width // edge_count % 128 else 16, width), BF16),
         ],
+        cost=pl.CostEstimate(
+            flops=2 * table * width * (width + 2 * nodes),
+            bytes_accessed=2 * width * (width + table + 2 * nodes) + 2 * nodes * lanes,
+            transcendentals=nodes * table * heads,
+        ),
     )
     got_ends = lax.all_to_all(send_ends, everyone, split_axis=0, concat_axis=0, tiled=True)
     tied = lax.optimization_barrier((*mlp_across, send_ends))[:-1]

time: 57.4 us -> 57.4 us (level)
  no operation moved by 1% of the time
where the time goes in v19:
time: 57.4 us; the launch traced here: 56.9 us
  waiting for transfers between devices  16.2 us (28%)
  starting transfers between devices  14.5 us (25%)
  Pallas kernels  13 us (23%)
  blocking collectives  10 us (17%)
  local copies, waits for them, and re-layouts  1.71 us (3%)
  between operations  1.42 us (2%)
    pallas_call x6, Pallas kernels, call(): pl.pallas_call(body, out_shape=outs, in_specs=[SPACES[space] for space, _...  13 us
    all_to_all x1, blocking collectives, local(): lax.all_to_all(send_back, everyone, split_axis=0, concat_axis=0, tiled=True)  10 us
    all_to_all x1, waiting for transfers between devices, local(): lax.all_to_all(send_rows, 'dom', split_axis=0, concat_axis=0, tiled=True)  8.2 us
    all_to_all x1, waiting for transfers between devices, local(): lax.all_to_all(send_ends, everyone, split_axis=0, concat_axis=0, tiled=True)  7.64 us
    all_to_all x1, starting transfers between devices, local(): lax.all_to_all(send_rows, 'dom', split_axis=0, concat_axis=0, tiled=True)  5.95 us
    ppermute x6, starting transfers between devices, swap(): return lax.ppermute(array, axis, [(i, i ^ k) for i in range(count)])  5.86 us
    all_to_all x1, starting transfers between devices, local(): lax.all_to_all(send_ends, everyone, split_axis=0, concat_axis=0, tiled=True)  2.73 us
  transfers between devices with their start and end apart: 8, of which 3 were waited for; matrix products, arithmetic and copies ran while one was open for 1% of the time, Pallas kernels for 17%

profile of v19, /device:TPU:0, one launch (start us, length us, event | category | flops | bytes accessed | tf_op | source)
XLA Modules:
  0.0 56.9 jit_solution(6843482185456143818)
XLA Ops:
  0.6 3.0 %collective-permute-start = (bf16[256,1024]{1,0:T(8,128)(2,1)}, bf16[256,1024]{1,0:T(8,128)(2,1)S(1)}, u32[]{:S(2)}, u32[]{:S(2)}) collective-permute-start(bf16[256,1024]{1,0:T(8,128)(2,1)} %refs_3_.3), channel_id=1, source_target_pairs={{0,2},{1,3},{2,0},{3,1},{4,6},{5,7},{6,4},{7,5},{8,10},{9,11},{10,... | collective-permute-start | bytes 1572872 | tf_op jit(solution)/shard_map/ppermute | solution.py:310
  3.7 2.4 %shard_map.157 = bf16[256,1024]{1,0:T(8,128)(2,1)} custom-call(s32[1,8]{1,0:T(1,128)} %bitcast.25, s32[8,32]{1,0:T(8,128)} %bitcast.20, bf16[128,1024]{1,0:T(8,128)(2,1)} %refs_0_.2), custom_call_target="tpu_custom_call" | custom-call | tf_op jit(solution)/shard_map/pallas_call | solution.py:46
  6.0 0.0 copy-start.6
  6.0 0.0 copy-start
  6.0 0.0 copy-start.1
  6.1 5.9 %all-to-all-start = ((bf16[8,32,1024]{2,1,0:T(8,128)(2,1)}), bf16[8,32,1024]{2,1,0:T(8,128)(2,1)S(1)}, u32[]{:S(2)}, u32[]{:S(2)}) async-start(bf16[8,32,1024]{2,1,0:T(8,128)(2,1)} %bitcast.18), calls=%async_computation | async-start | bytes 1048576 | tf_op jit(solution)/shard_map/all_to_all | solution.py:357
  12.7 0.1 copy.18
  12.8 0.6 %reshape.25.refs_5_ = s32[1,64]{1,0:T(1,128)} reshape(s32[1,1,8,4,2]{4,3,2,1,0:T(4,128)S(1)} %copy.18) | data formatting | bytes 512 | tf_op jit(solution)/shard_map/reshape | solution.py:374
  13.4 2.0 %shard_map.158 = (bf16[128,1024]{1,0:T(8,128)(2,1)}, bf16[96,512]{1,0:T(8,128)(2,1)}, bf16[128,64]{1,0:T(8,128)(2,1)}) custom-call(s32[1,1]{1,0:T(1,128)S(6)} %copy.19.refs_0_, s32[16,128]{1,0:T(8,128)} %bitcast.19, s32[1,128]{1,0:T(1,128)} %bitcast.24, f32[8,128]{1,0:T(8,128)} %refs_3_.2, f32[8,128]{1,0:T(8,128)} %refs_4_.1, s32[1,64]{1,0:T(1,128)} %reshape.25.refs_5_, ...), custom_call_target="tpu_custom_call" | custom-call | tf_op jit(solution)/shard_map/pallas_call | solution.py:46
  15.4 0.4 collective-permute-done.refs_5_
  15.8 0.0 collective-permute-start.1
  15.8 0.5 collective-permute-start.2
  16.3 0.0 copy-done
  16.3 1.7 %collective-permute-start.3 = (bf16[512,512]{1,0:T(8,128)(2,1)S(1)}, bf16[512,512]{1,0:T(8,128)(2,1)S(1)}, u32[]{:S(2)}, u32[]{:S(2)}) collective-permute-start(bf16[512,512]{1,0:T(8,128)(2,1)S(1)} %copy-done), channel_id=1, source_target_pairs={{0,2},{1,3},{2,0},{3,1},{4,6},{5,7},{6,4},{7,5},{8,10},{9,11},{10,... | collective-permute-start | bytes 1572872 | tf_op jit(solution)/shard_map/ppermute | solution.py:310
  18.1 8.2 %all-to-all-done = bf16[8,32,1024]{2,1,0:T(8,128)(2,1)S(1)} async-done(((bf16[8,32,1024]{2,1,0:T(8,128)(2,1)}), bf16[8,32,1024]{2,1,0:T(8,128)(2,1)S(1)}, u32[]{:S(2)}, u32[]{:S(2)}) %all-to-all-start) | async-done | bytes 524320 | tf_op jit(solution)/shard_map/all_to_all | solution.py:357
  26.3 0.0 collective-permute-done.1.refs_4_
  26.3 0.0 collective-permute-done.2.refs_6_
  26.3 0.0 copy-start.5
  26.3 0.9 %copy-done.5 = bf16[128,1024]{1,0:T(8,128)(2,1)S(1)} copy-done((bf16[128,1024]{1,0:T(8,128)(2,1)S(1)}, bf16[128,1024]{1,0:T(8,128)(2,1)}, u32[]{:S(2)}) %copy-start.5) | copy-done | bytes 262168
  27.2 4.8 %shard_map.159 = (bf16[128,1024]{1,0:T(8,128)(2,1)}, bf16[512,128]{1,0:T(8,128)(2,1)}) custom-call(bf16[128,1024]{1,0:T(8,128)(2,1)S(1)} %copy-done.1, bf16[256,1024]{1,0:T(8,128)(2,1)S(1)} %bitcast.14, bf16[128,1024]{1,0:T(8,128)(2,1)S(1)} %copy-done.5, bf16[256,1024]{1,0:T(8,128)(2,1)S(1)} %copy-done.4, ...), custom_call_target="tpu_custom_call" | custom-call | flops 1006632960 | bytes 3670016 | tf_op jit(solution)/shard_map/pallas_call | solution.py:46
  32.0 2.7 %all-to-all-start.1 = ((bf16[32,16,128]{2,1,0:T(8,128)(2,1)}), bf16[32,16,128]{2,1,0:T(8,128)(2,1)S(1)}, u32[]{:S(2)}, u32[]{:S(2)}) async-start(bf16[32,16,128]{2,1,0:T(8,128)(2,1)} %bitcast.9), calls=%async_computation.1 | async-start | bytes 262144 | tf_op jit(solution)/shard_map/all_to_all | solution.py:402
  34.8 0.0 collective-permute-done.3.refs_3_.refs_5_
  34.8 0.3 collective-permute-start.4
  35.1 0.3 collective-permute-start.5
  35.3 7.6 %all-to-all-done.1 = bf16[32,16,128]{2,1,0:T(8,128)(2,1)S(1)} async-done(((bf16[32,16,128]{2,1,0:T(8,128)(2,1)}), bf16[32,16,128]{2,1,0:T(8,128)(2,1)S(1)}, u32[]{:S(2)}, u32[]{:S(2)}) %all-to-all-start.1) | async-done | bytes 131104 | tf_op jit(solution)/shard_map/all_to_all | solution.py:402
  43.0 0.4 shard_map.160
  43.3 0.0 collective-permute-done.4.refs_4_
  43.4 0.0 collective-permute-done.5.refs_6_
  43.4 2.5 %shard_map.161 = (f32[1,256]{1,0:T(1,128)}, bf16[512,128]{1,0:T(8,128)(2,1)S(1)}) custom-call(bf16[64,1024]{1,0:T(8,128)(2,1)S(1)} %get-tuple-element.22.refs_0_, f32[2,64,512]{2,1,0:T(8,128)S(1)} %get-tuple-element.23.refs_1_, bf16[96,512]{1,0:T(8,128)(2,1)S(1)} %copy-done.2, bf16[512,512]{1,0:T(8,128)(2,1)S(1)} %copy-done, ...), custom_call_target="tpu_custom_call" | custom-call | tf_op jit(solution)/shard_map/pallas_call | solution.py:46
  45.9 10.0 %all_to_all.33 = bf16[32,16,128]{2,1,0:T(8,128)(2,1)S(1)} all-to-all(bf16[32,16,128]{2,1,0:T(8,128)(2,1)S(1)} %bitcast.17), channel_id=1, replica_groups=mesh['dom'=8,'edge'=4] {'dom','edge'}, dimensions={0} | all-to-all | bytes 262144 | tf_op jit(solution)/shard_map/all_to_all | solution.py:431
  55.9 0.0 copy-done.3
  55.9 1.0 %shard_map.162 = f32[128,1024]{1,0:T(8,128)} custom-call(bf16[128,64]{1,0:T(8,128)(2,1)S(1)} %copy-done.3, bf16[512,128]{1,0:T(8,128)(2,1)S(1)} %bitcast.15), custom_call_target="tpu_custom_call" | custom-call | tf_op jit(solution)/shard_map/pallas_call | solution.py:46
  (7 shorter events, 0.0 us)
Async XLA Ops:
  0.6 15.2 %collective-permute-start = (bf16[256,1024]{1,0:T(8,128)(2,1)}, bf16[256,1024]{1,0:T(8,128)(2,1)S(1)}, u32[]{:S(2)}, u32[]{:S(2)}) collective-permute-start(bf16[256,1024]{1,0:T(8,128)(2,1)} %refs_3_.3), channel_id=1, source_target_pairs={{0,2},{1,3},{2,0},{3,1},{4,6},{5,7},{6,4},{7,5},{8,10},{9,11},{10,... | collective-permute-start | bytes 1572872 | tf_op jit(solution)/shard_map/ppermute | solution.py:310
  3.7 12.1 %copy-start.4 = (bf16[256,1024]{1,0:T(8,128)(2,1)S(1)}, bf16[256,1024]{1,0:T(8,128)(2,1)}, u32[]{:S(2)}) copy-start(bf16[256,1024]{1,0:T(8,128)(2,1)} %refs_3_.3) | copy-start | bytes 1572868
  6.0 6.6 %copy-start.6 = (s32[1,1,8,4,2]{2,4,3,1,0:T(2,128)S(1)}, s32[1,1,8,4,2]{2,4,3,1,0:T(2,128)}, u32[]{:S(2)}) copy-start(s32[1,1,8,4,2]{2,4,3,1,0:T(2,128)} %param.22) | copy-start | bytes 772
  6.0 10.3 %copy-start = (bf16[512,512]{1,0:T(8,128)(2,1)S(1)}, bf16[512,512]{1,0:T(8,128)(2,1)}, u32[]{:S(2)}) copy-start(bf16[512,512]{1,0:T(8,128)(2,1)} %refs_3_.4) | copy-start | bytes 1572868
  6.0 20.2 %copy-start.1 = (bf16[128,1024]{1,0:T(8,128)(2,1)S(1)}, bf16[128,1024]{1,0:T(8,128)(2,1)}, u32[]{:S(2)}) copy-start(bf16[128,1024]{1,0:T(8,128)(2,1)} %refs_0_.2) | copy-start | bytes 786436
  6.1 20.2 %all-to-all-start = ((bf16[8,32,1024]{2,1,0:T(8,128)(2,1)}), bf16[8,32,1024]{2,1,0:T(8,128)(2,1)S(1)}, u32[]{:S(2)}, u32[]{:S(2)}) async-start(bf16[8,32,1024]{2,1,0:T(8,128)(2,1)} %bitcast.18), calls=%async_computation | async-start | bytes 1048576 | tf_op jit(solution)/shard_map/all_to_all | solution.py:357
  15.8 10.5 %collective-permute-start.1 = (bf16[256,1024]{1,0:T(8,128)(2,1)S(1)}, bf16[256,1024]{1,0:T(8,128)(2,1)S(1)}, u32[]{:S(2)}, u32[]{:S(2)}) collective-permute-start(bf16[256,1024]{1,0:T(8,128)(2,1)S(1)} %copy-done.4), channel_id=1, source_target_pairs={{0,1},{1,0},{2,3},{3,2},{4,5},{5,4},{6,7},{7,6},{8,9},{9,8},{10,11... | collective-permute-start | bytes 1572872 | tf_op jit(solution)/shard_map/ppermute | solution.py:310
  15.8 10.5 %collective-permute-start.2 = (bf16[256,1024]{1,0:T(8,128)(2,1)S(1)}, bf16[256,1024]{1,0:T(8,128)(2,1)}, u32[]{:S(2)}, u32[]{:S(2)}) collective-permute-start(bf16[256,1024]{1,0:T(8,128)(2,1)S(1)} %collective-permute-done.refs_5_), channel_id=1, source_target_pairs={{0,1},{1,0},{2,3},{3,2},{4,5},{5,4},{6,7},{7,6},{8,9},{9,8},{10,11... | collective-permute-start | bytes 1572872 | tf_op jit(solution)/shard_map/ppermute | solution.py:310
  16.3 18.4 %collective-permute-start.3 = (bf16[512,512]{1,0:T(8,128)(2,1)S(1)}, bf16[512,512]{1,0:T(8,128)(2,1)S(1)}, u32[]{:S(2)}, u32[]{:S(2)}) collective-permute-start(bf16[512,512]{1,0:T(8,128)(2,1)S(1)} %copy-done), channel_id=1, source_target_pairs={{0,2},{1,3},{2,0},{3,1},{4,6},{5,7},{6,4},{7,5},{8,10},{9,11},{10,... | collective-permute-start | bytes 1572872 | tf_op jit(solution)/shard_map/ppermute | solution.py:310
  26.3 1.0 %copy-start.5 = (bf16[128,1024]{1,0:T(8,128)(2,1)S(1)}, bf16[128,1024]{1,0:T(8,128)(2,1)}, u32[]{:S(2)}) copy-start(bf16[128,1024]{1,0:T(8,128)(2,1)} %get-tuple-element.16.refs_2_) | copy-start | bytes 786436
  32.0 11.0 %copy-start.2 = (bf16[96,512]{1,0:T(8,128)(2,1)S(1)}, bf16[96,512]{1,0:T(8,128)(2,1)}, u32[]{:S(2)}) copy-start(bf16[96,512]{1,0:T(8,128)(2,1)} %get-tuple-element.21.refs_1_.refs_2_) | copy-start | bytes 294916
  32.0 11.0 %all-to-all-start.1 = ((bf16[32,16,128]{2,1,0:T(8,128)(2,1)}), bf16[32,16,128]{2,1,0:T(8,128)(2,1)S(1)}, u32[]{:S(2)}, u32[]{:S(2)}) async-start(bf16[32,16,128]{2,1,0:T(8,128)(2,1)} %bitcast.9), calls=%async_computation.1 | async-start | bytes 262144 | tf_op jit(solution)/shard_map/all_to_all | solution.py:402
  34.8 8.6 %collective-permute-start.4 = (bf16[512,512]{1,0:T(8,128)(2,1)S(1)}, bf16[512,512]{1,0:T(8,128)(2,1)S(1)}, u32[]{:S(2)}, u32[]{:S(2)}) collective-permute-start(bf16[512,512]{1,0:T(8,128)(2,1)S(1)} %copy-done), channel_id=1, source_target_pairs={{0,1},{1,0},{2,3},{3,2},{4,5},{5,4},{6,7},{7,6},{8,9},{9,8},{10,11... | collective-permute-start | bytes 1572872 | tf_op jit(solution)/shard_map/ppermute | solution.py:310
  35.1 8.3 %collective-permute-start.5 = (bf16[512,512]{1,0:T(8,128)(2,1)S(1)}, bf16[512,512]{1,0:T(8,128)(2,1)S(1)}, u32[]{:S(2)}, u32[]{:S(2)}) collective-permute-start(bf16[512,512]{1,0:T(8,128)(2,1)S(1)} %collective-permute-done.3.refs_3_.refs_5_), channel_id=1, source_target_pairs={{0,1},{1,0},{2,3},{3,2},{4,5},{5,4},{6,7},{7,6},{8,9},{9,8},{10,11... | collective-permute-start | bytes 1572872 | tf_op jit(solution)/shard_map/ppermute | solution.py:310
  45.9 10.0 %copy-start.3 = (bf16[128,64]{1,0:T(8,128)(2,1)S(1)}, bf16[128,64]{1,0:T(8,128)(2,1)}, u32[]{:S(2)}) copy-start(bf16[128,64]{1,0:T(8,128)(2,1)} %get-tuple-element.27.refs_0_) | copy-start | bytes 49156
